TPU v7x, 32 devices: a whole 2x2x4 slice. The times are simulated.
32 devices in a mesh: dp: 4 (over y, x), graph: 8 (over z, core).
Axes of the slice: x: 2, y: 2, z: 4, core: 2. Of those that a mesh axis runs over, the one named last changes fastest.
Arguments:
- edge_emb: bfloat16 [4, 4096, 512], P('dp', 'graph'), may hold values from -6 to 6
- atom_emb: bfloat16 [4, 256, 512], P('dp', 'graph'), may hold values from -6 to 6
- edge_target: int32 [4, 4096], P('dp', 'graph'), may hold values from 0 to 255, as said below
- trip_in: int32 [4, 131072], P('dp', 'graph'), may hold values from 0 to 4095, as said below
- trip_out: int32 [4, 131072], P('dp', 'graph'), may hold values from 0 to 511
- trip_count: int32 [4, 8], P('dp', 'graph'), may hold values from 8192 to 16384, as said below
- trip_basis: bfloat16 [4, 16, 131072], P('dp', None, 'graph'), may hold values from -3 to 3
- grad_edge: bfloat16 [4, 4096, 512], P('dp', 'graph'), may hold values from -6 to 6
- grad_atom: bfloat16 [4, 256, 512], P('dp', 'graph'), may hold values from -6 to 6
- w_down: bfloat16 [512, 64], replicated, may hold values from -0.25 to 0.25
- w_bil: bfloat16 [1024, 64], replicated, may hold values from -0.1875 to 0.1875
- w_up: bfloat16 [64, 512], replicated, may hold values from -0.75 to 0.75
- w_atom: bfloat16 [512, 512], replicated, may hold values from -0.25 to 0.25
Outputs:
- edge_new: bfloat16 [4, 4096, 512], P('dp', 'graph')
- atom_new: bfloat16 [4, 256, 512], P('dp', 'graph')
- grad_edge_in: float32 [4, 4096, 512], P('dp', 'graph')
- grad_wdown: float32 [512, 64], replicated
- grad_wbil: float32 [1024, 64], replicated
- grad_wup: float32 [64, 512], replicated
- grad_watom: float32 [512, 512], replicated
Inputs may be any that keep to these rules, and one draw needn't show every extreme that they name: `trip_in`: among the 16384 slots of one device, the incoming edges held by any one device of the batch number at most 128 distinct ones; on every device some one device gives exactly 128. `trip_count`: every batch has a device with all 16384 slots used. `edge_target`: among the 512 edges of one device, those whose target atom is held by any one device (target // 32) number at most 128; on every device some one holder gets exactly 128.
All inputs are finite; a program needn't handle non-finite values.
Results may differ from a plain program's by a relative error of at most 0.0077.
Values may be sent and summed in bfloat16 or wider, within the bound.
No kernel may reach another device: no remote copies, remote signals or barrier semaphores. Data moves between devices by JAX's collectives and lax.ppermute only.
A program may use at most 64 MiB of HBM per device.

v0:
```python
import math

import jax
import jax.numpy as jnp
from jax import lax
from jax.sharding import PartitionSpec as P

ATOM_SCALE = 0.25
BLOCK_LIMIT = 2048


def silu_slope(value):
    logistic = jax.nn.sigmoid(value)
    return logistic * (1.0 + value * (1.0 - logistic))


def spread_cols(basis_part, feat_part):
    outer = basis_part.astype(jnp.float32)[:, None, :] * feat_part.astype(jnp.float32)[None, :, :]
    return outer.reshape(-1, basis_part.shape[1]).astype(jnp.bfloat16)


def body(
    edge_emb,
    atom_emb,
    edge_target,
    trip_in,
    trip_out,
    trip_count,
    trip_basis,
    grad_edge,
    grad_atom,
    w_down,
    w_bil,
    w_up,
    w_atom,
):
    members = lax.axis_size("graph")
    edge_rows = edge_emb[0]
    edge_dev = edge_rows.shape[0]
    atom_dev = atom_emb.shape[1]
    trip_dev = trip_in.shape[1]
    width_trip = w_down.shape[1]
    basis_width = trip_basis.shape[1]
    block_rows = math.gcd(trip_dev, BLOCK_LIMIT)
    block_count = trip_dev // block_rows
    incoming = trip_in[0]
    outgoing = trip_out[0]
    basis_cols = trip_basis[0]
    targets = edge_target[0]
    edge_iota = jnp.arange(edge_dev, dtype=jnp.int32)
    usable = (jnp.arange(trip_dev, dtype=jnp.int32) < trip_count[0, 0]).astype(jnp.float32)
    contract_first = (((0,), (0,)), ((), ()))
    contract_last = (((1,), (1,)), ((), ()))
    projected = jnp.dot(edge_rows, w_down, preferred_element_type=jnp.float32)
    edge_feat = jax.nn.silu(projected).astype(jnp.bfloat16)
    edge_table_all = lax.all_gather(edge_feat, "graph", axis=0, tiled=True)
    feat_in = jnp.take(edge_table_all, incoming, axis=0).T

    def forward_step(step_index, running):
        offset_at = step_index * block_rows
        feat_part = lax.dynamic_slice_in_dim(feat_in, offset_at, block_rows, 1)
        basis_part = lax.dynamic_slice_in_dim(basis_cols, offset_at, block_rows, 1)
        usable_part = lax.dynamic_slice_in_dim(usable, offset_at, block_rows, 0)
        target_part = lax.dynamic_slice_in_dim(outgoing, offset_at, block_rows, 0)
        spread = spread_cols(basis_part, feat_part)
        mixed = (
            lax.dot_general(w_bil, spread, contract_first, preferred_element_type=jnp.float32)
            * usable_part[None, :]
        )
        one_hot = (target_part[:, None] == edge_iota[None, :]).astype(jnp.float32)
        return running + jnp.dot(
            mixed, one_hot, precision=lax.Precision.HIGHEST, preferred_element_type=jnp.float32
        )

    gathered = lax.fori_loop(
        0, block_count, forward_step, jnp.zeros((width_trip, edge_dev), jnp.float32)
    ).astype(jnp.bfloat16)
    update = lax.dot_general(gathered, w_up, contract_first, preferred_element_type=jnp.float32)
    edge_new = (edge_rows.astype(jnp.float32) + jax.nn.silu(update)).astype(jnp.bfloat16)
    atoms_all = atom_dev * members
    atom_hot_all = (jnp.arange(atoms_all, dtype=jnp.int32)[:, None] == targets[None, :]).astype(
        jnp.bfloat16
    )
    partial_value = jnp.dot(atom_hot_all, edge_new, preferred_element_type=jnp.float32)
    atom_sum = lax.psum_scatter(partial_value, "graph", scatter_dimension=0, tiled=True).astype(
        jnp.bfloat16
    )
    atom_pre = ATOM_SCALE * jnp.dot(atom_sum, w_atom, preferred_element_type=jnp.float32)
    atom_new = (atom_emb[0].astype(jnp.float32) + jax.nn.silu(atom_pre)).astype(jnp.bfloat16)
    grad_pre = (grad_atom[0].astype(jnp.float32) * silu_slope(atom_pre)).astype(jnp.bfloat16)
    watom_term = ATOM_SCALE * lax.dot_general(
        atom_sum, grad_pre, contract_first, preferred_element_type=jnp.float32
    )
    grad_sum = (
        ATOM_SCALE
        * lax.dot_general(grad_pre, w_atom, contract_last, preferred_element_type=jnp.float32)
    ).astype(jnp.bfloat16)
    grad_all = lax.all_gather(grad_sum, "graph", axis=0, tiled=True)
    target_grad = jnp.take(grad_all, targets, axis=0)
    grad_new = grad_edge[0].astype(jnp.float32) + target_grad.astype(jnp.float32)
    grad_update = (grad_new * silu_slope(update)).astype(jnp.bfloat16)
    wup_term = jnp.dot(gathered, grad_update, preferred_element_type=jnp.float32)
    grad_gathered = lax.dot_general(
        w_up, grad_update, contract_last, preferred_element_type=jnp.float32
    ).astype(jnp.bfloat16)

    def backward_step(step_index, carried):
        running, grad_feat = carried
        offset_at = step_index * block_rows
        feat_part = lax.dynamic_slice_in_dim(feat_in, offset_at, block_rows, 1)
        basis_part = lax.dynamic_slice_in_dim(basis_cols, offset_at, block_rows, 1)
        usable_part = lax.dynamic_slice_in_dim(usable, offset_at, block_rows, 0)
        target_part = lax.dynamic_slice_in_dim(outgoing, offset_at, block_rows, 0)
        pick_hot = (edge_iota[:, None] == target_part[None, :]).astype(jnp.bfloat16)
        grad_part = jnp.dot(grad_gathered, pick_hot, preferred_element_type=jnp.float32).astype(
            jnp.bfloat16
        )
        grad_part = grad_part * usable_part.astype(jnp.bfloat16)[None, :]
        spread = spread_cols(basis_part, feat_part)
        running = running + lax.dot_general(
            spread, grad_part, contract_last, preferred_element_type=jnp.float32
        )
        backed = jnp.dot(w_bil, grad_part, preferred_element_type=jnp.float32).reshape(
            basis_width, width_trip, block_rows
        )
        feat_grad = jnp.sum(basis_part.astype(jnp.float32)[:, None, :] * backed, axis=0)
        return (running, lax.dynamic_update_slice_in_dim(grad_feat, feat_grad, offset_at, 1))

    wbil_term, grad_feat = lax.fori_loop(
        0,
        block_count,
        backward_step,
        (jnp.zeros(w_bil.shape, jnp.float32), jnp.zeros((width_trip, trip_dev), jnp.float32)),
    )
    grad_feat_rows = grad_feat.T
    spread_back = jax.ops.segment_sum(grad_feat_rows, incoming, num_segments=members * edge_dev)
    grad_edge_feat = lax.psum_scatter(spread_back, "graph", scatter_dimension=0, tiled=True)
    grad_project = (grad_edge_feat * silu_slope(projected)).astype(jnp.bfloat16)
    grad_edge_in = grad_new + lax.dot_general(
        grad_project, w_down, contract_last, preferred_element_type=jnp.float32
    )
    wdown_term = lax.dot_general(
        edge_rows, grad_project, contract_first, preferred_element_type=jnp.float32
    )
    totals = lax.psum((wdown_term, wbil_term, wup_term, watom_term), ("dp", "graph"))
    factor = 1.0 / math.sqrt(lax.axis_size("dp") * members * edge_dev)
    return (
        edge_new[None],
        atom_new[None],
        grad_edge_in[None],
        totals[0] * factor,
        totals[1] * factor,
        totals[2] * factor,
        totals[3] * factor,
    )


def solution(mesh):
    return jax.shard_map(
        body,
        mesh=mesh,
        in_specs=(
            P("dp", "graph", None),
            P("dp", "graph", None),
            P("dp", "graph"),
            P("dp", "graph"),
            P("dp", "graph"),
            P("dp", "graph"),
            P("dp", None, "graph"),
            P("dp", "graph", None),
            P("dp", "graph", None),
            P(),
            P(),
            P(),
            P(),
        ),
        out_specs=(
            P("dp", "graph", None),
            P("dp", "graph", None),
            P("dp", "graph", None),
            P(),
            P(),
            P(),
            P(),
        ),
        check_vma=False,
    )
```

profile of v0, /device:TPU:0, one launch (start us, length us, event | category | flops | bytes accessed | tf_op | source)
XLA Modules:
  0.0 594.9 jit_solution(7198902080952378741)
XLA Ops:
  7.2 1.4 multiply_convert_fusion.4
  8.6 16.6 %all_gather.6 = bf16[4096,64]{0,1:T(8,128)(2,1)S(1)} all-gather(bf16[512,64]{0,1:T(8,128)(2,1)S(1)} %get-tuple-element.449), channel_id=1, replica_groups=mesh['dp'=4,'graph'=8] {'graph'}, dimensions={0}, use_global_device_ids=true | all-gather | bytes 589824 | tf_op jit(solution)/shard_map/all_gather | solution.py:56
  27.5 57.4 %gather_fusion = bf16[16384,64]{1,0:T(8,128)(2,1)} fusion(bf16[4096,64]{1,0:T(8,128)(2,1)S(1)} %copy.25, s32[16384]{0:T(1024)S(1)} %broadcast_clamp_fusion), kind=kCustom, calls=%fused_computation | custom fusion | bytes 4259840 | tf_op jit(solution)/shard_map/jit(_take)/gather | solution.py:57
  84.9 11.5 %select_bitcast_fusion = bf16[64,16384]{0,1:T(8,128)(2,1)} fusion(bf16[16384,64]{1,0:T(8,128)(2,1)} %gather_fusion, pred[16384]{0:T(1024)(128)(4,1)S(1)} %compare_and_fusion), kind=kLoop, calls=%fused_computation.25 | loop fusion | flops 1048576 | bytes 4210688 | tf_op jit(solution)/shard_map/jit(_take)/select_n | solution.py:57
  96.4 4.8 copy.26
  101.9 53.6 %while.30 = (s32[]{:T(128)}, f32[64,512]{1,0:T(8,128)S(1)}, bf16[16,16384]{1,0:T(8,128)(2,1)}, bf16[64,16384]{1,0:T(8,128)(2,1)}, bf16[1024,64]{0,1:T(8,128)(2,1...) while((s32[]{:T(128)}, f32[64,512]{1,0:T(8,128)S(1)}, ...), condition=%wide.region_1.2_spmd.clone, body=%wide.region_0.1_spmd.clone.sunk | while | flops 1079345152 | bytes 11518133 | solution.py:75
  104.8 1.5 convolution_multiply_fusion.5
  107.0 1.6 fusion.69
  111.5 1.5 convolution_multiply_fusion.5
  113.7 1.6 fusion.69
  118.2 1.5 convolution_multiply_fusion.5
  120.4 1.6 fusion.69
  124.9 1.5 convolution_multiply_fusion.5
  127.1 1.6 fusion.69
  131.6 1.5 convolution_multiply_fusion.5
  133.8 1.6 fusion.69
  138.3 1.5 convolution_multiply_fusion.5
  140.5 1.6 fusion.69
  145.0 1.5 convolution_multiply_fusion.5
  147.2 1.6 fusion.69
  151.7 1.5 convolution_multiply_fusion.5
  153.9 1.6 fusion.69
  156.2 1.4 add_convert_fusion
  159.6 32.1 %reduce-scatter.3.cloned.1.call-done = f32[32,512]{1,0:T(8,128)} async-done(((f32[256,512]{1,0:T(8,128)}), f32[32,512]{1,0:T(8,128)}) %reduce-scatter.3.cloned.1.call-update) | async-done | bytes 65552 | tf_op jit(solution)/shard_map/reduce_scatter | solution.py:85
  193.0 14.4 %all_gather.7 = bf16[256,512]{1,0:T(8,128)(2,1)S(1)} all-gather(bf16[32,512]{1,0:T(8,128)(2,1)S(1)} %fusion.13), channel_id=1, replica_groups=mesh['dp'=4,'graph'=8] {'graph'}, dimensions={0}, use_global_device_ids=true | all-gather | bytes 294912 | tf_op jit(solution)/shard_map/all_gather | solution.py:98
  207.4 2.0 gather_fusion.1
  211.8 2.3 broadcast_in_dim.82
  214.1 100.8 %while.31 = (s32[]{:T(128)}, f32[1024,64]{0,1:T(8,128)S(1)}, f32[64,16384]{1,0:T(8,128)}, bf16[16,16384]{1,0:T(8,128)(2,1)}, bf16[64,16384]{1,0:T(8,128)(2,1)}, ...) while((s32[]{:T(128)}, f32[1024,64]{0,1:T(8,128)S(1)}, ...), condition=%wide.region_5.6_spmd.clone, body=%wide.region_3.5_spmd.clone.sunk | while | flops 680951808 | bytes 29921480 | solution.py:129
  215.7 1.3 fusion.76
  218.9 3.4 multiply_reduce_fusion.2
  223.1 3.6 convolution_add_fusion.3
  228.3 1.3 fusion.76
  231.5 3.4 multiply_reduce_fusion.2
  235.7 3.6 convolution_add_fusion.3
  240.9 1.3 fusion.76
  244.1 3.4 multiply_reduce_fusion.2
  248.4 3.6 convolution_add_fusion.3
  253.5 1.3 fusion.76
  256.7 3.4 multiply_reduce_fusion.2
  261.0 3.6 convolution_add_fusion.3
  266.1 1.3 fusion.76
  269.3 3.4 multiply_reduce_fusion.2
  273.5 3.6 convolution_add_fusion.3
  278.7 1.3 fusion.76
  281.9 3.4 multiply_reduce_fusion.2
  286.2 3.6 convolution_add_fusion.3
  291.3 1.3 fusion.76
  294.5 3.4 multiply_reduce_fusion.2
  298.8 3.6 convolution_add_fusion.3
  304.0 1.3 fusion.76
  307.1 3.4 multiply_reduce_fusion.2
  311.4 3.6 convolution_add_fusion.3
  315.0 7.0 %copy.28 = f32[16384,64]{1,0:T(8,128)} copy(f32[16384,64]{0,1:T(8,128)} %bitcast.95) | data formatting | bytes 8388608 | tf_op jit(solution)/shard_map/transpose | solution.py:135
  322.0 88.1 %scatter_custom_fusion = f32[4096,64]{1,0:T(8,128)S(1)} fusion(s32[16384]{0:T(1024)} %bitcast.99, f32[16384,64]{1,0:T(8,128)} %copy.28, f32[]{:T(128)} %constant.107.clone.1), kind=kCustom, calls=%fused_computation.37 | custom fusion | flops 1048576 | bytes 1049088 | tf_op jit(solution)/shard_map/scatter-add | solution.py:136
  410.2 1.6 copy.29
  411.8 2.0 fusion.24
  413.8 1.3 convolution_multiply_fusion.1
  415.1 27.5 %reduce-scatter.5.cloned.1.call-done = f32[512,64]{0,1:T(8,128)} async-done(((f32[4096,64]{0,1:T(8,128)}), f32[512,64]{0,1:T(8,128)}) %reduce-scatter.5.cloned.1.call-update) | async-done | bytes 131088 | tf_op jit(solution)/shard_map/reduce_scatter | solution.py:137
  443.5 1.9 convolution_bitcast_fusion
  447.4 133.8 %all-reduce.3.cloned.1.call-done = (f32[512,64]{0,1:T(8,128)}, f32[1024,64]{0,1:T(8,128)}, f32[64,512]{1,0:T(8,128)}, f32[512,512]{1,0:T(8,128)}) async-done(((f32[512,64]{0,1:T(8,128)}, f32[1024,64]{0,1:T(8,128)}, f32[64,512]{1,0:T(8,128)}, f32[512,512]{1,0:T(8,128)}), (f32[512,64]{0,1:T(8,128)}, f32[1024,64]{0,1:T(8,128)}, f32[64,512]{1,0:T(8,128)}, f32[512,512]{1,0:T(8,128)})) %all-reduce.3.cloned.1.call-update) | async-done | bytes 1572880 | tf_op jit(solution)/shard_map/psum | solution.py:145
  581.3 2.3 broadcast_multiply_fusion
  583.5 1.7 broadcast_multiply_fusion.1
  585.2 1.6 broadcast_multiply_fusion.2
  586.8 1.6 broadcast_multiply_fusion.3
  (146 shorter events, 73.9 us)
Async XLA Ops:
  7.2 184.5 %copy-start = (bf16[512,512]{1,0:T(8,128)(2,1)S(1)}, bf16[512,512]{1,0:T(8,128)(2,1)}, u32[]{:S(2)}) copy-start(bf16[512,512]{1,0:T(8,128)(2,1)} %param.29) | copy-start | bytes 1572868
  7.2 184.5 %reduce-scatter.3.cloned.1.call-start = ((), (), s32[]{:S(2)}) async-start(), calls=%async_computation.2 | async-start | bytes 589824 | tf_op jit(solution)/shard_map/reduce_scatter | solution.py:85
  96.4 5.5 copy-start.2
  101.9 54.3 %copy-start.8 = (bf16[1,512,512]{2,1,0:T(8,128)(2,1)S(1)}, bf16[1,512,512]{2,1,0:T(8,128)(2,1)}, u32[]{:S(2)}) copy-start(bf16[1,512,512]{2,1,0:T(8,128)(2,1)} %param.17) | copy-start | bytes 1572868
  101.9 54.3 %copy-start.12 = (bf16[64,512]{1,0:T(8,128)(2,1)S(1)}, bf16[64,512]{1,0:T(8,128)(2,1)}, u32[]{:S(2)}) copy-start(bf16[64,512]{1,0:T(8,128)(2,1)} %param.28) | copy-start | bytes 196612
  155.5 0.7 copy-start.11
  156.2 2.2 copy-start.16
  156.2 36.5 %copy-start.14 = (bf16[1,32,512]{2,1,0:T(8,128)(2,1)S(1)}, bf16[1,32,512]{2,1,0:T(8,128)(2,1)}, u32[]{:S(2)}) copy-start(bf16[1,32,512]{2,1,0:T(8,128)(2,1)} %param.25) | copy-start | bytes 98308
  157.6 0.8 copy-start.9
  157.6 51.8 %copy-start.6 = (bf16[1,512,512]{2,1,0:T(8,128)(2,1)S(1)}, bf16[1,512,512]{2,1,0:T(8,128)(2,1)}, u32[]{:S(2)}) copy-start(bf16[1,512,512]{2,1,0:T(8,128)(2,1)} %param.24) | copy-start | bytes 1572868
  159.5 283.1 %reduce-scatter.5.cloned.1.call-start = ((), (), s32[]{:S(2)}) async-start(), calls=%async_computation.3 | async-start | bytes 1179648 | tf_op jit(solution)/shard_map/reduce_scatter | solution.py:137
  209.3 4.8 copy-start.3
  209.9 0.8 copy-start.5
  315.0 7.0 %copy-start.1 = (f32[1024,64]{0,1:T(8,128)}, f32[1024,64]{0,1:T(8,128)S(1)}, u32[]{:S(2)}) copy-start(f32[1024,64]{0,1:T(8,128)S(1)} %get-tuple-element.318) | copy-start | bytes 786436
  322.0 91.8 %copy-start.10 = (f32[32,512]{1,0:T(8,128)S(1)}, f32[32,512]{1,0:T(8,128)}, u32[]{:S(2)}) copy-start(f32[32,512]{1,0:T(8,128)} %reduce-scatter.3.cloned.1.call-done) | copy-start | bytes 196612
  410.1 35.4 %copy-start.15 = (bf16[1,32,512]{2,1,0:T(8,128)(2,1)S(1)}, bf16[1,32,512]{2,1,0:T(8,128)(2,1)}, u32[]{:S(2)}) copy-start(bf16[1,32,512]{2,1,0:T(8,128)(2,1)} %param.18) | copy-start | bytes 98308
  410.1 36.0 %copy-start.4 = (bf16[512,512]{1,0:T(8,128)(2,1)S(1)}, bf16[512,512]{1,0:T(8,128)(2,1)}, u32[]{:S(2)}) copy-start(bf16[512,512]{1,0:T(8,128)(2,1)} %copy-done.3) | copy-start | bytes 1572868
  410.1 36.0 %copy-start.13 = (bf16[512,64]{0,1:T(8,128)(2,1)S(1)}, bf16[512,64]{0,1:T(8,128)(2,1)}, u32[]{:S(2)}) copy-start(bf16[512,64]{0,1:T(8,128)(2,1)} %param.26) | copy-start | bytes 196612
  411.7 34.4 %copy-start.7 = (bf16[1,512,512]{2,1,0:T(8,128)(2,1)S(1)}, bf16[1,512,512]{2,1,0:T(8,128)(2,1)}, u32[]{:S(2)}) copy-start(bf16[1,512,512]{2,1,0:T(8,128)(2,1)} %param.24) | copy-start | bytes 1572868
  411.7 169.5 %all-reduce.3.cloned.1.call-start = ((), (), s32[]{:S(2)}) async-start(), calls=%async_computation.4 | async-start | bytes 3145728 | tf_op jit(solution)/shard_map/psum | solution.py:145
Sparse Core Ops, SparseCore 0:
  159.6 32.0 reduce-scatter.2
  411.9 30.6 reduce-scatter.4
  449.9 131.3 all-reduce.2
where the time goes:
time: 598 us; the launch traced here: 595 us
  waiting for transfers between devices  193 us (32%)
  other arithmetic  175 us (29%)
  local copies, waits for them, and re-layouts  96 us (16%)
  matrix products  83.7 us (14%)
  blocking collectives  30.9 us (5%)
  between operations  14.7 us (2%)
    psum x1, waiting for transfers between devices, body(): lax.psum((wdown_term, wbil_term, wup_term, watom_term), ('dp', 'graph'))  134 us
    scatter-add x1, other arithmetic, body(): jax.ops.segment_sum(grad_feat_rows, incoming, num_segments=members * edge...  88.1 us
    gather x1, local copies, waits for them, and re-layouts, body(): feat_in = jnp.take(edge_table_all, incoming, axis=0).T  57.4 us
    reduce_scatter x1, waiting for transfers between devices, body(): lax.psum_scatter(partial_value, 'graph', scatter_dimension=0, tiled=True)  32.1 us
    dot_general x8, matrix products, backward_step(): lax.dot_general(spread, grad_part, contract_last, preferred_element_type=...  28.9 us
    reduce_scatter x1, waiting for transfers between devices, body(): lax.psum_scatter(spread_back, 'graph', scatter_dimension=0, tiled=True)  27.5 us
    reduce_sum x8, other arithmetic, backward_step(): jnp.sum(basis_part.astype(jnp.float32)[:, None, :] * backed, axis=0)  27.3 us
    all_gather x1, blocking collectives, body(): edge_table_all = lax.all_gather(edge_feat, 'graph', axis=0, tiled=True)  16.6 us
  transfers between devices with their start and end apart: 3, of which 3 were waited for; matrix products, arithmetic and copies ran while one was open for 1% of the time, Pallas kernels for 0%

commit v1 on v0

v1 whole, which is shorter than its diff:
```python
import functools
import math

import jax
import jax.numpy as jnp
from jax import lax
from jax.experimental import pallas as pl
from jax.experimental.pallas import tpu as pltpu
from jax.sharding import PartitionSpec as P

ATOM_SCALE = 0.25
BLOCK = 256
TILE_LIMIT = 1024
VMEM_BYTES = 48 * 1024 * 1024

FIRST_FIRST = (((0,), (0,)), ((), ()))
FIRST_LAST = (((0,), (1,)), ((), ()))
LAST_LAST = (((1,), (1,)), ((), ()))


def dot32(left, right, dims=(((1,), (0,)), ((), ()))):
    return lax.dot_general(left, right, dims, preferred_element_type=jnp.float32)


def silu(value):
    return value / (1.0 + jnp.exp(-value))


def silu_slope(value):
    logistic = 1.0 / (1.0 + jnp.exp(-value))
    return logistic * (1.0 + value * (1.0 - logistic))


def row_hot(rows, index):
    iota = lax.broadcasted_iota(jnp.int32, (rows, index.shape[1]), 0)
    return (iota == index).astype(jnp.float32).astype(jnp.bfloat16)


def feature_kernel(emb_ref, down_ref, projected_ref, table_ref):
    projected = dot32(down_ref[...], emb_ref[...], FIRST_LAST)
    projected_ref[...] = projected
    feat = silu(projected).astype(jnp.bfloat16)
    width = feat.shape[0]
    for part in range(feat.shape[1] // BLOCK):
        table_ref[part * width : (part + 1) * width, :] = feat[:, part * BLOCK : (part + 1) * BLOCK]


def forward_kernel(
    count_ref,
    in_ref,
    out_ref,
    basis_ref,
    table_ref,
    bil_ref,
    up_ref,
    emb_ref,
    target_ref,
    new_ref,
    atoms_ref,
    gathered_ref,
    moment_ref,
    total,
    spread,
):
    step = pl.program_id(0)
    tile = in_ref.shape[1]
    width = bil_ref.shape[1]
    edges = emb_ref.shape[0]
    groups = table_ref.shape[0] // width

    @pl.when(step == 0)
    def _():
        total[...] = jnp.zeros_like(total)

    incoming = in_ref[...]
    low = incoming & (BLOCK - 1)
    high = incoming // BLOCK
    hot = row_hot(BLOCK, low)
    feat = jnp.zeros((width, tile), jnp.float32)
    per = BLOCK // width
    for chunk in range(groups // per):
        picked = dot32(table_ref[chunk * BLOCK : (chunk + 1) * BLOCK, :], hot)
        for part in range(per):
            feat = jnp.where(
                high == chunk * per + part, picked[part * width : (part + 1) * width, :], feat
            )
    feat = feat.astype(jnp.bfloat16)
    for row in range(basis_ref.shape[0]):
        spread[row * width : (row + 1) * width, :] = feat * basis_ref[row : row + 1, :]
    place = step * tile + lax.broadcasted_iota(jnp.int32, (1, tile), 1)
    outgoing = jnp.where(place < count_ref[0, 0], out_ref[...], -1)
    total[...] += dot32(spread[...], row_hot(edges, outgoing), LAST_LAST)

    @pl.when(step == pl.num_programs(0) - 1)
    def _():
        summed = total[...]
        head = summed.astype(jnp.bfloat16)
        rest = (summed - head.astype(jnp.float32)).astype(jnp.bfloat16)
        moment_ref[...] = head
        gathered = (
            dot32(bil_ref[...], head, FIRST_FIRST) + dot32(bil_ref[...], rest, FIRST_FIRST)
        ).astype(jnp.bfloat16)
        gathered_ref[...] = gathered
        update = dot32(gathered, up_ref[...], FIRST_FIRST)
        fresh = (emb_ref[...].astype(jnp.float32) + silu(update)).astype(jnp.bfloat16)
        new_ref[...] = fresh
        atoms_ref[...] = dot32(row_hot(atoms_ref.shape[0], target_ref[...]), fresh).astype(
            jnp.bfloat16
        )


def atom_kernel(parts_ref, emb_ref, grad_ref, weight_ref, new_ref, pair_ref, weight_grad_ref):
    total = parts_ref[0].astype(jnp.float32)
    for part in range(1, parts_ref.shape[0]):
        total = total + parts_ref[part].astype(jnp.float32)
    total = total.astype(jnp.bfloat16)
    pre = ATOM_SCALE * dot32(total, weight_ref[...])
    new_ref[...] = (emb_ref[...].astype(jnp.float32) + silu(pre)).astype(jnp.bfloat16)
    grad_pre = (grad_ref[...].astype(jnp.float32) * silu_slope(pre)).astype(jnp.bfloat16)
    pair_ref[...] = (ATOM_SCALE * dot32(grad_pre, weight_ref[...], LAST_LAST)).astype(jnp.bfloat16)
    weight_grad_ref[...] = (ATOM_SCALE * dot32(total, grad_pre, FIRST_FIRST)).astype(jnp.bfloat16)


def backward_kernel(
    count_ref,
    in_ref,
    out_ref,
    basis_ref,
    bil_ref,
    up_ref,
    gathered_ref,
    moment_ref,
    grad_edge_ref,
    grad_sum_ref,
    target_ref,
    grad_new_ref,
    up_grad_ref,
    bil_grad_ref,
    parts_ref,
    table,
    spread,
    total,
):
    step = pl.program_id(0)
    tile = in_ref.shape[1]
    width = bil_ref.shape[1]
    edges = grad_edge_ref.shape[0]
    groups = total.shape[0] // width

    @pl.when(step == 0)
    def _():
        total[...] = jnp.zeros_like(total)
        update = dot32(gathered_ref[...], up_ref[...], FIRST_FIRST)
        hot = row_hot(grad_sum_ref.shape[0], target_ref[...])
        grad_new = grad_edge_ref[...].astype(jnp.float32) + dot32(
            hot, grad_sum_ref[...], FIRST_FIRST
        )
        grad_new_ref[...] = grad_new
        grad_update = (grad_new * silu_slope(update)).astype(jnp.bfloat16)
        up_grad_ref[...] = dot32(gathered_ref[...], grad_update).astype(jnp.bfloat16)
        grad_gathered = dot32(up_ref[...], grad_update, LAST_LAST).astype(jnp.bfloat16)
        bil_grad_ref[...] = dot32(grad_gathered, moment_ref[...], LAST_LAST).astype(jnp.bfloat16)
        for part in range(edges // BLOCK):
            table[part * width : (part + 1) * width, :] = grad_gathered[
                :, part * BLOCK : (part + 1) * BLOCK
            ]

    place = step * tile + lax.broadcasted_iota(jnp.int32, (1, tile), 1)
    outgoing = jnp.where(place < count_ref[0, 0], out_ref[...], -1)
    picked = dot32(table[...], row_hot(BLOCK, outgoing & (BLOCK - 1)))
    high = outgoing // BLOCK
    grad = jnp.zeros((width, tile), jnp.float32)
    for part in range(edges // BLOCK):
        grad = jnp.where(
            (high == part) & (outgoing >= 0), picked[part * width : (part + 1) * width, :], grad
        )
    grad = grad.astype(jnp.bfloat16)
    for row in range(basis_ref.shape[0]):
        spread[row * width : (row + 1) * width, :] = grad * basis_ref[row : row + 1, :]
    feat_grad = dot32(bil_ref[...], spread[...], FIRST_FIRST)
    incoming = in_ref[...]
    hot_in = row_hot(BLOCK, incoming & (BLOCK - 1))
    high_in = incoming // BLOCK
    for part in range(groups):
        masked = jnp.where(high_in == part, feat_grad, 0.0).astype(jnp.bfloat16)
        total[part * width : (part + 1) * width, :] += dot32(masked, hot_in, LAST_LAST)

    @pl.when(step == pl.num_programs(0) - 1)
    def _():
        parts_ref[...] = total[...].astype(jnp.bfloat16)


def edge_kernel(
    parts_ref, projected_ref, emb_ref, down_ref, grad_new_ref, grad_in_ref, down_grad_ref
):
    total = parts_ref[0].astype(jnp.float32)
    for part in range(1, parts_ref.shape[0]):
        total = total + parts_ref[part].astype(jnp.float32)
    width = projected_ref.shape[0]
    grad_feat = jnp.concatenate(
        [total[at : at + width, :] for at in range(0, total.shape[0], width)], axis=1
    )
    grad_project = (grad_feat * silu_slope(projected_ref[...])).astype(jnp.bfloat16)
    grad_in_ref[...] = grad_new_ref[...] + dot32(grad_project, down_ref[...], FIRST_LAST)
    down_grad_ref[...] = dot32(grad_project, emb_ref[...]).astype(jnp.bfloat16)


def whole(shape):
    return pl.BlockSpec(shape, lambda step: (0,) * len(shape))


def params():
    return pltpu.CompilerParams(vmem_limit_bytes=VMEM_BYTES)


def body(
    edge_emb,
    atom_emb,
    edge_target,
    trip_in,
    trip_out,
    trip_count,
    trip_basis,
    grad_edge,
    grad_atom,
    w_down,
    w_bil,
    w_up,
    w_atom,
):
    members = lax.axis_size("graph")
    devices = members * lax.axis_size("dp")
    edge_rows = edge_emb[0]
    edge_dev, model = edge_rows.shape
    atom_dev = atom_emb.shape[1]
    trips = trip_in.shape[1]
    width = w_down.shape[1]
    basis_width = trip_basis.shape[1]
    tile = math.gcd(trips, TILE_LIMIT)
    rows_dev = edge_dev // BLOCK * width
    f32, b16 = jnp.float32, jnp.bfloat16
    shaped = jax.ShapeDtypeStruct

    projected, table = pl.pallas_call(
        feature_kernel,
        out_shape=(shaped((width, edge_dev), f32), shaped((rows_dev, BLOCK), b16)),
        compiler_params=params(),
        name="features",
    )(edge_rows, w_down)
    table_all = lax.all_gather(table, "graph", axis=0, tiled=True)

    along = lambda rows: pl.BlockSpec((rows, tile), lambda step: (0, step))
    smem = pl.BlockSpec(memory_space=pltpu.SMEM)
    atoms_all = atom_dev * members
    edge_new, atom_parts, gathered, moment = pl.pallas_call(
        forward_kernel,
        grid=(trips // tile,),
        in_specs=[
            smem,
            along(1),
            along(1),
            along(basis_width),
            whole(table_all.shape),
            whole(w_bil.shape),
            whole(w_up.shape),
            whole(edge_rows.shape),
            whole(edge_target.shape),
        ],
        out_specs=(
            whole(edge_rows.shape),
            whole((atoms_all, model)),
            whole((width, edge_dev)),
            whole((w_bil.shape[0], edge_dev)),
        ),
        out_shape=(
            shaped(edge_rows.shape, b16),
            shaped((atoms_all, model), b16),
            shaped((width, edge_dev), b16),
            shaped((w_bil.shape[0], edge_dev), b16),
        ),
        scratch_shapes=[
            pltpu.VMEM((w_bil.shape[0], edge_dev), f32),
            pltpu.VMEM((w_bil.shape[0], tile), b16),
        ],
        compiler_params=params(),
        name="forward_triplets",
    )(trip_count, trip_in, trip_out, trip_basis[0], table_all, w_bil, w_up, edge_rows, edge_target)

    atom_parts = lax.all_to_all(
        atom_parts.reshape(members, atom_dev, model), "graph", 0, 0, tiled=True
    )
    atom_new, grad_sum, watom_term = pl.pallas_call(
        atom_kernel,
        out_shape=(
            shaped((atom_dev, model), b16),
            shaped((atom_dev, model), b16),
            shaped((model, model), b16),
        ),
        compiler_params=params(),
        name="atoms",
    )(atom_parts, atom_emb[0], grad_atom[0], w_atom)
    grad_sum_all = lax.all_gather(grad_sum, "graph", axis=0, tiled=True)

    grad_new, wup_term, wbil_term, feat_parts = pl.pallas_call(
        backward_kernel,
        grid=(trips // tile,),
        in_specs=[
            smem,
            along(1),
            along(1),
            along(basis_width),
            whole(w_bil.shape),
            whole(w_up.shape),
            whole(gathered.shape),
            whole(moment.shape),
            whole(edge_rows.shape),
            whole(grad_sum_all.shape),
            whole(edge_target.shape),
        ],
        out_specs=(
            whole(edge_rows.shape),
            whole(w_up.shape),
            whole((width, w_bil.shape[0])),
            whole((members * rows_dev, BLOCK)),
        ),
        out_shape=(
            shaped(edge_rows.shape, f32),
            shaped(w_up.shape, b16),
            shaped((width, w_bil.shape[0]), b16),
            shaped((members * rows_dev, BLOCK), b16),
        ),
        scratch_shapes=[
            pltpu.VMEM((rows_dev, BLOCK), b16),
            pltpu.VMEM((w_bil.shape[0], tile), b16),
            pltpu.VMEM((members * rows_dev, BLOCK), f32),
        ],
        compiler_params=params(),
        name="backward_triplets",
    )(
        trip_count,
        trip_in,
        trip_out,
        trip_basis[0],
        jnp.transpose(w_bil.reshape(basis_width, width, width), (0, 2, 1)).reshape(w_bil.shape),
        w_up,
        gathered,
        moment,
        grad_edge[0],
        grad_sum_all,
        edge_target,
    )
    feat_parts = lax.all_to_all(
        feat_parts.reshape(members, rows_dev, BLOCK), "graph", 0, 0, tiled=True
    )
    grad_in, wdown_term = pl.pallas_call(
        edge_kernel,
        out_shape=(shaped(edge_rows.shape, f32), shaped((width, model), b16)),
        compiler_params=params(),
        name="edges",
    )(feat_parts, projected, edge_rows, w_down, grad_new)

    factor = 1.0 / math.sqrt(lax.axis_size("dp") * members * edge_dev)
    terms = (wdown_term, wbil_term, wup_term, watom_term)
    lanes = 128
    packed = jnp.concatenate([term.reshape(-1, lanes) for term in terms], axis=0)
    packed = lax.all_to_all(
        packed.reshape(devices, -1, lanes), ("dp", "graph"), 0, 0, tiled=True
    )
    share = (jnp.sum(packed.astype(f32), axis=0) * factor).astype(b16)
    totals = lax.all_to_all(
        jnp.broadcast_to(share[None], packed.shape), ("dp", "graph"), 0, 0, tiled=True
    ).reshape(-1, lanes)
    sums, at = [], 0
    for term in terms:
        rows = term.size // lanes
        sums.append(totals[at : at + rows].reshape(term.shape).astype(f32))
        at += rows
    return (
        edge_new[None],
        atom_new[None],
        grad_in[None],
        sums[0].T,
        sums[1].T,
        sums[2],
        sums[3],
    )


def solution(mesh):
    return jax.shard_map(
        body,
        mesh=mesh,
        in_specs=(
            P("dp", "graph", None),
            P("dp", "graph", None),
            P("dp", "graph"),
            P("dp", "graph"),
            P("dp", "graph"),
            P("dp", "graph"),
            P("dp", None, "graph"),
            P("dp", "graph", None),
            P("dp", "graph", None),
            P(),
            P(),
            P(),
            P(),
        ),
        out_specs=(
            P("dp", "graph", None),
            P("dp", "graph", None),
            P("dp", "graph", None),
            P(),
            P(),
            P(),
            P(),
        ),
        check_vma=False,
    )
```

time: 598 us -> 218 us (0.36)
  other arithmetic: 175 us -> 0.29 us
  waiting for transfers between devices: 193 us -> 22 us
  Pallas kernels: 0 us -> 89.4 us
  matrix products: 83.7 us -> 0 us
  local copies, waits for them, and re-layouts: 96 us -> 15.6 us
  blocking collectives: 30.9 us -> 80.1 us
  between operations: 14.7 us -> 1.56 us
  starting transfers between devices: 0.12 us -> 8.41 us
    psum x1 -> x0, waiting for transfers between devices: 134 us -> none  [body(): lax.psum((wdown_term, wbil_term, wup_term, watom_term), ('dp', 'graph'))]
    pallas_call x0 -> x5, Pallas kernels: none -> 89.4 us  [the longest x1 53.8 us: body(): pl.pallas_call(backward_kernel, grid=(trips // tile,), in_specs=[smem, al...]
    scatter-add x1 -> x0, other arithmetic: 88.1 us -> none  [body(): jax.ops.segment_sum(grad_feat_rows, incoming, num_segments=members * edge...]
    dot_general x50 -> x0, matrix products: 83.7 us -> none  [the longest x8 28.9 us: backward_step(): lax.dot_general(spread, grad_part, contract_last, preferred_element_type=...]
    reduce_scatter x2 -> x0, waiting for transfers between devices: 59.5 us -> none  [the longest x1 32.1 us: body(): lax.psum_scatter(partial_value, 'graph', scatter_dimension=0, tiled=True)]
    gather x2 -> x0, local copies, waits for them, and re-layouts: 59.4 us -> none  [the longest x1 57.4 us: body(): feat_in = jnp.take(edge_table_all, incoming, axis=0).T]
    all_to_all x0 -> x2, blocking collectives: none -> 49.3 us  [the longest x1 25.3 us: body(): lax.all_to_all(packed.reshape(devices, -1, lanes), ('dp', 'graph'), 0, 0,...]
    convert_element_type x42 -> x3, other arithmetic: 38.8 us -> 0.1 us  [the longest x2 0.09 us: body(): sums.append(totals[at:at + rows].reshape(term.shape).astype(f32))]
  transfers between devices with their start and end apart: 3 -> 2, of which waited for: 3 -> 2; matrix products, arithmetic and copies ran while one was open for 1% -> 1% of each run, Pallas kernels for 0% -> 0%
where the time goes in v1:
time: 218 us; the launch traced here: 217 us
  Pallas kernels  89.4 us (41%)
  blocking collectives  80.1 us (37%)
  waiting for transfers between devices  22 us (10%)
  local copies, waits for them, and re-layouts  15.6 us (7%)
  starting transfers between devices  8.41 us (4%)
    pallas_call x1, Pallas kernels, body(): pl.pallas_call(backward_kernel, grid=(trips // tile,), in_specs=[smem, al...  53.8 us
    pallas_call x1, Pallas kernels, body(): pl.pallas_call(forward_kernel, grid=(trips // tile,), in_specs=[smem, alo...  33.1 us
    all_to_all x1, blocking collectives, body(): lax.all_to_all(packed.reshape(devices, -1, lanes), ('dp', 'graph'), 0, 0,...  25.3 us
    all_to_all x1, blocking collectives, body(): lax.all_to_all(jnp.broadcast_to(share[None], packed.shape), ('dp', 'graph...  24 us
    all_gather x1, blocking collectives, body(): table_all = lax.all_gather(table, 'graph', axis=0, tiled=True)  16.6 us
    all_gather x1, blocking collectives, body(): grad_sum_all = lax.all_gather(grad_sum, 'graph', axis=0, tiled=True)  14.2 us
    all_to_all x1, waiting for transfers between devices, body(): lax.all_to_all(feat_parts.reshape(members, rows_dev, BLOCK), 'graph', 0,...  14.2 us
    unnamed x54, local copies, waits for them, and re-layouts  9.21 us
  transfers between devices with their start and end apart: 2, of which 2 were waited for; matrix products, arithmetic and copies ran while one was open for 1% of the time, Pallas kernels for 0%

profile of v1, /device:TPU:0, one launch (start us, length us, event | category | flops | bytes accessed | tf_op | source)
XLA Modules:
  0.0 217.2 jit_solution(3824804946271784206)
XLA Ops:
  0.6 0.0 copy-start.7
  0.6 0.0 copy-start.23
  0.7 0.0 copy-start.2
  1.4 1.0 copy.20.down_ref
  2.3 1.1 copy.21.bil_ref
  3.4 0.0 copy-start
  3.4 1.0 copy-done
  4.5 0.0 copy-start.9
  4.5 0.3 features.1
  4.8 0.0 copy-start.13
  4.8 16.6 %all_gather.6.table_ref = bf16[1024,256]{1,0:T(8,128)(2,1)S(1)} all-gather(bf16[128,256]{1,0:T(8,128)(2,1)S(1)} %get-tuple-element.22), channel_id=1, replica_groups=mesh['dp'=4,'graph'=8] {'graph'}, dimensions={0}, use_global_device_ids=true | all-gather | bytes 589824 | tf_op jit(solution)/shard_map/all_gather | solution.py:250
  21.4 0.0 copy-done.13
  21.4 0.0 copy-done.7
  21.4 0.0 copy-done.23
  21.4 0.0 copy-done.2
  21.4 0.0 copy-done.9
  21.4 0.0 copy-done.11
  21.4 0.0 copy-start.24
  21.4 33.1 %forward_triplets.1 = (bf16[512,512]{1,0:T(8,128)(2,1)}, bf16[256,512]{1,0:T(8,128)(2,1)}, bf16[64,512]{1,0:T(8,128)(2,1)S(1)}, bf16[1024,512]{1,0:T(8,128)(2,1)S(1)}) custom-call(s32[1,1]{1,0:T(1,128)S(6)} %copy.24.count_ref, s32[1,16384]{1,0:T(1,128)S(1)} %copy-done.7, s32[1,16384]{1,0:T(1,128)S(1)} %copy-done.9, bf16[16,16384]{1,0:T(8,128)(2,1)S(1)} %bitcast.22, ...), custom_call_target="tpu_custom_call" | custom-call | tf_op jit(solution)/shard_map/forward_triplets/pallas_call | solution.py:255
  54.5 0.6 copy-done.17
  55.1 4.8 %all-to-all-start = ((bf16[8,32,512]{2,1,0:T(8,128)(2,1)}), bf16[8,32,512]{2,1,0:T(8,128)(2,1)S(1)}, u32[]{:S(2)}, u32[]{:S(2)}) async-start(bf16[8,32,512]{2,1,0:T(8,128)(2,1)} %bitcast.3), calls=%async_computation | async-start | bytes 524288 | tf_op jit(solution)/shard_map/all_to_all | solution.py:289
  59.9 0.0 copy-done.24
  59.9 0.0 copy-start.6
  59.9 0.9 reshape.61
  60.8 1.0 copy.22
  61.8 7.8 %all-to-all-done.parts_ref = bf16[8,32,512]{2,1,0:T(8,128)(2,1)S(1)} async-done(((bf16[8,32,512]{2,1,0:T(8,128)(2,1)}), bf16[8,32,512]{2,1,0:T(8,128)(2,1)S(1)}, u32[]{:S(2)}, u32[]{:S(2)}) %all-to-all-start) | async-done | bytes 262176 | tf_op jit(solution)/shard_map/all_to_all | solution.py:289
  69.6 0.0 copy-done.5
  69.6 0.0 copy-done.21
  69.6 0.0 copy-done.22
  69.6 0.9 atoms.1
  70.5 0.8 copy-done.3
  71.3 14.2 %all_gather.7.grad_sum_ref = bf16[256,512]{1,0:T(8,128)(2,1)S(1)} all-gather(bf16[32,512]{1,0:T(8,128)(2,1)S(1)} %get-tuple-element.28), channel_id=1, replica_groups=mesh['dp'=4,'graph'=8] {'graph'}, dimensions={0}, use_global_device_ids=true | all-gather | bytes 294912 | tf_op jit(solution)/shard_map/all_gather | solution.py:302
  85.5 0.0 copy-done.6
  85.5 0.8 copy-done.8
  86.4 0.8 copy-done.10
  87.2 0.8 copy-done.12
  88.0 0.8 copy-done.18
  88.9 53.8 %backward_triplets.1 = (f32[512,512]{1,0:T(8,128)S(1)}, bf16[64,512]{1,0:T(8,128)(2,1)S(1)}, bf16[64,1024]{1,0:T(8,128)(2,1)S(1)}, bf16[1024,256]{1,0:T(8,128)(2,1)}) custom-call(s32[1,1]{1,0:T(1,128)S(6)} %copy.24.count_ref, s32[1,16384]{1,0:T(1,128)S(1)} %copy-done.8, s32[1,16384]{1,0:T(1,128)S(1)} %copy-done.10, bf16[16,16384]{1,0:T(8,128)(2,1)S(1)} %bitcast.23, ...), custom_call_target="tpu_custom_call" | custom-call | tf_op jit(solution)/shard_map/backward_triplets/pallas_call | solution.py:304
  142.7 0.7 copy-done.15
  143.3 0.6 copy-done.19
  144.0 0.0 copy-start.14
  144.0 3.6 %all-to-all-start.1 = ((bf16[8,128,256]{2,1,0:T(8,128)(2,1)}), bf16[8,128,256]{2,1,0:T(8,128)(2,1)S(1)}, u32[]{:S(2)}, u32[]{:S(2)}) async-start(bf16[8,128,256]{2,1,0:T(8,128)(2,1)} %bitcast.10), calls=%async_computation.1 | async-start | bytes 1048576 | tf_op jit(solution)/shard_map/all_to_all | solution.py:352
  147.6 0.0 copy-done.20
  147.7 0.7 reshape.66
  148.3 0.0 copy-done.16
  148.3 0.1 reshape.65
  148.4 0.0 copy-done.4
  148.4 0.3 reshape.67
  148.7 14.2 %all-to-all-done.1.parts_ref = bf16[8,128,256]{2,1,0:T(8,128)(2,1)S(1)} async-done(((bf16[8,128,256]{2,1,0:T(8,128)(2,1)}), bf16[8,128,256]{2,1,0:T(8,128)(2,1)S(1)}, u32[]{:S(2)}, u32[]{:S(2)}) %all-to-all-start.1) | async-done | bytes 524320 | tf_op jit(solution)/shard_map/all_to_all | solution.py:352
  162.9 0.0 copy-done.1
  162.9 0.0 copy-done.14
  162.9 1.3 edges.1
  164.3 0.1 reshape.64
  164.3 0.0 copy-done.25
  164.3 0.1 pad_maximum_fusion
  164.4 25.3 %all_to_all.20 = bf16[32,96,128]{2,1,0:T(8,128)(2,1)S(1)} all-to-all(bf16[32,96,128]{2,1,0:T(8,128)(2,1)S(1)} %bitcast.31), channel_id=1, replica_groups=mesh['dp'=4,'graph'=8] {'dp','graph'}, dimensions={0} | all-to-all | bytes 1572864 | tf_op jit(solution)/shard_map/all_to_all | solution.py:366
  189.6 0.1 convert_reduce_fusion
  189.8 0.1 broadcast_in_dim.18
  189.9 24.0 %all_to_all.21 = bf16[32,96,128]{2,1,0:T(8,128)(2,1)S(1)} all-to-all(bf16[32,96,128]{2,1,0:T(8,128)(2,1)S(1)} %broadcast_in_dim.18), channel_id=1, replica_groups=mesh['dp'=4,'graph'=8] {'dp','graph'}, dimensions={0} | all-to-all | bytes 1572864 | tf_op jit(solution)/shard_map/all_to_all | solution.py:370
  213.9 0.1 slice_convert_fusion
  214.0 0.7 reshape.73
  214.8 0.7 reshape.70
  215.4 0.7 reshape.72
  216.1 1.1 reshape.71
  (20 shorter events, 0.1 us)
Async XLA Ops:
  0.6 20.8 %copy-start.7 = (s32[1,16384]{1,0:T(1,128)S(1)}, s32[1,16384]{1,0:T(1,128)}, u32[]{:S(2)}) copy-start(s32[1,16384]{1,0:T(1,128)} %in_ref.3) | copy-start | bytes 196612
  0.6 20.7 %copy-start.23 = (s32[1,512]{1,0:T(1,128)S(1)}, s32[1,512]{1,0:T(1,128)}, u32[]{:S(2)}) copy-start(s32[1,512]{1,0:T(1,128)} %target_ref.3) | copy-start | bytes 6148
  0.7 20.7 %copy-start.2 = (bf16[1,16,16384]{2,1,0:T(8,128)(2,1)S(1)}, bf16[1,16,16384]{2,1,0:T(8,128)(2,1)}, u32[]{:S(2)}) copy-start(bf16[1,16,16384]{2,1,0:T(8,128)(2,1)} %param.19) | copy-start | bytes 1572868
  3.4 1.0 copy-start
  4.5 16.9 %copy-start.9 = (s32[1,16384]{1,0:T(1,128)S(1)}, s32[1,16384]{1,0:T(1,128)}, u32[]{:S(2)}) copy-start(s32[1,16384]{1,0:T(1,128)} %out_ref.3) | copy-start | bytes 196612
  4.5 16.9 %copy-start.11 = (bf16[64,512]{1,0:T(8,128)(2,1)S(1)}, bf16[64,512]{1,0:T(8,128)(2,1)}, u32[]{:S(2)}) copy-start(bf16[64,512]{1,0:T(8,128)(2,1)} %up_ref.3) | copy-start | bytes 196612
  4.8 16.6 %copy-start.13 = (f32[64,512]{1,0:T(8,128)}, f32[64,512]{1,0:T(8,128)S(1)}, u32[]{:S(2)}) copy-start(f32[64,512]{1,0:T(8,128)S(1)} %get-tuple-element.30.projected_ref) | copy-start | bytes 393220
  21.4 38.5 %copy-start.24 = (bf16[1024,64]{0,1:T(8,128)(2,1)S(1)}, bf16[1024,64]{0,1:T(8,128)(2,1)}, u32[]{:S(2)}) copy-start(bf16[1024,64]{0,1:T(8,128)(2,1)} %param.23) | copy-start | bytes 393220
  54.5 0.6 copy-start.17
  55.1 14.5 %copy-start.5 = (bf16[512,512]{1,0:T(8,128)(2,1)S(1)}, bf16[512,512]{1,0:T(8,128)(2,1)}, u32[]{:S(2)}) copy-start(bf16[512,512]{1,0:T(8,128)(2,1)} %weight_ref.1) | copy-start | bytes 1572868
  55.1 14.5 %copy-start.21 = (bf16[1,32,512]{2,1,0:T(8,128)(2,1)S(1)}, bf16[1,32,512]{2,1,0:T(8,128)(2,1)}, u32[]{:S(2)}) copy-start(bf16[1,32,512]{2,1,0:T(8,128)(2,1)} %param.14) | copy-start | bytes 98308
  55.1 14.5 %copy-start.22 = (bf16[1,32,512]{2,1,0:T(8,128)(2,1)S(1)}, bf16[1,32,512]{2,1,0:T(8,128)(2,1)}, u32[]{:S(2)}) copy-start(bf16[1,32,512]{2,1,0:T(8,128)(2,1)} %param.21) | copy-start | bytes 98308
  55.1 14.5 %all-to-all-start = ((bf16[8,32,512]{2,1,0:T(8,128)(2,1)}), bf16[8,32,512]{2,1,0:T(8,128)(2,1)S(1)}, u32[]{:S(2)}, u32[]{:S(2)}) async-start(bf16[8,32,512]{2,1,0:T(8,128)(2,1)} %bitcast.3), calls=%async_computation | async-start | bytes 524288 | tf_op jit(solution)/shard_map/all_to_all | solution.py:289
  59.9 25.6 %copy-start.6 = (bf16[1,512,512]{2,1,0:T(8,128)(2,1)S(1)}, bf16[1,512,512]{2,1,0:T(8,128)(2,1)}, u32[]{:S(2)}) copy-start(bf16[1,512,512]{2,1,0:T(8,128)(2,1)} %param.20) | copy-start | bytes 1572868
  70.5 0.8 copy-start.3
  85.5 0.8 copy-start.8
  86.4 0.8 copy-start.10
  87.2 0.8 copy-start.12
  88.0 0.8 copy-start.18
  142.7 0.7 copy-start.15
  143.3 0.6 copy-start.19
  144.0 4.4 %copy-start.4 = (bf16[512,512]{1,0:T(8,128)(2,1)S(1)}, bf16[512,512]{1,0:T(8,128)(2,1)}, u32[]{:S(2)}) copy-start(bf16[512,512]{1,0:T(8,128)(2,1)} %copy-done.3) | copy-start | bytes 1572868
  144.0 3.7 %copy-start.20 = (bf16[64,512]{1,0:T(8,128)(2,1)S(1)}, bf16[64,512]{1,0:T(8,128)(2,1)}, u32[]{:S(2)}) copy-start(bf16[64,512]{1,0:T(8,128)(2,1)} %copy-done.19) | copy-start | bytes 196612
  144.0 4.4 %copy-start.16 = (bf16[64,1024]{1,0:T(8,128)(2,1)S(1)}, bf16[64,1024]{1,0:T(8,128)(2,1)}, u32[]{:S(2)}) copy-start(bf16[64,1024]{1,0:T(8,128)(2,1)} %copy-done.15) | copy-start | bytes 393220
  144.0 18.9 %copy-start.1 = (bf16[1,512,512]{2,1,0:T(8,128)(2,1)S(1)}, bf16[1,512,512]{2,1,0:T(8,128)(2,1)}, u32[]{:S(2)}) copy-start(bf16[1,512,512]{2,1,0:T(8,128)(2,1)} %param.13) | copy-start | bytes 1572868
  144.0 18.9 %copy-start.14 = (f32[64,512]{1,0:T(8,128)S(1)}, f32[64,512]{1,0:T(8,128)}, u32[]{:S(2)}) copy-start(f32[64,512]{1,0:T(8,128)} %copy-done.13) | copy-start | bytes 393220
  144.0 18.9 %all-to-all-start.1 = ((bf16[8,128,256]{2,1,0:T(8,128)(2,1)}), bf16[8,128,256]{2,1,0:T(8,128)(2,1)S(1)}, u32[]{:S(2)}, u32[]{:S(2)}) async-start(bf16[8,128,256]{2,1,0:T(8,128)(2,1)} %bitcast.10), calls=%async_computation.1 | async-start | bytes 1048576 | tf_op jit(solution)/shard_map/all_to_all | solution.py:352
  162.9 1.4 copy-start.25

commit v2 on v1

v2 whole, which is shorter than its diff:
```python
import functools
import math

import jax
import jax.numpy as jnp
from jax import lax
from jax.experimental import pallas as pl
from jax.experimental.pallas import tpu as pltpu
from jax.sharding import PartitionSpec as P

ATOM_SCALE = 0.25
BLOCK = 256
CAP = 128
TILE_LIMIT = 1024
INDEX_TILE = 2048
VMEM_BYTES = 48 * 1024 * 1024

FIRST_FIRST = (((0,), (0,)), ((), ()))
LAST_LAST = (((1,), (1,)), ((), ()))


def dot32(left, right, dims=(((1,), (0,)), ((), ()))):
    return lax.dot_general(left, right, dims, preferred_element_type=jnp.float32)


def silu(value):
    return value / (1.0 + jnp.exp(-value))


def silu_slope(value):
    logistic = 1.0 / (1.0 + jnp.exp(-value))
    return logistic * (1.0 + value * (1.0 - logistic))


def row_hot(rows, index):
    iota = lax.broadcasted_iota(jnp.int32, (rows, index.shape[1]), 0)
    return (iota == index).astype(jnp.float32).astype(jnp.bfloat16)


def feature_kernel(emb_ref, down_ref, bil_ref, projected_ref, feat_ref, back_ref):
    projected = dot32(down_ref[...], emb_ref[...], LAST_LAST)
    projected_ref[...] = projected
    feat_ref[...] = silu(projected).astype(jnp.bfloat16)
    width = down_ref.shape[0]
    turned = bil_ref[...].astype(jnp.float32).T
    back_ref[...] = jnp.concatenate(
        [turned[at : at + width] for at in range(0, turned.shape[0], width)], axis=1
    ).astype(jnp.bfloat16)


def index_kernel(members, in_ref, slot_ref, rank_ref, hots, counts):
    trips = in_ref.shape[1]
    rows = rank_ref.shape[0]
    tile = math.gcd(trips, INDEX_TILE)
    spans = [slice(at, at + tile) for at in range(0, trips, tile)]
    counts[...] = jnp.zeros_like(counts)
    for span in spans:
        incoming = in_ref[:, span]
        hot = row_hot(CAP, incoming & (CAP - 1))
        hots[:, span] = hot
        counts[...] += dot32(row_hot(rows, incoming // CAP), hot, LAST_LAST)
    named = (counts[...] > 0.0).astype(jnp.float32)
    per = rows // members
    ahead = (
        lax.broadcasted_iota(jnp.int32, (CAP, CAP), 0)
        < lax.broadcasted_iota(jnp.int32, (CAP, CAP), 1)
    ).astype(jnp.bfloat16)
    row = lax.broadcasted_iota(jnp.int32, (rows, rows), 0)
    other = lax.broadcasted_iota(jnp.int32, (rows, rows), 1)
    above = ((other < row) & (other // per == row // per)).astype(jnp.bfloat16)
    sums = dot32(above, named.astype(jnp.bfloat16))
    before = jnp.sum(sums, axis=1, keepdims=True)
    rank = dot32(named.astype(jnp.bfloat16), ahead) + before
    rank = jnp.where(named > 0.0, rank, -1.0)
    rank_ref[...] = rank
    lookup = rank.astype(jnp.bfloat16)
    for span in spans:
        incoming = in_ref[:, span]
        place = incoming // CAP
        found = dot32(lookup, hots[:, span])
        iota = lax.broadcasted_iota(jnp.int32, found.shape, 0)
        found = jnp.sum(jnp.where(iota == place, found, 0.0), axis=0, keepdims=True)
        slot_ref[:, span] = (place // per) * CAP + found.astype(jnp.int32)


def rank_row(rank_ref, source, per):
    return jnp.concatenate(
        [rank_ref[source * per + part : source * per + part + 1, :] for part in range(per)], axis=1
    )


def rank_hot(row):
    iota = lax.broadcasted_iota(jnp.int32, (CAP, row.shape[1]), 0).astype(jnp.float32)
    return (iota == row).astype(jnp.float32).astype(jnp.bfloat16)


def forward_kernel(
    count_ref,
    slot_ref,
    out_ref,
    basis_ref,
    feat_ref,
    rank_ref,
    bil_ref,
    up_ref,
    emb_ref,
    target_ref,
    new_ref,
    atoms_ref,
    gathered_ref,
    moment_ref,
    table,
    total,
    spread,
):
    step = pl.program_id(0)
    tile = slot_ref.shape[1]
    width = bil_ref.shape[0]
    edges = emb_ref.shape[0]
    members = feat_ref.shape[0] // width
    groups = table.shape[0] // width

    @pl.when(step == 0)
    def _():
        total[...] = jnp.zeros_like(total)
        for source in range(members):
            row = rank_row(rank_ref, source, edges // CAP)
            chosen = dot32(
                feat_ref[source * width : (source + 1) * width, :], rank_hot(row), LAST_LAST
            )
            group, lane = divmod(source * CAP, BLOCK)
            table[group * width : (group + 1) * width, lane : lane + CAP] = chosen.astype(
                jnp.bfloat16
            )

    slot = slot_ref[...]
    high = slot // BLOCK
    hot = row_hot(BLOCK, slot & (BLOCK - 1))
    feat = jnp.zeros((width, tile), jnp.float32)
    per = BLOCK // width
    for chunk in range(groups // per):
        picked = dot32(table[chunk * BLOCK : (chunk + 1) * BLOCK, :], hot)
        for part in range(per):
            feat = jnp.where(
                high == chunk * per + part, picked[part * width : (part + 1) * width, :], feat
            )
    feat = feat.astype(jnp.bfloat16)
    basis = basis_ref[...]
    for row in range(basis.shape[0]):
        spread[row * width : (row + 1) * width, :] = feat * basis[row : row + 1, :]
    place = step * tile + lax.broadcasted_iota(jnp.int32, (1, tile), 1)
    outgoing = jnp.where(place < count_ref[0, 0], out_ref[...], -1)
    total[...] += dot32(spread[...], row_hot(edges, outgoing), LAST_LAST)

    @pl.when(step == pl.num_programs(0) - 1)
    def _():
        summed = total[...]
        head = summed.astype(jnp.bfloat16)
        rest = (summed - head.astype(jnp.float32)).astype(jnp.bfloat16)
        moment_ref[...] = head
        gathered = (dot32(bil_ref[...], head) + dot32(bil_ref[...], rest)).astype(jnp.bfloat16)
        gathered_ref[...] = gathered
        update = dot32(gathered, up_ref[...], FIRST_FIRST)
        fresh = (emb_ref[...].astype(jnp.float32) + silu(update)).astype(jnp.bfloat16)
        new_ref[...] = fresh
        atoms_ref[...] = dot32(row_hot(atoms_ref.shape[0], target_ref[...]), fresh).astype(
            jnp.bfloat16
        )


def atom_kernel(parts_ref, emb_ref, grad_ref, weight_ref, new_ref, grad_sum_ref, pair_ref):
    total = parts_ref[0].astype(jnp.float32)
    for part in range(1, parts_ref.shape[0]):
        total = total + parts_ref[part].astype(jnp.float32)
    total = total.astype(jnp.bfloat16)
    pre = ATOM_SCALE * dot32(total, weight_ref[...])
    new_ref[...] = (emb_ref[...].astype(jnp.float32) + silu(pre)).astype(jnp.bfloat16)
    grad_pre = (grad_ref[...].astype(jnp.float32) * silu_slope(pre)).astype(jnp.bfloat16)
    grad_sum_ref[...] = (ATOM_SCALE * dot32(grad_pre, weight_ref[...], LAST_LAST)).astype(
        jnp.bfloat16
    )
    pair_ref[0] = total
    pair_ref[1] = grad_pre


def atom_weight_kernel(factor, pairs_ref, out_ref):
    devices, _, rows, model = pairs_ref.shape
    sums = pairs_ref[:, 0].reshape(devices * rows, model)
    grads = pairs_ref[:, 1].reshape(devices * rows, model)
    out_ref[...] = dot32(sums, grads, FIRST_FIRST) * (ATOM_SCALE * factor)


def backward_kernel(
    count_ref,
    slot_ref,
    out_ref,
    basis_ref,
    rank_ref,
    back_ref,
    up_ref,
    gathered_ref,
    moment_ref,
    grad_edge_ref,
    grad_sum_ref,
    target_ref,
    grad_new_ref,
    up_grad_ref,
    bil_grad_ref,
    parts_ref,
    table,
    spread,
    masked,
    total,
):
    step = pl.program_id(0)
    tile = slot_ref.shape[1]
    width = back_ref.shape[0]
    edges = grad_edge_ref.shape[0]
    groups = total.shape[0] // width

    @pl.when(step == 0)
    def _():
        total[...] = jnp.zeros_like(total)
        update = dot32(gathered_ref[...], up_ref[...], FIRST_FIRST)
        hot = row_hot(grad_sum_ref.shape[0], target_ref[...])
        grad_new = grad_edge_ref[...].astype(jnp.float32) + dot32(
            hot, grad_sum_ref[...], FIRST_FIRST
        )
        grad_new_ref[...] = grad_new
        grad_update = (grad_new * silu_slope(update)).astype(jnp.bfloat16)
        up_grad_ref[...] = dot32(gathered_ref[...], grad_update).astype(jnp.bfloat16)
        grad_gathered = dot32(up_ref[...], grad_update, LAST_LAST).astype(jnp.bfloat16)
        bil_grad_ref[...] = dot32(grad_gathered, moment_ref[...], LAST_LAST).astype(jnp.bfloat16)
        for part in range(edges // BLOCK):
            table[part * width : (part + 1) * width, :] = grad_gathered[
                :, part * BLOCK : (part + 1) * BLOCK
            ]

    place = step * tile + lax.broadcasted_iota(jnp.int32, (1, tile), 1)
    outgoing = jnp.where(place < count_ref[0, 0], out_ref[...], -1)
    picked = dot32(table[...], row_hot(BLOCK, outgoing & (BLOCK - 1)))
    high = jnp.where(outgoing >= 0, outgoing // BLOCK, -1)
    grad = jnp.zeros((width, tile), jnp.float32)
    for part in range(edges // BLOCK):
        grad = jnp.where(high == part, picked[part * width : (part + 1) * width, :], grad)
    grad = grad.astype(jnp.bfloat16)
    basis = basis_ref[...]
    for row in range(basis.shape[0]):
        spread[row * width : (row + 1) * width, :] = grad * basis[row : row + 1, :]
    feat_grad = dot32(back_ref[...], spread[...])
    slot = slot_ref[...]
    high_in = slot // BLOCK
    for part in range(groups):
        masked[part * width : (part + 1) * width, :] = jnp.where(
            high_in == part, feat_grad, 0.0
        ).astype(jnp.bfloat16)
    total[...] += dot32(masked[...], row_hot(BLOCK, slot & (BLOCK - 1)), LAST_LAST)

    @pl.when(step == pl.num_programs(0) - 1)
    def _():
        members = parts_ref.shape[0]
        per = rank_ref.shape[0] // members
        for source in range(members):
            group, lane = divmod(source * CAP, BLOCK)
            piece = total[group * width : (group + 1) * width, lane : lane + CAP]
            ranks = rank_ref[source * per : (source + 1) * per, :]
            spare = jnp.zeros((parts_ref.shape[1] - width - per, CAP), jnp.float32)
            parts_ref[source] = jnp.concatenate([piece, ranks, spare], axis=0).astype(jnp.bfloat16)


def edge_kernel(
    parts_ref,
    projected_ref,
    emb_ref,
    down_ref,
    grad_new_ref,
    bil_grad_ref,
    up_grad_ref,
    grad_in_ref,
    packed_ref,
):
    members = parts_ref.shape[0]
    width, edges = projected_ref.shape
    per = edges // CAP
    grad_feat = jnp.zeros((width, edges), jnp.float32)
    for source in range(members):
        part = parts_ref[source].astype(jnp.float32)
        row = jnp.concatenate([part[width + at : width + at + 1] for at in range(per)], axis=1)
        grad_feat = grad_feat + dot32(part[:width].astype(jnp.bfloat16), rank_hot(row))
    grad_project = (grad_feat * silu_slope(projected_ref[...])).astype(jnp.bfloat16)
    grad_in_ref[...] = grad_new_ref[...] + dot32(grad_project, down_ref[...], FIRST_FIRST)
    down_grad = dot32(grad_project, emb_ref[...])
    devices, rows, lanes = packed_ref.shape
    at = 0
    for term in (down_grad, bil_grad_ref[...].astype(jnp.float32), up_grad_ref[...].astype(jnp.float32)):
        for column in range(0, term.shape[1], lanes):
            for first in range(0, width, rows):
                packed_ref[at] = term[first : first + rows, column : column + lanes].astype(
                    jnp.bfloat16
                )
                at += 1


def share_kernel(factor, parts_ref, out_ref):
    total = parts_ref[0].astype(jnp.float32)
    for part in range(1, parts_ref.shape[0]):
        total = total + parts_ref[part].astype(jnp.float32)
    total = (total * factor).astype(jnp.bfloat16)
    for part in range(out_ref.shape[0]):
        out_ref[part] = total


def unpack_kernel(parts_ref, down_ref, bil_ref, up_ref):
    devices, rows, lanes = parts_ref.shape
    at = 0
    for out in (down_ref, bil_ref, up_ref):
        for column in range(0, out.shape[1], lanes):
            for first in range(0, out.shape[0], rows):
                out[first : first + rows, column : column + lanes] = parts_ref[at].astype(
                    jnp.float32
                )
                at += 1


def whole(shape):
    return pl.BlockSpec(shape, lambda step: (0,) * len(shape))


def params():
    return pltpu.CompilerParams(vmem_limit_bytes=VMEM_BYTES)


def body(
    edge_emb,
    atom_emb,
    edge_target,
    trip_in,
    trip_out,
    trip_count,
    trip_basis,
    grad_edge,
    grad_atom,
    w_down,
    w_bil,
    w_up,
    w_atom,
):
    members = lax.axis_size("graph")
    devices = members * lax.axis_size("dp")
    edge_rows = edge_emb[0]
    edge_dev, model = edge_rows.shape
    atom_dev = atom_emb.shape[1]
    trips = trip_in.shape[1]
    width = w_down.shape[1]
    basis_width = trip_basis.shape[1]
    tile = math.gcd(trips, TILE_LIMIT)
    f32, b16 = jnp.float32, jnp.bfloat16
    shaped = jax.ShapeDtypeStruct

    down_rows = w_down.T
    bil_rows = w_bil.T
    projected, feat, back = pl.pallas_call(
        feature_kernel,
        out_shape=(
            shaped((width, edge_dev), f32),
            shaped((width, edge_dev), b16),
            shaped((width, w_bil.shape[0]), b16),
        ),
        compiler_params=params(),
        name="features",
    )(edge_rows, down_rows, bil_rows)
    feat_all = lax.all_gather(feat, "graph", axis=0, tiled=True)
    rank_rows = members * edge_dev // CAP
    slot, rank = pl.pallas_call(
        functools.partial(index_kernel, members),
        out_shape=(shaped(trip_in.shape, jnp.int32), shaped((rank_rows, CAP), f32)),
        scratch_shapes=[pltpu.VMEM((CAP, trips), b16), pltpu.VMEM((rank_rows, CAP), f32)],
        compiler_params=params(),
        name="slots",
    )(trip_in)

    along = lambda rows: pl.BlockSpec((rows, tile), lambda step: (0, step))
    smem = pl.BlockSpec(memory_space=pltpu.SMEM)
    atoms_all = atom_dev * members
    named_rows = members * CAP // BLOCK * width
    edge_new, atom_parts, gathered, moment = pl.pallas_call(
        forward_kernel,
        grid=(trips // tile,),
        in_specs=[
            smem,
            along(1),
            along(1),
            along(basis_width),
            whole(feat_all.shape),
            whole(rank.shape),
            whole(bil_rows.shape),
            whole(w_up.shape),
            whole(edge_rows.shape),
            whole(edge_target.shape),
        ],
        out_specs=(
            whole(edge_rows.shape),
            whole((atoms_all, model)),
            whole((width, edge_dev)),
            whole((w_bil.shape[0], edge_dev)),
        ),
        out_shape=(
            shaped(edge_rows.shape, b16),
            shaped((atoms_all, model), b16),
            shaped((width, edge_dev), b16),
            shaped((w_bil.shape[0], edge_dev), b16),
        ),
        scratch_shapes=[
            pltpu.VMEM((named_rows, BLOCK), b16),
            pltpu.VMEM((w_bil.shape[0], edge_dev), f32),
            pltpu.VMEM((w_bil.shape[0], tile), b16),
        ],
        compiler_params=params(),
        name="forward_triplets",
    )(
        trip_count,
        slot,
        trip_out,
        trip_basis[0],
        feat_all,
        rank,
        bil_rows,
        w_up,
        edge_rows,
        edge_target,
    )

    atom_parts = lax.all_to_all(
        atom_parts.reshape(members, atom_dev, model), "graph", 0, 0, tiled=True
    )
    atom_new, grad_sum, pair = pl.pallas_call(
        atom_kernel,
        out_shape=(
            shaped((atom_dev, model), b16),
            shaped((atom_dev, model), b16),
            shaped((2, atom_dev, model), b16),
        ),
        compiler_params=params(),
        name="atoms",
    )(atom_parts, atom_emb[0], grad_atom[0], w_atom)
    grad_sum_all = lax.all_gather(grad_sum, "graph", axis=0, tiled=True)
    pairs = lax.all_gather(pair, ("dp", "graph"), axis=0)

    piece_rows = width + -(-(edge_dev // CAP) // 16) * 16
    grad_new, wup_term, wbil_term, feat_parts = pl.pallas_call(
        backward_kernel,
        grid=(trips // tile,),
        in_specs=[
            smem,
            along(1),
            along(1),
            along(basis_width),
            whole(rank.shape),
            whole(back.shape),
            whole(w_up.shape),
            whole(gathered.shape),
            whole(moment.shape),
            whole(edge_rows.shape),
            whole(grad_sum_all.shape),
            whole(edge_target.shape),
        ],
        out_specs=(
            whole(edge_rows.shape),
            whole(w_up.shape),
            whole((width, w_bil.shape[0])),
            whole((members, piece_rows, CAP)),
        ),
        out_shape=(
            shaped(edge_rows.shape, f32),
            shaped(w_up.shape, b16),
            shaped((width, w_bil.shape[0]), b16),
            shaped((members, piece_rows, CAP), b16),
        ),
        scratch_shapes=[
            pltpu.VMEM((edge_dev // BLOCK * width, BLOCK), b16),
            pltpu.VMEM((w_bil.shape[0], tile), b16),
            pltpu.VMEM((named_rows, tile), b16),
            pltpu.VMEM((named_rows, BLOCK), f32),
        ],
        compiler_params=params(),
        name="backward_triplets",
    )(
        trip_count,
        slot,
        trip_out,
        trip_basis[0],
        rank,
        back,
        w_up,
        gathered,
        moment,
        grad_edge[0],
        grad_sum_all,
        edge_target,
    )
    feat_parts = lax.all_to_all(feat_parts, "graph", 0, 0, tiled=True)
    lanes = CAP
    weights = width * (2 * model + w_bil.shape[0])
    packed_shape = (devices, weights // devices // lanes, lanes)
    grad_in, packed = pl.pallas_call(
        edge_kernel,
        out_shape=(shaped(edge_rows.shape, f32), shaped(packed_shape, b16)),
        compiler_params=params(),
        name="edges",
    )(feat_parts, projected, edge_rows, down_rows, grad_new, wbil_term, wup_term)

    factor = 1.0 / math.sqrt(lax.axis_size("dp") * members * edge_dev)
    packed = lax.all_to_all(packed, ("dp", "graph"), 0, 0, tiled=True)
    share = pl.pallas_call(
        functools.partial(share_kernel, factor),
        out_shape=shaped(packed_shape, b16),
        compiler_params=params(),
        name="share",
    )(packed)
    totals = lax.all_to_all(share, ("dp", "graph"), 0, 0, tiled=True)
    grad_watom = pl.pallas_call(
        functools.partial(atom_weight_kernel, factor),
        out_shape=shaped((model, model), f32),
        compiler_params=params(),
        name="atom_weights",
    )(pairs)
    grad_wdown, grad_wbil, grad_wup = pl.pallas_call(
        unpack_kernel,
        out_shape=(
            shaped((width, model), f32),
            shaped((width, w_bil.shape[0]), f32),
            shaped(w_up.shape, f32),
        ),
        compiler_params=params(),
        name="unpack",
    )(totals)
    return (
        edge_new[None],
        atom_new[None],
        grad_in[None],
        grad_wdown.T,
        grad_wbil.T,
        grad_wup,
        grad_watom,
    )


def solution(mesh):
    return jax.shard_map(
        body,
        mesh=mesh,
        in_specs=(
            P("dp", "graph", None),
            P("dp", "graph", None),
            P("dp", "graph"),
            P("dp", "graph"),
            P("dp", "graph"),
            P("dp", "graph"),
            P("dp", None, "graph"),
            P("dp", "graph", None),
            P("dp", "graph", None),
            P(),
            P(),
            P(),
            P(),
        ),
        out_specs=(
            P("dp", "graph", None),
            P("dp", "graph", None),
            P("dp", "graph", None),
            P(),
            P(),
            P(),
            P(),
        ),
        check_vma=False,
    )
```

time: 218 us -> 162 us (0.74)
  Pallas kernels: 89.4 us -> 52.4 us
  waiting for transfers between devices: 22 us -> 0.02 us
  between operations: 1.56 us -> 14.8 us
  starting transfers between devices: 8.41 us -> 0.04 us
  local copies, waits for them, and re-layouts: 15.6 us -> 10.6 us
  blocking collectives: 80.1 us -> 83.6 us
    pallas_call x1, Pallas kernels: 53.8 us -> 16.6 us  [body(): pl.pallas_call(backward_kernel, grid=(trips // tile,), in_specs=[smem, al...]
    all_to_all x2 -> x0, waiting for transfers between devices: 22 us -> none  [the longest x1 14.2 us: body(): lax.all_to_all(feat_parts.reshape(members, rows_dev, BLOCK), 'graph', 0,...]
    all_to_all x2 -> x0, starting transfers between devices: 8.41 us -> none  [the longest x1 4.78 us: body(): lax.all_to_all(atom_parts.reshape(members, atom_dev, model), 'graph', 0,...]
    pallas_call x1, Pallas kernels: 33.1 us -> 27.2 us  [body(): pl.pallas_call(forward_kernel, grid=(trips // tile,), in_specs=[smem, alo...]
    pallas_call x0 -> x4, Pallas kernels: none -> 5.84 us  [the longest x1 3.28 us: body(): pl.pallas_call(functools.partial(index_kernel, members), out_shape=(shape...]
    all_to_all x2 -> x4, blocking collectives: 49.3 us -> 52.6 us  [the longest x1 16.4 us: body(): packed = lax.all_to_all(packed, ('dp', 'graph'), 0, 0, tiled=True)]
    reshape x6 -> x0, local copies, waits for them, and re-layouts: 3.02 us -> none  [the longest x2 1.91 us: body(): w_bil.reshape(basis_width, width, width)]
    unnamed x54 -> x42, local copies, waits for them, and re-layouts: 9.21 us -> 10.6 us
  transfers between devices with their start and end apart: 2 -> 1, of which waited for: 2 -> 0; matrix products, arithmetic and copies ran while one was open for 1% -> 0% of each run, Pallas kernels for 0% -> 12%
where the time goes in v2:
time: 162 us; the launch traced here: 161 us
  blocking collectives  83.6 us (52%)
  Pallas kernels  52.4 us (32%)
  between operations  14.8 us (9%)
  local copies, waits for them, and re-layouts  10.6 us (7%)
    pallas_call x1, Pallas kernels, body(): pl.pallas_call(forward_kernel, grid=(trips // tile,), in_specs=[smem, alo...  27.2 us
    all_gather x1, blocking collectives, body(): feat_all = lax.all_gather(feat, 'graph', axis=0, tiled=True)  16.7 us
    pallas_call x1, Pallas kernels, body(): pl.pallas_call(backward_kernel, grid=(trips // tile,), in_specs=[smem, al...  16.6 us
    all_to_all x1, blocking collectives, body(): packed = lax.all_to_all(packed, ('dp', 'graph'), 0, 0, tiled=True)  16.4 us
    all_gather x1, blocking collectives, body(): grad_sum_all = lax.all_gather(grad_sum, 'graph', axis=0, tiled=True)  14.3 us
    all_to_all x1, blocking collectives, body(): lax.all_to_all(atom_parts.reshape(members, atom_dev, model), 'graph', 0,...  14.2 us
    all_to_all x1, blocking collectives, body(): totals = lax.all_to_all(share, ('dp', 'graph'), 0, 0, tiled=True)  12.4 us
    unnamed x42, local copies, waits for them, and re-layouts  10.6 us
  transfers between devices with their start and end apart: 1, of which 0 were waited for; matrix products, arithmetic and copies ran while one was open for 0% of the time, Pallas kernels for 12%

profile of v2, /device:TPU:0, one launch (start us, length us, event | category | flops | bytes accessed | tf_op | source)
XLA Modules:
  0.0 161.4 jit_solution(5891813372492157266)
XLA Ops:
  7.2 0.0 all-gather.3.cloned.1.call-start
  7.9 0.0 copy-start.16
  7.9 0.8 copy-done.16
  8.7 0.0 copy-start.17
  8.7 0.0 copy-start.18
  8.7 3.3 %slots.1 = (s32[1,16384]{1,0:T(1,128)S(1)}, f32[32,128]{1,0:T(8,128)S(1)}) custom-call(s32[1,16384]{1,0:T(1,128)S(1)} %copy-done.16), custom_call_target="tpu_custom_call" | custom-call | tf_op jit(solution)/shard_map/slots/pallas_call | solution.py:374
  12.0 0.0 copy-start
  12.0 1.0 copy-done
  13.0 0.0 copy-start.6
  13.0 0.9 copy-done.6
  13.9 0.0 copy-start.10
  13.9 0.8 copy-done.10
  14.8 0.0 copy-start.8
  14.8 0.0 copy-start.15
  14.8 0.3 features.1
  15.1 0.0 copy-start.5
  15.1 0.0 copy-start.13
  15.1 0.0 copy-start.20
  15.1 16.7 %all_gather.12.feat_ref = bf16[512,512]{1,0:T(8,128)(2,1)S(1)} all-gather(bf16[64,512]{1,0:T(8,128)(2,1)S(1)} %get-tuple-element.29), channel_id=1, replica_groups=mesh['dp'=4,'graph'=8] {'graph'}, dimensions={0}, use_global_device_ids=true | all-gather | bytes 589824 | tf_op jit(solution)/shard_map/all_gather | solution.py:372
  31.8 0.0 copy-start.1
  31.8 1.0 copy-done.1
  32.9 0.0 copy-start.4
  32.9 1.0 copy-done.4
  33.9 0.0 copy-start.7
  33.9 0.9 copy-done.7
  34.8 0.0 copy-start.12
  34.8 0.8 copy-done.12
  35.7 0.0 copy-start.14
  35.7 0.8 copy-done.14
  36.5 0.0 copy-start.19
  36.5 0.7 copy-done.19
  37.2 0.0 copy-start.9
  37.2 27.2 %forward_triplets.1 = (bf16[512,512]{1,0:T(8,128)(2,1)}, bf16[256,512]{1,0:T(8,128)(2,1)S(1)}, bf16[64,512]{1,0:T(8,128)(2,1)S(1)}, bf16[1024,512]{1,0:T(8,128)(2,1)S(1)}) custom-call(s32[1,1]{1,0:T(1,128)S(6)} %copy.20.count_ref, s32[1,16384]{1,0:T(1,128)S(1)} %get-tuple-element.28.slot_ref, s32[1,16384]{1,0:T(1,128)S(1)} %copy-done.12, ...), custom_call_target="tpu_custom_call" | custom-call | tf_op jit(solution)/shard_map/forward_triplets/pallas_call | solution.py:386
  64.4 14.2 %all_to_all.20.parts_ref = bf16[8,32,512]{2,1,0:T(8,128)(2,1)S(1)} all-to-all(bf16[8,32,512]{2,1,0:T(8,128)(2,1)S(1)} %bitcast.23), channel_id=1, replica_groups=mesh['dp'=4,'graph'=8] {'graph'}, dimensions={0} | all-to-all | bytes 524288 | tf_op jit(solution)/shard_map/all_to_all | solution.py:433
  78.5 0.0 copy-done.17
  78.5 0.0 copy-done.18
  78.5 0.0 copy-done.8
  78.5 0.0 copy-start.2
  78.6 0.0 copy-start.11
  78.6 0.9 atoms.1
  79.5 0.0 all-gather.3.cloned.1.call-update
  79.5 14.3 %all_gather.13.grad_sum_ref = bf16[256,512]{1,0:T(8,128)(2,1)S(1)} all-gather(bf16[32,512]{1,0:T(8,128)(2,1)S(1)} %get-tuple-element.37), channel_id=1, replica_groups=mesh['dp'=4,'graph'=8] {'graph'}, dimensions={0}, use_global_device_ids=true | all-gather | bytes 294912 | tf_op jit(solution)/shard_map/all_gather | solution.py:446
  93.8 0.0 copy-done.15
  93.8 0.0 copy-done.5
  93.8 0.0 copy-done.13
  93.8 0.0 copy-done.20
  93.8 0.0 copy-done.9
  93.8 16.6 %backward_triplets.1 = (f32[512,512]{1,0:T(8,128)S(1)}, bf16[64,512]{1,0:T(8,128)(2,1)S(1)}, bf16[64,1024]{1,0:T(8,128)(2,1)S(1)}, bf16[8,80,128]{2,1,0:T(8,128)(2,1)S(1)}) custom-call(s32[1,1]{1,0:T(1,128)S(6)} %copy.20.count_ref, s32[1,16384]{1,0:T(1,128)S(1)} %get-tuple-element.28.slot_ref, s32[1,16384]{1,0:T(1,128)S(1)} %copy-done.13, ...), custom_call_target="tpu_custom_call" | custom-call | tf_op jit(solution)/shard_map/backward_triplets/pallas_call | solution.py:450
  110.4 9.6 %all_to_all.21.parts_ref = bf16[8,80,128]{2,1,0:T(8,128)(2,1)S(1)} all-to-all(bf16[8,80,128]{2,1,0:T(8,128)(2,1)S(1)} %get-tuple-element.38), channel_id=1, replica_groups=mesh['dp'=4,'graph'=8] {'graph'}, dimensions={0} | all-to-all | bytes 327680 | tf_op jit(solution)/shard_map/all_to_all | solution.py:501
  120.0 0.0 copy-done.2
  120.0 0.0 copy-done.11
  120.0 1.6 %edges.1 = (f32[512,512]{1,0:T(8,128)}, bf16[32,32,128]{2,1,0:T(8,128)(2,1)S(1)}) custom-call(bf16[8,80,128]{2,1,0:T(8,128)(2,1)S(1)} %all_to_all.21.parts_ref, f32[64,512]{1,0:T(8,128)S(1)} %get-tuple-element.39.projected_ref, bf16[512,512]{1,0:T(8,128)(2,1)S(1)} %bitcast.16, bf16[64,512]{1,0:T(8,128)(2,1)S(1)} %bitcast.25, ...), custom_call_target="tpu_custom_call" | custom-call | tf_op jit(solution)/shard_map/edges/pallas_call | solution.py:505
  121.6 16.4 %all_to_all.22.parts_ref = bf16[32,32,128]{2,1,0:T(8,128)(2,1)S(1)} all-to-all(bf16[32,32,128]{2,1,0:T(8,128)(2,1)S(1)} %get-tuple-element.44), channel_id=1, replica_groups=mesh['dp'=4,'graph'=8] {'dp','graph'}, dimensions={0} | all-to-all | bytes 524288 | tf_op jit(solution)/shard_map/all_to_all | solution.py:513
  138.0 0.1 share.1
  138.1 12.4 %all_to_all.23.parts_ref = bf16[32,32,128]{2,1,0:T(8,128)(2,1)S(1)} all-to-all(bf16[32,32,128]{2,1,0:T(8,128)(2,1)S(1)} %share.1), channel_id=1, replica_groups=mesh['dp'=4,'graph'=8] {'dp','graph'}, dimensions={0} | all-to-all | bytes 524288 | tf_op jit(solution)/shard_map/all_to_all | solution.py:520
  150.5 0.8 unpack.1
  151.3 0.0 all-gather.3.cloned.1.call-done
  151.3 0.0 copy-start.3
  151.3 1.6 copy-done.3
  152.9 1.7 %atom_weights.1 = f32[512,512]{1,0:T(8,128)} custom-call(bf16[32,2,32,512]{3,2,1,0:T(8,128)(2,1)S(1)} %bitcast.17), custom_call_target="tpu_custom_call" | custom-call | tf_op jit(solution)/shard_map/atom_weights/pallas_call | solution.py:521
Async XLA Ops:
  7.2 144.1 %all-gather.3.cloned.1.call-start = ((), (), s32[]{:S(2)}) async-start(), calls=%async_computation.4 | async-start | bytes 2162688 | tf_op jit(solution)/shard_map/all_gather | solution.py:447
  7.9 0.8 copy-start.16
  8.7 69.8 %copy-start.17 = (bf16[1,32,512]{2,1,0:T(8,128)(2,1)S(1)}, bf16[1,32,512]{2,1,0:T(8,128)(2,1)}, u32[]{:S(2)}) copy-start(bf16[1,32,512]{2,1,0:T(8,128)(2,1)} %param.14) | copy-start | bytes 98308
  8.7 69.8 %copy-start.18 = (bf16[1,32,512]{2,1,0:T(8,128)(2,1)S(1)}, bf16[1,32,512]{2,1,0:T(8,128)(2,1)}, u32[]{:S(2)}) copy-start(bf16[1,32,512]{2,1,0:T(8,128)(2,1)} %param.21) | copy-start | bytes 98308
  12.0 1.0 copy-start
  13.0 0.9 copy-start.6
  13.9 0.8 copy-start.10
  14.8 63.8 %copy-start.8 = (bf16[512,512]{1,0:T(8,128)(2,1)S(1)}, bf16[512,512]{1,0:T(8,128)(2,1)}, u32[]{:S(2)}) copy-start(bf16[512,512]{1,0:T(8,128)(2,1)} %weight_ref.1) | copy-start | bytes 1572868
  14.8 79.0 %copy-start.15 = (bf16[64,512]{1,0:T(8,128)(2,1)S(1)}, bf16[64,512]{1,0:T(8,128)(2,1)}, u32[]{:S(2)}) copy-start(bf16[64,512]{1,0:T(8,128)(2,1)} %up_ref.3) | copy-start | bytes 196612
  15.1 78.7 %copy-start.5 = (bf16[1,16,16384]{2,1,0:T(8,128)(2,1)S(1)}, bf16[1,16,16384]{2,1,0:T(8,128)(2,1)}, u32[]{:S(2)}) copy-start(bf16[1,16,16384]{2,1,0:T(8,128)(2,1)} %param.19) | copy-start | bytes 1572868
  15.1 78.7 %copy-start.13 = (s32[1,16384]{1,0:T(1,128)S(1)}, s32[1,16384]{1,0:T(1,128)}, u32[]{:S(2)}) copy-start(s32[1,16384]{1,0:T(1,128)} %out_ref.3) | copy-start | bytes 196612
  15.1 78.7 %copy-start.20 = (s32[1,512]{1,0:T(1,128)S(1)}, s32[1,512]{1,0:T(1,128)}, u32[]{:S(2)}) copy-start(s32[1,512]{1,0:T(1,128)} %target_ref.3) | copy-start | bytes 6148
  31.8 1.0 copy-start.1
  32.9 1.0 copy-start.4
  33.9 0.9 copy-start.7
  34.8 0.8 copy-start.12
  35.7 0.8 copy-start.14
  36.5 0.7 copy-start.19
  37.2 56.6 %copy-start.9 = (bf16[1,512,512]{2,1,0:T(8,128)(2,1)S(1)}, bf16[1,512,512]{2,1,0:T(8,128)(2,1)}, u32[]{:S(2)}) copy-start(bf16[1,512,512]{2,1,0:T(8,128)(2,1)} %param.20) | copy-start | bytes 1572868
  78.5 41.5 %copy-start.2 = (bf16[1,512,512]{2,1,0:T(8,128)(2,1)S(1)}, bf16[1,512,512]{2,1,0:T(8,128)(2,1)}, u32[]{:S(2)}) copy-start(bf16[1,512,512]{2,1,0:T(8,128)(2,1)} %param.13) | copy-start | bytes 1572868
  78.6 41.5 %copy-start.11 = (bf16[512,64]{0,1:T(8,128)(2,1)S(1)}, bf16[512,64]{0,1:T(8,128)(2,1)}, u32[]{:S(2)}) copy-start(bf16[512,64]{0,1:T(8,128)(2,1)} %param.22) | copy-start | bytes 196612
  151.3 1.6 copy-start.3
Sparse Core Ops, SparseCore 0:
  79.6 56.9 all-gather.2

commit v3 on v2

v3 whole, which is shorter than its diff:
```python
import functools
import math

import jax
import jax.numpy as jnp
from jax import lax
from jax.experimental import pallas as pl
from jax.experimental.pallas import tpu as pltpu
from jax.sharding import PartitionSpec as P

ATOM_SCALE = 0.25
BLOCK = 256
CAP = 128
TILE_LIMIT = 2048
INDEX_TILE = 2048
VMEM_BYTES = 24 * 1024 * 1024
VMEM_MOST = 60 * 1024 * 1024

FIRST_FIRST = (((0,), (0,)), ((), ()))
LAST_LAST = (((1,), (1,)), ((), ()))


def dot32(left, right, dims=(((1,), (0,)), ((), ()))):
    return lax.dot_general(left, right, dims, preferred_element_type=jnp.float32)


def silu(value):
    return value / (1.0 + jnp.exp(-value))


def silu_slope(value):
    logistic = 1.0 / (1.0 + jnp.exp(-value))
    return logistic * (1.0 + value * (1.0 - logistic))


def row_hot(rows, index):
    iota = lax.broadcasted_iota(jnp.int32, (rows, index.shape[1]), 0)
    return (iota == index).astype(jnp.float32).astype(jnp.bfloat16)


def start_copies(pairs, sems):
    copies = [
        pltpu.make_async_copy(source, target, sems.at[place])
        for place, (source, target) in enumerate(pairs)
    ]
    for copy in copies:
        copy.start()
    return copies


def feature_kernel(emb_hbm, down_hbm, projected_ref, feat_ref, emb_ref, down_ref, sems):
    for copy in start_copies(((emb_hbm, emb_ref), (down_hbm, down_ref)), sems):
        copy.wait()
    projected = dot32(down_ref[...], emb_ref[...], LAST_LAST)
    projected_ref[...] = projected
    feat_ref[...] = silu(projected).astype(jnp.bfloat16)


def index_kernel(members, in_ref, *refs):
    slot_ref, rank_ref, hots, counts = refs[-4:]
    trips = in_ref.shape[1]
    rows = rank_ref.shape[0]
    turn = lax.axis_index("graph") * (rows // members * CAP)
    tile = math.gcd(trips, INDEX_TILE)
    spans = [slice(at, at + tile) for at in range(0, trips, tile)]
    counts[...] = jnp.zeros_like(counts)
    for span in spans:
        incoming = in_ref[:, span] ^ turn
        hot = row_hot(CAP, incoming & (CAP - 1))
        hots[:, span] = hot
        counts[...] += dot32(row_hot(rows, incoming // CAP), hot, LAST_LAST)
    named = (counts[...] > 0.0).astype(jnp.float32)
    per = rows // members
    ahead = (
        lax.broadcasted_iota(jnp.int32, (CAP, CAP), 0)
        < lax.broadcasted_iota(jnp.int32, (CAP, CAP), 1)
    ).astype(jnp.bfloat16)
    row = lax.broadcasted_iota(jnp.int32, (rows, rows), 0)
    other = lax.broadcasted_iota(jnp.int32, (rows, rows), 1)
    above = ((other < row) & (other // per == row // per)).astype(jnp.bfloat16)
    sums = dot32(above, named.astype(jnp.bfloat16))
    before = jnp.sum(sums, axis=1, keepdims=True)
    rank = dot32(named.astype(jnp.bfloat16), ahead) + before
    rank = jnp.where(named > 0.0, rank, -1.0)
    rank_ref[...] = rank
    lookup = rank.astype(jnp.bfloat16)
    for span in spans:
        incoming = in_ref[:, span] ^ turn
        place = incoming // CAP
        found = dot32(lookup, hots[:, span])
        iota = lax.broadcasted_iota(jnp.int32, found.shape, 0)
        found = jnp.sum(jnp.where(iota == place, found, 0.0), axis=0, keepdims=True)
        slot_ref[:, span] = (place // per) * CAP + found.astype(jnp.int32)


def rank_row(rank_ref, source, per):
    return jnp.concatenate(
        [rank_ref[source * per + part : source * per + part + 1, :] for part in range(per)], axis=1
    )


def rank_hot(row):
    iota = lax.broadcasted_iota(jnp.int32, (CAP, row.shape[1]), 0).astype(jnp.float32)
    return (iota == row).astype(jnp.float32).astype(jnp.bfloat16)


def forward_kernel(
    members,
    count_ref,
    slot_ref,
    rank_ref,
    out_ref,
    basis_ref,
    bil_ref,
    up_ref,
    emb_ref,
    target_ref,
    *refs,
):
    feat_refs, refs = refs[:members], refs[members:]
    new_ref, near_ref, far_ref, gathered_ref, moment_ref, back_ref, *refs = refs
    table, total, spread = refs
    trips = slot_ref.shape[1]
    tile = spread.shape[1]
    width = bil_ref.shape[0]
    edges = emb_ref.shape[0]
    groups = table.shape[0] // width
    per = BLOCK // width
    count = count_ref[0, 0]
    total[...] = jnp.zeros_like(total)
    for source in range(members):
        row = rank_row(rank_ref, source, edges // CAP)
        chosen = dot32(feat_refs[source][...], rank_hot(row), LAST_LAST)
        group, lane = divmod(source * CAP, BLOCK)
        table[group * width : (group + 1) * width, lane : lane + CAP] = chosen.astype(jnp.bfloat16)

    def one_tile(step, carry):
        span = pl.ds(pl.multiple_of(step * tile, tile), tile)
        slot = slot_ref[:, span]
        high = slot // BLOCK
        hot = row_hot(BLOCK, slot & (BLOCK - 1))
        feat = jnp.zeros((width, tile), jnp.float32)
        for chunk in range(groups // per):
            picked = dot32(table[chunk * BLOCK : (chunk + 1) * BLOCK, :], hot)
            for part in range(per):
                feat = jnp.where(
                    high == chunk * per + part, picked[part * width : (part + 1) * width, :], feat
                )
        feat = feat.astype(jnp.bfloat16)
        basis = basis_ref[:, span]
        for row in range(basis.shape[0]):
            spread[row * width : (row + 1) * width, :] = feat * basis[row : row + 1, :]
        place = step * tile + lax.broadcasted_iota(jnp.int32, (1, tile), 1)
        outgoing = jnp.where(place < count, out_ref[:, span], -1)
        total[...] += dot32(spread[...], row_hot(edges, outgoing), LAST_LAST)
        return carry

    lax.fori_loop(0, trips // tile, one_tile, 0)
    turned = bil_ref[...].astype(jnp.float32).T
    back_ref[...] = jnp.concatenate(
        [turned[at : at + width] for at in range(0, turned.shape[0], width)], axis=1
    ).astype(jnp.bfloat16)
    summed = total[...]
    head = summed.astype(jnp.bfloat16)
    rest = (summed - head.astype(jnp.float32)).astype(jnp.bfloat16)
    moment_ref[...] = head
    gathered = (dot32(bil_ref[...], head) + dot32(bil_ref[...], rest)).astype(jnp.bfloat16)
    gathered_ref[...] = gathered
    update = dot32(gathered, up_ref[...], FIRST_FIRST)
    fresh = (emb_ref[...].astype(jnp.float32) + silu(update)).astype(jnp.bfloat16)
    new_ref[...] = fresh
    held = near_ref.shape[1]
    turn = lax.axis_index("graph") * held
    sums = dot32(row_hot(members * held, target_ref[...] ^ turn), fresh)
    for pair in range(members // 2):
        near_ref[pair] = sums[2 * pair * held : (2 * pair + 1) * held].astype(jnp.bfloat16)
        far_ref[pair] = sums[(2 * pair + 1) * held : (2 * pair + 2) * held].astype(jnp.bfloat16)


def chip_kernel(near_ref, far_ref, *out_refs):
    for pair, out_ref in enumerate(out_refs):
        out_ref[...] = (
            near_ref[pair].astype(jnp.float32) + far_ref[pair].astype(jnp.float32)
        ).astype(jnp.bfloat16)


def atom_kernel(emb_ref, grad_ref, weight_ref, *refs):
    part_refs, (new_ref, pair_ref) = refs[:-2], refs[-2:]
    total = part_refs[0][...].astype(jnp.float32)
    for part_ref in part_refs[1:]:
        total = total + part_ref[...].astype(jnp.float32)
    total = total.astype(jnp.bfloat16)
    pre = ATOM_SCALE * dot32(total, weight_ref[...])
    new_ref[...] = (emb_ref[...].astype(jnp.float32) + silu(pre)).astype(jnp.bfloat16)
    grad_pre = (grad_ref[...].astype(jnp.float32) * silu_slope(pre)).astype(jnp.bfloat16)
    pair_ref[0] = total
    pair_ref[1] = grad_pre


def backward_kernel(
    members,
    count_ref,
    slot_ref,
    out_ref,
    basis_ref,
    rank_ref,
    back_ref,
    up_ref,
    gathered_ref,
    moment_ref,
    grad_edge_ref,
    target_ref,
    atom_weight_ref,
    *refs,
):
    pair_refs, refs = refs[:members], refs[members:]
    grad_new_ref, up_grad_ref, bil_grad_ref, slab_ref, parts_ref, *refs = refs
    table, spread, masked, total, sums, grads, atom_grad = refs
    trips = slot_ref.shape[1]
    tile = spread.shape[1]
    width = back_ref.shape[0]
    edges = grad_edge_ref.shape[0]
    groups = total.shape[0] // width
    count = count_ref[0, 0]
    me = lax.axis_index("graph")
    held, model = pair_refs[0].shape[1:]
    for source, pair_ref in enumerate(pair_refs):
        sums[source * held : (source + 1) * held, :] = pair_ref[0]
        grads[source * held : (source + 1) * held, :] = pair_ref[1]
    grad_sum = (ATOM_SCALE * dot32(grads[...], atom_weight_ref[...], LAST_LAST)).astype(
        jnp.bfloat16
    )
    atom_grad[...] = ATOM_SCALE * dot32(sums[...], grads[...], FIRST_FIRST)
    share = model // members
    mine = atom_grad[pl.ds(pl.multiple_of(me * share, share), share), :]
    for column in range(0, model, CAP):
        slab_ref[column // CAP] = mine[:, column : column + CAP].astype(jnp.bfloat16)
    total[...] = jnp.zeros_like(total)
    update = dot32(gathered_ref[...], up_ref[...], FIRST_FIRST)
    hot = row_hot(members * held, target_ref[...] ^ (me * held))
    grad_new = grad_edge_ref[...].astype(jnp.float32) + dot32(hot, grad_sum, FIRST_FIRST)
    grad_new_ref[...] = grad_new
    grad_update = (grad_new * silu_slope(update)).astype(jnp.bfloat16)
    up_grad_ref[...] = dot32(gathered_ref[...], grad_update).astype(jnp.bfloat16)
    grad_gathered = dot32(up_ref[...], grad_update, LAST_LAST).astype(jnp.bfloat16)
    bil_grad_ref[...] = dot32(grad_gathered, moment_ref[...], LAST_LAST).astype(jnp.bfloat16)
    for part in range(edges // BLOCK):
        table[part * width : (part + 1) * width, :] = grad_gathered[
            :, part * BLOCK : (part + 1) * BLOCK
        ]

    def one_tile(step, carry):
        span = pl.ds(pl.multiple_of(step * tile, tile), tile)
        place = step * tile + lax.broadcasted_iota(jnp.int32, (1, tile), 1)
        outgoing = jnp.where(place < count, out_ref[:, span], -1)
        picked = dot32(table[...], row_hot(BLOCK, outgoing & (BLOCK - 1)))
        high = jnp.where(outgoing >= 0, outgoing // BLOCK, -1)
        grad = jnp.zeros((width, tile), jnp.float32)
        for part in range(edges // BLOCK):
            grad = jnp.where(high == part, picked[part * width : (part + 1) * width, :], grad)
        grad = grad.astype(jnp.bfloat16)
        basis = basis_ref[:, span]
        for row in range(basis.shape[0]):
            spread[row * width : (row + 1) * width, :] = grad * basis[row : row + 1, :]
        feat_grad = dot32(back_ref[...], spread[...])
        slot = slot_ref[:, span]
        high_in = slot // BLOCK
        for part in range(groups):
            masked[part * width : (part + 1) * width, :] = jnp.where(
                high_in == part, feat_grad, 0.0
            ).astype(jnp.bfloat16)
        total[...] += dot32(masked[...], row_hot(BLOCK, slot & (BLOCK - 1)), LAST_LAST)
        return carry

    lax.fori_loop(0, trips // tile, one_tile, 0)
    per = rank_ref.shape[0] // members
    for source in range(members):
        group, lane = divmod(source * CAP, BLOCK)
        piece = total[group * width : (group + 1) * width, lane : lane + CAP]
        ranks = rank_ref[source * per : (source + 1) * per, :]
        spare = jnp.zeros((parts_ref.shape[1] - width - per, CAP), jnp.float32)
        parts_ref[me ^ source] = jnp.concatenate([piece, ranks, spare], axis=0).astype(jnp.bfloat16)


def edge_kernel(
    parts_ref,
    projected_ref,
    emb_ref,
    down_ref,
    grad_new_ref,
    bil_grad_ref,
    up_grad_ref,
    grad_in_ref,
    near_ref,
    far_ref,
    flat,
):
    members = parts_ref.shape[0]
    width, edges = projected_ref.shape
    per = edges // CAP
    grad_feat = jnp.zeros((width, edges), jnp.float32)
    for source in range(members):
        part = parts_ref[source].astype(jnp.float32)
        row = jnp.concatenate([part[width + at : width + at + 1] for at in range(per)], axis=1)
        grad_feat = grad_feat + dot32(part[:width].astype(jnp.bfloat16), rank_hot(row))
    grad_project = (grad_feat * silu_slope(projected_ref[...])).astype(jnp.bfloat16)
    grad_in_ref[...] = grad_new_ref[...] + dot32(grad_project, down_ref[...], FIRST_FIRST)
    down_grad = dot32(grad_project, emb_ref[...]).astype(jnp.bfloat16)
    at = 0
    for term in (down_grad, bil_grad_ref[...], up_grad_ref[...]):
        for column in range(0, term.shape[1], CAP):
            flat[at : at + width, :] = term[:, column : column + CAP]
            at += width
    me = lax.axis_index("graph")
    rows = near_ref.shape[1]
    for pair in range(members // 2):
        near_ref[pair] = flat[pl.ds(pl.multiple_of((me ^ (2 * pair)) * rows, rows), rows), :]
        far_ref[pair] = flat[pl.ds(pl.multiple_of((me ^ (2 * pair + 1)) * rows, rows), rows), :]


def share_kernel(slab_ref, *refs):
    part_refs, out_ref = refs[:-1], refs[-1]
    total = part_refs[0][...].astype(jnp.float32)
    for part_ref in part_refs[1:]:
        total = total + part_ref[...].astype(jnp.float32)
    rows = total.shape[0]
    out_ref[:rows, :] = total.astype(jnp.bfloat16)
    slab = slab_ref[...]
    out_ref[rows:, :] = slab.reshape(slab.shape[0] * slab.shape[1], CAP)


def total_kernel(factor, *refs):
    part_refs, out_ref = refs[:-1], refs[-1]
    total = part_refs[0][...].astype(jnp.float32)
    for part_ref in part_refs[1:]:
        total = total + part_ref[...].astype(jnp.float32)
    out_ref[...] = (total * factor).astype(jnp.bfloat16)


def last_kernel(members, *refs):
    part_refs, (down_ref, bil_ref, up_ref, atom_ref, flat) = refs[:members], refs[members:]
    me = lax.axis_index("graph")
    model = atom_ref.shape[1]
    rows = flat.shape[0] // members
    held = model // members
    for place, part_ref in enumerate(part_refs):
        source = me ^ place
        flat[pl.ds(pl.multiple_of(source * rows, rows), rows), :] = part_ref[:rows, :]
        for block in range(model // CAP):
            first = rows + block * held
            atom_ref[
                pl.ds(pl.multiple_of(source * held, held), held), block * CAP : (block + 1) * CAP
            ] = part_ref[first : first + held, :].astype(jnp.float32)
    at = 0
    for out in (down_ref, bil_ref, up_ref):
        width = out.shape[0]
        for column in range(0, out.shape[1], CAP):
            out[:, column : column + CAP] = flat[at : at + width, :].astype(jnp.float32)
            at += width


HBM = pl.BlockSpec(memory_space=pltpu.HBM)
VMEM = pl.BlockSpec(memory_space=pltpu.VMEM)
SMEM = pl.BlockSpec(memory_space=pltpu.SMEM)


def swap(value, members, mask, axis="graph"):
    return lax.ppermute(value, axis, [(at, at ^ mask) for at in range(members)])


def scatter_near(near, far, members):
    shape = jax.ShapeDtypeStruct(near.shape[1:], near.dtype)
    sums = pl.pallas_call(
        chip_kernel,
        out_shape=[shape] * (members // 2),
        compiler_params=params(),
        name="chip_sums",
    )(near, swap(far, members, 1))
    return [sums[0]] + [swap(part, members, 2 * at) for at, part in enumerate(sums) if at > 0]


def gather_near(value, members, beside=None):
    even = [value] + [swap(value, members, mask) for mask in range(2, members, 2)]
    if beside is not None:
        even, beside = lax.optimization_barrier((even, beside))
    odd = [swap(piece, members, 1) for piece in even]
    return [piece for pair in zip(even, odd) for piece in pair], beside


def params(limit=VMEM_BYTES):
    return pltpu.CompilerParams(vmem_limit_bytes=limit)


def body(
    edge_emb,
    atom_emb,
    edge_target,
    trip_in,
    trip_out,
    trip_count,
    trip_basis,
    grad_edge,
    grad_atom,
    w_down,
    w_bil,
    w_up,
    w_atom,
):
    members = lax.axis_size("graph")
    edge_rows = edge_emb[0]
    edge_dev, model = edge_rows.shape
    atom_dev = atom_emb.shape[1]
    trips = trip_in.shape[1]
    width = w_down.shape[1]
    tile = math.gcd(trips, TILE_LIMIT)
    f32, b16 = jnp.float32, jnp.bfloat16
    shaped = jax.ShapeDtypeStruct

    down_rows = w_down.T
    bil_rows = w_bil.T
    basis = trip_basis[0]
    projected, feat = pl.pallas_call(
        feature_kernel,
        in_specs=[HBM] * 2,
        out_shape=(
            shaped((width, edge_dev), f32),
            shaped((width, edge_dev), b16),
        ),
        scratch_shapes=[
            pltpu.VMEM(edge_rows.shape, b16),
            pltpu.VMEM(down_rows.shape, b16),
            pltpu.SemaphoreType.DMA((2,)),
        ],
        compiler_params=params(VMEM_MOST),
        name="features",
    )(edge_rows, down_rows)
    rank_rows = members * edge_dev // CAP
    staged = (trip_out, basis, bil_rows, w_up, edge_rows, edge_target)
    slot, rank = pl.pallas_call(
        functools.partial(index_kernel, members),
        in_specs=[VMEM] + [pl.BlockSpec(memory_space=pl.ANY)] * len(staged),
        out_shape=(shaped(trip_in.shape, jnp.int32), shaped((rank_rows, CAP), f32)),
        scratch_shapes=[
            pltpu.VMEM((CAP, trips), b16),
            pltpu.VMEM((rank_rows, CAP), f32),
        ],
        compiler_params=params(),
        cost_estimate=pl.CostEstimate(
            flops=8 * CAP * CAP * trips, bytes_accessed=8 * trips, transcendentals=0
        ),
        name="slots",
    )(trip_in, *staged)
    feats, (slot, rank) = gather_near(feat, members, (slot, rank))

    named_rows = members * CAP // BLOCK * width
    half = shaped((members // 2, atom_dev, model), b16)
    edge_new, near, far, gathered, moment, back = pl.pallas_call(
        functools.partial(forward_kernel, members),
        in_specs=[SMEM] + [VMEM] * (8 + members),
        out_shape=(
            shaped(edge_rows.shape, b16),
            half,
            half,
            shaped((width, edge_dev), b16),
            shaped((w_bil.shape[0], edge_dev), b16),
            shaped((width, w_bil.shape[0]), b16),
        ),
        scratch_shapes=[
            pltpu.VMEM((named_rows, BLOCK), b16),
            pltpu.VMEM((w_bil.shape[0], edge_dev), f32),
            pltpu.VMEM((w_bil.shape[0], tile), b16),
        ],
        compiler_params=params(),
        name="forward_triplets",
    )(
        trip_count,
        slot,
        rank,
        trip_out,
        basis,
        bil_rows,
        w_up,
        edge_rows,
        edge_target,
        *feats,
    )

    atom_block = shaped((atom_dev, model), b16)
    sums = scatter_near(near, far, members)
    atom_new, pair = pl.pallas_call(
        atom_kernel,
        out_shape=(atom_block, shaped((2, atom_dev, model), b16)),
        compiler_params=params(),
        name="atoms",
    )(atom_emb[0], grad_atom[0], w_atom, *sums)
    pairs, _ = gather_near(pair, members)

    piece_rows = width + -(-(edge_dev // CAP) // 16) * 16
    grad_new, wup_term, wbil_term, slab, feat_parts = pl.pallas_call(
        functools.partial(backward_kernel, members),
        in_specs=[SMEM] + [VMEM] * (11 + members),
        out_shape=(
            shaped(edge_rows.shape, f32),
            shaped(w_up.shape, b16),
            shaped((width, w_bil.shape[0]), b16),
            shaped((model // CAP, model // members, CAP), b16),
            shaped((members, piece_rows, CAP), b16),
        ),
        scratch_shapes=[
            pltpu.VMEM((edge_dev // BLOCK * width, BLOCK), b16),
            pltpu.VMEM((w_bil.shape[0], tile), b16),
            pltpu.VMEM((named_rows, tile), b16),
            pltpu.VMEM((named_rows, BLOCK), f32),
            pltpu.VMEM((members * atom_dev, model), b16),
            pltpu.VMEM((members * atom_dev, model), b16),
            pltpu.VMEM((model, model), f32),
        ],
        compiler_params=params(),
        name="backward_triplets",
    )(
        trip_count,
        slot,
        trip_out,
        basis,
        rank,
        back,
        w_up,
        gathered,
        moment,
        grad_edge[0],
        edge_target,
        w_atom,
        *pairs,
    )
    feat_parts = lax.all_to_all(feat_parts, "graph", 0, 0, tiled=True)
    flat_rows = width * (2 * model + w_bil.shape[0]) // CAP
    piece = shaped((members // 2, flat_rows // members, CAP), b16)
    grad_in, near, far = pl.pallas_call(
        edge_kernel,
        out_shape=(shaped(edge_rows.shape, f32), piece, piece),
        scratch_shapes=[pltpu.VMEM((flat_rows, CAP), b16)],
        compiler_params=params(),
        name="edges",
    )(feat_parts, projected, edge_rows, down_rows, grad_new, wbil_term, wup_term)

    batches = lax.axis_size("dp")
    factor = 1.0 / math.sqrt(batches * members * edge_dev)
    share_rows = (flat_rows + model * model // CAP) // members
    share = pl.pallas_call(
        share_kernel,
        out_shape=shaped((share_rows, CAP), b16),
        compiler_params=params(),
        name="share",
    )(slab, *scatter_near(near, far, members))
    share = pl.pallas_call(
        functools.partial(total_kernel, factor),
        out_shape=shaped((share_rows, CAP), b16),
        compiler_params=params(),
        name="total",
    )(share, *[swap(share, batches, mask, "dp") for mask in range(1, batches)])
    shares, _ = gather_near(share, members)
    grad_wdown, grad_wbil, grad_wup, grad_watom = pl.pallas_call(
        functools.partial(last_kernel, members),
        out_shape=(
            shaped((width, model), f32),
            shaped((width, w_bil.shape[0]), f32),
            shaped(w_up.shape, f32),
            shaped((model, model), f32),
        ),
        scratch_shapes=[pltpu.VMEM((flat_rows, CAP), b16)],
        compiler_params=params(),
        name="weights",
    )(*shares)
    return (
        edge_new[None],
        atom_new[None],
        grad_in[None],
        grad_wdown.T,
        grad_wbil.T,
        grad_wup,
        grad_watom,
    )


def solution(mesh):
    return jax.shard_map(
        body,
        mesh=mesh,
        in_specs=(
            P("dp", "graph", None),
            P("dp", "graph", None),
            P("dp", "graph"),
            P("dp", "graph"),
            P("dp", "graph"),
            P("dp", "graph"),
            P("dp", None, "graph"),
            P("dp", "graph", None),
            P("dp", "graph", None),
            P(),
            P(),
            P(),
            P(),
        ),
        out_specs=(
            P("dp", "graph", None),
            P("dp", "graph", None),
            P("dp", "graph", None),
            P(),
            P(),
            P(),
            P(),
        ),
        check_vma=False,
    )
```

time: 162 us -> 118 us (0.73)
  blocking collectives: 83.6 us -> 10.5 us
  starting transfers between devices: 0.04 us -> 29.5 us
  waiting for transfers between devices: 0.02 us -> 25 us
  between operations: 14.8 us -> 1.47 us
  local copies, waits for them, and re-layouts: 10.6 us -> 3.67 us
  Pallas kernels: 52.4 us -> 47 us
    all_to_all x3 -> x0, blocking collectives: 42.9 us -> none  [the longest x1 16.4 us: body(): packed = lax.all_to_all(packed, ('dp', 'graph'), 0, 0, tiled=True)]
    all_gather x2 -> x0, blocking collectives: 31 us -> none  [the longest x1 16.7 us: body(): feat_all = lax.all_gather(feat, 'graph', axis=0, tiled=True)]
    ppermute x0 -> x32, starting transfers between devices: none -> 29.5 us  [swap(): return lax.ppermute(value, axis, [(at, at ^ mask) for at in range(members)])]
    ppermute x0 -> x32, waiting for transfers between devices: none -> 25 us  [swap(): return lax.ppermute(value, axis, [(at, at ^ mask) for at in range(members)])]
    unnamed x42 -> x32, local copies, waits for them, and re-layouts: 10.6 us -> 3.67 us
    pallas_call x9 -> x11, Pallas kernels: 52.4 us -> 47 us  [the longest x1 24.6 us: body(): pl.pallas_call(functools.partial(forward_kernel, members), in_specs=[SMEM...]
  transfers between devices with their start and end apart: 1 -> 32, of which waited for: 0 -> 19; matrix products, arithmetic and copies ran while one was open for 0% -> 0% of each run, Pallas kernels for 12% -> 3%
where the time goes in v3:
time: 118 us; the launch traced here: 117 us
  Pallas kernels  47 us (40%)
  starting transfers between devices  29.5 us (25%)
  waiting for transfers between devices  25 us (21%)
  blocking collectives  10.5 us (9%)
  local copies, waits for them, and re-layouts  3.67 us (3%)
  between operations  1.47 us (1%)
    ppermute x32, starting transfers between devices, swap(): return lax.ppermute(value, axis, [(at, at ^ mask) for at in range(members)])  29.5 us
    ppermute x32, waiting for transfers between devices, swap(): return lax.ppermute(value, axis, [(at, at ^ mask) for at in range(members)])  25 us
    pallas_call x1, Pallas kernels, body(): pl.pallas_call(functools.partial(forward_kernel, members), in_specs=[SMEM...  24.6 us
    pallas_call x1, Pallas kernels, body(): pl.pallas_call(functools.partial(backward_kernel, members), in_specs=[SME...  13.2 us
    all_to_all x1, blocking collectives, body(): feat_parts = lax.all_to_all(feat_parts, 'graph', 0, 0, tiled=True)  10.5 us
    unnamed x32, local copies, waits for them, and re-layouts  3.67 us
    pallas_call x1, Pallas kernels, body(): pl.pallas_call(functools.partial(index_kernel, members), in_specs=[VMEM]...  3.28 us
  transfers between devices with their start and end apart: 32, of which 19 were waited for; matrix products, arithmetic and copies ran while one was open for 0% of the time, Pallas kernels for 3%

profile of v3, /device:TPU:0, one launch (start us, length us, event | category | flops | bytes accessed | tf_op | source)
XLA Modules:
  0.0 117.2 jit_solution(12080203042231851897)
XLA Ops:
  0.7 2.1 %features.1 = (f32[64,512]{1,0:T(8,128)}, bf16[64,512]{1,0:T(8,128)(2,1)}) custom-call(bf16[512,512]{1,0:T(8,128)(2,1)} %bitcast.12, bf16[64,512]{1,0:T(8,128)(2,1)} %bitcast.20), custom_call_target="tpu_custom_call" | custom-call | tf_op jit(solution)/shard_map/features/pallas_call | solution.py:422
  2.7 0.0 copy-start.14
  2.7 5.1 %collective-permute-start.2 = (bf16[64,512]{1,0:T(8,128)(2,1)}, bf16[64,512]{1,0:T(8,128)(2,1)S(1)}, u32[]{:S(2)}, u32[]{:S(2)}) collective-permute-start(bf16[64,512]{1,0:T(8,128)(2,1)} %get-tuple-element.50.refs_0_), channel_id=1, source_target_pairs={{0,6},{1,7},{2,4},{3,5},{4,2},{5,3},{6,0},{7,1},{8,14},{9,15},{10,... | collective-permute-start | bytes 196616 | tf_op jit(solution)/shard_map/ppermute | solution.py:368
  7.9 0.0 collective-permute-start.1
  7.9 0.6 collective-permute-start
  8.5 1.0 copy-done.1
  9.6 0.8 copy-done.6
  10.4 0.9 copy-done.9
  11.3 0.8 copy-done.15
  12.1 3.3 %slots.1 = (s32[1,16384]{1,0:T(1,128)S(1)}, f32[32,128]{1,0:T(8,128)S(1)}) custom-call(s32[1,16384]{1,0:T(1,128)S(1)} %copy-done.15, s32[1,16384]{1,0:T(1,128)S(1)} %copy-done.5, bf16[16,16384]{1,0:T(8,128)(2,1)S(1)} %bitcast.16, bf16[64,1024]{1,0:T(8,128)(2,1)S(1)} %bitcast.22, bf16[64,512]{1,0:T(8,128)(2,1)S(1)} %copy-done.6, ...), custom_call_target="tpu_custom_call" | custom-call | flops 2147483648 | bytes 131072 | tf_op jit(solution)/shard_map/slots/pallas_call | solution.py:439
  15.4 0.0 collective-permute-done.2.refs_6_
  15.4 0.0 collective-permute-done.1.refs_4_
  15.5 0.1 collective-permute-start.3
  15.6 0.5 collective-permute-start.4
  16.0 0.1 collective-permute-start.5
  16.1 0.4 collective-permute-start.6
  17.2 0.0 collective-permute-done.3.refs_1_
  17.2 0.1 collective-permute-done.5.refs_5_
  17.3 0.2 collective-permute-done.6.refs_7_
  17.5 24.6 %forward_triplets.1 = (bf16[512,512]{1,0:T(8,128)(2,1)}, bf16[4,32,512]{2,1,0:T(8,128)(2,1)S(1)}, bf16[4,32,512]{2,1,0:T(8,128)(2,1)S(1)}, bf16[64,512]{1,0:T(8,...) custom-call(s32[1,1]{1,0:T(1,128)S(6)} %copy.20.count_ref, ...), custom_call_target="tpu_custom_call" | custom-call | tf_op jit(solution)/shard_map/forward_triplets/pallas_call | solution.py:457
  42.1 0.4 collective-permute-start.7
  42.5 1.0 collective-permute-done.7.far_ref
  43.5 1.5 %collective-permute-start.8 = (bf16[32,512]{1,0:T(8,128)(2,1)S(1)}, bf16[32,512]{1,0:T(8,128)(2,1)S(1)}, u32[]{:S(2)}, u32[]{:S(2)}) collective-permute-start(bf16[32,512]{1,0:T(8,128)(2,1)S(1)} %get-tuple-element.58), channel_id=1, source_target_pairs={{0,2},{1,3},{2,0},{3,1},{4,6},{5,7},{6,4},{7,5},{8,10},{9,11},{10,... | collective-permute-start | bytes 98312 | tf_op jit(solution)/shard_map/ppermute | solution.py:368
  45.0 2.9 %collective-permute-start.9 = (bf16[32,512]{1,0:T(8,128)(2,1)S(1)}, bf16[32,512]{1,0:T(8,128)(2,1)S(1)}, u32[]{:S(2)}, u32[]{:S(2)}) collective-permute-start(bf16[32,512]{1,0:T(8,128)(2,1)S(1)} %get-tuple-element.59), channel_id=1, source_target_pairs={{0,4},{1,5},{2,6},{3,7},{4,0},{5,1},{6,2},{7,3},{8,12},{9,13},{10,... | collective-permute-start | bytes 98312 | tf_op jit(solution)/shard_map/ppermute | solution.py:368
  47.9 0.1 collective-permute-start.10
  48.0 0.0 collective-permute-done.8.refs_1_
  48.0 2.4 %collective-permute-done.9.refs_2_ = bf16[32,512]{1,0:T(8,128)(2,1)S(1)} collective-permute-done((bf16[32,512]{1,0:T(8,128)(2,1)S(1)}, bf16[32,512]{1,0:T(8,128)(2,1)S(1)}, u32[]{:S(2)}, u32[]{:S(2)}) %collective-permute-start.9) | collective-permute-done | bytes 32800 | tf_op jit(solution)/shard_map/ppermute | solution.py:368
  50.4 3.2 %collective-permute-done.10.refs_3_ = bf16[32,512]{1,0:T(8,128)(2,1)S(1)} collective-permute-done((bf16[32,512]{1,0:T(8,128)(2,1)S(1)}, bf16[32,512]{1,0:T(8,128)(2,1)S(1)}, u32[]{:S(2)}, u32[]{:S(2)}) %collective-permute-start.10) | collective-permute-done | bytes 32800 | tf_op jit(solution)/shard_map/ppermute | solution.py:368
  53.6 0.0 copy-start.7
  53.6 0.9 atoms.1
  54.5 0.4 collective-permute-start.16
  54.9 0.0 collective-permute-start.14
  54.9 4.0 %collective-permute-start.12 = (bf16[2,32,512]{2,1,0:T(8,128)(2,1)S(1)}, bf16[2,32,512]{2,1,0:T(8,128)(2,1)S(1)}, u32[]{:S(2)}, u32[]{:S(2)}) collective-permute-start(bf16[2,32,512]{2,1,0:T(8,128)(2,1)S(1)} %get-tuple-element.65.refs_0_), channel_id=1, source_target_pairs={{0,2},{1,3},{2,0},{3,1},{4,6},{5,7},{6,4},{7,5},{8,10},{9,11},{10,... | collective-permute-start | bytes 196616 | tf_op jit(solution)/shard_map/ppermute | solution.py:368
  58.9 1.8 %collective-permute-done.16.refs_6_ = bf16[2,32,512]{2,1,0:T(8,128)(2,1)S(1)} collective-permute-done((bf16[2,32,512]{2,1,0:T(8,128)(2,1)S(1)}, bf16[2,32,512]{2,1,0:T(8,128)(2,1)S(1)}, u32[]{:S(2)}, u32[]{:S(2)}) %collective-permute-start.16) | collective-permute-done | bytes 65568 | tf_op jit(solution)/shard_map/ppermute | solution.py:368
  60.7 0.8 collective-permute-done.14.refs_4_
  61.5 0.5 collective-permute-start.13
  62.0 0.7 collective-permute-done.15.refs_5_
  62.7 0.2 collective-permute-done.13.refs_3_
  62.9 13.2 %backward_triplets.1 = (f32[512,512]{1,0:T(8,128)S(1)}, bf16[64,512]{1,0:T(8,128)(2,1)S(1)}, bf16[64,1024]{1,0:T(8,128)(2,1)S(1)}, bf16[4,64,128]{2,1,0:T(8,128)(2,1)S(1)}, bf16[8,80,128]{2,1,0:T(8,128)(2,1)S(1)}) custom-call(s32[1,1]{1,0:T(1,128)S(6)} %copy.20.count_ref, s32[1,16384]{1,0:T(1,128)S(1)} %get-tuple-element.48.slot_ref, ...), custom_call_target="tpu_custom_call" | custom-call | tf_op jit(solution)/shard_map/backward_triplets/pallas_call | solution.py:499
  76.1 0.0 copy-start.8
  76.1 0.0 copy-start.10
  76.1 10.5 %all_to_all.5.parts_ref = bf16[8,80,128]{2,1,0:T(8,128)(2,1)S(1)} all-to-all(bf16[8,80,128]{2,1,0:T(8,128)(2,1)S(1)} %get-tuple-element.66), channel_id=1, replica_groups=mesh['dp'=4,'graph'=8] {'graph'}, dimensions={0} | all-to-all | bytes 327680 | tf_op jit(solution)/shard_map/all_to_all | solution.py:535
  86.7 1.6 %edges.1 = (f32[512,512]{1,0:T(8,128)}, bf16[4,128,128]{2,1,0:T(8,128)(2,1)S(1)}, bf16[4,128,128]{2,1,0:T(8,128)(2,1)S(1)}) custom-call(bf16[8,80,128]{2,1,0:T(8,128)(2,1)S(1)} %all_to_all.5.parts_ref, f32[64,512]{1,0:T(8,128)S(1)} %copy-done.10, bf16[512,512]{1,0:T(8,128)(2,1)S(1)} %bitcast.15, bf16[64,512]{1,0:T(8,128)(2,1)S(1)} %bitcast.21, ...), custom_call_target="tpu_custom_call" | custom-call | tf_op jit(solution)/shard_map/edges/pallas_call | solution.py:538
  88.3 1.3 %collective-permute-done.18.far_ref = bf16[4,128,128]{2,1,0:T(8,128)(2,1)S(1)} collective-permute-done((bf16[4,128,128]{2,1,0:T(8,128)(2,1)S(1)}, bf16[4,128,128]{2,1,0:T(8,128)(2,1)S(1)}, u32[]{:S(2)}, u32[]{:S(2)}) %collective-permute-start.18) | collective-permute-done | bytes 131104 | tf_op jit(solution)/shard_map/ppermute | solution.py:368
  89.7 1.1 collective-permute-start.19
  90.7 1.2 %collective-permute-start.20 = (bf16[128,128]{1,0:T(8,128)(2,1)S(1)}, bf16[128,128]{1,0:T(8,128)(2,1)S(1)}, u32[]{:S(2)}, u32[]{:S(2)}) collective-permute-start(bf16[128,128]{1,0:T(8,128)(2,1)S(1)} %get-tuple-element.77), channel_id=1, source_target_pairs={{0,4},{1,5},{2,6},{3,7},{4,0},{5,1},{6,2},{7,3},{8,12},{9,13},{10,... | collective-permute-start | bytes 98312 | tf_op jit(solution)/shard_map/ppermute | solution.py:368
  92.0 2.1 %collective-permute-start.21 = (bf16[128,128]{1,0:T(8,128)(2,1)S(1)}, bf16[128,128]{1,0:T(8,128)(2,1)S(1)}, u32[]{:S(2)}, u32[]{:S(2)}) collective-permute-start(bf16[128,128]{1,0:T(8,128)(2,1)S(1)} %get-tuple-element.78), channel_id=1, source_target_pairs={{0,6},{1,7},{2,4},{3,5},{4,2},{5,3},{6,0},{7,1},{8,14},{9,15},{10,... | collective-permute-start | bytes 98312 | tf_op jit(solution)/shard_map/ppermute | solution.py:368
  94.1 1.4 %collective-permute-done.20.refs_2_ = bf16[128,128]{1,0:T(8,128)(2,1)S(1)} collective-permute-done((bf16[128,128]{1,0:T(8,128)(2,1)S(1)}, bf16[128,128]{1,0:T(8,128)(2,1)S(1)}, u32[]{:S(2)}, u32[]{:S(2)}) %collective-permute-start.20) | collective-permute-done | bytes 32800 | tf_op jit(solution)/shard_map/ppermute | solution.py:368
  95.5 2.1 %collective-permute-done.21.refs_3_ = bf16[128,128]{1,0:T(8,128)(2,1)S(1)} collective-permute-done((bf16[128,128]{1,0:T(8,128)(2,1)S(1)}, bf16[128,128]{1,0:T(8,128)(2,1)S(1)}, u32[]{:S(2)}, u32[]{:S(2)}) %collective-permute-start.21) | collective-permute-done | bytes 32800 | tf_op jit(solution)/shard_map/ppermute | solution.py:368
  97.7 2.5 %collective-permute-start.24 = (bf16[384,128]{1,0:T(8,128)(2,1)S(1)}, bf16[384,128]{1,0:T(8,128)(2,1)S(1)}, u32[]{:S(2)}, u32[]{:S(2)}) collective-permute-start(bf16[384,128]{1,0:T(8,128)(2,1)S(1)} %share.1.refs_0_), channel_id=1, source_target_pairs={{0,24},{8,16},{16,8},{24,0},{1,25},{9,17},{17,9},{25,1},{2,26},{10... | collective-permute-start | bytes 294920 | tf_op jit(solution)/shard_map/ppermute | solution.py:368
  100.2 0.5 collective-permute-start.23
  100.7 0.5 collective-permute-start.22
  101.3 3.0 %collective-permute-done.24.refs_3_ = bf16[384,128]{1,0:T(8,128)(2,1)S(1)} collective-permute-done((bf16[384,128]{1,0:T(8,128)(2,1)S(1)}, bf16[384,128]{1,0:T(8,128)(2,1)S(1)}, u32[]{:S(2)}, u32[]{:S(2)}) %collective-permute-start.24) | collective-permute-done | bytes 98336 | tf_op jit(solution)/shard_map/ppermute | solution.py:368
  104.3 0.8 collective-permute-done.23.refs_2_
  105.1 0.3 collective-permute-done.22.refs_1_
  105.3 0.1 total.1.refs_0_
  105.4 2.2 %collective-permute-start.30 = (bf16[384,128]{1,0:T(8,128)(2,1)S(1)}, bf16[384,128]{1,0:T(8,128)(2,1)S(1)}, u32[]{:S(2)}, u32[]{:S(2)}) collective-permute-start(bf16[384,128]{1,0:T(8,128)(2,1)S(1)} %total.1.refs_0_), channel_id=1, source_target_pairs={{0,6},{1,7},{2,4},{3,5},{4,2},{5,3},{6,0},{7,1},{8,14},{9,15},{10,... | collective-permute-start | bytes 294920 | tf_op jit(solution)/shard_map/ppermute | solution.py:368
  107.6 2.2 %collective-permute-start.26 = (bf16[384,128]{1,0:T(8,128)(2,1)S(1)}, bf16[384,128]{1,0:T(8,128)(2,1)S(1)}, u32[]{:S(2)}, u32[]{:S(2)}) collective-permute-start(bf16[384,128]{1,0:T(8,128)(2,1)S(1)} %total.1.refs_0_), channel_id=1, source_target_pairs={{0,2},{1,3},{2,0},{3,1},{4,6},{5,7},{6,4},{7,5},{8,10},{9,11},{10,... | collective-permute-start | bytes 294920 | tf_op jit(solution)/shard_map/ppermute | solution.py:368
  109.9 2.2 %collective-permute-done.30.refs_6_ = bf16[384,128]{1,0:T(8,128)(2,1)S(1)} collective-permute-done((bf16[384,128]{1,0:T(8,128)(2,1)S(1)}, bf16[384,128]{1,0:T(8,128)(2,1)S(1)}, u32[]{:S(2)}, u32[]{:S(2)}) %collective-permute-start.30) | collective-permute-done | bytes 98336 | tf_op jit(solution)/shard_map/ppermute | solution.py:368
  112.0 2.5 %collective-permute-done.28.refs_4_ = bf16[384,128]{1,0:T(8,128)(2,1)S(1)} collective-permute-done((bf16[384,128]{1,0:T(8,128)(2,1)S(1)}, bf16[384,128]{1,0:T(8,128)(2,1)S(1)}, u32[]{:S(2)}, u32[]{:S(2)}) %collective-permute-start.28) | collective-permute-done | bytes 98336 | tf_op jit(solution)/shard_map/ppermute | solution.py:368
  114.6 0.5 collective-permute-start.27
  115.1 0.8 collective-permute-done.29.refs_5_
  115.9 0.2 collective-permute-done.27.refs_3_
  116.0 1.2 %weights.1 = (f32[64,512]{1,0:T(8,128)}, f32[64,1024]{1,0:T(8,128)}, f32[64,512]{1,0:T(8,128)}, f32[512,512]{1,0:T(8,128)}) custom-call(bf16[384,128]{1,0:T(8,128)(2,1)S(1)} %total.1.refs_0_, bf16[384,128]{1,0:T(8,128)(2,1)S(1)} %collective-permute-done.25.refs_1_, bf16[384,128]{1,0:T(8,128)(2,1)S(1)} %collective-permute-done.26.refs_2_, ...), custom_call_target="tpu_custom_call" | custom-call | tf_op jit(solution)/shard_map/weights/pallas_call | solution.py:562
  (44 shorter events, 0.2 us)
Async XLA Ops:
  0.6 7.9 %copy-start = (bf16[1,512,512]{2,1,0:T(8,128)(2,1)S(1)}, bf16[1,512,512]{2,1,0:T(8,128)(2,1)}, u32[]{:S(2)}) copy-start(bf16[1,512,512]{2,1,0:T(8,128)(2,1)} %param.13) | copy-start | bytes 1572868
  0.6 7.9 %copy-start.5 = (s32[1,16384]{1,0:T(1,128)S(1)}, s32[1,16384]{1,0:T(1,128)}, u32[]{:S(2)}) copy-start(s32[1,16384]{1,0:T(1,128)} %out_ref.3) | copy-start | bytes 196612
  2.7 5.8 %copy-start.14 = (s32[1,512]{1,0:T(1,128)S(1)}, s32[1,512]{1,0:T(1,128)}, u32[]{:S(2)}) copy-start(s32[1,512]{1,0:T(1,128)} %target_ref.3) | copy-start | bytes 6148
  2.7 12.7 %collective-permute-start.2 = (bf16[64,512]{1,0:T(8,128)(2,1)}, bf16[64,512]{1,0:T(8,128)(2,1)S(1)}, u32[]{:S(2)}, u32[]{:S(2)}) collective-permute-start(bf16[64,512]{1,0:T(8,128)(2,1)} %get-tuple-element.50.refs_0_), channel_id=1, source_target_pairs={{0,6},{1,7},{2,4},{3,5},{4,2},{5,3},{6,0},{7,1},{8,14},{9,15},{10,... | collective-permute-start | bytes 196616 | tf_op jit(solution)/shard_map/ppermute | solution.py:368
  7.9 7.6 %collective-permute-start.1 = (bf16[64,512]{1,0:T(8,128)(2,1)}, bf16[64,512]{1,0:T(8,128)(2,1)S(1)}, u32[]{:S(2)}, u32[]{:S(2)}) collective-permute-start(bf16[64,512]{1,0:T(8,128)(2,1)} %get-tuple-element.50.refs_0_), channel_id=1, source_target_pairs={{0,4},{1,5},{2,6},{3,7},{4,0},{5,1},{6,2},{7,3},{8,12},{9,13},{10,... | collective-permute-start | bytes 196616 | tf_op jit(solution)/shard_map/ppermute | solution.py:368
  7.9 7.6 %collective-permute-start = (bf16[64,512]{1,0:T(8,128)(2,1)}, bf16[64,512]{1,0:T(8,128)(2,1)S(1)}, u32[]{:S(2)}, u32[]{:S(2)}) collective-permute-start(bf16[64,512]{1,0:T(8,128)(2,1)} %get-tuple-element.50.refs_0_), channel_id=1, source_target_pairs={{0,2},{1,3},{2,0},{3,1},{4,6},{5,7},{6,4},{7,5},{8,10},{9,11},{10,... | collective-permute-start | bytes 196616 | tf_op jit(solution)/shard_map/ppermute | solution.py:368
  8.5 1.0 copy-start.1
  9.6 0.8 copy-start.6
  10.4 0.9 copy-start.9
  11.3 0.8 copy-start.15
  12.1 3.3 %copy-start.11 = (bf16[64,512]{1,0:T(8,128)(2,1)S(1)}, bf16[64,512]{1,0:T(8,128)(2,1)}, u32[]{:S(2)}) copy-start(bf16[64,512]{1,0:T(8,128)(2,1)} %get-tuple-element.50.refs_0_) | copy-start | bytes 196612
  12.1 5.3 %copy-start.2 = (bf16[1,16,16384]{2,1,0:T(8,128)(2,1)S(1)}, bf16[1,16,16384]{2,1,0:T(8,128)(2,1)}, u32[]{:S(2)}) copy-start(bf16[1,16,16384]{2,1,0:T(8,128)(2,1)} %param.19) | copy-start | bytes 1572868
  15.5 1.7 %collective-permute-start.3 = (bf16[64,512]{1,0:T(8,128)(2,1)S(1)}, bf16[64,512]{1,0:T(8,128)(2,1)S(1)}, u32[]{:S(2)}, u32[]{:S(2)}) collective-permute-start(bf16[64,512]{1,0:T(8,128)(2,1)S(1)} %copy-done.11), channel_id=1, source_target_pairs={{0,1},{1,0},{2,3},{3,2},{4,5},{5,4},{6,7},{7,6},{8,9},{9,8},{10,11... | collective-permute-start | bytes 196616 | tf_op jit(solution)/shard_map/ppermute | solution.py:368
  15.6 1.7 %collective-permute-start.4 = (bf16[64,512]{1,0:T(8,128)(2,1)S(1)}, bf16[64,512]{1,0:T(8,128)(2,1)S(1)}, u32[]{:S(2)}, u32[]{:S(2)}) collective-permute-start(bf16[64,512]{1,0:T(8,128)(2,1)S(1)} %collective-permute-done.refs_2_), channel_id=1, source_target_pairs={{0,1},{1,0},{2,3},{3,2},{4,5},{5,4},{6,7},{7,6},{8,9},{9,8},{10,11... | collective-permute-start | bytes 196616 | tf_op jit(solution)/shard_map/ppermute | solution.py:368
  16.0 1.3 %collective-permute-start.5 = (bf16[64,512]{1,0:T(8,128)(2,1)S(1)}, bf16[64,512]{1,0:T(8,128)(2,1)S(1)}, u32[]{:S(2)}, u32[]{:S(2)}) collective-permute-start(bf16[64,512]{1,0:T(8,128)(2,1)S(1)} %collective-permute-done.1.refs_4_), channel_id=1, source_target_pairs={{0,1},{1,0},{2,3},{3,2},{4,5},{5,4},{6,7},{7,6},{8,9},{9,8},{10,11... | collective-permute-start | bytes 196616 | tf_op jit(solution)/shard_map/ppermute | solution.py:368
  16.1 1.3 %collective-permute-start.6 = (bf16[64,512]{1,0:T(8,128)(2,1)S(1)}, bf16[64,512]{1,0:T(8,128)(2,1)S(1)}, u32[]{:S(2)}, u32[]{:S(2)}) collective-permute-start(bf16[64,512]{1,0:T(8,128)(2,1)S(1)} %collective-permute-done.2.refs_6_), channel_id=1, source_target_pairs={{0,1},{1,0},{2,3},{3,2},{4,5},{5,4},{6,7},{7,6},{8,9},{9,8},{10,11... | collective-permute-start | bytes 196616 | tf_op jit(solution)/shard_map/ppermute | solution.py:368
  17.5 36.2 %copy-start.3 = (bf16[512,512]{1,0:T(8,128)(2,1)S(1)}, bf16[512,512]{1,0:T(8,128)(2,1)}, u32[]{:S(2)}) copy-start(bf16[512,512]{1,0:T(8,128)(2,1)} %atom_weight_ref.1) | copy-start | bytes 1572868
  17.5 36.2 %copy-start.12 = (bf16[1,32,512]{2,1,0:T(8,128)(2,1)S(1)}, bf16[1,32,512]{2,1,0:T(8,128)(2,1)}, u32[]{:S(2)}) copy-start(bf16[1,32,512]{2,1,0:T(8,128)(2,1)} %param.14) | copy-start | bytes 98308
  17.5 36.2 %copy-start.13 = (bf16[1,32,512]{2,1,0:T(8,128)(2,1)S(1)}, bf16[1,32,512]{2,1,0:T(8,128)(2,1)}, u32[]{:S(2)}) copy-start(bf16[1,32,512]{2,1,0:T(8,128)(2,1)} %param.21) | copy-start | bytes 98308
  42.1 20.8 %copy-start.4 = (bf16[1,512,512]{2,1,0:T(8,128)(2,1)S(1)}, bf16[1,512,512]{2,1,0:T(8,128)(2,1)}, u32[]{:S(2)}) copy-start(bf16[1,512,512]{2,1,0:T(8,128)(2,1)} %param.20) | copy-start | bytes 1572868
  42.1 1.3 %collective-permute-start.7 = (bf16[4,32,512]{2,1,0:T(8,128)(2,1)S(1)}, bf16[4,32,512]{2,1,0:T(8,128)(2,1)S(1)}, u32[]{:S(2)}, u32[]{:S(2)}) collective-permute-start(bf16[4,32,512]{2,1,0:T(8,128)(2,1)S(1)} %get-tuple-element.56), channel_id=1, source_target_pairs={{0,1},{1,0},{2,3},{3,2},{4,5},{5,4},{6,7},{7,6},{8,9},{9,8},{10,11... | collective-permute-start | bytes 393224 | tf_op jit(solution)/shard_map/ppermute | solution.py:368
  43.5 4.5 %collective-permute-start.8 = (bf16[32,512]{1,0:T(8,128)(2,1)S(1)}, bf16[32,512]{1,0:T(8,128)(2,1)S(1)}, u32[]{:S(2)}, u32[]{:S(2)}) collective-permute-start(bf16[32,512]{1,0:T(8,128)(2,1)S(1)} %get-tuple-element.58), channel_id=1, source_target_pairs={{0,2},{1,3},{2,0},{3,1},{4,6},{5,7},{6,4},{7,5},{8,10},{9,11},{10,... | collective-permute-start | bytes 98312 | tf_op jit(solution)/shard_map/ppermute | solution.py:368
  45.0 5.4 %collective-permute-start.9 = (bf16[32,512]{1,0:T(8,128)(2,1)S(1)}, bf16[32,512]{1,0:T(8,128)(2,1)S(1)}, u32[]{:S(2)}, u32[]{:S(2)}) collective-permute-start(bf16[32,512]{1,0:T(8,128)(2,1)S(1)} %get-tuple-element.59), channel_id=1, source_target_pairs={{0,4},{1,5},{2,6},{3,7},{4,0},{5,1},{6,2},{7,3},{8,12},{9,13},{10,... | collective-permute-start | bytes 98312 | tf_op jit(solution)/shard_map/ppermute | solution.py:368
  47.9 5.7 %collective-permute-start.10 = (bf16[32,512]{1,0:T(8,128)(2,1)S(1)}, bf16[32,512]{1,0:T(8,128)(2,1)S(1)}, u32[]{:S(2)}, u32[]{:S(2)}) collective-permute-start(bf16[32,512]{1,0:T(8,128)(2,1)S(1)} %get-tuple-element.60), channel_id=1, source_target_pairs={{0,6},{1,7},{2,4},{3,5},{4,2},{5,3},{6,0},{7,1},{8,14},{9,15},{10,... | collective-permute-start | bytes 98312 | tf_op jit(solution)/shard_map/ppermute | solution.py:368
  53.6 9.3 %copy-start.7 = (bf16[64,512]{1,0:T(8,128)(2,1)S(1)}, bf16[64,512]{1,0:T(8,128)(2,1)}, u32[]{:S(2)}) copy-start(bf16[64,512]{1,0:T(8,128)(2,1)} %up_ref.3) | copy-start | bytes 196612
  54.5 6.2 %collective-permute-start.16 = (bf16[2,32,512]{2,1,0:T(8,128)(2,1)S(1)}, bf16[2,32,512]{2,1,0:T(8,128)(2,1)S(1)}, u32[]{:S(2)}, u32[]{:S(2)}) collective-permute-start(bf16[2,32,512]{2,1,0:T(8,128)(2,1)S(1)} %get-tuple-element.65.refs_0_), channel_id=1, source_target_pairs={{0,6},{1,7},{2,4},{3,5},{4,2},{5,3},{6,0},{7,1},{8,14},{9,15},{10,... | collective-permute-start | bytes 196616 | tf_op jit(solution)/shard_map/ppermute | solution.py:368
  54.9 6.6 %collective-permute-start.14 = (bf16[2,32,512]{2,1,0:T(8,128)(2,1)S(1)}, bf16[2,32,512]{2,1,0:T(8,128)(2,1)S(1)}, u32[]{:S(2)}, u32[]{:S(2)}) collective-permute-start(bf16[2,32,512]{2,1,0:T(8,128)(2,1)S(1)} %get-tuple-element.65.refs_0_), channel_id=1, source_target_pairs={{0,4},{1,5},{2,6},{3,7},{4,0},{5,1},{6,2},{7,3},{8,12},{9,13},{10,... | collective-permute-start | bytes 196616 | tf_op jit(solution)/shard_map/ppermute | solution.py:368
  54.9 6.6 %collective-permute-start.12 = (bf16[2,32,512]{2,1,0:T(8,128)(2,1)S(1)}, bf16[2,32,512]{2,1,0:T(8,128)(2,1)S(1)}, u32[]{:S(2)}, u32[]{:S(2)}) collective-permute-start(bf16[2,32,512]{2,1,0:T(8,128)(2,1)S(1)} %get-tuple-element.65.refs_0_), channel_id=1, source_target_pairs={{0,2},{1,3},{2,0},{3,1},{4,6},{5,7},{6,4},{7,5},{8,10},{9,11},{10,... | collective-permute-start | bytes 196616 | tf_op jit(solution)/shard_map/ppermute | solution.py:368
  58.9 3.1 %collective-permute-start.11 = (bf16[2,32,512]{2,1,0:T(8,128)(2,1)S(1)}, bf16[2,32,512]{2,1,0:T(8,128)(2,1)S(1)}, u32[]{:S(2)}, u32[]{:S(2)}) collective-permute-start(bf16[2,32,512]{2,1,0:T(8,128)(2,1)S(1)} %get-tuple-element.65.refs_0_), channel_id=1, source_target_pairs={{0,1},{1,0},{2,3},{3,2},{4,5},{5,4},{6,7},{7,6},{8,9},{9,8},{10,11... | collective-permute-start | bytes 196616 | tf_op jit(solution)/shard_map/ppermute | solution.py:368
  60.7 1.3 %collective-permute-start.17 = (bf16[2,32,512]{2,1,0:T(8,128)(2,1)S(1)}, bf16[2,32,512]{2,1,0:T(8,128)(2,1)S(1)}, u32[]{:S(2)}, u32[]{:S(2)}) collective-permute-start(bf16[2,32,512]{2,1,0:T(8,128)(2,1)S(1)} %collective-permute-done.16.refs_6_), channel_id=1, source_target_pairs={{0,1},{1,0},{2,3},{3,2},{4,5},{5,4},{6,7},{7,6},{8,9},{9,8},{10,11... | collective-permute-start | bytes 196616 | tf_op jit(solution)/shard_map/ppermute | solution.py:368
  61.5 1.3 %collective-permute-start.15 = (bf16[2,32,512]{2,1,0:T(8,128)(2,1)S(1)}, bf16[2,32,512]{2,1,0:T(8,128)(2,1)S(1)}, u32[]{:S(2)}, u32[]{:S(2)}) collective-permute-start(bf16[2,32,512]{2,1,0:T(8,128)(2,1)S(1)} %collective-permute-done.14.refs_4_), channel_id=1, source_target_pairs={{0,1},{1,0},{2,3},{3,2},{4,5},{5,4},{6,7},{7,6},{8,9},{9,8},{10,11... | collective-permute-start | bytes 196616 | tf_op jit(solution)/shard_map/ppermute | solution.py:368
  61.5 1.4 %collective-permute-start.13 = (bf16[2,32,512]{2,1,0:T(8,128)(2,1)S(1)}, bf16[2,32,512]{2,1,0:T(8,128)(2,1)S(1)}, u32[]{:S(2)}, u32[]{:S(2)}) collective-permute-start(bf16[2,32,512]{2,1,0:T(8,128)(2,1)S(1)} %collective-permute-done.12.refs_2_), channel_id=1, source_target_pairs={{0,1},{1,0},{2,3},{3,2},{4,5},{5,4},{6,7},{7,6},{8,9},{9,8},{10,11... | collective-permute-start | bytes 196616 | tf_op jit(solution)/shard_map/ppermute | solution.py:368
  76.1 10.6 %copy-start.8 = (bf16[512,64]{0,1:T(8,128)(2,1)S(1)}, bf16[512,64]{0,1:T(8,128)(2,1)}, u32[]{:S(2)}) copy-start(bf16[512,64]{0,1:T(8,128)(2,1)} %param.22) | copy-start | bytes 196612
  76.1 10.6 %copy-start.10 = (f32[64,512]{1,0:T(8,128)S(1)}, f32[64,512]{1,0:T(8,128)}, u32[]{:S(2)}) copy-start(f32[64,512]{1,0:T(8,128)} %get-tuple-element.67.projected_ref) | copy-start | bytes 393220
  88.3 1.3 %collective-permute-start.18 = (bf16[4,128,128]{2,1,0:T(8,128)(2,1)S(1)}, bf16[4,128,128]{2,1,0:T(8,128)(2,1)S(1)}, u32[]{:S(2)}, u32[]{:S(2)}) collective-permute-start(bf16[4,128,128]{2,1,0:T(8,128)(2,1)S(1)} %get-tuple-element.74), channel_id=1, source_target_pairs={{0,1},{1,0},{2,3},{3,2},{4,5},{5,4},{6,7},{7,6},{8,9},{9,8},{10,11... | collective-permute-start | bytes 393224 | tf_op jit(solution)/shard_map/ppermute | solution.py:368
  89.7 4.5 %collective-permute-start.19 = (bf16[128,128]{1,0:T(8,128)(2,1)S(1)}, bf16[128,128]{1,0:T(8,128)(2,1)S(1)}, u32[]{:S(2)}, u32[]{:S(2)}) collective-permute-start(bf16[128,128]{1,0:T(8,128)(2,1)S(1)} %get-tuple-element.76), channel_id=1, source_target_pairs={{0,2},{1,3},{2,0},{3,1},{4,6},{5,7},{6,4},{7,5},{8,10},{9,11},{10,... | collective-permute-start | bytes 98312 | tf_op jit(solution)/shard_map/ppermute | solution.py:368
  90.7 4.8 %collective-permute-start.20 = (bf16[128,128]{1,0:T(8,128)(2,1)S(1)}, bf16[128,128]{1,0:T(8,128)(2,1)S(1)}, u32[]{:S(2)}, u32[]{:S(2)}) collective-permute-start(bf16[128,128]{1,0:T(8,128)(2,1)S(1)} %get-tuple-element.77), channel_id=1, source_target_pairs={{0,4},{1,5},{2,6},{3,7},{4,0},{5,1},{6,2},{7,3},{8,12},{9,13},{10,... | collective-permute-start | bytes 98312 | tf_op jit(solution)/shard_map/ppermute | solution.py:368
  92.0 5.7 %collective-permute-start.21 = (bf16[128,128]{1,0:T(8,128)(2,1)S(1)}, bf16[128,128]{1,0:T(8,128)(2,1)S(1)}, u32[]{:S(2)}, u32[]{:S(2)}) collective-permute-start(bf16[128,128]{1,0:T(8,128)(2,1)S(1)} %get-tuple-element.78), channel_id=1, source_target_pairs={{0,6},{1,7},{2,4},{3,5},{4,2},{5,3},{6,0},{7,1},{8,14},{9,15},{10,... | collective-permute-start | bytes 98312 | tf_op jit(solution)/shard_map/ppermute | solution.py:368
  97.7 6.5 %collective-permute-start.24 = (bf16[384,128]{1,0:T(8,128)(2,1)S(1)}, bf16[384,128]{1,0:T(8,128)(2,1)S(1)}, u32[]{:S(2)}, u32[]{:S(2)}) collective-permute-start(bf16[384,128]{1,0:T(8,128)(2,1)S(1)} %share.1.refs_0_), channel_id=1, source_target_pairs={{0,24},{8,16},{16,8},{24,0},{1,25},{9,17},{17,9},{25,1},{2,26},{10... | collective-permute-start | bytes 294920 | tf_op jit(solution)/shard_map/ppermute | solution.py:368
  100.2 4.9 %collective-permute-start.23 = (bf16[384,128]{1,0:T(8,128)(2,1)S(1)}, bf16[384,128]{1,0:T(8,128)(2,1)S(1)}, u32[]{:S(2)}, u32[]{:S(2)}) collective-permute-start(bf16[384,128]{1,0:T(8,128)(2,1)S(1)} %share.1.refs_0_), channel_id=1, source_target_pairs={{0,16},{8,24},{16,0},{24,8},{1,17},{9,25},{17,1},{25,9},{2,18},{10... | collective-permute-start | bytes 294920 | tf_op jit(solution)/shard_map/ppermute | solution.py:368
  100.7 4.6 %collective-permute-start.22 = (bf16[384,128]{1,0:T(8,128)(2,1)S(1)}, bf16[384,128]{1,0:T(8,128)(2,1)S(1)}, u32[]{:S(2)}, u32[]{:S(2)}) collective-permute-start(bf16[384,128]{1,0:T(8,128)(2,1)S(1)} %share.1.refs_0_), channel_id=1, source_target_pairs={{0,8},{8,0},{16,24},{24,16},{1,9},{9,1},{17,25},{25,17},{2,10},{10... | collective-permute-start | bytes 294920 | tf_op jit(solution)/shard_map/ppermute | solution.py:368
  105.4 6.6 %collective-permute-start.30 = (bf16[384,128]{1,0:T(8,128)(2,1)S(1)}, bf16[384,128]{1,0:T(8,128)(2,1)S(1)}, u32[]{:S(2)}, u32[]{:S(2)}) collective-permute-start(bf16[384,128]{1,0:T(8,128)(2,1)S(1)} %total.1.refs_0_), channel_id=1, source_target_pairs={{0,6},{1,7},{2,4},{3,5},{4,2},{5,3},{6,0},{7,1},{8,14},{9,15},{10,... | collective-permute-start | bytes 294920 | tf_op jit(solution)/shard_map/ppermute | solution.py:368
  107.6 6.9 %collective-permute-start.28 = (bf16[384,128]{1,0:T(8,128)(2,1)S(1)}, bf16[384,128]{1,0:T(8,128)(2,1)S(1)}, u32[]{:S(2)}, u32[]{:S(2)}) collective-permute-start(bf16[384,128]{1,0:T(8,128)(2,1)S(1)} %total.1.refs_0_), channel_id=1, source_target_pairs={{0,4},{1,5},{2,6},{3,7},{4,0},{5,1},{6,2},{7,3},{8,12},{9,13},{10,... | collective-permute-start | bytes 294920 | tf_op jit(solution)/shard_map/ppermute | solution.py:368
  107.6 6.9 %collective-permute-start.26 = (bf16[384,128]{1,0:T(8,128)(2,1)S(1)}, bf16[384,128]{1,0:T(8,128)(2,1)S(1)}, u32[]{:S(2)}, u32[]{:S(2)}) collective-permute-start(bf16[384,128]{1,0:T(8,128)(2,1)S(1)} %total.1.refs_0_), channel_id=1, source_target_pairs={{0,2},{1,3},{2,0},{3,1},{4,6},{5,7},{6,4},{7,5},{8,10},{9,11},{10,... | collective-permute-start | bytes 294920 | tf_op jit(solution)/shard_map/ppermute | solution.py:368
  109.9 5.2 %collective-permute-start.25 = (bf16[384,128]{1,0:T(8,128)(2,1)S(1)}, bf16[384,128]{1,0:T(8,128)(2,1)S(1)}, u32[]{:S(2)}, u32[]{:S(2)}) collective-permute-start(bf16[384,128]{1,0:T(8,128)(2,1)S(1)} %total.1.refs_0_), channel_id=1, source_target_pairs={{0,1},{1,0},{2,3},{3,2},{4,5},{5,4},{6,7},{7,6},{8,9},{9,8},{10,11... | collective-permute-start | bytes 294920 | tf_op jit(solution)/shard_map/ppermute | solution.py:368
  112.0 3.0 %collective-permute-start.31 = (bf16[384,128]{1,0:T(8,128)(2,1)S(1)}, bf16[384,128]{1,0:T(8,128)(2,1)S(1)}, u32[]{:S(2)}, u32[]{:S(2)}) collective-permute-start(bf16[384,128]{1,0:T(8,128)(2,1)S(1)} %collective-permute-done.30.refs_6_), channel_id=1, source_target_pairs={{0,1},{1,0},{2,3},{3,2},{4,5},{5,4},{6,7},{7,6},{8,9},{9,8},{10,11... | collective-permute-start | bytes 294920 | tf_op jit(solution)/shard_map/ppermute | solution.py:368
  114.6 1.3 %collective-permute-start.29 = (bf16[384,128]{1,0:T(8,128)(2,1)S(1)}, bf16[384,128]{1,0:T(8,128)(2,1)S(1)}, u32[]{:S(2)}, u32[]{:S(2)}) collective-permute-start(bf16[384,128]{1,0:T(8,128)(2,1)S(1)} %collective-permute-done.28.refs_4_), channel_id=1, source_target_pairs={{0,1},{1,0},{2,3},{3,2},{4,5},{5,4},{6,7},{7,6},{8,9},{9,8},{10,11... | collective-permute-start | bytes 294920 | tf_op jit(solution)/shard_map/ppermute | solution.py:368
  114.6 1.5 %collective-permute-start.27 = (bf16[384,128]{1,0:T(8,128)(2,1)S(1)}, bf16[384,128]{1,0:T(8,128)(2,1)S(1)}, u32[]{:S(2)}, u32[]{:S(2)}) collective-permute-start(bf16[384,128]{1,0:T(8,128)(2,1)S(1)} %collective-permute-done.26.refs_2_), channel_id=1, source_target_pairs={{0,1},{1,0},{2,3},{3,2},{4,5},{5,4},{6,7},{7,6},{8,9},{9,8},{10,11... | collective-permute-start | bytes 294920 | tf_op jit(solution)/shard_map/ppermute | solution.py:368

commit v4 on v3

--- a/solution.py
+++ b/solution.py
@@ -14,7 +14,6 @@
 TILE_LIMIT = 2048
 INDEX_TILE = 2048
 VMEM_BYTES = 24 * 1024 * 1024
-VMEM_MOST = 60 * 1024 * 1024
 
 FIRST_FIRST = (((0,), (0,)), ((), ()))
 LAST_LAST = (((1,), (1,)), ((), ()))
@@ -35,7 +34,10 @@
 
 def row_hot(rows, index):
     iota = lax.broadcasted_iota(jnp.int32, (rows, index.shape[1]), 0)
-    return (iota == index).astype(jnp.float32).astype(jnp.bfloat16)
+    if rows > BLOCK:
+        return (iota == index).astype(jnp.float32).astype(jnp.bfloat16)
+    match = iota.astype(jnp.bfloat16) == index.astype(jnp.bfloat16)
+    return jnp.where(match, jnp.bfloat16(1), jnp.bfloat16(0))
 
 
 def start_copies(pairs, sems):
@@ -48,6 +50,11 @@
     return copies
 
 
+def tile_copy(source, target, sems, step, tile):
+    span = pl.ds(pl.multiple_of(step * tile, tile), tile)
+    return pltpu.make_async_copy(source.at[:, span], target.at[:, span], sems.at[step])
+
+
 def feature_kernel(emb_hbm, down_hbm, projected_ref, feat_ref, emb_ref, down_ref, sems):
     for copy in start_copies(((emb_hbm, emb_ref), (down_hbm, down_ref)), sems):
         copy.wait()
@@ -56,14 +63,18 @@
     feat_ref[...] = silu(projected).astype(jnp.bfloat16)
 
 
-def index_kernel(members, in_ref, *refs):
-    slot_ref, rank_ref, hots, counts = refs[-4:]
+def index_kernel(members, in_hbm, *refs):
+    held = (len(refs) - 6) // 2
+    staged, (slot_ref, rank_ref), kept = refs[:held], refs[held : held + 2], refs[held + 2 : -4]
+    in_ref, hots, counts, sems = refs[-4:]
+    copy, *copies = start_copies(((in_hbm, in_ref), *zip(staged, kept)), sems)
     trips = in_ref.shape[1]
     rows = rank_ref.shape[0]
     turn = lax.axis_index("graph") * (rows // members * CAP)
     tile = math.gcd(trips, INDEX_TILE)
     spans = [slice(at, at + tile) for at in range(0, trips, tile)]
     counts[...] = jnp.zeros_like(counts)
+    copy.wait()
     for span in spans:
         incoming = in_ref[:, span] ^ turn
         hot = row_hot(CAP, incoming & (CAP - 1))
@@ -91,6 +102,8 @@
         iota = lax.broadcasted_iota(jnp.int32, found.shape, 0)
         found = jnp.sum(jnp.where(iota == place, found, 0.0), axis=0, keepdims=True)
         slot_ref[:, span] = (place // per) * CAP + found.astype(jnp.int32)
+    for copy in copies:
+        copy.wait()
 
 
 def rank_row(rank_ref, source, per):
@@ -109,17 +122,12 @@
     count_ref,
     slot_ref,
     rank_ref,
-    out_ref,
-    basis_ref,
-    bil_ref,
-    up_ref,
-    emb_ref,
-    target_ref,
     *refs,
 ):
+    out_ref, basis_ref, bil_ref, up_ref, emb_ref, target_ref, *refs = refs
     feat_refs, refs = refs[:members], refs[members:]
-    new_ref, near_ref, far_ref, gathered_ref, moment_ref, back_ref, *refs = refs
-    table, total, spread = refs
+    new_ref, near_ref, far_ref, gathered_ref, picked_hbm, back_ref, *refs = refs
+    table, total, spread, masked, picked_ref, sems = refs
     trips = slot_ref.shape[1]
     tile = spread.shape[1]
     width = bil_ref.shape[0]
@@ -147,24 +155,32 @@
                     high == chunk * per + part, picked[part * width : (part + 1) * width, :], feat
                 )
         feat = feat.astype(jnp.bfloat16)
+        picked_ref[:, span] = feat
+        tile_copy(picked_ref, picked_hbm, sems, step, tile).start()
         basis = basis_ref[:, span]
         for row in range(basis.shape[0]):
             spread[row * width : (row + 1) * width, :] = feat * basis[row : row + 1, :]
         place = step * tile + lax.broadcasted_iota(jnp.int32, (1, tile), 1)
-        outgoing = jnp.where(place < count, out_ref[:, span], -1)
-        total[...] += dot32(spread[...], row_hot(edges, outgoing), LAST_LAST)
+        outgoing = out_ref[:, span]
+        high = jnp.where(place < count, outgoing // BLOCK, -1)
+        mixed = dot32(bil_ref[...], spread[...])
+        for part in range(edges // BLOCK):
+            masked[part * width : (part + 1) * width, :] = jnp.where(
+                high == part, mixed, 0.0
+            ).astype(jnp.bfloat16)
+        total[...] += dot32(masked[...], row_hot(BLOCK, outgoing & (BLOCK - 1)), LAST_LAST)
         return carry
 
     lax.fori_loop(0, trips // tile, one_tile, 0)
+    for step in range(trips // tile):
+        tile_copy(picked_ref, picked_hbm, sems, step, tile).wait()
     turned = bil_ref[...].astype(jnp.float32).T
     back_ref[...] = jnp.concatenate(
         [turned[at : at + width] for at in range(0, turned.shape[0], width)], axis=1
     ).astype(jnp.bfloat16)
-    summed = total[...]
-    head = summed.astype(jnp.bfloat16)
-    rest = (summed - head.astype(jnp.float32)).astype(jnp.bfloat16)
-    moment_ref[...] = head
-    gathered = (dot32(bil_ref[...], head) + dot32(bil_ref[...], rest)).astype(jnp.bfloat16)
+    gathered = jnp.concatenate(
+        [total[at : at + width, :] for at in range(0, total.shape[0], width)], axis=1
+    ).astype(jnp.bfloat16)
     gathered_ref[...] = gathered
     update = dot32(gathered, up_ref[...], FIRST_FIRST)
     fresh = (emb_ref[...].astype(jnp.float32) + silu(update)).astype(jnp.bfloat16)
@@ -207,15 +223,14 @@
     back_ref,
     up_ref,
     gathered_ref,
-    moment_ref,
     grad_edge_ref,
     target_ref,
     atom_weight_ref,
     *refs,
 ):
     pair_refs, refs = refs[:members], refs[members:]
-    grad_new_ref, up_grad_ref, bil_grad_ref, slab_ref, parts_ref, *refs = refs
-    table, spread, masked, total, sums, grads, atom_grad = refs
+    grad_new_ref, up_grad_ref, mixed_hbm, slab_ref, parts_ref, *refs = refs
+    table, spread, masked, total, sums, grads, atom_grad, mixed_ref, sems = refs
     trips = slot_ref.shape[1]
     tile = spread.shape[1]
     width = back_ref.shape[0]
@@ -243,7 +258,6 @@
     grad_update = (grad_new * silu_slope(update)).astype(jnp.bfloat16)
     up_grad_ref[...] = dot32(gathered_ref[...], grad_update).astype(jnp.bfloat16)
     grad_gathered = dot32(up_ref[...], grad_update, LAST_LAST).astype(jnp.bfloat16)
-    bil_grad_ref[...] = dot32(grad_gathered, moment_ref[...], LAST_LAST).astype(jnp.bfloat16)
     for part in range(edges // BLOCK):
         table[part * width : (part + 1) * width, :] = grad_gathered[
             :, part * BLOCK : (part + 1) * BLOCK
@@ -259,6 +273,8 @@
         for part in range(edges // BLOCK):
             grad = jnp.where(high == part, picked[part * width : (part + 1) * width, :], grad)
         grad = grad.astype(jnp.bfloat16)
+        mixed_ref[:, span] = grad
+        tile_copy(mixed_ref, mixed_hbm, sems, step, tile).start()
         basis = basis_ref[:, span]
         for row in range(basis.shape[0]):
             spread[row * width : (row + 1) * width, :] = grad * basis[row : row + 1, :]
@@ -273,6 +289,8 @@
         return carry
 
     lax.fori_loop(0, trips // tile, one_tile, 0)
+    for step in range(trips // tile):
+        tile_copy(mixed_ref, mixed_hbm, sems, step, tile).wait()
     per = rank_ref.shape[0] // members
     for source in range(members):
         group, lane = divmod(source * CAP, BLOCK)
@@ -280,6 +298,30 @@
         ranks = rank_ref[source * per : (source + 1) * per, :]
         spare = jnp.zeros((parts_ref.shape[1] - width - per, CAP), jnp.float32)
         parts_ref[me ^ source] = jnp.concatenate([piece, ranks, spare], axis=0).astype(jnp.bfloat16)
+
+
+def weight_kernel(basis_ref, picked_hbm, mixed_hbm, out_ref, picked, mixed, spread, total, sems):
+    width, trips = picked.shape
+    tile = spread.shape[1]
+    steps = trips // tile
+    for step in range(steps):
+        tile_copy(picked_hbm, picked, sems.at[0], step, tile).start()
+        tile_copy(mixed_hbm, mixed, sems.at[1], step, tile).start()
+    total[...] = jnp.zeros_like(total)
+
+    def one_tile(step, carry):
+        span = pl.ds(pl.multiple_of(step * tile, tile), tile)
+        tile_copy(picked_hbm, picked, sems.at[0], step, tile).wait()
+        tile_copy(mixed_hbm, mixed, sems.at[1], step, tile).wait()
+        feat = picked[:, span]
+        basis = basis_ref[:, span]
+        for row in range(basis.shape[0]):
+            spread[row * width : (row + 1) * width, :] = feat * basis[row : row + 1, :]
+        total[...] += dot32(spread[...], mixed[:, span], LAST_LAST)
+        return carry
+
+    lax.fori_loop(0, steps, one_tile, 0)
+    out_ref[...] = total[...].T.astype(jnp.bfloat16)
 
 
 def edge_kernel(
@@ -364,6 +406,10 @@
 SMEM = pl.BlockSpec(memory_space=pltpu.SMEM)
 
 
+def hbm(value):
+    return pltpu.with_memory_space_constraint(value, pltpu.HBM)
+
+
 def swap(value, members, mask, axis="graph"):
     return lax.ppermute(value, axis, [(at, at ^ mask) for at in range(members)])
 
@@ -389,6 +435,10 @@
 
 def params(limit=VMEM_BYTES):
     return pltpu.CompilerParams(vmem_limit_bytes=limit)
+
+
+def cost(flops):
+    return pl.CostEstimate(flops=flops, bytes_accessed=1 << 20, transcendentals=0)
 
 
 def body(
@@ -431,57 +481,62 @@
             pltpu.VMEM(down_rows.shape, b16),
             pltpu.SemaphoreType.DMA((2,)),
         ],
-        compiler_params=params(VMEM_MOST),
+        compiler_params=params(),
+        cost_estimate=cost(16 * edge_rows.size * width),
         name="features",
-    )(edge_rows, down_rows)
+    )(hbm(edge_rows), hbm(down_rows))
     rank_rows = members * edge_dev // CAP
     staged = (trip_out, basis, bil_rows, w_up, edge_rows, edge_target)
-    slot, rank = pl.pallas_call(
+    slot, rank, *kept = pl.pallas_call(
         functools.partial(index_kernel, members),
-        in_specs=[VMEM] + [pl.BlockSpec(memory_space=pl.ANY)] * len(staged),
-        out_shape=(shaped(trip_in.shape, jnp.int32), shaped((rank_rows, CAP), f32)),
+        in_specs=[HBM] * (1 + len(staged)),
+        out_shape=(
+            shaped(trip_in.shape, jnp.int32),
+            shaped((rank_rows, CAP), f32),
+            *[shaped(value.shape, value.dtype) for value in staged],
+        ),
         scratch_shapes=[
+            pltpu.VMEM(trip_in.shape, jnp.int32),
             pltpu.VMEM((CAP, trips), b16),
             pltpu.VMEM((rank_rows, CAP), f32),
+            pltpu.SemaphoreType.DMA((1 + len(staged),)),
         ],
         compiler_params=params(),
-        cost_estimate=pl.CostEstimate(
-            flops=8 * CAP * CAP * trips, bytes_accessed=8 * trips, transcendentals=0
-        ),
+        cost_estimate=cost(8 * CAP * CAP * trips),
         name="slots",
-    )(trip_in, *staged)
-    feats, (slot, rank) = gather_near(feat, members, (slot, rank))
+    )(*[hbm(value) for value in (trip_in, *staged)])
+    feats, (slot, rank, *kept) = gather_near(feat, members, (slot, rank, *kept))
 
     named_rows = members * CAP // BLOCK * width
     half = shaped((members // 2, atom_dev, model), b16)
-    edge_new, near, far, gathered, moment, back = pl.pallas_call(
+    edge_new, near, far, gathered, picked, back = pl.pallas_call(
         functools.partial(forward_kernel, members),
-        in_specs=[SMEM] + [VMEM] * (8 + members),
+        in_specs=[SMEM] + [VMEM] * (2 + len(kept) + members),
+        out_specs=(VMEM, VMEM, VMEM, VMEM, HBM, VMEM),
         out_shape=(
             shaped(edge_rows.shape, b16),
             half,
             half,
             shaped((width, edge_dev), b16),
-            shaped((w_bil.shape[0], edge_dev), b16),
+            pltpu.HBM((width, trips), b16),
             shaped((width, w_bil.shape[0]), b16),
         ),
         scratch_shapes=[
             pltpu.VMEM((named_rows, BLOCK), b16),
-            pltpu.VMEM((w_bil.shape[0], edge_dev), f32),
+            pltpu.VMEM((edge_dev // BLOCK * width, BLOCK), f32),
             pltpu.VMEM((w_bil.shape[0], tile), b16),
+            pltpu.VMEM((edge_dev // BLOCK * width, tile), b16),
+            pltpu.VMEM((width, trips), b16),
+            pltpu.SemaphoreType.DMA((trips // tile,)),
         ],
         compiler_params=params(),
+        cost_estimate=cost(12 * w_bil.size * trips),
         name="forward_triplets",
     )(
         trip_count,
         slot,
         rank,
-        trip_out,
-        basis,
-        bil_rows,
-        w_up,
-        edge_rows,
-        edge_target,
+        *kept,
         *feats,
     )
 
@@ -491,18 +546,20 @@
         atom_kernel,
         out_shape=(atom_block, shaped((2, atom_dev, model), b16)),
         compiler_params=params(),
+        cost_estimate=cost(16 * atom_dev * w_atom.size),
         name="atoms",
     )(atom_emb[0], grad_atom[0], w_atom, *sums)
     pairs, _ = gather_near(pair, members)
 
     piece_rows = width + -(-(edge_dev // CAP) // 16) * 16
-    grad_new, wup_term, wbil_term, slab, feat_parts = pl.pallas_call(
+    grad_new, wup_term, mixed, slab, feat_parts = pl.pallas_call(
         functools.partial(backward_kernel, members),
-        in_specs=[SMEM] + [VMEM] * (11 + members),
+        in_specs=[SMEM] + [VMEM] * (10 + members),
+        out_specs=(VMEM, VMEM, HBM, VMEM, VMEM),
         out_shape=(
             shaped(edge_rows.shape, f32),
             shaped(w_up.shape, b16),
-            shaped((width, w_bil.shape[0]), b16),
+            pltpu.HBM((width, trips), b16),
             shaped((model // CAP, model // members, CAP), b16),
             shaped((members, piece_rows, CAP), b16),
         ),
@@ -514,25 +571,43 @@
             pltpu.VMEM((members * atom_dev, model), b16),
             pltpu.VMEM((members * atom_dev, model), b16),
             pltpu.VMEM((model, model), f32),
+            pltpu.VMEM((width, trips), b16),
+            pltpu.SemaphoreType.DMA((trips // tile,)),
         ],
         compiler_params=params(),
+        cost_estimate=cost(12 * w_bil.size * trips),
         name="backward_triplets",
     )(
         trip_count,
         slot,
-        trip_out,
-        basis,
+        kept[0],
+        kept[1],
         rank,
         back,
-        w_up,
+        kept[3],
         gathered,
-        moment,
         grad_edge[0],
-        edge_target,
+        kept[5],
         w_atom,
         *pairs,
     )
     feat_parts = lax.all_to_all(feat_parts, "graph", 0, 0, tiled=True)
+    wide = math.gcd(trips, 2 * tile)
+    wbil_term = pl.pallas_call(
+        weight_kernel,
+        in_specs=[VMEM, HBM, HBM],
+        out_shape=shaped((width, w_bil.shape[0]), b16),
+        scratch_shapes=[
+            pltpu.VMEM((width, trips), b16),
+            pltpu.VMEM((width, trips), b16),
+            pltpu.VMEM((w_bil.shape[0], wide), b16),
+            pltpu.VMEM((w_bil.shape[0], width), f32),
+            pltpu.SemaphoreType.DMA((2, trips // wide)),
+        ],
+        compiler_params=params(),
+        cost_estimate=cost(8 * w_bil.size * trips),
+        name="bilinear_weights",
+    )(kept[1], hbm(picked), hbm(mixed))
     flat_rows = width * (2 * model + w_bil.shape[0]) // CAP
     piece = shaped((members // 2, flat_rows // members, CAP), b16)
     grad_in, near, far = pl.pallas_call(
@@ -540,6 +615,7 @@
         out_shape=(shaped(edge_rows.shape, f32), piece, piece),
         scratch_shapes=[pltpu.VMEM((flat_rows, CAP), b16)],
         compiler_params=params(),
+        cost_estimate=cost(64 * edge_rows.size * width),
         name="edges",
     )(feat_parts, projected, edge_rows, down_rows, grad_new, wbil_term, wup_term)
 

time: 118 us -> 110 us (0.932)
  blocking collectives: 10.5 us -> 0 us
  starting transfers between devices: 29.5 us -> 33.4 us
  local copies, waits for them, and re-layouts: 3.67 us -> 0.04 us
  Pallas kernels: 47 us -> 48.7 us
  waiting for transfers between devices: 25 us -> 26.5 us
    pallas_call x1 -> x2, Pallas kernels: 3.28 us -> 14.9 us  [the longest x1 10.8 us: body(): pl.pallas_call(weight_kernel, in_specs=[VMEM, HBM, HBM], out_shape=shaped...]
    all_to_all x1 -> x0, blocking collectives: 10.5 us -> none  [body(): feat_parts = lax.all_to_all(feat_parts, 'graph', 0, 0, tiled=True)]
    pallas_call x1, Pallas kernels: 24.6 us -> 15.1 us  [body(): pl.pallas_call(functools.partial(forward_kernel, members), in_specs=[SMEM...]
    unnamed x32 -> x12, local copies, waits for them, and re-layouts: 3.67 us -> 0.04 us
    all_to_all x0 -> x1, starting transfers between devices: none -> 3.57 us  [body(): feat_parts = lax.all_to_all(feat_parts, 'graph', 0, 0, tiled=True)]
    ppermute x32, waiting for transfers between devices: 25 us -> 26.5 us  [swap(): return lax.ppermute(value, axis, [(at, at ^ mask) for at in range(members)])]
  transfers between devices with their start and end apart: 32 -> 33, of which waited for: 19 -> 19; matrix products, arithmetic and copies ran while one was open for 0% -> 0% of each run, Pallas kernels for 3% -> 14%
where the time goes in v4:
time: 110 us
  Pallas kernels  48.7 us (44%)
  starting transfers between devices  33.4 us (30%)
  waiting for transfers between devices  26.5 us (24%)
  between operations  1.47 us (1%)
    ppermute x32, starting transfers between devices, swap(): return lax.ppermute(value, axis, [(at, at ^ mask) for at in range(members)])  29.9 us
    ppermute x32, waiting for transfers between devices, swap(): return lax.ppermute(value, axis, [(at, at ^ mask) for at in range(members)])  26.5 us
    pallas_call x1, Pallas kernels, body(): pl.pallas_call(functools.partial(forward_kernel, members), in_specs=[SMEM...  15.1 us
    pallas_call x1, Pallas kernels, body(): pl.pallas_call(functools.partial(backward_kernel, members), in_specs=[SME...  13.5 us
    pallas_call x1, Pallas kernels, body(): pl.pallas_call(weight_kernel, in_specs=[VMEM, HBM, HBM], out_shape=shaped...  10.8 us
    pallas_call x1, Pallas kernels, body(): pl.pallas_call(functools.partial(index_kernel, members), in_specs=[HBM] *...  4.08 us
    all_to_all x1, starting transfers between devices, body(): feat_parts = lax.all_to_all(feat_parts, 'graph', 0, 0, tiled=True)  3.57 us
  transfers between devices with their start and end apart: 33, of which 19 were waited for; matrix products, arithmetic and copies ran while one was open for 0% of the time, Pallas kernels for 14%

profile of v4, /device:TPU:0, one launch (start us, length us, event | category | flops | bytes accessed | tf_op | source)
XLA Modules:
  0.0 110.1 jit_solution(11960384541349816898)
XLA Ops:
  0.6 1.4 %features.1 = (f32[64,512]{1,0:T(8,128)S(1)}, bf16[64,512]{1,0:T(8,128)(2,1)S(1)}) custom-call(bf16[512,512]{1,0:T(8,128)(2,1)} %bitcast.15, bf16[64,512]{1,0:T(8,128)(2,1)} %bitcast.18), custom_call_target="tpu_custom_call" | custom-call | flops 268435456 | bytes 1048576 | tf_op jit(solution)/shard_map/features/pallas_call | solution.py:472
  2.0 5.1 %collective-permute-start.2 = (bf16[64,512]{1,0:T(8,128)(2,1)S(1)}, bf16[64,512]{1,0:T(8,128)(2,1)S(1)}, u32[]{:S(2)}, u32[]{:S(2)}) collective-permute-start(bf16[64,512]{1,0:T(8,128)(2,1)S(1)} %get-tuple-element.74.refs_6_), channel_id=1, source_target_pairs={{0,6},{1,7},{2,4},{3,5},{4,2},{5,3},{6,0},{7,1},{8,14},{9,15},{10,... | collective-permute-start | bytes 196616 | tf_op jit(solution)/shard_map/ppermute | solution.py:414
  7.1 0.0 collective-permute-start.1
  7.1 0.6 collective-permute-start
  7.8 4.1 %slots.1 = (s32[1,16384]{1,0:T(1,128)S(1)}, f32[32,128]{1,0:T(8,128)S(1)}, s32[1,16384]{1,0:T(1,128)S(1)}, bf16[16,16384]{1,0:T(8,128)(2,1)S(1)}, bf16[64,1024]{...) custom-call(s32[1,16384]{1,0:T(1,128)} %in_hbm.1, ...), custom_call_target="tpu_custom_call" | custom-call | flops 2147483648 | bytes 1048576 | tf_op jit(solution)/shard_map/slots/pallas_call | solution.py:490
  11.9 0.0 collective-permute-done.2.refs_12_
  11.9 0.9 collective-permute-done.1.refs_10_
  12.7 0.0 collective-permute-done.refs_8_
  12.7 0.0 collective-permute-start.3
  12.7 0.5 collective-permute-start.4
  13.3 0.0 collective-permute-start.5
  13.3 0.5 collective-permute-start.6
  14.4 0.0 copy-start
  14.4 0.0 copy-start.1
  14.4 0.0 copy-start.2
  14.5 0.0 copy-start.3
  14.5 0.0 collective-permute-done.3.refs_7_
  14.5 0.0 collective-permute-done.4.refs_9_
  14.5 0.0 collective-permute-done.5.refs_11_
  14.5 0.2 collective-permute-done.6.refs_13_
  14.7 15.1 %forward_triplets.1 = (bf16[512,512]{1,0:T(8,128)(2,1)}, bf16[4,32,512]{2,1,0:T(8,128)(2,1)S(1)}, bf16[4,32,512]{2,1,0:T(8,128)(2,1)S(1)}, bf16[64,512]{1,0:T(8,...) custom-call(s32[1,1]{1,0:T(1,128)S(6)} %copy.20.count_ref, ...), custom_call_target="tpu_custom_call" | custom-call | flops 12884901888 | bytes 1048576 | tf_op jit(solution)/shard_map/forward_triplets/pallas_call | solution.py:512
  29.8 0.4 collective-permute-start.7
  30.2 1.0 collective-permute-done.7.far_ref
  31.2 1.2 %collective-permute-start.8 = (bf16[32,512]{1,0:T(8,128)(2,1)S(1)}, bf16[32,512]{1,0:T(8,128)(2,1)S(1)}, u32[]{:S(2)}, u32[]{:S(2)}) collective-permute-start(bf16[32,512]{1,0:T(8,128)(2,1)S(1)} %get-tuple-element.82), channel_id=1, source_target_pairs={{0,2},{1,3},{2,0},{3,1},{4,6},{5,7},{6,4},{7,5},{8,10},{9,11},{10,... | collective-permute-start | bytes 98312 | tf_op jit(solution)/shard_map/ppermute | solution.py:414
  32.4 2.5 %collective-permute-start.9 = (bf16[32,512]{1,0:T(8,128)(2,1)S(1)}, bf16[32,512]{1,0:T(8,128)(2,1)S(1)}, u32[]{:S(2)}, u32[]{:S(2)}) collective-permute-start(bf16[32,512]{1,0:T(8,128)(2,1)S(1)} %get-tuple-element.83), channel_id=1, source_target_pairs={{0,4},{1,5},{2,6},{3,7},{4,0},{5,1},{6,2},{7,3},{8,12},{9,13},{10,... | collective-permute-start | bytes 98312 | tf_op jit(solution)/shard_map/ppermute | solution.py:414
  34.9 0.8 collective-permute-start.10
  35.7 2.0 %collective-permute-done.9.refs_2_ = bf16[32,512]{1,0:T(8,128)(2,1)S(1)} collective-permute-done((bf16[32,512]{1,0:T(8,128)(2,1)S(1)}, bf16[32,512]{1,0:T(8,128)(2,1)S(1)}, u32[]{:S(2)}, u32[]{:S(2)}) %collective-permute-start.9) | collective-permute-done | bytes 32800 | tf_op jit(solution)/shard_map/ppermute | solution.py:414
  37.7 2.9 %collective-permute-done.10.refs_3_ = bf16[32,512]{1,0:T(8,128)(2,1)S(1)} collective-permute-done((bf16[32,512]{1,0:T(8,128)(2,1)S(1)}, bf16[32,512]{1,0:T(8,128)(2,1)S(1)}, u32[]{:S(2)}, u32[]{:S(2)}) %collective-permute-start.10) | collective-permute-done | bytes 32800 | tf_op jit(solution)/shard_map/ppermute | solution.py:414
  40.6 0.9 atoms.1
  41.4 0.8 collective-permute-start.16
  42.3 3.5 %collective-permute-start.12 = (bf16[2,32,512]{2,1,0:T(8,128)(2,1)S(1)}, bf16[2,32,512]{2,1,0:T(8,128)(2,1)S(1)}, u32[]{:S(2)}, u32[]{:S(2)}) collective-permute-start(bf16[2,32,512]{2,1,0:T(8,128)(2,1)S(1)} %get-tuple-element.88.refs_0_), channel_id=1, source_target_pairs={{0,2},{1,3},{2,0},{3,1},{4,6},{5,7},{6,4},{7,5},{8,10},{9,11},{10,... | collective-permute-start | bytes 196616 | tf_op jit(solution)/shard_map/ppermute | solution.py:414
  45.8 1.8 %collective-permute-done.16.refs_6_ = bf16[2,32,512]{2,1,0:T(8,128)(2,1)S(1)} collective-permute-done((bf16[2,32,512]{2,1,0:T(8,128)(2,1)S(1)}, bf16[2,32,512]{2,1,0:T(8,128)(2,1)S(1)}, u32[]{:S(2)}, u32[]{:S(2)}) %collective-permute-start.16) | collective-permute-done | bytes 65568 | tf_op jit(solution)/shard_map/ppermute | solution.py:414
  47.6 1.2 %collective-permute-done.14.refs_4_ = bf16[2,32,512]{2,1,0:T(8,128)(2,1)S(1)} collective-permute-done((bf16[2,32,512]{2,1,0:T(8,128)(2,1)S(1)}, bf16[2,32,512]{2,1,0:T(8,128)(2,1)S(1)}, u32[]{:S(2)}, u32[]{:S(2)}) %collective-permute-start.14) | collective-permute-done | bytes 65568 | tf_op jit(solution)/shard_map/ppermute | solution.py:414
  48.9 0.5 collective-permute-start.13
  49.4 0.7 collective-permute-done.15.refs_5_
  50.1 0.2 collective-permute-done.13.refs_3_
  50.3 13.5 %backward_triplets.1 = (f32[512,512]{1,0:T(8,128)S(1)}, bf16[64,512]{1,0:T(8,128)(2,1)S(1)}, bf16[64,16384]{1,0:T(8,128)(2,1)}, bf16[4,64,128]{2,1,0:T(8,128)(2,1)S(1)}, bf16[8,80,128]{2,1,0:T(8,128)(2,1)}) custom-call(s32[1,1]{1,0:T(1,128)S(6)} %copy.20.count_ref, s32[1,16384]{1,0:T(1,128)S(1)} %get-tuple-element.66.slot_ref, ...), custom_call_target="tpu_custom_call" | custom-call | flops 12884901888 | bytes 1048576 | tf_op jit(solution)/shard_map/backward_triplets/pallas_call | solution.py:555
  63.8 3.6 %all-to-all-start = ((bf16[8,80,128]{2,1,0:T(8,128)(2,1)}), bf16[8,80,128]{2,1,0:T(8,128)(2,1)S(1)}, u32[]{:S(2)}, u32[]{:S(2)}) async-start(bf16[8,80,128]{2,1,0:T(8,128)(2,1)} %get-tuple-element.89), calls=%async_computation | async-start | bytes 327680 | tf_op jit(solution)/shard_map/all_to_all | solution.py:594
  67.4 0.0 copy-start.4
  67.4 0.0 copy-start.5
  67.4 10.8 %bilinear_weights.1.bil_grad_ref = bf16[64,1024]{1,0:T(8,128)(2,1)S(1)} custom-call(bf16[16,16384]{1,0:T(8,128)(2,1)S(1)} %get-tuple-element.69.refs_1_.basis_ref, bf16[64,16384]{1,0:T(8,128)(2,1)} %get-tuple-element.92.picked_hbm, bf16[64,16384]{1,0:T(8,128)(2,1)} %get-tuple-element.93.mixed_hbm), custom_call_target="tpu_custom_call" | custom-call | flops 8589934592 | bytes 1048576 | tf_op jit(solution)/shard_map/bilinear_weights/pallas_call | solution.py:596
  78.2 1.6 %edges.1 = (f32[512,512]{1,0:T(8,128)}, bf16[4,128,128]{2,1,0:T(8,128)(2,1)S(1)}, bf16[4,128,128]{2,1,0:T(8,128)(2,1)S(1)}) custom-call(bf16[8,80,128]{2,1,0:T(8,128)(2,1)S(1)} %all-to-all-done.parts_ref, f32[64,512]{1,0:T(8,128)S(1)} %get-tuple-element.90.projected_ref, bf16[512,512]{1,0:T(8,128)(2,1)S(1)} %bitcast.17, bf16[64,512]{1,0:T(8,128)(2,1)S(1)} %bitcast.19, ...), custom_call_target="tpu_custom_call" | custom-call | flops 1073741824 | bytes 1048576 | tf_op jit(solution)/shard_map/edges/pallas_call | solution.py:613
  79.8 0.3 collective-permute-start.18
  80.1 1.0 collective-permute-done.18.far_ref
  81.2 1.8 %collective-permute-start.19 = (bf16[128,128]{1,0:T(8,128)(2,1)S(1)}, bf16[128,128]{1,0:T(8,128)(2,1)S(1)}, u32[]{:S(2)}, u32[]{:S(2)}) collective-permute-start(bf16[128,128]{1,0:T(8,128)(2,1)S(1)} %get-tuple-element.100), channel_id=1, source_target_pairs={{0,2},{1,3},{2,0},{3,1},{4,6},{5,7},{6,4},{7,5},{8,10},{9,11},{10,... | collective-permute-start | bytes 98312 | tf_op jit(solution)/shard_map/ppermute | solution.py:414
  83.0 2.4 %collective-permute-start.20 = (bf16[128,128]{1,0:T(8,128)(2,1)S(1)}, bf16[128,128]{1,0:T(8,128)(2,1)S(1)}, u32[]{:S(2)}, u32[]{:S(2)}) collective-permute-start(bf16[128,128]{1,0:T(8,128)(2,1)S(1)} %get-tuple-element.101), channel_id=1, source_target_pairs={{0,4},{1,5},{2,6},{3,7},{4,0},{5,1},{6,2},{7,3},{8,12},{9,13},{10,... | collective-permute-start | bytes 98312 | tf_op jit(solution)/shard_map/ppermute | solution.py:414
  85.4 0.3 collective-permute-start.21
  85.7 2.6 %collective-permute-done.20.refs_2_ = bf16[128,128]{1,0:T(8,128)(2,1)S(1)} collective-permute-done((bf16[128,128]{1,0:T(8,128)(2,1)S(1)}, bf16[128,128]{1,0:T(8,128)(2,1)S(1)}, u32[]{:S(2)}, u32[]{:S(2)}) %collective-permute-start.20) | collective-permute-done | bytes 32800 | tf_op jit(solution)/shard_map/ppermute | solution.py:414
  88.3 2.8 %collective-permute-done.21.refs_3_ = bf16[128,128]{1,0:T(8,128)(2,1)S(1)} collective-permute-done((bf16[128,128]{1,0:T(8,128)(2,1)S(1)}, bf16[128,128]{1,0:T(8,128)(2,1)S(1)}, u32[]{:S(2)}, u32[]{:S(2)}) %collective-permute-start.21) | collective-permute-done | bytes 32800 | tf_op jit(solution)/shard_map/ppermute | solution.py:414
  91.1 2.5 %collective-permute-start.24 = (bf16[384,128]{1,0:T(8,128)(2,1)S(1)}, bf16[384,128]{1,0:T(8,128)(2,1)S(1)}, u32[]{:S(2)}, u32[]{:S(2)}) collective-permute-start(bf16[384,128]{1,0:T(8,128)(2,1)S(1)} %share.1.refs_0_), channel_id=1, source_target_pairs={{0,24},{8,16},{16,8},{24,0},{1,25},{9,17},{17,9},{25,1},{2,26},{10... | collective-permute-start | bytes 294920 | tf_op jit(solution)/shard_map/ppermute | solution.py:414
  93.7 0.5 collective-permute-start.23
  94.2 0.5 collective-permute-start.22
  94.7 3.1 %collective-permute-done.24.refs_3_ = bf16[384,128]{1,0:T(8,128)(2,1)S(1)} collective-permute-done((bf16[384,128]{1,0:T(8,128)(2,1)S(1)}, bf16[384,128]{1,0:T(8,128)(2,1)S(1)}, u32[]{:S(2)}, u32[]{:S(2)}) %collective-permute-start.24) | collective-permute-done | bytes 98336 | tf_op jit(solution)/shard_map/ppermute | solution.py:414
  97.8 0.7 collective-permute-done.23.refs_2_
  98.6 0.2 collective-permute-done.22.refs_1_
  98.8 0.1 total.1.refs_0_
  98.8 0.5 collective-permute-start.30
  99.3 4.0 %collective-permute-start.26 = (bf16[384,128]{1,0:T(8,128)(2,1)S(1)}, bf16[384,128]{1,0:T(8,128)(2,1)S(1)}, u32[]{:S(2)}, u32[]{:S(2)}) collective-permute-start(bf16[384,128]{1,0:T(8,128)(2,1)S(1)} %total.1.refs_0_), channel_id=1, source_target_pairs={{0,2},{1,3},{2,0},{3,1},{4,6},{5,7},{6,4},{7,5},{8,10},{9,11},{10,... | collective-permute-start | bytes 294920 | tf_op jit(solution)/shard_map/ppermute | solution.py:414
  103.3 2.2 %collective-permute-done.30.refs_6_ = bf16[384,128]{1,0:T(8,128)(2,1)S(1)} collective-permute-done((bf16[384,128]{1,0:T(8,128)(2,1)S(1)}, bf16[384,128]{1,0:T(8,128)(2,1)S(1)}, u32[]{:S(2)}, u32[]{:S(2)}) %collective-permute-start.30) | collective-permute-done | bytes 98336 | tf_op jit(solution)/shard_map/ppermute | solution.py:414
  105.5 2.0 %collective-permute-done.28.refs_4_ = bf16[384,128]{1,0:T(8,128)(2,1)S(1)} collective-permute-done((bf16[384,128]{1,0:T(8,128)(2,1)S(1)}, bf16[384,128]{1,0:T(8,128)(2,1)S(1)}, u32[]{:S(2)}, u32[]{:S(2)}) %collective-permute-start.28) | collective-permute-done | bytes 98336 | tf_op jit(solution)/shard_map/ppermute | solution.py:414
  107.5 0.5 collective-permute-start.27
  108.0 0.8 collective-permute-done.29.refs_5_
  108.8 0.2 collective-permute-done.27.refs_3_
  108.9 1.2 %weights.1 = (f32[64,512]{1,0:T(8,128)}, f32[64,1024]{1,0:T(8,128)}, f32[64,512]{1,0:T(8,128)}, f32[512,512]{1,0:T(8,128)}) custom-call(bf16[384,128]{1,0:T(8,128)(2,1)S(1)} %total.1.refs_0_, bf16[384,128]{1,0:T(8,128)(2,1)S(1)} %collective-permute-done.25.refs_1_, bf16[384,128]{1,0:T(8,128)(2,1)S(1)} %collective-permute-done.26.refs_2_, ...), custom_call_target="tpu_custom_call" | custom-call | tf_op jit(solution)/shard_map/weights/pallas_call | solution.py:638
  (26 shorter events, 0.1 us)
Async XLA Ops:
  2.0 9.9 %collective-permute-start.2 = (bf16[64,512]{1,0:T(8,128)(2,1)S(1)}, bf16[64,512]{1,0:T(8,128)(2,1)S(1)}, u32[]{:S(2)}, u32[]{:S(2)}) collective-permute-start(bf16[64,512]{1,0:T(8,128)(2,1)S(1)} %get-tuple-element.74.refs_6_), channel_id=1, source_target_pairs={{0,6},{1,7},{2,4},{3,5},{4,2},{5,3},{6,0},{7,1},{8,14},{9,15},{10,... | collective-permute-start | bytes 196616 | tf_op jit(solution)/shard_map/ppermute | solution.py:414
  7.1 5.6 %collective-permute-start.1 = (bf16[64,512]{1,0:T(8,128)(2,1)S(1)}, bf16[64,512]{1,0:T(8,128)(2,1)S(1)}, u32[]{:S(2)}, u32[]{:S(2)}) collective-permute-start(bf16[64,512]{1,0:T(8,128)(2,1)S(1)} %get-tuple-element.74.refs_6_), channel_id=1, source_target_pairs={{0,4},{1,5},{2,6},{3,7},{4,0},{5,1},{6,2},{7,3},{8,12},{9,13},{10,... | collective-permute-start | bytes 196616 | tf_op jit(solution)/shard_map/ppermute | solution.py:414
  7.1 5.6 %collective-permute-start = (bf16[64,512]{1,0:T(8,128)(2,1)S(1)}, bf16[64,512]{1,0:T(8,128)(2,1)S(1)}, u32[]{:S(2)}, u32[]{:S(2)}) collective-permute-start(bf16[64,512]{1,0:T(8,128)(2,1)S(1)} %get-tuple-element.74.refs_6_), channel_id=1, source_target_pairs={{0,2},{1,3},{2,0},{3,1},{4,6},{5,7},{6,4},{7,5},{8,10},{9,11},{10,... | collective-permute-start | bytes 196616 | tf_op jit(solution)/shard_map/ppermute | solution.py:414
  12.7 1.7 %collective-permute-start.3 = (bf16[64,512]{1,0:T(8,128)(2,1)S(1)}, bf16[64,512]{1,0:T(8,128)(2,1)S(1)}, u32[]{:S(2)}, u32[]{:S(2)}) collective-permute-start(bf16[64,512]{1,0:T(8,128)(2,1)S(1)} %get-tuple-element.74.refs_6_), channel_id=1, source_target_pairs={{0,1},{1,0},{2,3},{3,2},{4,5},{5,4},{6,7},{7,6},{8,9},{9,8},{10,11... | collective-permute-start | bytes 196616 | tf_op jit(solution)/shard_map/ppermute | solution.py:414
  12.7 1.7 %collective-permute-start.4 = (bf16[64,512]{1,0:T(8,128)(2,1)S(1)}, bf16[64,512]{1,0:T(8,128)(2,1)S(1)}, u32[]{:S(2)}, u32[]{:S(2)}) collective-permute-start(bf16[64,512]{1,0:T(8,128)(2,1)S(1)} %collective-permute-done.refs_8_), channel_id=1, source_target_pairs={{0,1},{1,0},{2,3},{3,2},{4,5},{5,4},{6,7},{7,6},{8,9},{9,8},{10,11... | collective-permute-start | bytes 196616 | tf_op jit(solution)/shard_map/ppermute | solution.py:414
  13.3 1.3 %collective-permute-start.5 = (bf16[64,512]{1,0:T(8,128)(2,1)S(1)}, bf16[64,512]{1,0:T(8,128)(2,1)S(1)}, u32[]{:S(2)}, u32[]{:S(2)}) collective-permute-start(bf16[64,512]{1,0:T(8,128)(2,1)S(1)} %collective-permute-done.1.refs_10_), channel_id=1, source_target_pairs={{0,1},{1,0},{2,3},{3,2},{4,5},{5,4},{6,7},{7,6},{8,9},{9,8},{10,11... | collective-permute-start | bytes 196616 | tf_op jit(solution)/shard_map/ppermute | solution.py:414
  13.3 1.4 %collective-permute-start.6 = (bf16[64,512]{1,0:T(8,128)(2,1)S(1)}, bf16[64,512]{1,0:T(8,128)(2,1)S(1)}, u32[]{:S(2)}, u32[]{:S(2)}) collective-permute-start(bf16[64,512]{1,0:T(8,128)(2,1)S(1)} %collective-permute-done.2.refs_12_), channel_id=1, source_target_pairs={{0,1},{1,0},{2,3},{3,2},{4,5},{5,4},{6,7},{7,6},{8,9},{9,8},{10,11... | collective-permute-start | bytes 196616 | tf_op jit(solution)/shard_map/ppermute | solution.py:414
  14.4 26.2 %copy-start = (bf16[512,512]{1,0:T(8,128)(2,1)S(1)}, bf16[512,512]{1,0:T(8,128)(2,1)}, u32[]{:S(2)}) copy-start(bf16[512,512]{1,0:T(8,128)(2,1)} %atom_weight_ref.1) | copy-start | bytes 1572868
  14.4 26.1 %copy-start.1 = (bf16[1,32,512]{2,1,0:T(8,128)(2,1)S(1)}, bf16[1,32,512]{2,1,0:T(8,128)(2,1)}, u32[]{:S(2)}) copy-start(bf16[1,32,512]{2,1,0:T(8,128)(2,1)} %param.14) | copy-start | bytes 98308
  14.4 26.1 %copy-start.2 = (bf16[1,32,512]{2,1,0:T(8,128)(2,1)S(1)}, bf16[1,32,512]{2,1,0:T(8,128)(2,1)}, u32[]{:S(2)}) copy-start(bf16[1,32,512]{2,1,0:T(8,128)(2,1)} %param.21) | copy-start | bytes 98308
  14.5 35.8 %copy-start.3 = (bf16[1,512,512]{2,1,0:T(8,128)(2,1)S(1)}, bf16[1,512,512]{2,1,0:T(8,128)(2,1)}, u32[]{:S(2)}) copy-start(bf16[1,512,512]{2,1,0:T(8,128)(2,1)} %param.20) | copy-start | bytes 1572868
  29.8 1.4 %collective-permute-start.7 = (bf16[4,32,512]{2,1,0:T(8,128)(2,1)S(1)}, bf16[4,32,512]{2,1,0:T(8,128)(2,1)S(1)}, u32[]{:S(2)}, u32[]{:S(2)}) collective-permute-start(bf16[4,32,512]{2,1,0:T(8,128)(2,1)S(1)} %get-tuple-element.80), channel_id=1, source_target_pairs={{0,1},{1,0},{2,3},{3,2},{4,5},{5,4},{6,7},{7,6},{8,9},{9,8},{10,11... | collective-permute-start | bytes 393224 | tf_op jit(solution)/shard_map/ppermute | solution.py:414
  31.2 4.5 %collective-permute-start.8 = (bf16[32,512]{1,0:T(8,128)(2,1)S(1)}, bf16[32,512]{1,0:T(8,128)(2,1)S(1)}, u32[]{:S(2)}, u32[]{:S(2)}) collective-permute-start(bf16[32,512]{1,0:T(8,128)(2,1)S(1)} %get-tuple-element.82), channel_id=1, source_target_pairs={{0,2},{1,3},{2,0},{3,1},{4,6},{5,7},{6,4},{7,5},{8,10},{9,11},{10,... | collective-permute-start | bytes 98312 | tf_op jit(solution)/shard_map/ppermute | solution.py:414
  32.4 5.3 %collective-permute-start.9 = (bf16[32,512]{1,0:T(8,128)(2,1)S(1)}, bf16[32,512]{1,0:T(8,128)(2,1)S(1)}, u32[]{:S(2)}, u32[]{:S(2)}) collective-permute-start(bf16[32,512]{1,0:T(8,128)(2,1)S(1)} %get-tuple-element.83), channel_id=1, source_target_pairs={{0,4},{1,5},{2,6},{3,7},{4,0},{5,1},{6,2},{7,3},{8,12},{9,13},{10,... | collective-permute-start | bytes 98312 | tf_op jit(solution)/shard_map/ppermute | solution.py:414
  34.9 5.7 %collective-permute-start.10 = (bf16[32,512]{1,0:T(8,128)(2,1)S(1)}, bf16[32,512]{1,0:T(8,128)(2,1)S(1)}, u32[]{:S(2)}, u32[]{:S(2)}) collective-permute-start(bf16[32,512]{1,0:T(8,128)(2,1)S(1)} %get-tuple-element.84), channel_id=1, source_target_pairs={{0,6},{1,7},{2,4},{3,5},{4,2},{5,3},{6,0},{7,1},{8,14},{9,15},{10,... | collective-permute-start | bytes 98312 | tf_op jit(solution)/shard_map/ppermute | solution.py:414
  41.4 6.2 %collective-permute-start.16 = (bf16[2,32,512]{2,1,0:T(8,128)(2,1)S(1)}, bf16[2,32,512]{2,1,0:T(8,128)(2,1)S(1)}, u32[]{:S(2)}, u32[]{:S(2)}) collective-permute-start(bf16[2,32,512]{2,1,0:T(8,128)(2,1)S(1)} %get-tuple-element.88.refs_0_), channel_id=1, source_target_pairs={{0,6},{1,7},{2,4},{3,5},{4,2},{5,3},{6,0},{7,1},{8,14},{9,15},{10,... | collective-permute-start | bytes 196616 | tf_op jit(solution)/shard_map/ppermute | solution.py:414
  42.3 6.6 %collective-permute-start.14 = (bf16[2,32,512]{2,1,0:T(8,128)(2,1)S(1)}, bf16[2,32,512]{2,1,0:T(8,128)(2,1)S(1)}, u32[]{:S(2)}, u32[]{:S(2)}) collective-permute-start(bf16[2,32,512]{2,1,0:T(8,128)(2,1)S(1)} %get-tuple-element.88.refs_0_), channel_id=1, source_target_pairs={{0,4},{1,5},{2,6},{3,7},{4,0},{5,1},{6,2},{7,3},{8,12},{9,13},{10,... | collective-permute-start | bytes 196616 | tf_op jit(solution)/shard_map/ppermute | solution.py:414
  42.3 6.6 %collective-permute-start.12 = (bf16[2,32,512]{2,1,0:T(8,128)(2,1)S(1)}, bf16[2,32,512]{2,1,0:T(8,128)(2,1)S(1)}, u32[]{:S(2)}, u32[]{:S(2)}) collective-permute-start(bf16[2,32,512]{2,1,0:T(8,128)(2,1)S(1)} %get-tuple-element.88.refs_0_), channel_id=1, source_target_pairs={{0,2},{1,3},{2,0},{3,1},{4,6},{5,7},{6,4},{7,5},{8,10},{9,11},{10,... | collective-permute-start | bytes 196616 | tf_op jit(solution)/shard_map/ppermute | solution.py:414
  45.8 3.5 %collective-permute-start.11 = (bf16[2,32,512]{2,1,0:T(8,128)(2,1)S(1)}, bf16[2,32,512]{2,1,0:T(8,128)(2,1)S(1)}, u32[]{:S(2)}, u32[]{:S(2)}) collective-permute-start(bf16[2,32,512]{2,1,0:T(8,128)(2,1)S(1)} %get-tuple-element.88.refs_0_), channel_id=1, source_target_pairs={{0,1},{1,0},{2,3},{3,2},{4,5},{5,4},{6,7},{7,6},{8,9},{9,8},{10,11... | collective-permute-start | bytes 196616 | tf_op jit(solution)/shard_map/ppermute | solution.py:414
  47.6 1.7 %collective-permute-start.17 = (bf16[2,32,512]{2,1,0:T(8,128)(2,1)S(1)}, bf16[2,32,512]{2,1,0:T(8,128)(2,1)S(1)}, u32[]{:S(2)}, u32[]{:S(2)}) collective-permute-start(bf16[2,32,512]{2,1,0:T(8,128)(2,1)S(1)} %collective-permute-done.16.refs_6_), channel_id=1, source_target_pairs={{0,1},{1,0},{2,3},{3,2},{4,5},{5,4},{6,7},{7,6},{8,9},{9,8},{10,11... | collective-permute-start | bytes 196616 | tf_op jit(solution)/shard_map/ppermute | solution.py:414
  48.9 1.3 %collective-permute-start.15 = (bf16[2,32,512]{2,1,0:T(8,128)(2,1)S(1)}, bf16[2,32,512]{2,1,0:T(8,128)(2,1)S(1)}, u32[]{:S(2)}, u32[]{:S(2)}) collective-permute-start(bf16[2,32,512]{2,1,0:T(8,128)(2,1)S(1)} %collective-permute-done.14.refs_4_), channel_id=1, source_target_pairs={{0,1},{1,0},{2,3},{3,2},{4,5},{5,4},{6,7},{7,6},{8,9},{9,8},{10,11... | collective-permute-start | bytes 196616 | tf_op jit(solution)/shard_map/ppermute | solution.py:414
  48.9 1.4 %collective-permute-start.13 = (bf16[2,32,512]{2,1,0:T(8,128)(2,1)S(1)}, bf16[2,32,512]{2,1,0:T(8,128)(2,1)S(1)}, u32[]{:S(2)}, u32[]{:S(2)}) collective-permute-start(bf16[2,32,512]{2,1,0:T(8,128)(2,1)S(1)} %collective-permute-done.12.refs_2_), channel_id=1, source_target_pairs={{0,1},{1,0},{2,3},{3,2},{4,5},{5,4},{6,7},{7,6},{8,9},{9,8},{10,11... | collective-permute-start | bytes 196616 | tf_op jit(solution)/shard_map/ppermute | solution.py:414
  63.8 14.4 %all-to-all-start = ((bf16[8,80,128]{2,1,0:T(8,128)(2,1)}), bf16[8,80,128]{2,1,0:T(8,128)(2,1)S(1)}, u32[]{:S(2)}, u32[]{:S(2)}) async-start(bf16[8,80,128]{2,1,0:T(8,128)(2,1)} %get-tuple-element.89), calls=%async_computation | async-start | bytes 327680 | tf_op jit(solution)/shard_map/all_to_all | solution.py:594
  67.4 10.8 %copy-start.4 = (bf16[1,512,512]{2,1,0:T(8,128)(2,1)S(1)}, bf16[1,512,512]{2,1,0:T(8,128)(2,1)}, u32[]{:S(2)}) copy-start(bf16[1,512,512]{2,1,0:T(8,128)(2,1)} %param.13) | copy-start | bytes 1572868
  67.4 10.8 %copy-start.5 = (bf16[512,64]{0,1:T(8,128)(2,1)S(1)}, bf16[512,64]{0,1:T(8,128)(2,1)}, u32[]{:S(2)}) copy-start(bf16[512,64]{0,1:T(8,128)(2,1)} %param.22) | copy-start | bytes 196612
  79.8 1.3 %collective-permute-start.18 = (bf16[4,128,128]{2,1,0:T(8,128)(2,1)S(1)}, bf16[4,128,128]{2,1,0:T(8,128)(2,1)S(1)}, u32[]{:S(2)}, u32[]{:S(2)}) collective-permute-start(bf16[4,128,128]{2,1,0:T(8,128)(2,1)S(1)} %get-tuple-element.98), channel_id=1, source_target_pairs={{0,1},{1,0},{2,3},{3,2},{4,5},{5,4},{6,7},{7,6},{8,9},{9,8},{10,11... | collective-permute-start | bytes 393224 | tf_op jit(solution)/shard_map/ppermute | solution.py:414
  81.2 4.5 %collective-permute-start.19 = (bf16[128,128]{1,0:T(8,128)(2,1)S(1)}, bf16[128,128]{1,0:T(8,128)(2,1)S(1)}, u32[]{:S(2)}, u32[]{:S(2)}) collective-permute-start(bf16[128,128]{1,0:T(8,128)(2,1)S(1)} %get-tuple-element.100), channel_id=1, source_target_pairs={{0,2},{1,3},{2,0},{3,1},{4,6},{5,7},{6,4},{7,5},{8,10},{9,11},{10,... | collective-permute-start | bytes 98312 | tf_op jit(solution)/shard_map/ppermute | solution.py:414
  83.0 5.3 %collective-permute-start.20 = (bf16[128,128]{1,0:T(8,128)(2,1)S(1)}, bf16[128,128]{1,0:T(8,128)(2,1)S(1)}, u32[]{:S(2)}, u32[]{:S(2)}) collective-permute-start(bf16[128,128]{1,0:T(8,128)(2,1)S(1)} %get-tuple-element.101), channel_id=1, source_target_pairs={{0,4},{1,5},{2,6},{3,7},{4,0},{5,1},{6,2},{7,3},{8,12},{9,13},{10,... | collective-permute-start | bytes 98312 | tf_op jit(solution)/shard_map/ppermute | solution.py:414
  85.4 5.7 %collective-permute-start.21 = (bf16[128,128]{1,0:T(8,128)(2,1)S(1)}, bf16[128,128]{1,0:T(8,128)(2,1)S(1)}, u32[]{:S(2)}, u32[]{:S(2)}) collective-permute-start(bf16[128,128]{1,0:T(8,128)(2,1)S(1)} %get-tuple-element.102), channel_id=1, source_target_pairs={{0,6},{1,7},{2,4},{3,5},{4,2},{5,3},{6,0},{7,1},{8,14},{9,15},{10,... | collective-permute-start | bytes 98312 | tf_op jit(solution)/shard_map/ppermute | solution.py:414
  91.1 6.7 %collective-permute-start.24 = (bf16[384,128]{1,0:T(8,128)(2,1)S(1)}, bf16[384,128]{1,0:T(8,128)(2,1)S(1)}, u32[]{:S(2)}, u32[]{:S(2)}) collective-permute-start(bf16[384,128]{1,0:T(8,128)(2,1)S(1)} %share.1.refs_0_), channel_id=1, source_target_pairs={{0,24},{8,16},{16,8},{24,0},{1,25},{9,17},{17,9},{25,1},{2,26},{10... | collective-permute-start | bytes 294920 | tf_op jit(solution)/shard_map/ppermute | solution.py:414
  93.7 4.9 %collective-permute-start.23 = (bf16[384,128]{1,0:T(8,128)(2,1)S(1)}, bf16[384,128]{1,0:T(8,128)(2,1)S(1)}, u32[]{:S(2)}, u32[]{:S(2)}) collective-permute-start(bf16[384,128]{1,0:T(8,128)(2,1)S(1)} %share.1.refs_0_), channel_id=1, source_target_pairs={{0,16},{8,24},{16,0},{24,8},{1,17},{9,25},{17,1},{25,9},{2,18},{10... | collective-permute-start | bytes 294920 | tf_op jit(solution)/shard_map/ppermute | solution.py:414
  94.2 4.6 %collective-permute-start.22 = (bf16[384,128]{1,0:T(8,128)(2,1)S(1)}, bf16[384,128]{1,0:T(8,128)(2,1)S(1)}, u32[]{:S(2)}, u32[]{:S(2)}) collective-permute-start(bf16[384,128]{1,0:T(8,128)(2,1)S(1)} %share.1.refs_0_), channel_id=1, source_target_pairs={{0,8},{8,0},{16,24},{24,16},{1,9},{9,1},{17,25},{25,17},{2,10},{10... | collective-permute-start | bytes 294920 | tf_op jit(solution)/shard_map/ppermute | solution.py:414
  98.8 6.6 %collective-permute-start.30 = (bf16[384,128]{1,0:T(8,128)(2,1)S(1)}, bf16[384,128]{1,0:T(8,128)(2,1)S(1)}, u32[]{:S(2)}, u32[]{:S(2)}) collective-permute-start(bf16[384,128]{1,0:T(8,128)(2,1)S(1)} %total.1.refs_0_), channel_id=1, source_target_pairs={{0,6},{1,7},{2,4},{3,5},{4,2},{5,3},{6,0},{7,1},{8,14},{9,15},{10,... | collective-permute-start | bytes 294920 | tf_op jit(solution)/shard_map/ppermute | solution.py:414
  99.3 8.2 %collective-permute-start.28 = (bf16[384,128]{1,0:T(8,128)(2,1)S(1)}, bf16[384,128]{1,0:T(8,128)(2,1)S(1)}, u32[]{:S(2)}, u32[]{:S(2)}) collective-permute-start(bf16[384,128]{1,0:T(8,128)(2,1)S(1)} %total.1.refs_0_), channel_id=1, source_target_pairs={{0,4},{1,5},{2,6},{3,7},{4,0},{5,1},{6,2},{7,3},{8,12},{9,13},{10,... | collective-permute-start | bytes 294920 | tf_op jit(solution)/shard_map/ppermute | solution.py:414
  99.3 8.2 %collective-permute-start.26 = (bf16[384,128]{1,0:T(8,128)(2,1)S(1)}, bf16[384,128]{1,0:T(8,128)(2,1)S(1)}, u32[]{:S(2)}, u32[]{:S(2)}) collective-permute-start(bf16[384,128]{1,0:T(8,128)(2,1)S(1)} %total.1.refs_0_), channel_id=1, source_target_pairs={{0,2},{1,3},{2,0},{3,1},{4,6},{5,7},{6,4},{7,5},{8,10},{9,11},{10,... | collective-permute-start | bytes 294920 | tf_op jit(solution)/shard_map/ppermute | solution.py:414
  103.3 4.7 %collective-permute-start.25 = (bf16[384,128]{1,0:T(8,128)(2,1)S(1)}, bf16[384,128]{1,0:T(8,128)(2,1)S(1)}, u32[]{:S(2)}, u32[]{:S(2)}) collective-permute-start(bf16[384,128]{1,0:T(8,128)(2,1)S(1)} %total.1.refs_0_), channel_id=1, source_target_pairs={{0,1},{1,0},{2,3},{3,2},{4,5},{5,4},{6,7},{7,6},{8,9},{9,8},{10,11... | collective-permute-start | bytes 294920 | tf_op jit(solution)/shard_map/ppermute | solution.py:414
  105.5 2.5 %collective-permute-start.31 = (bf16[384,128]{1,0:T(8,128)(2,1)S(1)}, bf16[384,128]{1,0:T(8,128)(2,1)S(1)}, u32[]{:S(2)}, u32[]{:S(2)}) collective-permute-start(bf16[384,128]{1,0:T(8,128)(2,1)S(1)} %collective-permute-done.30.refs_6_), channel_id=1, source_target_pairs={{0,1},{1,0},{2,3},{3,2},{4,5},{5,4},{6,7},{7,6},{8,9},{9,8},{10,11... | collective-permute-start | bytes 294920 | tf_op jit(solution)/shard_map/ppermute | solution.py:414
  107.5 1.3 %collective-permute-start.29 = (bf16[384,128]{1,0:T(8,128)(2,1)S(1)}, bf16[384,128]{1,0:T(8,128)(2,1)S(1)}, u32[]{:S(2)}, u32[]{:S(2)}) collective-permute-start(bf16[384,128]{1,0:T(8,128)(2,1)S(1)} %collective-permute-done.28.refs_4_), channel_id=1, source_target_pairs={{0,1},{1,0},{2,3},{3,2},{4,5},{5,4},{6,7},{7,6},{8,9},{9,8},{10,11... | collective-permute-start | bytes 294920 | tf_op jit(solution)/shard_map/ppermute | solution.py:414
  107.5 1.5 %collective-permute-start.27 = (bf16[384,128]{1,0:T(8,128)(2,1)S(1)}, bf16[384,128]{1,0:T(8,128)(2,1)S(1)}, u32[]{:S(2)}, u32[]{:S(2)}) collective-permute-start(bf16[384,128]{1,0:T(8,128)(2,1)S(1)} %collective-permute-done.26.refs_2_), channel_id=1, source_target_pairs={{0,1},{1,0},{2,3},{3,2},{4,5},{5,4},{6,7},{7,6},{8,9},{9,8},{10,11... | collective-permute-start | bytes 294920 | tf_op jit(solution)/shard_map/ppermute | solution.py:414

commit v5 on v4

--- a/solution.py
+++ b/solution.py
@@ -11,9 +11,10 @@
 ATOM_SCALE = 0.25
 BLOCK = 256
 CAP = 128
-TILE_LIMIT = 2048
+TILE_LIMIT = 4096
+FORWARD_LIMIT = 8192
 INDEX_TILE = 2048
-VMEM_BYTES = 24 * 1024 * 1024
+VMEM_BYTES = 32 * 1024 * 1024
 
 FIRST_FIRST = (((0,), (0,)), ((), ()))
 LAST_LAST = (((1,), (1,)), ((), ()))
@@ -64,8 +65,9 @@
 
 
 def index_kernel(members, in_hbm, *refs):
-    held = (len(refs) - 6) // 2
-    staged, (slot_ref, rank_ref), kept = refs[:held], refs[held : held + 2], refs[held + 2 : -4]
+    held = (len(refs) - 7) // 2
+    staged, (slot_ref, rank_ref, back_ref) = refs[:held], refs[held : held + 3]
+    kept = refs[held + 3 : -4]
     in_ref, hots, counts, sems = refs[-4:]
     copy, *copies = start_copies(((in_hbm, in_ref), *zip(staged, kept)), sems)
     trips = in_ref.shape[1]
@@ -104,6 +106,12 @@
         slot_ref[:, span] = (place // per) * CAP + found.astype(jnp.int32)
     for copy in copies:
         copy.wait()
+    bil_ref = kept[2]
+    width = bil_ref.shape[0]
+    turned = bil_ref[...].astype(jnp.float32).T
+    back_ref[...] = jnp.concatenate(
+        [turned[at : at + width] for at in range(0, turned.shape[0], width)], axis=1
+    ).astype(jnp.bfloat16)
 
 
 def rank_row(rank_ref, source, per):
@@ -125,8 +133,8 @@
     *refs,
 ):
     out_ref, basis_ref, bil_ref, up_ref, emb_ref, target_ref, *refs = refs
-    feat_refs, refs = refs[:members], refs[members:]
-    new_ref, near_ref, far_ref, gathered_ref, picked_hbm, back_ref, *refs = refs
+    feat_refs, refs = refs[:members][::-1], refs[members:]
+    new_ref, near_ref, far_ref, gathered_ref, picked_hbm, *refs = refs
     table, total, spread, masked, picked_ref, sems = refs
     trips = slot_ref.shape[1]
     tile = spread.shape[1]
@@ -174,10 +182,6 @@
     lax.fori_loop(0, trips // tile, one_tile, 0)
     for step in range(trips // tile):
         tile_copy(picked_ref, picked_hbm, sems, step, tile).wait()
-    turned = bil_ref[...].astype(jnp.float32).T
-    back_ref[...] = jnp.concatenate(
-        [turned[at : at + width] for at in range(0, turned.shape[0], width)], axis=1
-    ).astype(jnp.bfloat16)
     gathered = jnp.concatenate(
         [total[at : at + width, :] for at in range(0, total.shape[0], width)], axis=1
     ).astype(jnp.bfloat16)
@@ -213,6 +217,24 @@
     pair_ref[1] = grad_pre
 
 
+def slope_kernel(gathered_ref, up_ref, slope_ref):
+    slope_ref[...] = silu_slope(dot32(gathered_ref[...], up_ref[...], FIRST_FIRST))
+
+
+def slab_kernel(members, *refs):
+    pair_refs, (slab_ref, sums, grads, atom_grad) = refs[:members], refs[members:]
+    me = lax.axis_index("graph")
+    held, model = pair_refs[0].shape[1:]
+    for source, pair_ref in enumerate(pair_refs):
+        sums[source * held : (source + 1) * held, :] = pair_ref[0]
+        grads[source * held : (source + 1) * held, :] = pair_ref[1]
+    atom_grad[...] = ATOM_SCALE * dot32(sums[...], grads[...], FIRST_FIRST)
+    share = model // members
+    mine = atom_grad[pl.ds(pl.multiple_of(me * share, share), share), :]
+    for column in range(0, model, CAP):
+        slab_ref[column // CAP] = mine[:, column : column + CAP].astype(jnp.bfloat16)
+
+
 def backward_kernel(
     members,
     count_ref,
@@ -223,14 +245,15 @@
     back_ref,
     up_ref,
     gathered_ref,
+    slope_ref,
     grad_edge_ref,
     target_ref,
     atom_weight_ref,
     *refs,
 ):
-    pair_refs, refs = refs[:members], refs[members:]
-    grad_new_ref, up_grad_ref, mixed_hbm, slab_ref, parts_ref, *refs = refs
-    table, spread, masked, total, sums, grads, atom_grad, mixed_ref, sems = refs
+    pair_refs, refs = refs[:members][::-1], refs[members:]
+    grad_new_ref, up_grad_ref, mixed_hbm, parts_ref, *refs = refs
+    table, spread, masked, total, grads, mixed_ref, sems = refs
     trips = slot_ref.shape[1]
     tile = spread.shape[1]
     width = back_ref.shape[0]
@@ -238,24 +261,17 @@
     groups = total.shape[0] // width
     count = count_ref[0, 0]
     me = lax.axis_index("graph")
-    held, model = pair_refs[0].shape[1:]
+    held = pair_refs[0].shape[1]
     for source, pair_ref in enumerate(pair_refs):
-        sums[source * held : (source + 1) * held, :] = pair_ref[0]
         grads[source * held : (source + 1) * held, :] = pair_ref[1]
     grad_sum = (ATOM_SCALE * dot32(grads[...], atom_weight_ref[...], LAST_LAST)).astype(
         jnp.bfloat16
     )
-    atom_grad[...] = ATOM_SCALE * dot32(sums[...], grads[...], FIRST_FIRST)
-    share = model // members
-    mine = atom_grad[pl.ds(pl.multiple_of(me * share, share), share), :]
-    for column in range(0, model, CAP):
-        slab_ref[column // CAP] = mine[:, column : column + CAP].astype(jnp.bfloat16)
     total[...] = jnp.zeros_like(total)
-    update = dot32(gathered_ref[...], up_ref[...], FIRST_FIRST)
     hot = row_hot(members * held, target_ref[...] ^ (me * held))
     grad_new = grad_edge_ref[...].astype(jnp.float32) + dot32(hot, grad_sum, FIRST_FIRST)
     grad_new_ref[...] = grad_new
-    grad_update = (grad_new * silu_slope(update)).astype(jnp.bfloat16)
+    grad_update = (grad_new * slope_ref[...]).astype(jnp.bfloat16)
     up_grad_ref[...] = dot32(gathered_ref[...], grad_update).astype(jnp.bfloat16)
     grad_gathered = dot32(up_ref[...], grad_update, LAST_LAST).astype(jnp.bfloat16)
     for part in range(edges // BLOCK):
@@ -324,15 +340,19 @@
     out_ref[...] = total[...].T.astype(jnp.bfloat16)
 
 
+def input_kernel(grad_project_ref, down_ref, grad_new_ref, grad_in_ref):
+    grad_in_ref[...] = grad_new_ref[...] + dot32(
+        grad_project_ref[...], down_ref[...], FIRST_FIRST
+    )
+
+
 def edge_kernel(
     parts_ref,
     projected_ref,
     emb_ref,
-    down_ref,
-    grad_new_ref,
     bil_grad_ref,
     up_grad_ref,
-    grad_in_ref,
+    grad_project_ref,
     near_ref,
     far_ref,
     flat,
@@ -346,7 +366,7 @@
         row = jnp.concatenate([part[width + at : width + at + 1] for at in range(per)], axis=1)
         grad_feat = grad_feat + dot32(part[:width].astype(jnp.bfloat16), rank_hot(row))
     grad_project = (grad_feat * silu_slope(projected_ref[...])).astype(jnp.bfloat16)
-    grad_in_ref[...] = grad_new_ref[...] + dot32(grad_project, down_ref[...], FIRST_FIRST)
+    grad_project_ref[...] = grad_project
     down_grad = dot32(grad_project, emb_ref[...]).astype(jnp.bfloat16)
     at = 0
     for term in (down_grad, bil_grad_ref[...], up_grad_ref[...]):
@@ -372,15 +392,14 @@
 
 
 def total_kernel(factor, *refs):
-    part_refs, out_ref = refs[:-1], refs[-1]
-    total = part_refs[0][...].astype(jnp.float32)
-    for part_ref in part_refs[1:]:
-        total = total + part_ref[...].astype(jnp.float32)
-    out_ref[...] = (total * factor).astype(jnp.bfloat16)
+    parts = [part_ref[...].astype(jnp.float32) for part_ref in refs[:-1]]
+    while len(parts) > 1:
+        parts = [left + right for left, right in zip(parts[::2], parts[1::2])]
+    refs[-1][...] = (parts[0] * factor).astype(jnp.bfloat16)
 
 
 def last_kernel(members, *refs):
-    part_refs, (down_ref, bil_ref, up_ref, atom_ref, flat) = refs[:members], refs[members:]
+    part_refs, (down_ref, bil_ref, up_ref, atom_ref, flat) = refs[:members][::-1], refs[members:]
     me = lax.axis_index("graph")
     model = atom_ref.shape[1]
     rows = flat.shape[0] // members
@@ -428,7 +447,8 @@
 def gather_near(value, members, beside=None):
     even = [value] + [swap(value, members, mask) for mask in range(2, members, 2)]
     if beside is not None:
-        even, beside = lax.optimization_barrier((even, beside))
+        back_even, beside = lax.optimization_barrier((even[::-1], beside))
+        even = back_even[::-1]
     odd = [swap(piece, members, 1) for piece in even]
     return [piece for pair in zip(even, odd) for piece in pair], beside
 
@@ -463,6 +483,7 @@
     trips = trip_in.shape[1]
     width = w_down.shape[1]
     tile = math.gcd(trips, TILE_LIMIT)
+    long = math.gcd(trips, FORWARD_LIMIT)
     f32, b16 = jnp.float32, jnp.bfloat16
     shaped = jax.ShapeDtypeStruct
 
@@ -487,12 +508,13 @@
     )(hbm(edge_rows), hbm(down_rows))
     rank_rows = members * edge_dev // CAP
     staged = (trip_out, basis, bil_rows, w_up, edge_rows, edge_target)
-    slot, rank, *kept = pl.pallas_call(
+    slot, rank, back, *kept = pl.pallas_call(
         functools.partial(index_kernel, members),
         in_specs=[HBM] * (1 + len(staged)),
         out_shape=(
             shaped(trip_in.shape, jnp.int32),
             shaped((rank_rows, CAP), f32),
+            shaped(bil_rows.shape, b16),
             *[shaped(value.shape, value.dtype) for value in staged],
         ),
         scratch_shapes=[
@@ -505,29 +527,28 @@
         cost_estimate=cost(8 * CAP * CAP * trips),
         name="slots",
     )(*[hbm(value) for value in (trip_in, *staged)])
-    feats, (slot, rank, *kept) = gather_near(feat, members, (slot, rank, *kept))
+    feats, (slot, rank, back, *kept) = gather_near(feat, members, (slot, rank, back, *kept))
 
     named_rows = members * CAP // BLOCK * width
     half = shaped((members // 2, atom_dev, model), b16)
-    edge_new, near, far, gathered, picked, back = pl.pallas_call(
+    edge_new, near, far, gathered, picked = pl.pallas_call(
         functools.partial(forward_kernel, members),
         in_specs=[SMEM] + [VMEM] * (2 + len(kept) + members),
-        out_specs=(VMEM, VMEM, VMEM, VMEM, HBM, VMEM),
+        out_specs=(VMEM, VMEM, VMEM, VMEM, HBM),
         out_shape=(
             shaped(edge_rows.shape, b16),
             half,
             half,
             shaped((width, edge_dev), b16),
             pltpu.HBM((width, trips), b16),
-            shaped((width, w_bil.shape[0]), b16),
         ),
         scratch_shapes=[
             pltpu.VMEM((named_rows, BLOCK), b16),
             pltpu.VMEM((edge_dev // BLOCK * width, BLOCK), f32),
-            pltpu.VMEM((w_bil.shape[0], tile), b16),
-            pltpu.VMEM((edge_dev // BLOCK * width, tile), b16),
+            pltpu.VMEM((w_bil.shape[0], long), b16),
+            pltpu.VMEM((edge_dev // BLOCK * width, long), b16),
             pltpu.VMEM((width, trips), b16),
-            pltpu.SemaphoreType.DMA((trips // tile,)),
+            pltpu.SemaphoreType.DMA((trips // long,)),
         ],
         compiler_params=params(),
         cost_estimate=cost(12 * w_bil.size * trips),
@@ -537,30 +558,38 @@
         slot,
         rank,
         *kept,
-        *feats,
+        *feats[::-1],
     )
 
     atom_block = shaped((atom_dev, model), b16)
+    slope = pl.pallas_call(
+        slope_kernel,
+        out_shape=shaped(edge_rows.shape, f32),
+        compiler_params=params(),
+        cost_estimate=cost(64 * edge_rows.size * width),
+        name="slopes",
+    )(gathered, kept[3])
     sums = scatter_near(near, far, members)
+    sums, slope = lax.optimization_barrier((sums[::-1], slope))
+    sums = sums[::-1]
     atom_new, pair = pl.pallas_call(
         atom_kernel,
         out_shape=(atom_block, shaped((2, atom_dev, model), b16)),
         compiler_params=params(),
         cost_estimate=cost(16 * atom_dev * w_atom.size),
         name="atoms",
-    )(atom_emb[0], grad_atom[0], w_atom, *sums)
+    )(atom_emb[0], grad_atom[0], w_atom, *sums[::-1])
     pairs, _ = gather_near(pair, members)
 
     piece_rows = width + -(-(edge_dev // CAP) // 16) * 16
-    grad_new, wup_term, mixed, slab, feat_parts = pl.pallas_call(
+    grad_new, wup_term, mixed, feat_parts = pl.pallas_call(
         functools.partial(backward_kernel, members),
-        in_specs=[SMEM] + [VMEM] * (10 + members),
-        out_specs=(VMEM, VMEM, HBM, VMEM, VMEM),
+        in_specs=[SMEM] + [VMEM] * (11 + members),
+        out_specs=(VMEM, VMEM, HBM, VMEM),
         out_shape=(
             shaped(edge_rows.shape, f32),
             shaped(w_up.shape, b16),
             pltpu.HBM((width, trips), b16),
-            shaped((model // CAP, model // members, CAP), b16),
             shaped((members, piece_rows, CAP), b16),
         ),
         scratch_shapes=[
@@ -569,8 +598,6 @@
             pltpu.VMEM((named_rows, tile), b16),
             pltpu.VMEM((named_rows, BLOCK), f32),
             pltpu.VMEM((members * atom_dev, model), b16),
-            pltpu.VMEM((members * atom_dev, model), b16),
-            pltpu.VMEM((model, model), f32),
             pltpu.VMEM((width, trips), b16),
             pltpu.SemaphoreType.DMA((trips // tile,)),
         ],
@@ -586,13 +613,14 @@
         back,
         kept[3],
         gathered,
+        slope,
         grad_edge[0],
         kept[5],
         w_atom,
-        *pairs,
+        *pairs[::-1],
     )
     feat_parts = lax.all_to_all(feat_parts, "graph", 0, 0, tiled=True)
-    wide = math.gcd(trips, 2 * tile)
+    wide = math.gcd(trips, tile)
     wbil_term = pl.pallas_call(
         weight_kernel,
         in_specs=[VMEM, HBM, HBM],
@@ -610,30 +638,52 @@
     )(kept[1], hbm(picked), hbm(mixed))
     flat_rows = width * (2 * model + w_bil.shape[0]) // CAP
     piece = shaped((members // 2, flat_rows // members, CAP), b16)
-    grad_in, near, far = pl.pallas_call(
+    grad_project, near, far = pl.pallas_call(
         edge_kernel,
-        out_shape=(shaped(edge_rows.shape, f32), piece, piece),
+        out_shape=(shaped((width, edge_dev), b16), piece, piece),
         scratch_shapes=[pltpu.VMEM((flat_rows, CAP), b16)],
         compiler_params=params(),
         cost_estimate=cost(64 * edge_rows.size * width),
         name="edges",
-    )(feat_parts, projected, edge_rows, down_rows, grad_new, wbil_term, wup_term)
-
+    )(feat_parts, projected, edge_rows, wbil_term, wup_term)
+    grad_in = pl.pallas_call(
+        input_kernel,
+        out_shape=shaped(edge_rows.shape, f32),
+        compiler_params=params(),
+        cost_estimate=cost(64 * edge_rows.size * width),
+        name="input_grads",
+    )(grad_project, down_rows, grad_new)
+
+    slab = pl.pallas_call(
+        functools.partial(slab_kernel, members),
+        out_shape=shaped((model // CAP, model // members, CAP), b16),
+        scratch_shapes=[
+            pltpu.VMEM((members * atom_dev, model), b16),
+            pltpu.VMEM((members * atom_dev, model), b16),
+            pltpu.VMEM((model, model), f32),
+        ],
+        compiler_params=params(),
+        cost_estimate=cost(16 * members * atom_dev * w_atom.size),
+        name="atom_slab",
+    )(*pairs)
     batches = lax.axis_size("dp")
     factor = 1.0 / math.sqrt(batches * members * edge_dev)
     share_rows = (flat_rows + model * model // CAP) // members
+    flat_sums = scatter_near(near, far, members)
+    flat_sums, slab, grad_in = lax.optimization_barrier((flat_sums[::-1], slab, grad_in))
+    flat_sums = flat_sums[::-1]
     share = pl.pallas_call(
         share_kernel,
         out_shape=shaped((share_rows, CAP), b16),
         compiler_params=params(),
         name="share",
-    )(slab, *scatter_near(near, far, members))
+    )(slab, *flat_sums[::-1])
     share = pl.pallas_call(
         functools.partial(total_kernel, factor),
         out_shape=shaped((share_rows, CAP), b16),
         compiler_params=params(),
         name="total",
-    )(share, *[swap(share, batches, mask, "dp") for mask in range(1, batches)])
+    )(*[swap(share, batches, mask, "dp") for mask in range(batches - 1, 0, -1)], share)
     shares, _ = gather_near(share, members)
     grad_wdown, grad_wbil, grad_wup, grad_watom = pl.pallas_call(
         functools.partial(last_kernel, members),
@@ -646,7 +696,7 @@
         scratch_shapes=[pltpu.VMEM((flat_rows, CAP), b16)],
         compiler_params=params(),
         name="weights",
-    )(*shares)
+    )(*shares[::-1])
     return (
         edge_new[None],
         atom_new[None],

time: 110 us -> 105 us (0.955)
  waiting for transfers between devices: 26.5 us -> 23.8 us
  Pallas kernels: 48.7 us -> 46.4 us
    ppermute x32, waiting for transfers between devices: 26.5 us -> 23.8 us  [swap(): return lax.ppermute(value, axis, [(at, at ^ mask) for at in range(members)])]
    pallas_call x1, Pallas kernels: 15.1 us -> 13.1 us  [body(): pl.pallas_call(functools.partial(forward_kernel, members), in_specs=[SMEM...]
    pallas_call x1, Pallas kernels: 13.5 us -> 12 us  [body(): pl.pallas_call(functools.partial(backward_kernel, members), in_specs=[SME...]
    pallas_call x1 -> x4, Pallas kernels: 1.61 us -> 2.63 us  [the longest x1 1.29 us: body(): pl.pallas_call(input_kernel, out_shape=shaped(edge_rows.shape, f32), comp...]
  transfers between devices with their start and end apart: 33 -> 33, of which waited for: 19 -> 20; matrix products, arithmetic and copies ran while one was open for 0% -> 0% of each run, Pallas kernels for 14% -> 16%
where the time goes in v5:
time: 105 us
  Pallas kernels  46.4 us (44%)
  starting transfers between devices  33.5 us (32%)
  waiting for transfers between devices  23.8 us (23%)
  between operations  1.47 us (1%)
    ppermute x32, starting transfers between devices, swap(): return lax.ppermute(value, axis, [(at, at ^ mask) for at in range(members)])  29.9 us
    ppermute x32, waiting for transfers between devices, swap(): return lax.ppermute(value, axis, [(at, at ^ mask) for at in range(members)])  23.8 us
    pallas_call x1, Pallas kernels, body(): pl.pallas_call(functools.partial(forward_kernel, members), in_specs=[SMEM...  13.1 us
    pallas_call x1, Pallas kernels, body(): pl.pallas_call(functools.partial(backward_kernel, members), in_specs=[SME...  12 us
    pallas_call x1, Pallas kernels, body(): pl.pallas_call(weight_kernel, in_specs=[VMEM, HBM, HBM], out_shape=shaped...  10.8 us
    pallas_call x1, Pallas kernels, body(): pl.pallas_call(functools.partial(index_kernel, members), in_specs=[HBM] *...  4.3 us
    all_to_all x1, starting transfers between devices, body(): feat_parts = lax.all_to_all(feat_parts, 'graph', 0, 0, tiled=True)  3.61 us
  transfers between devices with their start and end apart: 33, of which 20 were waited for; matrix products, arithmetic and copies ran while one was open for 0% of the time, Pallas kernels for 16%

profile of v5, /device:TPU:0, one launch (start us, length us, event | category | flops | bytes accessed | tf_op | source)
XLA Modules:
  0.0 105.2 jit_solution(13139589163943479481)
XLA Ops:
  0.6 1.4 %features.1 = (f32[64,512]{1,0:T(8,128)S(1)}, bf16[64,512]{1,0:T(8,128)(2,1)S(1)}) custom-call(bf16[512,512]{1,0:T(8,128)(2,1)} %bitcast.15, bf16[64,512]{1,0:T(8,128)(2,1)} %bitcast.18), custom_call_target="tpu_custom_call" | custom-call | flops 268435456 | bytes 1048576 | tf_op jit(solution)/shard_map/features/pallas_call | solution.py:493
  2.0 5.1 %collective-permute-start = (bf16[64,512]{1,0:T(8,128)(2,1)S(1)}, bf16[64,512]{1,0:T(8,128)(2,1)S(1)}, u32[]{:S(2)}, u32[]{:S(2)}) collective-permute-start(bf16[64,512]{1,0:T(8,128)(2,1)S(1)} %get-tuple-element.89.refs_13_), channel_id=1, source_target_pairs={{0,6},{1,7},{2,4},{3,5},{4,2},{5,3},{6,0},{7,1},{8,14},{9,15},{10,... | collective-permute-start | bytes 196616 | tf_op jit(solution)/shard_map/ppermute | solution.py:433
  7.1 0.0 collective-permute-start.1
  7.1 0.6 collective-permute-start.2
  7.8 4.3 %slots.1 = (s32[1,16384]{1,0:T(1,128)S(1)}, f32[32,128]{1,0:T(8,128)S(1)}, bf16[64,1024]{1,0:T(8,128)(2,1)S(1)}, s32[1,16384]{1,0:T(1,128)S(1)}, bf16[16,16384]{...) custom-call(s32[1,16384]{1,0:T(1,128)} %in_hbm.1, ...), custom_call_target="tpu_custom_call" | custom-call | flops 2147483648 | bytes 1048576 | tf_op jit(solution)/shard_map/slots/pallas_call | solution.py:511
  12.1 0.6 collective-permute-done.1.refs_9_
  12.7 0.0 collective-permute-done.2.refs_11_
  12.7 0.0 collective-permute-start.3
  12.7 0.5 collective-permute-start.4
  13.3 0.0 collective-permute-start.5
  13.3 0.5 collective-permute-start.6
  14.4 0.0 collective-permute-done.3.refs_6_
  14.4 0.1 collective-permute-done.5.refs_10_
  14.5 0.2 collective-permute-done.6.refs_12_
  14.7 13.1 %forward_triplets.1 = (bf16[512,512]{1,0:T(8,128)(2,1)}, bf16[4,32,512]{2,1,0:T(8,128)(2,1)S(1)}, bf16[4,32,512]{2,1,0:T(8,128)(2,1)S(1)}, bf16[64,512]{1,0:T(8,128)(2,1)S(1)}, bf16[64,16384]{1,0:T(8,128)(2,1)}) custom-call(s32[1,1]{1,0:T(1,128)S(6)} %copy.20.count_ref, s32[1,16384]{1,0:T(1,128)S(1)} %get-tuple-element.78.slot_ref, ...), custom_call_target="tpu_custom_call" | custom-call | flops 12884901888 | bytes 1048576 | tf_op jit(solution)/shard_map/forward_triplets/pallas_call | solution.py:534
  27.8 0.4 collective-permute-start.7
  28.2 1.0 collective-permute-done.7.far_ref
  29.2 3.3 %collective-permute-start.8 = (bf16[32,512]{1,0:T(8,128)(2,1)S(1)}, bf16[32,512]{1,0:T(8,128)(2,1)S(1)}, u32[]{:S(2)}, u32[]{:S(2)}) collective-permute-start(bf16[32,512]{1,0:T(8,128)(2,1)S(1)} %get-tuple-element.93), channel_id=1, source_target_pairs={{0,6},{1,7},{2,4},{3,5},{4,2},{5,3},{6,0},{7,1},{8,14},{9,15},{10,... | collective-permute-start | bytes 98312 | tf_op jit(solution)/shard_map/ppermute | solution.py:433
  32.5 0.0 collective-permute-start.9
  32.5 1.2 %collective-permute-start.10 = (bf16[32,512]{1,0:T(8,128)(2,1)S(1)}, bf16[32,512]{1,0:T(8,128)(2,1)S(1)}, u32[]{:S(2)}, u32[]{:S(2)}) collective-permute-start(bf16[32,512]{1,0:T(8,128)(2,1)S(1)} %get-tuple-element.95), channel_id=1, source_target_pairs={{0,2},{1,3},{2,0},{3,1},{4,6},{5,7},{6,4},{7,5},{8,10},{9,11},{10,... | collective-permute-start | bytes 98312 | tf_op jit(solution)/shard_map/ppermute | solution.py:433
  33.7 0.5 slopes.1.slope_ref
  34.2 1.2 %collective-permute-done.8.refs_0_ = bf16[32,512]{1,0:T(8,128)(2,1)S(1)} collective-permute-done((bf16[32,512]{1,0:T(8,128)(2,1)S(1)}, bf16[32,512]{1,0:T(8,128)(2,1)S(1)}, u32[]{:S(2)}, u32[]{:S(2)}) %collective-permute-start.8) | collective-permute-done | bytes 32800 | tf_op jit(solution)/shard_map/ppermute | solution.py:433
  35.4 1.9 %collective-permute-done.9.refs_1_ = bf16[32,512]{1,0:T(8,128)(2,1)S(1)} collective-permute-done((bf16[32,512]{1,0:T(8,128)(2,1)S(1)}, bf16[32,512]{1,0:T(8,128)(2,1)S(1)}, u32[]{:S(2)}, u32[]{:S(2)}) %collective-permute-start.9) | collective-permute-done | bytes 32800 | tf_op jit(solution)/shard_map/ppermute | solution.py:433
  37.3 0.0 collective-permute-done.10.refs_2_
  37.3 0.9 atoms.1
  38.2 1.7 %collective-permute-start.11 = (bf16[2,32,512]{2,1,0:T(8,128)(2,1)S(1)}, bf16[2,32,512]{2,1,0:T(8,128)(2,1)S(1)}, u32[]{:S(2)}, u32[]{:S(2)}) collective-permute-start(bf16[2,32,512]{2,1,0:T(8,128)(2,1)S(1)} %get-tuple-element.105.refs_7_.refs_0_), channel_id=1, source_target_pairs={{0,6},{1,7},{2,4},{3,5},{4,2},{5,3},{6,0},{7,1},{8,14},{9,15},{10,... | collective-permute-start | bytes 196616 | tf_op jit(solution)/shard_map/ppermute | solution.py:433
  39.8 0.3 collective-permute-start.13
  40.2 2.4 %collective-permute-start.15 = (bf16[2,32,512]{2,1,0:T(8,128)(2,1)S(1)}, bf16[2,32,512]{2,1,0:T(8,128)(2,1)S(1)}, u32[]{:S(2)}, u32[]{:S(2)}) collective-permute-start(bf16[2,32,512]{2,1,0:T(8,128)(2,1)S(1)} %get-tuple-element.105.refs_7_.refs_0_), channel_id=1, source_target_pairs={{0,2},{1,3},{2,0},{3,1},{4,6},{5,7},{6,4},{7,5},{8,10},{9,11},{10,... | collective-permute-start | bytes 196616 | tf_op jit(solution)/shard_map/ppermute | solution.py:433
  42.5 0.0 collective-permute-start.17
  42.5 2.4 %collective-permute-done.11.refs_1_.refs_6_ = bf16[2,32,512]{2,1,0:T(8,128)(2,1)S(1)} collective-permute-done((bf16[2,32,512]{2,1,0:T(8,128)(2,1)S(1)}, bf16[2,32,512]{2,1,0:T(8,128)(2,1)S(1)}, u32[]{:S(2)}, u32[]{:S(2)}) %collective-permute-start.11) | collective-permute-done | bytes 65568 | tf_op jit(solution)/shard_map/ppermute | solution.py:433
  45.0 1.4 %collective-permute-done.13.refs_3_.refs_4_ = bf16[2,32,512]{2,1,0:T(8,128)(2,1)S(1)} collective-permute-done((bf16[2,32,512]{2,1,0:T(8,128)(2,1)S(1)}, bf16[2,32,512]{2,1,0:T(8,128)(2,1)S(1)}, u32[]{:S(2)}, u32[]{:S(2)}) %collective-permute-start.13) | collective-permute-done | bytes 65568 | tf_op jit(solution)/shard_map/ppermute | solution.py:433
  46.4 0.5 collective-permute-start.16
  46.9 0.7 collective-permute-done.14.refs_2_.refs_5_
  47.7 0.2 collective-permute-done.16.refs_4_.refs_3_
  47.8 12.0 %backward_triplets.1 = (f32[512,512]{1,0:T(8,128)S(1)}, bf16[64,512]{1,0:T(8,128)(2,1)S(1)}, bf16[64,16384]{1,0:T(8,128)(2,1)}, bf16[8,80,128]{2,1,0:T(8,128)(2,1)}) custom-call(s32[1,1]{1,0:T(1,128)S(6)} %copy.20.count_ref, s32[1,16384]{1,0:T(1,128)S(1)} %get-tuple-element.78.slot_ref, s32[1,16384]{1,0:T(1,128)S(1)} %get-tuple-element.80.refs_0_.out_ref, ...), custom_call_target="tpu_custom_call" | custom-call | flops 12884901888 | bytes 1048576 | tf_op jit(solution)/shard_map/backward_triplets/pallas_call | solution.py:585
  59.9 3.6 %all-to-all-start = ((bf16[8,80,128]{2,1,0:T(8,128)(2,1)}), bf16[8,80,128]{2,1,0:T(8,128)(2,1)S(1)}, u32[]{:S(2)}, u32[]{:S(2)}) async-start(bf16[8,80,128]{2,1,0:T(8,128)(2,1)} %get-tuple-element.106), calls=%async_computation | async-start | bytes 327680 | tf_op jit(solution)/shard_map/all_to_all | solution.py:622
  63.5 0.0 copy-start.4
  63.5 10.8 %bilinear_weights.1.bil_grad_ref = bf16[64,1024]{1,0:T(8,128)(2,1)S(1)} custom-call(bf16[16,16384]{1,0:T(8,128)(2,1)S(1)} %get-tuple-element.81.refs_1_.basis_ref, bf16[64,16384]{1,0:T(8,128)(2,1)} %get-tuple-element.108.picked_hbm, bf16[64,16384]{1,0:T(8,128)(2,1)} %get-tuple-element.109.mixed_hbm), custom_call_target="tpu_custom_call" | custom-call | flops 8589934592 | bytes 1048576 | tf_op jit(solution)/shard_map/bilinear_weights/pallas_call | solution.py:624
  74.3 0.5 edges.1
  74.8 0.0 copy-start.5
  74.8 0.4 collective-permute-start.18
  75.2 0.3 atom_slab.1.slab_ref
  75.5 0.7 collective-permute-done.18.far_ref
  76.3 3.6 %collective-permute-start.19 = (bf16[128,128]{1,0:T(8,128)(2,1)S(1)}, bf16[128,128]{1,0:T(8,128)(2,1)S(1)}, u32[]{:S(2)}, u32[]{:S(2)}) collective-permute-start(bf16[128,128]{1,0:T(8,128)(2,1)S(1)} %get-tuple-element.113), channel_id=1, source_target_pairs={{0,6},{1,7},{2,4},{3,5},{4,2},{5,3},{6,0},{7,1},{8,14},{9,15},{10,... | collective-permute-start | bytes 98312 | tf_op jit(solution)/shard_map/ppermute | solution.py:433
  79.9 0.9 collective-permute-start.21
  80.7 1.3 %input_grads.1 = f32[512,512]{1,0:T(8,128)} custom-call(bf16[64,512]{1,0:T(8,128)(2,1)S(1)} %get-tuple-element.117.grad_project_ref, bf16[64,512]{1,0:T(8,128)(2,1)S(1)} %bitcast.19, f32[512,512]{1,0:T(8,128)S(1)} %get-tuple-element.118.grad_new_ref), custom_call_target="tpu_custom_call" | custom-call | flops 1073741824 | bytes 1048576 | tf_op jit(solution)/shard_map/input_grads/pallas_call | solution.py:649
  82.0 0.1 collective-permute-done.19.refs_0_
  82.1 2.6 %collective-permute-done.20.refs_1_ = bf16[128,128]{1,0:T(8,128)(2,1)S(1)} collective-permute-done((bf16[128,128]{1,0:T(8,128)(2,1)S(1)}, bf16[128,128]{1,0:T(8,128)(2,1)S(1)}, u32[]{:S(2)}, u32[]{:S(2)}) %collective-permute-start.20) | collective-permute-done | bytes 32800 | tf_op jit(solution)/shard_map/ppermute | solution.py:433
  84.7 2.5 %collective-permute-start.22 = (bf16[384,128]{1,0:T(8,128)(2,1)S(1)}, bf16[384,128]{1,0:T(8,128)(2,1)S(1)}, u32[]{:S(2)}, u32[]{:S(2)}) collective-permute-start(bf16[384,128]{1,0:T(8,128)(2,1)S(1)} %share.1.refs_3_), channel_id=1, source_target_pairs={{0,24},{8,16},{16,8},{24,0},{1,25},{9,17},{17,9},{25,1},{2,26},{10... | collective-permute-start | bytes 294920 | tf_op jit(solution)/shard_map/ppermute | solution.py:433
  87.2 0.5 collective-permute-start.23
  87.7 0.5 collective-permute-start.24
  88.2 2.6 %collective-permute-done.22.refs_0_ = bf16[384,128]{1,0:T(8,128)(2,1)S(1)} collective-permute-done((bf16[384,128]{1,0:T(8,128)(2,1)S(1)}, bf16[384,128]{1,0:T(8,128)(2,1)S(1)}, u32[]{:S(2)}, u32[]{:S(2)}) %collective-permute-start.22) | collective-permute-done | bytes 98336 | tf_op jit(solution)/shard_map/ppermute | solution.py:433
  90.8 1.0 collective-permute-done.23.refs_1_
  91.9 0.5 collective-permute-done.24.refs_2_
  92.3 0.1 total.1.refs_7_
  92.4 1.5 %collective-permute-start.25 = (bf16[384,128]{1,0:T(8,128)(2,1)S(1)}, bf16[384,128]{1,0:T(8,128)(2,1)S(1)}, u32[]{:S(2)}, u32[]{:S(2)}) collective-permute-start(bf16[384,128]{1,0:T(8,128)(2,1)S(1)} %total.1.refs_7_), channel_id=1, source_target_pairs={{0,6},{1,7},{2,4},{3,5},{4,2},{5,3},{6,0},{7,1},{8,14},{9,15},{10,... | collective-permute-start | bytes 294920 | tf_op jit(solution)/shard_map/ppermute | solution.py:433
  93.9 0.6 collective-permute-start.27
  94.6 2.3 %collective-permute-start.29 = (bf16[384,128]{1,0:T(8,128)(2,1)S(1)}, bf16[384,128]{1,0:T(8,128)(2,1)S(1)}, u32[]{:S(2)}, u32[]{:S(2)}) collective-permute-start(bf16[384,128]{1,0:T(8,128)(2,1)S(1)} %total.1.refs_7_), channel_id=1, source_target_pairs={{0,2},{1,3},{2,0},{3,1},{4,6},{5,7},{6,4},{7,5},{8,10},{9,11},{10,... | collective-permute-start | bytes 294920 | tf_op jit(solution)/shard_map/ppermute | solution.py:433
  96.8 2.7 %collective-permute-done.25.refs_1_ = bf16[384,128]{1,0:T(8,128)(2,1)S(1)} collective-permute-done((bf16[384,128]{1,0:T(8,128)(2,1)S(1)}, bf16[384,128]{1,0:T(8,128)(2,1)S(1)}, u32[]{:S(2)}, u32[]{:S(2)}) %collective-permute-start.25) | collective-permute-done | bytes 98336 | tf_op jit(solution)/shard_map/ppermute | solution.py:433
  99.6 3.0 %collective-permute-done.27.refs_3_ = bf16[384,128]{1,0:T(8,128)(2,1)S(1)} collective-permute-done((bf16[384,128]{1,0:T(8,128)(2,1)S(1)}, bf16[384,128]{1,0:T(8,128)(2,1)S(1)}, u32[]{:S(2)}, u32[]{:S(2)}) %collective-permute-start.27) | collective-permute-done | bytes 98336 | tf_op jit(solution)/shard_map/ppermute | solution.py:433
  102.6 0.5 collective-permute-start.30
  103.1 0.8 collective-permute-done.28.refs_2_
  103.9 0.2 collective-permute-done.30.refs_4_
  104.0 1.2 %weights.1 = (f32[64,512]{1,0:T(8,128)}, f32[64,1024]{1,0:T(8,128)}, f32[64,512]{1,0:T(8,128)}, f32[512,512]{1,0:T(8,128)}) custom-call(bf16[384,128]{1,0:T(8,128)(2,1)S(1)} %collective-permute-done.26.refs_0_, bf16[384,128]{1,0:T(8,128)(2,1)S(1)} %collective-permute-done.25.refs_1_, bf16[384,128]{1,0:T(8,128)(2,1)S(1)} %collective-permute-done.28.refs_2_, ...), custom_call_target="tpu_custom_call" | custom-call | tf_op jit(solution)/shard_map/weights/pallas_call | solution.py:688
  (29 shorter events, 0.1 us)
Async XLA Ops:
  2.0 10.1 %collective-permute-start = (bf16[64,512]{1,0:T(8,128)(2,1)S(1)}, bf16[64,512]{1,0:T(8,128)(2,1)S(1)}, u32[]{:S(2)}, u32[]{:S(2)}) collective-permute-start(bf16[64,512]{1,0:T(8,128)(2,1)S(1)} %get-tuple-element.89.refs_13_), channel_id=1, source_target_pairs={{0,6},{1,7},{2,4},{3,5},{4,2},{5,3},{6,0},{7,1},{8,14},{9,15},{10,... | collective-permute-start | bytes 196616 | tf_op jit(solution)/shard_map/ppermute | solution.py:433
  7.1 5.6 %collective-permute-start.1 = (bf16[64,512]{1,0:T(8,128)(2,1)S(1)}, bf16[64,512]{1,0:T(8,128)(2,1)S(1)}, u32[]{:S(2)}, u32[]{:S(2)}) collective-permute-start(bf16[64,512]{1,0:T(8,128)(2,1)S(1)} %get-tuple-element.89.refs_13_), channel_id=1, source_target_pairs={{0,4},{1,5},{2,6},{3,7},{4,0},{5,1},{6,2},{7,3},{8,12},{9,13},{10,... | collective-permute-start | bytes 196616 | tf_op jit(solution)/shard_map/ppermute | solution.py:433
  7.1 5.6 %collective-permute-start.2 = (bf16[64,512]{1,0:T(8,128)(2,1)S(1)}, bf16[64,512]{1,0:T(8,128)(2,1)S(1)}, u32[]{:S(2)}, u32[]{:S(2)}) collective-permute-start(bf16[64,512]{1,0:T(8,128)(2,1)S(1)} %get-tuple-element.89.refs_13_), channel_id=1, source_target_pairs={{0,2},{1,3},{2,0},{3,1},{4,6},{5,7},{6,4},{7,5},{8,10},{9,11},{10,... | collective-permute-start | bytes 196616 | tf_op jit(solution)/shard_map/ppermute | solution.py:433
  12.7 1.7 %collective-permute-start.3 = (bf16[64,512]{1,0:T(8,128)(2,1)S(1)}, bf16[64,512]{1,0:T(8,128)(2,1)S(1)}, u32[]{:S(2)}, u32[]{:S(2)}) collective-permute-start(bf16[64,512]{1,0:T(8,128)(2,1)S(1)} %collective-permute-done.refs_7_), channel_id=1, source_target_pairs={{0,1},{1,0},{2,3},{3,2},{4,5},{5,4},{6,7},{7,6},{8,9},{9,8},{10,11... | collective-permute-start | bytes 196616 | tf_op jit(solution)/shard_map/ppermute | solution.py:433
  12.7 1.7 %collective-permute-start.4 = (bf16[64,512]{1,0:T(8,128)(2,1)S(1)}, bf16[64,512]{1,0:T(8,128)(2,1)S(1)}, u32[]{:S(2)}, u32[]{:S(2)}) collective-permute-start(bf16[64,512]{1,0:T(8,128)(2,1)S(1)} %collective-permute-done.1.refs_9_), channel_id=1, source_target_pairs={{0,1},{1,0},{2,3},{3,2},{4,5},{5,4},{6,7},{7,6},{8,9},{9,8},{10,11... | collective-permute-start | bytes 196616 | tf_op jit(solution)/shard_map/ppermute | solution.py:433
  13.3 1.3 %collective-permute-start.5 = (bf16[64,512]{1,0:T(8,128)(2,1)S(1)}, bf16[64,512]{1,0:T(8,128)(2,1)S(1)}, u32[]{:S(2)}, u32[]{:S(2)}) collective-permute-start(bf16[64,512]{1,0:T(8,128)(2,1)S(1)} %collective-permute-done.2.refs_11_), channel_id=1, source_target_pairs={{0,1},{1,0},{2,3},{3,2},{4,5},{5,4},{6,7},{7,6},{8,9},{9,8},{10,11... | collective-permute-start | bytes 196616 | tf_op jit(solution)/shard_map/ppermute | solution.py:433
  13.3 1.4 %collective-permute-start.6 = (bf16[64,512]{1,0:T(8,128)(2,1)S(1)}, bf16[64,512]{1,0:T(8,128)(2,1)S(1)}, u32[]{:S(2)}, u32[]{:S(2)}) collective-permute-start(bf16[64,512]{1,0:T(8,128)(2,1)S(1)} %get-tuple-element.89.refs_13_), channel_id=1, source_target_pairs={{0,1},{1,0},{2,3},{3,2},{4,5},{5,4},{6,7},{7,6},{8,9},{9,8},{10,11... | collective-permute-start | bytes 196616 | tf_op jit(solution)/shard_map/ppermute | solution.py:433
  27.8 1.4 %collective-permute-start.7 = (bf16[4,32,512]{2,1,0:T(8,128)(2,1)S(1)}, bf16[4,32,512]{2,1,0:T(8,128)(2,1)S(1)}, u32[]{:S(2)}, u32[]{:S(2)}) collective-permute-start(bf16[4,32,512]{2,1,0:T(8,128)(2,1)S(1)} %get-tuple-element.92), channel_id=1, source_target_pairs={{0,1},{1,0},{2,3},{3,2},{4,5},{5,4},{6,7},{7,6},{8,9},{9,8},{10,11... | collective-permute-start | bytes 393224 | tf_op jit(solution)/shard_map/ppermute | solution.py:433
  29.2 8.1 %copy-start = (bf16[512,512]{1,0:T(8,128)(2,1)S(1)}, bf16[512,512]{1,0:T(8,128)(2,1)}, u32[]{:S(2)}) copy-start(bf16[512,512]{1,0:T(8,128)(2,1)} %atom_weight_ref.1) | copy-start | bytes 1572868
  29.2 8.1 %copy-start.1 = (bf16[1,32,512]{2,1,0:T(8,128)(2,1)S(1)}, bf16[1,32,512]{2,1,0:T(8,128)(2,1)}, u32[]{:S(2)}) copy-start(bf16[1,32,512]{2,1,0:T(8,128)(2,1)} %param.14) | copy-start | bytes 98308
  29.2 8.1 %copy-start.2 = (bf16[1,32,512]{2,1,0:T(8,128)(2,1)S(1)}, bf16[1,32,512]{2,1,0:T(8,128)(2,1)}, u32[]{:S(2)}) copy-start(bf16[1,32,512]{2,1,0:T(8,128)(2,1)} %param.21) | copy-start | bytes 98308
  29.2 6.2 %collective-permute-start.8 = (bf16[32,512]{1,0:T(8,128)(2,1)S(1)}, bf16[32,512]{1,0:T(8,128)(2,1)S(1)}, u32[]{:S(2)}, u32[]{:S(2)}) collective-permute-start(bf16[32,512]{1,0:T(8,128)(2,1)S(1)} %get-tuple-element.93), channel_id=1, source_target_pairs={{0,6},{1,7},{2,4},{3,5},{4,2},{5,3},{6,0},{7,1},{8,14},{9,15},{10,... | collective-permute-start | bytes 98312 | tf_op jit(solution)/shard_map/ppermute | solution.py:433
  32.5 4.8 %collective-permute-start.9 = (bf16[32,512]{1,0:T(8,128)(2,1)S(1)}, bf16[32,512]{1,0:T(8,128)(2,1)S(1)}, u32[]{:S(2)}, u32[]{:S(2)}) collective-permute-start(bf16[32,512]{1,0:T(8,128)(2,1)S(1)} %get-tuple-element.94), channel_id=1, source_target_pairs={{0,4},{1,5},{2,6},{3,7},{4,0},{5,1},{6,2},{7,3},{8,12},{9,13},{10,... | collective-permute-start | bytes 98312 | tf_op jit(solution)/shard_map/ppermute | solution.py:433
  32.5 4.8 %collective-permute-start.10 = (bf16[32,512]{1,0:T(8,128)(2,1)S(1)}, bf16[32,512]{1,0:T(8,128)(2,1)S(1)}, u32[]{:S(2)}, u32[]{:S(2)}) collective-permute-start(bf16[32,512]{1,0:T(8,128)(2,1)S(1)} %get-tuple-element.95), channel_id=1, source_target_pairs={{0,2},{1,3},{2,0},{3,1},{4,6},{5,7},{6,4},{7,5},{8,10},{9,11},{10,... | collective-permute-start | bytes 98312 | tf_op jit(solution)/shard_map/ppermute | solution.py:433
  33.7 14.2 %copy-start.3 = (bf16[1,512,512]{2,1,0:T(8,128)(2,1)S(1)}, bf16[1,512,512]{2,1,0:T(8,128)(2,1)}, u32[]{:S(2)}) copy-start(bf16[1,512,512]{2,1,0:T(8,128)(2,1)} %param.20) | copy-start | bytes 1572868
  38.2 6.8 %collective-permute-start.11 = (bf16[2,32,512]{2,1,0:T(8,128)(2,1)S(1)}, bf16[2,32,512]{2,1,0:T(8,128)(2,1)S(1)}, u32[]{:S(2)}, u32[]{:S(2)}) collective-permute-start(bf16[2,32,512]{2,1,0:T(8,128)(2,1)S(1)} %get-tuple-element.105.refs_7_.refs_0_), channel_id=1, source_target_pairs={{0,6},{1,7},{2,4},{3,5},{4,2},{5,3},{6,0},{7,1},{8,14},{9,15},{10,... | collective-permute-start | bytes 196616 | tf_op jit(solution)/shard_map/ppermute | solution.py:433
  39.8 6.6 %collective-permute-start.13 = (bf16[2,32,512]{2,1,0:T(8,128)(2,1)S(1)}, bf16[2,32,512]{2,1,0:T(8,128)(2,1)S(1)}, u32[]{:S(2)}, u32[]{:S(2)}) collective-permute-start(bf16[2,32,512]{2,1,0:T(8,128)(2,1)S(1)} %get-tuple-element.105.refs_7_.refs_0_), channel_id=1, source_target_pairs={{0,4},{1,5},{2,6},{3,7},{4,0},{5,1},{6,2},{7,3},{8,12},{9,13},{10,... | collective-permute-start | bytes 196616 | tf_op jit(solution)/shard_map/ppermute | solution.py:433
  40.2 6.2 %collective-permute-start.15 = (bf16[2,32,512]{2,1,0:T(8,128)(2,1)S(1)}, bf16[2,32,512]{2,1,0:T(8,128)(2,1)S(1)}, u32[]{:S(2)}, u32[]{:S(2)}) collective-permute-start(bf16[2,32,512]{2,1,0:T(8,128)(2,1)S(1)} %get-tuple-element.105.refs_7_.refs_0_), channel_id=1, source_target_pairs={{0,2},{1,3},{2,0},{3,1},{4,6},{5,7},{6,4},{7,5},{8,10},{9,11},{10,... | collective-permute-start | bytes 196616 | tf_op jit(solution)/shard_map/ppermute | solution.py:433
  42.5 4.4 %collective-permute-start.17 = (bf16[2,32,512]{2,1,0:T(8,128)(2,1)S(1)}, bf16[2,32,512]{2,1,0:T(8,128)(2,1)S(1)}, u32[]{:S(2)}, u32[]{:S(2)}) collective-permute-start(bf16[2,32,512]{2,1,0:T(8,128)(2,1)S(1)} %get-tuple-element.105.refs_7_.refs_0_), channel_id=1, source_target_pairs={{0,1},{1,0},{2,3},{3,2},{4,5},{5,4},{6,7},{7,6},{8,9},{9,8},{10,11... | collective-permute-start | bytes 196616 | tf_op jit(solution)/shard_map/ppermute | solution.py:433
  45.0 2.0 %collective-permute-start.12 = (bf16[2,32,512]{2,1,0:T(8,128)(2,1)S(1)}, bf16[2,32,512]{2,1,0:T(8,128)(2,1)S(1)}, u32[]{:S(2)}, u32[]{:S(2)}) collective-permute-start(bf16[2,32,512]{2,1,0:T(8,128)(2,1)S(1)} %collective-permute-done.11.refs_1_.refs_6_), channel_id=1, source_target_pairs={{0,1},{1,0},{2,3},{3,2},{4,5},{5,4},{6,7},{7,6},{8,9},{9,8},{10,11... | collective-permute-start | bytes 196616 | tf_op jit(solution)/shard_map/ppermute | solution.py:433
  46.4 1.3 %collective-permute-start.14 = (bf16[2,32,512]{2,1,0:T(8,128)(2,1)S(1)}, bf16[2,32,512]{2,1,0:T(8,128)(2,1)S(1)}, u32[]{:S(2)}, u32[]{:S(2)}) collective-permute-start(bf16[2,32,512]{2,1,0:T(8,128)(2,1)S(1)} %collective-permute-done.13.refs_3_.refs_4_), channel_id=1, source_target_pairs={{0,1},{1,0},{2,3},{3,2},{4,5},{5,4},{6,7},{7,6},{8,9},{9,8},{10,11... | collective-permute-start | bytes 196616 | tf_op jit(solution)/shard_map/ppermute | solution.py:433
  46.4 1.4 %collective-permute-start.16 = (bf16[2,32,512]{2,1,0:T(8,128)(2,1)S(1)}, bf16[2,32,512]{2,1,0:T(8,128)(2,1)S(1)}, u32[]{:S(2)}, u32[]{:S(2)}) collective-permute-start(bf16[2,32,512]{2,1,0:T(8,128)(2,1)S(1)} %collective-permute-done.15.refs_5_.refs_2_), channel_id=1, source_target_pairs={{0,1},{1,0},{2,3},{3,2},{4,5},{5,4},{6,7},{7,6},{8,9},{9,8},{10,11... | collective-permute-start | bytes 196616 | tf_op jit(solution)/shard_map/ppermute | solution.py:433
  59.9 14.4 %all-to-all-start = ((bf16[8,80,128]{2,1,0:T(8,128)(2,1)}), bf16[8,80,128]{2,1,0:T(8,128)(2,1)S(1)}, u32[]{:S(2)}, u32[]{:S(2)}) async-start(bf16[8,80,128]{2,1,0:T(8,128)(2,1)} %get-tuple-element.106), calls=%async_computation | async-start | bytes 327680 | tf_op jit(solution)/shard_map/all_to_all | solution.py:622
  63.5 10.8 %copy-start.4 = (bf16[1,512,512]{2,1,0:T(8,128)(2,1)S(1)}, bf16[1,512,512]{2,1,0:T(8,128)(2,1)}, u32[]{:S(2)}) copy-start(bf16[1,512,512]{2,1,0:T(8,128)(2,1)} %param.13) | copy-start | bytes 1572868
  74.8 5.9 %copy-start.5 = (bf16[512,64]{0,1:T(8,128)(2,1)S(1)}, bf16[512,64]{0,1:T(8,128)(2,1)}, u32[]{:S(2)}) copy-start(bf16[512,64]{0,1:T(8,128)(2,1)} %param.22) | copy-start | bytes 196612
  74.8 1.4 %collective-permute-start.18 = (bf16[4,128,128]{2,1,0:T(8,128)(2,1)S(1)}, bf16[4,128,128]{2,1,0:T(8,128)(2,1)S(1)}, u32[]{:S(2)}, u32[]{:S(2)}) collective-permute-start(bf16[4,128,128]{2,1,0:T(8,128)(2,1)S(1)} %get-tuple-element.112), channel_id=1, source_target_pairs={{0,1},{1,0},{2,3},{3,2},{4,5},{5,4},{6,7},{7,6},{8,9},{9,8},{10,11... | collective-permute-start | bytes 393224 | tf_op jit(solution)/shard_map/ppermute | solution.py:433
  76.3 5.8 %collective-permute-start.19 = (bf16[128,128]{1,0:T(8,128)(2,1)S(1)}, bf16[128,128]{1,0:T(8,128)(2,1)S(1)}, u32[]{:S(2)}, u32[]{:S(2)}) collective-permute-start(bf16[128,128]{1,0:T(8,128)(2,1)S(1)} %get-tuple-element.113), channel_id=1, source_target_pairs={{0,6},{1,7},{2,4},{3,5},{4,2},{5,3},{6,0},{7,1},{8,14},{9,15},{10,... | collective-permute-start | bytes 98312 | tf_op jit(solution)/shard_map/ppermute | solution.py:433
  79.9 4.8 %collective-permute-start.20 = (bf16[128,128]{1,0:T(8,128)(2,1)S(1)}, bf16[128,128]{1,0:T(8,128)(2,1)S(1)}, u32[]{:S(2)}, u32[]{:S(2)}) collective-permute-start(bf16[128,128]{1,0:T(8,128)(2,1)S(1)} %get-tuple-element.114), channel_id=1, source_target_pairs={{0,4},{1,5},{2,6},{3,7},{4,0},{5,1},{6,2},{7,3},{8,12},{9,13},{10,... | collective-permute-start | bytes 98312 | tf_op jit(solution)/shard_map/ppermute | solution.py:433
  79.9 4.8 %collective-permute-start.21 = (bf16[128,128]{1,0:T(8,128)(2,1)S(1)}, bf16[128,128]{1,0:T(8,128)(2,1)S(1)}, u32[]{:S(2)}, u32[]{:S(2)}) collective-permute-start(bf16[128,128]{1,0:T(8,128)(2,1)S(1)} %get-tuple-element.115), channel_id=1, source_target_pairs={{0,2},{1,3},{2,0},{3,1},{4,6},{5,7},{6,4},{7,5},{8,10},{9,11},{10,... | collective-permute-start | bytes 98312 | tf_op jit(solution)/shard_map/ppermute | solution.py:433
  84.7 6.1 %collective-permute-start.22 = (bf16[384,128]{1,0:T(8,128)(2,1)S(1)}, bf16[384,128]{1,0:T(8,128)(2,1)S(1)}, u32[]{:S(2)}, u32[]{:S(2)}) collective-permute-start(bf16[384,128]{1,0:T(8,128)(2,1)S(1)} %share.1.refs_3_), channel_id=1, source_target_pairs={{0,24},{8,16},{16,8},{24,0},{1,25},{9,17},{17,9},{25,1},{2,26},{10... | collective-permute-start | bytes 294920 | tf_op jit(solution)/shard_map/ppermute | solution.py:433
  87.2 4.7 %collective-permute-start.23 = (bf16[384,128]{1,0:T(8,128)(2,1)S(1)}, bf16[384,128]{1,0:T(8,128)(2,1)S(1)}, u32[]{:S(2)}, u32[]{:S(2)}) collective-permute-start(bf16[384,128]{1,0:T(8,128)(2,1)S(1)} %share.1.refs_3_), channel_id=1, source_target_pairs={{0,16},{8,24},{16,0},{24,8},{1,17},{9,25},{17,1},{25,9},{2,18},{10... | collective-permute-start | bytes 294920 | tf_op jit(solution)/shard_map/ppermute | solution.py:433
  87.7 4.6 %collective-permute-start.24 = (bf16[384,128]{1,0:T(8,128)(2,1)S(1)}, bf16[384,128]{1,0:T(8,128)(2,1)S(1)}, u32[]{:S(2)}, u32[]{:S(2)}) collective-permute-start(bf16[384,128]{1,0:T(8,128)(2,1)S(1)} %share.1.refs_3_), channel_id=1, source_target_pairs={{0,8},{8,0},{16,24},{24,16},{1,9},{9,1},{17,25},{25,17},{2,10},{10... | collective-permute-start | bytes 294920 | tf_op jit(solution)/shard_map/ppermute | solution.py:433
  92.4 7.2 %collective-permute-start.25 = (bf16[384,128]{1,0:T(8,128)(2,1)S(1)}, bf16[384,128]{1,0:T(8,128)(2,1)S(1)}, u32[]{:S(2)}, u32[]{:S(2)}) collective-permute-start(bf16[384,128]{1,0:T(8,128)(2,1)S(1)} %total.1.refs_7_), channel_id=1, source_target_pairs={{0,6},{1,7},{2,4},{3,5},{4,2},{5,3},{6,0},{7,1},{8,14},{9,15},{10,... | collective-permute-start | bytes 294920 | tf_op jit(solution)/shard_map/ppermute | solution.py:433
  93.9 8.6 %collective-permute-start.27 = (bf16[384,128]{1,0:T(8,128)(2,1)S(1)}, bf16[384,128]{1,0:T(8,128)(2,1)S(1)}, u32[]{:S(2)}, u32[]{:S(2)}) collective-permute-start(bf16[384,128]{1,0:T(8,128)(2,1)S(1)} %total.1.refs_7_), channel_id=1, source_target_pairs={{0,4},{1,5},{2,6},{3,7},{4,0},{5,1},{6,2},{7,3},{8,12},{9,13},{10,... | collective-permute-start | bytes 294920 | tf_op jit(solution)/shard_map/ppermute | solution.py:433
  94.6 8.0 %collective-permute-start.29 = (bf16[384,128]{1,0:T(8,128)(2,1)S(1)}, bf16[384,128]{1,0:T(8,128)(2,1)S(1)}, u32[]{:S(2)}, u32[]{:S(2)}) collective-permute-start(bf16[384,128]{1,0:T(8,128)(2,1)S(1)} %total.1.refs_7_), channel_id=1, source_target_pairs={{0,2},{1,3},{2,0},{3,1},{4,6},{5,7},{6,4},{7,5},{8,10},{9,11},{10,... | collective-permute-start | bytes 294920 | tf_op jit(solution)/shard_map/ppermute | solution.py:433
  96.8 6.2 %collective-permute-start.31 = (bf16[384,128]{1,0:T(8,128)(2,1)S(1)}, bf16[384,128]{1,0:T(8,128)(2,1)S(1)}, u32[]{:S(2)}, u32[]{:S(2)}) collective-permute-start(bf16[384,128]{1,0:T(8,128)(2,1)S(1)} %total.1.refs_7_), channel_id=1, source_target_pairs={{0,1},{1,0},{2,3},{3,2},{4,5},{5,4},{6,7},{7,6},{8,9},{9,8},{10,11... | collective-permute-start | bytes 294920 | tf_op jit(solution)/shard_map/ppermute | solution.py:433
  99.6 3.5 %collective-permute-start.26 = (bf16[384,128]{1,0:T(8,128)(2,1)S(1)}, bf16[384,128]{1,0:T(8,128)(2,1)S(1)}, u32[]{:S(2)}, u32[]{:S(2)}) collective-permute-start(bf16[384,128]{1,0:T(8,128)(2,1)S(1)} %collective-permute-done.25.refs_1_), channel_id=1, source_target_pairs={{0,1},{1,0},{2,3},{3,2},{4,5},{5,4},{6,7},{7,6},{8,9},{9,8},{10,11... | collective-permute-start | bytes 294920 | tf_op jit(solution)/shard_map/ppermute | solution.py:433
  102.6 1.3 %collective-permute-start.28 = (bf16[384,128]{1,0:T(8,128)(2,1)S(1)}, bf16[384,128]{1,0:T(8,128)(2,1)S(1)}, u32[]{:S(2)}, u32[]{:S(2)}) collective-permute-start(bf16[384,128]{1,0:T(8,128)(2,1)S(1)} %collective-permute-done.27.refs_3_), channel_id=1, source_target_pairs={{0,1},{1,0},{2,3},{3,2},{4,5},{5,4},{6,7},{7,6},{8,9},{9,8},{10,11... | collective-permute-start | bytes 294920 | tf_op jit(solution)/shard_map/ppermute | solution.py:433
  102.6 1.5 %collective-permute-start.30 = (bf16[384,128]{1,0:T(8,128)(2,1)S(1)}, bf16[384,128]{1,0:T(8,128)(2,1)S(1)}, u32[]{:S(2)}, u32[]{:S(2)}) collective-permute-start(bf16[384,128]{1,0:T(8,128)(2,1)S(1)} %collective-permute-done.29.refs_5_), channel_id=1, source_target_pairs={{0,1},{1,0},{2,3},{3,2},{4,5},{5,4},{6,7},{7,6},{8,9},{9,8},{10,11... | collective-permute-start | bytes 294920 | tf_op jit(solution)/shard_map/ppermute | solution.py:433

commit v6 on v5

--- a/solution.py
+++ b/solution.py
@@ -316,10 +316,13 @@
         parts_ref[me ^ source] = jnp.concatenate([piece, ranks, spare], axis=0).astype(jnp.bfloat16)
 
 
-def weight_kernel(basis_ref, picked_hbm, mixed_hbm, out_ref, picked, mixed, spread, total, sems):
+def weight_kernel(
+    basis_ref, picked_hbm, mixed_hbm, out_ref, picked, mixed, spread, scaled, total, sems
+):
     width, trips = picked.shape
     tile = spread.shape[1]
     steps = trips // tile
+    moved = scaled.shape[0] // width - 1
     for step in range(steps):
         tile_copy(picked_hbm, picked, sems.at[0], step, tile).start()
         tile_copy(mixed_hbm, mixed, sems.at[1], step, tile).start()
@@ -327,17 +330,26 @@
 
     def one_tile(step, carry):
         span = pl.ds(pl.multiple_of(step * tile, tile), tile)
+        basis = basis_ref[:, span]
         tile_copy(picked_hbm, picked, sems.at[0], step, tile).wait()
         tile_copy(mixed_hbm, mixed, sems.at[1], step, tile).wait()
         feat = picked[:, span]
-        basis = basis_ref[:, span]
-        for row in range(basis.shape[0]):
-            spread[row * width : (row + 1) * width, :] = feat * basis[row : row + 1, :]
-        total[...] += dot32(spread[...], mixed[:, span], LAST_LAST)
+        spread[:width, :] = feat
+        for row in range(moved, basis.shape[0]):
+            at = (row - moved + 1) * width
+            spread[at : at + width, :] = feat * basis[row : row + 1, :]
+        grad = mixed[:, span]
+        scaled[:width, :] = grad
+        for row in range(moved):
+            at = (row + 1) * width
+            scaled[at : at + width, :] = grad * basis[row : row + 1, :]
+        total[...] += dot32(spread[...], scaled[...], LAST_LAST)
         return carry
 
     lax.fori_loop(0, steps, one_tile, 0)
-    out_ref[...] = total[...].T.astype(jnp.bfloat16)
+    first = [total[:width, (row + 1) * width : (row + 2) * width] for row in range(moved)]
+    whole = jnp.concatenate([*first, total[width:, :width]], axis=0)
+    out_ref[...] = whole.T.astype(jnp.bfloat16)
 
 
 def input_kernel(grad_project_ref, down_ref, grad_new_ref, grad_in_ref):
@@ -620,7 +632,7 @@
         *pairs[::-1],
     )
     feat_parts = lax.all_to_all(feat_parts, "graph", 0, 0, tiled=True)
-    wide = math.gcd(trips, tile)
+    wide = math.gcd(trips, 2 * tile)
     wbil_term = pl.pallas_call(
         weight_kernel,
         in_specs=[VMEM, HBM, HBM],
@@ -628,8 +640,9 @@
         scratch_shapes=[
             pltpu.VMEM((width, trips), b16),
             pltpu.VMEM((width, trips), b16),
-            pltpu.VMEM((w_bil.shape[0], wide), b16),
-            pltpu.VMEM((w_bil.shape[0], width), f32),
+            pltpu.VMEM((w_bil.shape[0] + 2 * width - BLOCK, wide), b16),
+            pltpu.VMEM((BLOCK, wide), b16),
+            pltpu.VMEM((w_bil.shape[0] + 2 * width - BLOCK, BLOCK), f32),
             pltpu.SemaphoreType.DMA((2, trips // wide)),
         ],
         compiler_params=params(),

time: 105 us -> 105 us (level)
  no operation moved by 1% of the time
where the time goes in v6:
time: 105 us; the launch traced here: 104 us
  Pallas kernels  45.5 us (43%)
  starting transfers between devices  33.5 us (32%)
  waiting for transfers between devices  23.8 us (23%)
  between operations  1.47 us (1%)
    ppermute x32, starting transfers between devices, swap(): return lax.ppermute(value, axis, [(at, at ^ mask) for at in range(members)])  29.9 us
    ppermute x32, waiting for transfers between devices, swap(): return lax.ppermute(value, axis, [(at, at ^ mask) for at in range(members)])  23.8 us
    pallas_call x1, Pallas kernels, body(): pl.pallas_call(functools.partial(forward_kernel, members), in_specs=[SMEM...  13.1 us
    pallas_call x1, Pallas kernels, body(): pl.pallas_call(functools.partial(backward_kernel, members), in_specs=[SME...  12 us
    pallas_call x1, Pallas kernels, body(): pl.pallas_call(weight_kernel, in_specs=[VMEM, HBM, HBM], out_shape=shaped...  9.87 us
    pallas_call x1, Pallas kernels, body(): pl.pallas_call(functools.partial(index_kernel, members), in_specs=[HBM] *...  4.3 us
    all_to_all x1, starting transfers between devices, body(): feat_parts = lax.all_to_all(feat_parts, 'graph', 0, 0, tiled=True)  3.61 us
  transfers between devices with their start and end apart: 33, of which 20 were waited for; matrix products, arithmetic and copies ran while one was open for 0% of the time, Pallas kernels for 16%

profile of v6, /device:TPU:0, one launch (start us, length us, event | category | flops | bytes accessed | tf_op | source)
XLA Modules:
  0.0 104.3 jit_solution(10594061769066541462)
XLA Ops:
  0.6 1.4 %features.1 = (f32[64,512]{1,0:T(8,128)S(1)}, bf16[64,512]{1,0:T(8,128)(2,1)S(1)}) custom-call(bf16[512,512]{1,0:T(8,128)(2,1)} %bitcast.15, bf16[64,512]{1,0:T(8,128)(2,1)} %bitcast.18), custom_call_target="tpu_custom_call" | custom-call | flops 268435456 | bytes 1048576 | tf_op jit(solution)/shard_map/features/pallas_call | solution.py:505
  2.0 5.1 %collective-permute-start = (bf16[64,512]{1,0:T(8,128)(2,1)S(1)}, bf16[64,512]{1,0:T(8,128)(2,1)S(1)}, u32[]{:S(2)}, u32[]{:S(2)}) collective-permute-start(bf16[64,512]{1,0:T(8,128)(2,1)S(1)} %get-tuple-element.89.refs_13_), channel_id=1, source_target_pairs={{0,6},{1,7},{2,4},{3,5},{4,2},{5,3},{6,0},{7,1},{8,14},{9,15},{10,... | collective-permute-start | bytes 196616 | tf_op jit(solution)/shard_map/ppermute | solution.py:445
  7.1 0.6 collective-permute-start.2
  7.8 4.3 %slots.1 = (s32[1,16384]{1,0:T(1,128)S(1)}, f32[32,128]{1,0:T(8,128)S(1)}, bf16[64,1024]{1,0:T(8,128)(2,1)S(1)}, s32[1,16384]{1,0:T(1,128)S(1)}, bf16[16,16384]{...) custom-call(s32[1,16384]{1,0:T(1,128)} %in_hbm.1, ...), custom_call_target="tpu_custom_call" | custom-call | flops 2147483648 | bytes 1048576 | tf_op jit(solution)/shard_map/slots/pallas_call | solution.py:523
  12.1 0.0 collective-permute-done.refs_7_
  12.1 0.6 collective-permute-done.1.refs_9_
  12.7 0.5 collective-permute-start.4
  13.3 0.0 collective-permute-start.5
  13.3 0.5 collective-permute-start.6
  14.4 0.1 collective-permute-done.5.refs_10_
  14.5 0.2 collective-permute-done.6.refs_12_
  14.7 13.1 %forward_triplets.1 = (bf16[512,512]{1,0:T(8,128)(2,1)}, bf16[4,32,512]{2,1,0:T(8,128)(2,1)S(1)}, bf16[4,32,512]{2,1,0:T(8,128)(2,1)S(1)}, bf16[64,512]{1,0:T(8,128)(2,1)S(1)}, bf16[64,16384]{1,0:T(8,128)(2,1)}) custom-call(s32[1,1]{1,0:T(1,128)S(6)} %copy.20.count_ref, s32[1,16384]{1,0:T(1,128)S(1)} %get-tuple-element.78.slot_ref, ...), custom_call_target="tpu_custom_call" | custom-call | flops 12884901888 | bytes 1048576 | tf_op jit(solution)/shard_map/forward_triplets/pallas_call | solution.py:546
  27.8 0.4 collective-permute-start.7
  28.2 1.0 collective-permute-done.7.far_ref
  29.2 3.3 %collective-permute-start.8 = (bf16[32,512]{1,0:T(8,128)(2,1)S(1)}, bf16[32,512]{1,0:T(8,128)(2,1)S(1)}, u32[]{:S(2)}, u32[]{:S(2)}) collective-permute-start(bf16[32,512]{1,0:T(8,128)(2,1)S(1)} %get-tuple-element.93), channel_id=1, source_target_pairs={{0,6},{1,7},{2,4},{3,5},{4,2},{5,3},{6,0},{7,1},{8,14},{9,15},{10,... | collective-permute-start | bytes 98312 | tf_op jit(solution)/shard_map/ppermute | solution.py:445
  32.5 1.2 %collective-permute-start.10 = (bf16[32,512]{1,0:T(8,128)(2,1)S(1)}, bf16[32,512]{1,0:T(8,128)(2,1)S(1)}, u32[]{:S(2)}, u32[]{:S(2)}) collective-permute-start(bf16[32,512]{1,0:T(8,128)(2,1)S(1)} %get-tuple-element.95), channel_id=1, source_target_pairs={{0,2},{1,3},{2,0},{3,1},{4,6},{5,7},{6,4},{7,5},{8,10},{9,11},{10,... | collective-permute-start | bytes 98312 | tf_op jit(solution)/shard_map/ppermute | solution.py:445
  33.7 0.5 slopes.1.slope_ref
  34.2 1.2 %collective-permute-done.8.refs_0_ = bf16[32,512]{1,0:T(8,128)(2,1)S(1)} collective-permute-done((bf16[32,512]{1,0:T(8,128)(2,1)S(1)}, bf16[32,512]{1,0:T(8,128)(2,1)S(1)}, u32[]{:S(2)}, u32[]{:S(2)}) %collective-permute-start.8) | collective-permute-done | bytes 32800 | tf_op jit(solution)/shard_map/ppermute | solution.py:445
  35.4 1.9 %collective-permute-done.9.refs_1_ = bf16[32,512]{1,0:T(8,128)(2,1)S(1)} collective-permute-done((bf16[32,512]{1,0:T(8,128)(2,1)S(1)}, bf16[32,512]{1,0:T(8,128)(2,1)S(1)}, u32[]{:S(2)}, u32[]{:S(2)}) %collective-permute-start.9) | collective-permute-done | bytes 32800 | tf_op jit(solution)/shard_map/ppermute | solution.py:445
  37.3 0.0 collective-permute-done.10.refs_2_
  37.3 0.9 atoms.1
  38.2 1.7 %collective-permute-start.11 = (bf16[2,32,512]{2,1,0:T(8,128)(2,1)S(1)}, bf16[2,32,512]{2,1,0:T(8,128)(2,1)S(1)}, u32[]{:S(2)}, u32[]{:S(2)}) collective-permute-start(bf16[2,32,512]{2,1,0:T(8,128)(2,1)S(1)} %get-tuple-element.105.refs_7_.refs_0_), channel_id=1, source_target_pairs={{0,6},{1,7},{2,4},{3,5},{4,2},{5,3},{6,0},{7,1},{8,14},{9,15},{10,... | collective-permute-start | bytes 196616 | tf_op jit(solution)/shard_map/ppermute | solution.py:445
  39.8 0.3 collective-permute-start.13
  40.2 2.4 %collective-permute-start.15 = (bf16[2,32,512]{2,1,0:T(8,128)(2,1)S(1)}, bf16[2,32,512]{2,1,0:T(8,128)(2,1)S(1)}, u32[]{:S(2)}, u32[]{:S(2)}) collective-permute-start(bf16[2,32,512]{2,1,0:T(8,128)(2,1)S(1)} %get-tuple-element.105.refs_7_.refs_0_), channel_id=1, source_target_pairs={{0,2},{1,3},{2,0},{3,1},{4,6},{5,7},{6,4},{7,5},{8,10},{9,11},{10,... | collective-permute-start | bytes 196616 | tf_op jit(solution)/shard_map/ppermute | solution.py:445
  42.5 2.4 %collective-permute-done.11.refs_1_.refs_6_ = bf16[2,32,512]{2,1,0:T(8,128)(2,1)S(1)} collective-permute-done((bf16[2,32,512]{2,1,0:T(8,128)(2,1)S(1)}, bf16[2,32,512]{2,1,0:T(8,128)(2,1)S(1)}, u32[]{:S(2)}, u32[]{:S(2)}) %collective-permute-start.11) | collective-permute-done | bytes 65568 | tf_op jit(solution)/shard_map/ppermute | solution.py:445
  45.0 0.0 collective-permute-start.12
  45.0 1.4 %collective-permute-done.13.refs_3_.refs_4_ = bf16[2,32,512]{2,1,0:T(8,128)(2,1)S(1)} collective-permute-done((bf16[2,32,512]{2,1,0:T(8,128)(2,1)S(1)}, bf16[2,32,512]{2,1,0:T(8,128)(2,1)S(1)}, u32[]{:S(2)}, u32[]{:S(2)}) %collective-permute-start.13) | collective-permute-done | bytes 65568 | tf_op jit(solution)/shard_map/ppermute | solution.py:445
  46.4 0.0 collective-permute-start.14
  46.4 0.0 collective-permute-done.15.refs_5_.refs_2_
  46.4 0.5 collective-permute-start.16
  46.9 0.0 collective-permute-done.17.refs_6_.refs_1_
  46.9 0.0 collective-permute-done.12.refs_0_.refs_7_
  46.9 0.7 collective-permute-done.14.refs_2_.refs_5_
  47.7 0.2 collective-permute-done.16.refs_4_.refs_3_
  47.8 12.0 %backward_triplets.1 = (f32[512,512]{1,0:T(8,128)S(1)}, bf16[64,512]{1,0:T(8,128)(2,1)S(1)}, bf16[64,16384]{1,0:T(8,128)(2,1)}, bf16[8,80,128]{2,1,0:T(8,128)(2,1)}) custom-call(s32[1,1]{1,0:T(1,128)S(6)} %copy.20.count_ref, s32[1,16384]{1,0:T(1,128)S(1)} %get-tuple-element.78.slot_ref, s32[1,16384]{1,0:T(1,128)S(1)} %get-tuple-element.80.refs_0_.out_ref, ...), custom_call_target="tpu_custom_call" | custom-call | flops 12884901888 | bytes 1048576 | tf_op jit(solution)/shard_map/backward_triplets/pallas_call | solution.py:597
  59.9 3.6 %all-to-all-start = ((bf16[8,80,128]{2,1,0:T(8,128)(2,1)}), bf16[8,80,128]{2,1,0:T(8,128)(2,1)S(1)}, u32[]{:S(2)}, u32[]{:S(2)}) async-start(bf16[8,80,128]{2,1,0:T(8,128)(2,1)} %get-tuple-element.106), calls=%async_computation | async-start | bytes 327680 | tf_op jit(solution)/shard_map/all_to_all | solution.py:634
  63.5 0.0 copy-start.4
  63.5 9.9 %bilinear_weights.1.bil_grad_ref = bf16[64,1024]{1,0:T(8,128)(2,1)S(1)} custom-call(bf16[16,16384]{1,0:T(8,128)(2,1)S(1)} %get-tuple-element.81.refs_1_.basis_ref, bf16[64,16384]{1,0:T(8,128)(2,1)} %get-tuple-element.108.picked_hbm, bf16[64,16384]{1,0:T(8,128)(2,1)} %get-tuple-element.109.mixed_hbm), custom_call_target="tpu_custom_call" | custom-call | flops 8589934592 | bytes 1048576 | tf_op jit(solution)/shard_map/bilinear_weights/pallas_call | solution.py:636
  73.4 0.5 edges.1
  73.9 0.0 copy-start.5
  73.9 0.4 collective-permute-start.18
  74.3 0.3 atom_slab.1.slab_ref
  74.6 0.7 collective-permute-done.18.far_ref
  75.3 3.6 %collective-permute-start.19 = (bf16[128,128]{1,0:T(8,128)(2,1)S(1)}, bf16[128,128]{1,0:T(8,128)(2,1)S(1)}, u32[]{:S(2)}, u32[]{:S(2)}) collective-permute-start(bf16[128,128]{1,0:T(8,128)(2,1)S(1)} %get-tuple-element.113), channel_id=1, source_target_pairs={{0,6},{1,7},{2,4},{3,5},{4,2},{5,3},{6,0},{7,1},{8,14},{9,15},{10,... | collective-permute-start | bytes 98312 | tf_op jit(solution)/shard_map/ppermute | solution.py:445
  78.9 0.9 collective-permute-start.21
  79.8 1.3 %input_grads.1 = f32[512,512]{1,0:T(8,128)} custom-call(bf16[64,512]{1,0:T(8,128)(2,1)S(1)} %get-tuple-element.117.grad_project_ref, bf16[64,512]{1,0:T(8,128)(2,1)S(1)} %bitcast.19, f32[512,512]{1,0:T(8,128)S(1)} %get-tuple-element.118.grad_new_ref), custom_call_target="tpu_custom_call" | custom-call | flops 1073741824 | bytes 1048576 | tf_op jit(solution)/shard_map/input_grads/pallas_call | solution.py:662
  81.1 0.1 collective-permute-done.19.refs_0_
  81.2 2.6 %collective-permute-done.20.refs_1_ = bf16[128,128]{1,0:T(8,128)(2,1)S(1)} collective-permute-done((bf16[128,128]{1,0:T(8,128)(2,1)S(1)}, bf16[128,128]{1,0:T(8,128)(2,1)S(1)}, u32[]{:S(2)}, u32[]{:S(2)}) %collective-permute-start.20) | collective-permute-done | bytes 32800 | tf_op jit(solution)/shard_map/ppermute | solution.py:445
  83.8 2.5 %collective-permute-start.22 = (bf16[384,128]{1,0:T(8,128)(2,1)S(1)}, bf16[384,128]{1,0:T(8,128)(2,1)S(1)}, u32[]{:S(2)}, u32[]{:S(2)}) collective-permute-start(bf16[384,128]{1,0:T(8,128)(2,1)S(1)} %share.1.refs_3_), channel_id=1, source_target_pairs={{0,24},{8,16},{16,8},{24,0},{1,25},{9,17},{17,9},{25,1},{2,26},{10... | collective-permute-start | bytes 294920 | tf_op jit(solution)/shard_map/ppermute | solution.py:445
  86.3 0.5 collective-permute-start.23
  86.8 0.5 collective-permute-start.24
  87.3 2.6 %collective-permute-done.22.refs_0_ = bf16[384,128]{1,0:T(8,128)(2,1)S(1)} collective-permute-done((bf16[384,128]{1,0:T(8,128)(2,1)S(1)}, bf16[384,128]{1,0:T(8,128)(2,1)S(1)}, u32[]{:S(2)}, u32[]{:S(2)}) %collective-permute-start.22) | collective-permute-done | bytes 98336 | tf_op jit(solution)/shard_map/ppermute | solution.py:445
  89.9 1.0 collective-permute-done.23.refs_1_
  90.9 0.5 collective-permute-done.24.refs_2_
  91.4 0.1 total.1.refs_7_
  91.5 1.5 %collective-permute-start.25 = (bf16[384,128]{1,0:T(8,128)(2,1)S(1)}, bf16[384,128]{1,0:T(8,128)(2,1)S(1)}, u32[]{:S(2)}, u32[]{:S(2)}) collective-permute-start(bf16[384,128]{1,0:T(8,128)(2,1)S(1)} %total.1.refs_7_), channel_id=1, source_target_pairs={{0,6},{1,7},{2,4},{3,5},{4,2},{5,3},{6,0},{7,1},{8,14},{9,15},{10,... | collective-permute-start | bytes 294920 | tf_op jit(solution)/shard_map/ppermute | solution.py:445
  93.0 0.6 collective-permute-start.27
  93.6 2.3 %collective-permute-start.29 = (bf16[384,128]{1,0:T(8,128)(2,1)S(1)}, bf16[384,128]{1,0:T(8,128)(2,1)S(1)}, u32[]{:S(2)}, u32[]{:S(2)}) collective-permute-start(bf16[384,128]{1,0:T(8,128)(2,1)S(1)} %total.1.refs_7_), channel_id=1, source_target_pairs={{0,2},{1,3},{2,0},{3,1},{4,6},{5,7},{6,4},{7,5},{8,10},{9,11},{10,... | collective-permute-start | bytes 294920 | tf_op jit(solution)/shard_map/ppermute | solution.py:445
  95.9 2.7 %collective-permute-done.25.refs_1_ = bf16[384,128]{1,0:T(8,128)(2,1)S(1)} collective-permute-done((bf16[384,128]{1,0:T(8,128)(2,1)S(1)}, bf16[384,128]{1,0:T(8,128)(2,1)S(1)}, u32[]{:S(2)}, u32[]{:S(2)}) %collective-permute-start.25) | collective-permute-done | bytes 98336 | tf_op jit(solution)/shard_map/ppermute | solution.py:445
  98.7 3.0 %collective-permute-done.27.refs_3_ = bf16[384,128]{1,0:T(8,128)(2,1)S(1)} collective-permute-done((bf16[384,128]{1,0:T(8,128)(2,1)S(1)}, bf16[384,128]{1,0:T(8,128)(2,1)S(1)}, u32[]{:S(2)}, u32[]{:S(2)}) %collective-permute-start.27) | collective-permute-done | bytes 98336 | tf_op jit(solution)/shard_map/ppermute | solution.py:445
  101.6 0.5 collective-permute-start.30
  102.2 0.8 collective-permute-done.28.refs_2_
  102.9 0.2 collective-permute-done.30.refs_4_
  103.1 1.2 %weights.1 = (f32[64,512]{1,0:T(8,128)}, f32[64,1024]{1,0:T(8,128)}, f32[64,512]{1,0:T(8,128)}, f32[512,512]{1,0:T(8,128)}) custom-call(bf16[384,128]{1,0:T(8,128)(2,1)S(1)} %collective-permute-done.26.refs_0_, bf16[384,128]{1,0:T(8,128)(2,1)S(1)} %collective-permute-done.25.refs_1_, bf16[384,128]{1,0:T(8,128)(2,1)S(1)} %collective-permute-done.28.refs_2_, ...), custom_call_target="tpu_custom_call" | custom-call | tf_op jit(solution)/shard_map/weights/pallas_call | solution.py:701
  (29 shorter events, 0.1 us)
Async XLA Ops:
  2.0 10.1 %collective-permute-start = (bf16[64,512]{1,0:T(8,128)(2,1)S(1)}, bf16[64,512]{1,0:T(8,128)(2,1)S(1)}, u32[]{:S(2)}, u32[]{:S(2)}) collective-permute-start(bf16[64,512]{1,0:T(8,128)(2,1)S(1)} %get-tuple-element.89.refs_13_), channel_id=1, source_target_pairs={{0,6},{1,7},{2,4},{3,5},{4,2},{5,3},{6,0},{7,1},{8,14},{9,15},{10,... | collective-permute-start | bytes 196616 | tf_op jit(solution)/shard_map/ppermute | solution.py:445
  7.1 5.6 %collective-permute-start.1 = (bf16[64,512]{1,0:T(8,128)(2,1)S(1)}, bf16[64,512]{1,0:T(8,128)(2,1)S(1)}, u32[]{:S(2)}, u32[]{:S(2)}) collective-permute-start(bf16[64,512]{1,0:T(8,128)(2,1)S(1)} %get-tuple-element.89.refs_13_), channel_id=1, source_target_pairs={{0,4},{1,5},{2,6},{3,7},{4,0},{5,1},{6,2},{7,3},{8,12},{9,13},{10,... | collective-permute-start | bytes 196616 | tf_op jit(solution)/shard_map/ppermute | solution.py:445
  7.1 5.6 %collective-permute-start.2 = (bf16[64,512]{1,0:T(8,128)(2,1)S(1)}, bf16[64,512]{1,0:T(8,128)(2,1)S(1)}, u32[]{:S(2)}, u32[]{:S(2)}) collective-permute-start(bf16[64,512]{1,0:T(8,128)(2,1)S(1)} %get-tuple-element.89.refs_13_), channel_id=1, source_target_pairs={{0,2},{1,3},{2,0},{3,1},{4,6},{5,7},{6,4},{7,5},{8,10},{9,11},{10,... | collective-permute-start | bytes 196616 | tf_op jit(solution)/shard_map/ppermute | solution.py:445
  12.7 1.7 %collective-permute-start.3 = (bf16[64,512]{1,0:T(8,128)(2,1)S(1)}, bf16[64,512]{1,0:T(8,128)(2,1)S(1)}, u32[]{:S(2)}, u32[]{:S(2)}) collective-permute-start(bf16[64,512]{1,0:T(8,128)(2,1)S(1)} %collective-permute-done.refs_7_), channel_id=1, source_target_pairs={{0,1},{1,0},{2,3},{3,2},{4,5},{5,4},{6,7},{7,6},{8,9},{9,8},{10,11... | collective-permute-start | bytes 196616 | tf_op jit(solution)/shard_map/ppermute | solution.py:445
  12.7 1.7 %collective-permute-start.4 = (bf16[64,512]{1,0:T(8,128)(2,1)S(1)}, bf16[64,512]{1,0:T(8,128)(2,1)S(1)}, u32[]{:S(2)}, u32[]{:S(2)}) collective-permute-start(bf16[64,512]{1,0:T(8,128)(2,1)S(1)} %collective-permute-done.1.refs_9_), channel_id=1, source_target_pairs={{0,1},{1,0},{2,3},{3,2},{4,5},{5,4},{6,7},{7,6},{8,9},{9,8},{10,11... | collective-permute-start | bytes 196616 | tf_op jit(solution)/shard_map/ppermute | solution.py:445
  13.3 1.3 %collective-permute-start.5 = (bf16[64,512]{1,0:T(8,128)(2,1)S(1)}, bf16[64,512]{1,0:T(8,128)(2,1)S(1)}, u32[]{:S(2)}, u32[]{:S(2)}) collective-permute-start(bf16[64,512]{1,0:T(8,128)(2,1)S(1)} %collective-permute-done.2.refs_11_), channel_id=1, source_target_pairs={{0,1},{1,0},{2,3},{3,2},{4,5},{5,4},{6,7},{7,6},{8,9},{9,8},{10,11... | collective-permute-start | bytes 196616 | tf_op jit(solution)/shard_map/ppermute | solution.py:445
  13.3 1.4 %collective-permute-start.6 = (bf16[64,512]{1,0:T(8,128)(2,1)S(1)}, bf16[64,512]{1,0:T(8,128)(2,1)S(1)}, u32[]{:S(2)}, u32[]{:S(2)}) collective-permute-start(bf16[64,512]{1,0:T(8,128)(2,1)S(1)} %get-tuple-element.89.refs_13_), channel_id=1, source_target_pairs={{0,1},{1,0},{2,3},{3,2},{4,5},{5,4},{6,7},{7,6},{8,9},{9,8},{10,11... | collective-permute-start | bytes 196616 | tf_op jit(solution)/shard_map/ppermute | solution.py:445
  27.8 1.4 %collective-permute-start.7 = (bf16[4,32,512]{2,1,0:T(8,128)(2,1)S(1)}, bf16[4,32,512]{2,1,0:T(8,128)(2,1)S(1)}, u32[]{:S(2)}, u32[]{:S(2)}) collective-permute-start(bf16[4,32,512]{2,1,0:T(8,128)(2,1)S(1)} %get-tuple-element.92), channel_id=1, source_target_pairs={{0,1},{1,0},{2,3},{3,2},{4,5},{5,4},{6,7},{7,6},{8,9},{9,8},{10,11... | collective-permute-start | bytes 393224 | tf_op jit(solution)/shard_map/ppermute | solution.py:445
  29.2 8.1 %copy-start = (bf16[512,512]{1,0:T(8,128)(2,1)S(1)}, bf16[512,512]{1,0:T(8,128)(2,1)}, u32[]{:S(2)}) copy-start(bf16[512,512]{1,0:T(8,128)(2,1)} %atom_weight_ref.1) | copy-start | bytes 1572868
  29.2 8.1 %copy-start.1 = (bf16[1,32,512]{2,1,0:T(8,128)(2,1)S(1)}, bf16[1,32,512]{2,1,0:T(8,128)(2,1)}, u32[]{:S(2)}) copy-start(bf16[1,32,512]{2,1,0:T(8,128)(2,1)} %param.14) | copy-start | bytes 98308
  29.2 8.1 %copy-start.2 = (bf16[1,32,512]{2,1,0:T(8,128)(2,1)S(1)}, bf16[1,32,512]{2,1,0:T(8,128)(2,1)}, u32[]{:S(2)}) copy-start(bf16[1,32,512]{2,1,0:T(8,128)(2,1)} %param.21) | copy-start | bytes 98308
  29.2 6.2 %collective-permute-start.8 = (bf16[32,512]{1,0:T(8,128)(2,1)S(1)}, bf16[32,512]{1,0:T(8,128)(2,1)S(1)}, u32[]{:S(2)}, u32[]{:S(2)}) collective-permute-start(bf16[32,512]{1,0:T(8,128)(2,1)S(1)} %get-tuple-element.93), channel_id=1, source_target_pairs={{0,6},{1,7},{2,4},{3,5},{4,2},{5,3},{6,0},{7,1},{8,14},{9,15},{10,... | collective-permute-start | bytes 98312 | tf_op jit(solution)/shard_map/ppermute | solution.py:445
  32.5 4.8 %collective-permute-start.9 = (bf16[32,512]{1,0:T(8,128)(2,1)S(1)}, bf16[32,512]{1,0:T(8,128)(2,1)S(1)}, u32[]{:S(2)}, u32[]{:S(2)}) collective-permute-start(bf16[32,512]{1,0:T(8,128)(2,1)S(1)} %get-tuple-element.94), channel_id=1, source_target_pairs={{0,4},{1,5},{2,6},{3,7},{4,0},{5,1},{6,2},{7,3},{8,12},{9,13},{10,... | collective-permute-start | bytes 98312 | tf_op jit(solution)/shard_map/ppermute | solution.py:445
  32.5 4.8 %collective-permute-start.10 = (bf16[32,512]{1,0:T(8,128)(2,1)S(1)}, bf16[32,512]{1,0:T(8,128)(2,1)S(1)}, u32[]{:S(2)}, u32[]{:S(2)}) collective-permute-start(bf16[32,512]{1,0:T(8,128)(2,1)S(1)} %get-tuple-element.95), channel_id=1, source_target_pairs={{0,2},{1,3},{2,0},{3,1},{4,6},{5,7},{6,4},{7,5},{8,10},{9,11},{10,... | collective-permute-start | bytes 98312 | tf_op jit(solution)/shard_map/ppermute | solution.py:445
  33.7 14.2 %copy-start.3 = (bf16[1,512,512]{2,1,0:T(8,128)(2,1)S(1)}, bf16[1,512,512]{2,1,0:T(8,128)(2,1)}, u32[]{:S(2)}) copy-start(bf16[1,512,512]{2,1,0:T(8,128)(2,1)} %param.20) | copy-start | bytes 1572868
  38.2 6.8 %collective-permute-start.11 = (bf16[2,32,512]{2,1,0:T(8,128)(2,1)S(1)}, bf16[2,32,512]{2,1,0:T(8,128)(2,1)S(1)}, u32[]{:S(2)}, u32[]{:S(2)}) collective-permute-start(bf16[2,32,512]{2,1,0:T(8,128)(2,1)S(1)} %get-tuple-element.105.refs_7_.refs_0_), channel_id=1, source_target_pairs={{0,6},{1,7},{2,4},{3,5},{4,2},{5,3},{6,0},{7,1},{8,14},{9,15},{10,... | collective-permute-start | bytes 196616 | tf_op jit(solution)/shard_map/ppermute | solution.py:445
  39.8 6.6 %collective-permute-start.13 = (bf16[2,32,512]{2,1,0:T(8,128)(2,1)S(1)}, bf16[2,32,512]{2,1,0:T(8,128)(2,1)S(1)}, u32[]{:S(2)}, u32[]{:S(2)}) collective-permute-start(bf16[2,32,512]{2,1,0:T(8,128)(2,1)S(1)} %get-tuple-element.105.refs_7_.refs_0_), channel_id=1, source_target_pairs={{0,4},{1,5},{2,6},{3,7},{4,0},{5,1},{6,2},{7,3},{8,12},{9,13},{10,... | collective-permute-start | bytes 196616 | tf_op jit(solution)/shard_map/ppermute | solution.py:445
  40.2 6.2 %collective-permute-start.15 = (bf16[2,32,512]{2,1,0:T(8,128)(2,1)S(1)}, bf16[2,32,512]{2,1,0:T(8,128)(2,1)S(1)}, u32[]{:S(2)}, u32[]{:S(2)}) collective-permute-start(bf16[2,32,512]{2,1,0:T(8,128)(2,1)S(1)} %get-tuple-element.105.refs_7_.refs_0_), channel_id=1, source_target_pairs={{0,2},{1,3},{2,0},{3,1},{4,6},{5,7},{6,4},{7,5},{8,10},{9,11},{10,... | collective-permute-start | bytes 196616 | tf_op jit(solution)/shard_map/ppermute | solution.py:445
  42.5 4.4 %collective-permute-start.17 = (bf16[2,32,512]{2,1,0:T(8,128)(2,1)S(1)}, bf16[2,32,512]{2,1,0:T(8,128)(2,1)S(1)}, u32[]{:S(2)}, u32[]{:S(2)}) collective-permute-start(bf16[2,32,512]{2,1,0:T(8,128)(2,1)S(1)} %get-tuple-element.105.refs_7_.refs_0_), channel_id=1, source_target_pairs={{0,1},{1,0},{2,3},{3,2},{4,5},{5,4},{6,7},{7,6},{8,9},{9,8},{10,11... | collective-permute-start | bytes 196616 | tf_op jit(solution)/shard_map/ppermute | solution.py:445
  45.0 2.0 %collective-permute-start.12 = (bf16[2,32,512]{2,1,0:T(8,128)(2,1)S(1)}, bf16[2,32,512]{2,1,0:T(8,128)(2,1)S(1)}, u32[]{:S(2)}, u32[]{:S(2)}) collective-permute-start(bf16[2,32,512]{2,1,0:T(8,128)(2,1)S(1)} %collective-permute-done.11.refs_1_.refs_6_), channel_id=1, source_target_pairs={{0,1},{1,0},{2,3},{3,2},{4,5},{5,4},{6,7},{7,6},{8,9},{9,8},{10,11... | collective-permute-start | bytes 196616 | tf_op jit(solution)/shard_map/ppermute | solution.py:445
  46.4 1.3 %collective-permute-start.14 = (bf16[2,32,512]{2,1,0:T(8,128)(2,1)S(1)}, bf16[2,32,512]{2,1,0:T(8,128)(2,1)S(1)}, u32[]{:S(2)}, u32[]{:S(2)}) collective-permute-start(bf16[2,32,512]{2,1,0:T(8,128)(2,1)S(1)} %collective-permute-done.13.refs_3_.refs_4_), channel_id=1, source_target_pairs={{0,1},{1,0},{2,3},{3,2},{4,5},{5,4},{6,7},{7,6},{8,9},{9,8},{10,11... | collective-permute-start | bytes 196616 | tf_op jit(solution)/shard_map/ppermute | solution.py:445
  46.4 1.4 %collective-permute-start.16 = (bf16[2,32,512]{2,1,0:T(8,128)(2,1)S(1)}, bf16[2,32,512]{2,1,0:T(8,128)(2,1)S(1)}, u32[]{:S(2)}, u32[]{:S(2)}) collective-permute-start(bf16[2,32,512]{2,1,0:T(8,128)(2,1)S(1)} %collective-permute-done.15.refs_5_.refs_2_), channel_id=1, source_target_pairs={{0,1},{1,0},{2,3},{3,2},{4,5},{5,4},{6,7},{7,6},{8,9},{9,8},{10,11... | collective-permute-start | bytes 196616 | tf_op jit(solution)/shard_map/ppermute | solution.py:445
  59.9 13.5 %all-to-all-start = ((bf16[8,80,128]{2,1,0:T(8,128)(2,1)}), bf16[8,80,128]{2,1,0:T(8,128)(2,1)S(1)}, u32[]{:S(2)}, u32[]{:S(2)}) async-start(bf16[8,80,128]{2,1,0:T(8,128)(2,1)} %get-tuple-element.106), calls=%async_computation | async-start | bytes 327680 | tf_op jit(solution)/shard_map/all_to_all | solution.py:634
  63.5 9.9 %copy-start.4 = (bf16[1,512,512]{2,1,0:T(8,128)(2,1)S(1)}, bf16[1,512,512]{2,1,0:T(8,128)(2,1)}, u32[]{:S(2)}) copy-start(bf16[1,512,512]{2,1,0:T(8,128)(2,1)} %param.13) | copy-start | bytes 1572868
  73.9 5.9 %copy-start.5 = (bf16[512,64]{0,1:T(8,128)(2,1)S(1)}, bf16[512,64]{0,1:T(8,128)(2,1)}, u32[]{:S(2)}) copy-start(bf16[512,64]{0,1:T(8,128)(2,1)} %param.22) | copy-start | bytes 196612
  73.9 1.4 %collective-permute-start.18 = (bf16[4,128,128]{2,1,0:T(8,128)(2,1)S(1)}, bf16[4,128,128]{2,1,0:T(8,128)(2,1)S(1)}, u32[]{:S(2)}, u32[]{:S(2)}) collective-permute-start(bf16[4,128,128]{2,1,0:T(8,128)(2,1)S(1)} %get-tuple-element.112), channel_id=1, source_target_pairs={{0,1},{1,0},{2,3},{3,2},{4,5},{5,4},{6,7},{7,6},{8,9},{9,8},{10,11... | collective-permute-start | bytes 393224 | tf_op jit(solution)/shard_map/ppermute | solution.py:445
  75.3 5.8 %collective-permute-start.19 = (bf16[128,128]{1,0:T(8,128)(2,1)S(1)}, bf16[128,128]{1,0:T(8,128)(2,1)S(1)}, u32[]{:S(2)}, u32[]{:S(2)}) collective-permute-start(bf16[128,128]{1,0:T(8,128)(2,1)S(1)} %get-tuple-element.113), channel_id=1, source_target_pairs={{0,6},{1,7},{2,4},{3,5},{4,2},{5,3},{6,0},{7,1},{8,14},{9,15},{10,... | collective-permute-start | bytes 98312 | tf_op jit(solution)/shard_map/ppermute | solution.py:445
  78.9 4.8 %collective-permute-start.20 = (bf16[128,128]{1,0:T(8,128)(2,1)S(1)}, bf16[128,128]{1,0:T(8,128)(2,1)S(1)}, u32[]{:S(2)}, u32[]{:S(2)}) collective-permute-start(bf16[128,128]{1,0:T(8,128)(2,1)S(1)} %get-tuple-element.114), channel_id=1, source_target_pairs={{0,4},{1,5},{2,6},{3,7},{4,0},{5,1},{6,2},{7,3},{8,12},{9,13},{10,... | collective-permute-start | bytes 98312 | tf_op jit(solution)/shard_map/ppermute | solution.py:445
  78.9 4.8 %collective-permute-start.21 = (bf16[128,128]{1,0:T(8,128)(2,1)S(1)}, bf16[128,128]{1,0:T(8,128)(2,1)S(1)}, u32[]{:S(2)}, u32[]{:S(2)}) collective-permute-start(bf16[128,128]{1,0:T(8,128)(2,1)S(1)} %get-tuple-element.115), channel_id=1, source_target_pairs={{0,2},{1,3},{2,0},{3,1},{4,6},{5,7},{6,4},{7,5},{8,10},{9,11},{10,... | collective-permute-start | bytes 98312 | tf_op jit(solution)/shard_map/ppermute | solution.py:445
  83.8 6.1 %collective-permute-start.22 = (bf16[384,128]{1,0:T(8,128)(2,1)S(1)}, bf16[384,128]{1,0:T(8,128)(2,1)S(1)}, u32[]{:S(2)}, u32[]{:S(2)}) collective-permute-start(bf16[384,128]{1,0:T(8,128)(2,1)S(1)} %share.1.refs_3_), channel_id=1, source_target_pairs={{0,24},{8,16},{16,8},{24,0},{1,25},{9,17},{17,9},{25,1},{2,26},{10... | collective-permute-start | bytes 294920 | tf_op jit(solution)/shard_map/ppermute | solution.py:445
  86.3 4.7 %collective-permute-start.23 = (bf16[384,128]{1,0:T(8,128)(2,1)S(1)}, bf16[384,128]{1,0:T(8,128)(2,1)S(1)}, u32[]{:S(2)}, u32[]{:S(2)}) collective-permute-start(bf16[384,128]{1,0:T(8,128)(2,1)S(1)} %share.1.refs_3_), channel_id=1, source_target_pairs={{0,16},{8,24},{16,0},{24,8},{1,17},{9,25},{17,1},{25,9},{2,18},{10... | collective-permute-start | bytes 294920 | tf_op jit(solution)/shard_map/ppermute | solution.py:445
  86.8 4.6 %collective-permute-start.24 = (bf16[384,128]{1,0:T(8,128)(2,1)S(1)}, bf16[384,128]{1,0:T(8,128)(2,1)S(1)}, u32[]{:S(2)}, u32[]{:S(2)}) collective-permute-start(bf16[384,128]{1,0:T(8,128)(2,1)S(1)} %share.1.refs_3_), channel_id=1, source_target_pairs={{0,8},{8,0},{16,24},{24,16},{1,9},{9,1},{17,25},{25,17},{2,10},{10... | collective-permute-start | bytes 294920 | tf_op jit(solution)/shard_map/ppermute | solution.py:445
  91.5 7.2 %collective-permute-start.25 = (bf16[384,128]{1,0:T(8,128)(2,1)S(1)}, bf16[384,128]{1,0:T(8,128)(2,1)S(1)}, u32[]{:S(2)}, u32[]{:S(2)}) collective-permute-start(bf16[384,128]{1,0:T(8,128)(2,1)S(1)} %total.1.refs_7_), channel_id=1, source_target_pairs={{0,6},{1,7},{2,4},{3,5},{4,2},{5,3},{6,0},{7,1},{8,14},{9,15},{10,... | collective-permute-start | bytes 294920 | tf_op jit(solution)/shard_map/ppermute | solution.py:445
  93.0 8.6 %collective-permute-start.27 = (bf16[384,128]{1,0:T(8,128)(2,1)S(1)}, bf16[384,128]{1,0:T(8,128)(2,1)S(1)}, u32[]{:S(2)}, u32[]{:S(2)}) collective-permute-start(bf16[384,128]{1,0:T(8,128)(2,1)S(1)} %total.1.refs_7_), channel_id=1, source_target_pairs={{0,4},{1,5},{2,6},{3,7},{4,0},{5,1},{6,2},{7,3},{8,12},{9,13},{10,... | collective-permute-start | bytes 294920 | tf_op jit(solution)/shard_map/ppermute | solution.py:445
  93.6 8.0 %collective-permute-start.29 = (bf16[384,128]{1,0:T(8,128)(2,1)S(1)}, bf16[384,128]{1,0:T(8,128)(2,1)S(1)}, u32[]{:S(2)}, u32[]{:S(2)}) collective-permute-start(bf16[384,128]{1,0:T(8,128)(2,1)S(1)} %total.1.refs_7_), channel_id=1, source_target_pairs={{0,2},{1,3},{2,0},{3,1},{4,6},{5,7},{6,4},{7,5},{8,10},{9,11},{10,... | collective-permute-start | bytes 294920 | tf_op jit(solution)/shard_map/ppermute | solution.py:445
  95.9 6.2 %collective-permute-start.31 = (bf16[384,128]{1,0:T(8,128)(2,1)S(1)}, bf16[384,128]{1,0:T(8,128)(2,1)S(1)}, u32[]{:S(2)}, u32[]{:S(2)}) collective-permute-start(bf16[384,128]{1,0:T(8,128)(2,1)S(1)} %total.1.refs_7_), channel_id=1, source_target_pairs={{0,1},{1,0},{2,3},{3,2},{4,5},{5,4},{6,7},{7,6},{8,9},{9,8},{10,11... | collective-permute-start | bytes 294920 | tf_op jit(solution)/shard_map/ppermute | solution.py:445
  98.7 3.5 %collective-permute-start.26 = (bf16[384,128]{1,0:T(8,128)(2,1)S(1)}, bf16[384,128]{1,0:T(8,128)(2,1)S(1)}, u32[]{:S(2)}, u32[]{:S(2)}) collective-permute-start(bf16[384,128]{1,0:T(8,128)(2,1)S(1)} %collective-permute-done.25.refs_1_), channel_id=1, source_target_pairs={{0,1},{1,0},{2,3},{3,2},{4,5},{5,4},{6,7},{7,6},{8,9},{9,8},{10,11... | collective-permute-start | bytes 294920 | tf_op jit(solution)/shard_map/ppermute | solution.py:445
  101.6 1.3 %collective-permute-start.28 = (bf16[384,128]{1,0:T(8,128)(2,1)S(1)}, bf16[384,128]{1,0:T(8,128)(2,1)S(1)}, u32[]{:S(2)}, u32[]{:S(2)}) collective-permute-start(bf16[384,128]{1,0:T(8,128)(2,1)S(1)} %collective-permute-done.27.refs_3_), channel_id=1, source_target_pairs={{0,1},{1,0},{2,3},{3,2},{4,5},{5,4},{6,7},{7,6},{8,9},{9,8},{10,11... | collective-permute-start | bytes 294920 | tf_op jit(solution)/shard_map/ppermute | solution.py:445
  101.6 1.5 %collective-permute-start.30 = (bf16[384,128]{1,0:T(8,128)(2,1)S(1)}, bf16[384,128]{1,0:T(8,128)(2,1)S(1)}, u32[]{:S(2)}, u32[]{:S(2)}) collective-permute-start(bf16[384,128]{1,0:T(8,128)(2,1)S(1)} %collective-permute-done.29.refs_5_), channel_id=1, source_target_pairs={{0,1},{1,0},{2,3},{3,2},{4,5},{5,4},{6,7},{7,6},{8,9},{9,8},{10,11... | collective-permute-start | bytes 294920 | tf_op jit(solution)/shard_map/ppermute | solution.py:445

commit v7 on v6

--- a/solution.py
+++ b/solution.py
@@ -133,7 +133,7 @@
     *refs,
 ):
     out_ref, basis_ref, bil_ref, up_ref, emb_ref, target_ref, *refs = refs
-    feat_refs, refs = refs[:members][::-1], refs[members:]
+    feat_refs, refs = restored(refs[:members]), refs[members:]
     new_ref, near_ref, far_ref, gathered_ref, picked_hbm, *refs = refs
     table, total, spread, masked, picked_ref, sems = refs
     trips = slot_ref.shape[1]
@@ -251,7 +251,7 @@
     atom_weight_ref,
     *refs,
 ):
-    pair_refs, refs = refs[:members][::-1], refs[members:]
+    pair_refs, refs = restored(refs[:members]), refs[members:]
     grad_new_ref, up_grad_ref, mixed_hbm, parts_ref, *refs = refs
     table, spread, masked, total, grads, mixed_ref, sems = refs
     trips = slot_ref.shape[1]
@@ -411,7 +411,7 @@
 
 
 def last_kernel(members, *refs):
-    part_refs, (down_ref, bil_ref, up_ref, atom_ref, flat) = refs[:members][::-1], refs[members:]
+    part_refs, (down_ref, bil_ref, up_ref, atom_ref, flat) = restored(refs[:members]), refs[members:]
     me = lax.axis_index("graph")
     model = atom_ref.shape[1]
     rows = flat.shape[0] // members
@@ -441,6 +441,24 @@
     return pltpu.with_memory_space_constraint(value, pltpu.HBM)
 
 
+def sending(count):
+    falling = list(range(count))[::-1]
+    return falling[1:2] + falling[:1] + falling[2:]
+
+
+def places(count):
+    return [2 * pair + 1 - odd for pair in sending(count // 2) for odd in range(2)]
+
+
+def ordered(items):
+    return [items[place] for place in places(len(items))]
+
+
+def restored(items):
+    found = dict(zip(places(len(items)), items))
+    return [found[place] for place in range(len(items))]
+
+
 def swap(value, members, mask, axis="graph"):
     return lax.ppermute(value, axis, [(at, at ^ mask) for at in range(members)])
 
@@ -459,8 +477,9 @@
 def gather_near(value, members, beside=None):
     even = [value] + [swap(value, members, mask) for mask in range(2, members, 2)]
     if beside is not None:
-        back_even, beside = lax.optimization_barrier((even[::-1], beside))
-        even = back_even[::-1]
+        turn = sending(len(even))
+        moved, beside = lax.optimization_barrier(([even[at] for at in turn], beside))
+        even = [moved[turn.index(at)] for at in range(len(even))]
     odd = [swap(piece, members, 1) for piece in even]
     return [piece for pair in zip(even, odd) for piece in pair], beside
 
@@ -570,7 +589,7 @@
         slot,
         rank,
         *kept,
-        *feats[::-1],
+        *ordered(feats),
     )
 
     atom_block = shaped((atom_dev, model), b16)
@@ -582,15 +601,16 @@
         name="slopes",
     )(gathered, kept[3])
     sums = scatter_near(near, far, members)
-    sums, slope = lax.optimization_barrier((sums[::-1], slope))
-    sums = sums[::-1]
+    turn = sending(len(sums))
+    moved, slope = lax.optimization_barrier(([sums[at] for at in turn], slope))
+    sums = [moved[turn.index(at)] for at in range(len(sums))]
     atom_new, pair = pl.pallas_call(
         atom_kernel,
         out_shape=(atom_block, shaped((2, atom_dev, model), b16)),
         compiler_params=params(),
         cost_estimate=cost(16 * atom_dev * w_atom.size),
         name="atoms",
-    )(atom_emb[0], grad_atom[0], w_atom, *sums[::-1])
+    )(atom_emb[0], grad_atom[0], w_atom, *[sums[at] for at in sending(len(sums))])
     pairs, _ = gather_near(pair, members)
 
     piece_rows = width + -(-(edge_dev // CAP) // 16) * 16
@@ -629,7 +649,7 @@
         grad_edge[0],
         kept[5],
         w_atom,
-        *pairs[::-1],
+        *ordered(pairs),
     )
     feat_parts = lax.all_to_all(feat_parts, "graph", 0, 0, tiled=True)
     wide = math.gcd(trips, 2 * tile)
@@ -683,14 +703,16 @@
     factor = 1.0 / math.sqrt(batches * members * edge_dev)
     share_rows = (flat_rows + model * model // CAP) // members
     flat_sums = scatter_near(near, far, members)
-    flat_sums, slab, grad_in = lax.optimization_barrier((flat_sums[::-1], slab, grad_in))
-    flat_sums = flat_sums[::-1]
+    moved, slab, grad_in = lax.optimization_barrier(
+        ([flat_sums[at] for at in turn], slab, grad_in)
+    )
+    flat_sums = [moved[turn.index(at)] for at in range(len(sums))]
     share = pl.pallas_call(
         share_kernel,
         out_shape=shaped((share_rows, CAP), b16),
         compiler_params=params(),
         name="share",
-    )(slab, *flat_sums[::-1])
+    )(slab, *[flat_sums[at] for at in sending(len(flat_sums))])
     share = pl.pallas_call(
         functools.partial(total_kernel, factor),
         out_shape=shaped((share_rows, CAP), b16),
@@ -709,7 +731,7 @@
         scratch_shapes=[pltpu.VMEM((flat_rows, CAP), b16)],
         compiler_params=params(),
         name="weights",
-    )(*shares[::-1])
+    )(*ordered(shares))
     return (
         edge_new[None],
         atom_new[None],

time: 105 us -> 103 us (0.981)
  starting transfers between devices: 33.5 us -> 30.8 us
    ppermute x32, starting transfers between devices: 29.9 us -> 27.2 us  [swap(): return lax.ppermute(value, axis, [(at, at ^ mask) for at in range(members)])]
where the time goes in v7:
time: 103 us; the launch traced here: 102 us
  Pallas kernels  45.5 us (44%)
  starting transfers between devices  30.8 us (30%)
  waiting for transfers between devices  24.5 us (24%)
  between operations  1.47 us (1%)
    ppermute x32, starting transfers between devices, swap(): return lax.ppermute(value, axis, [(at, at ^ mask) for at in range(members)])  27.2 us
    ppermute x32, waiting for transfers between devices, swap(): return lax.ppermute(value, axis, [(at, at ^ mask) for at in range(members)])  24.5 us
    pallas_call x1, Pallas kernels, body(): pl.pallas_call(functools.partial(forward_kernel, members), in_specs=[SMEM...  13.1 us
    pallas_call x1, Pallas kernels, body(): pl.pallas_call(functools.partial(backward_kernel, members), in_specs=[SME...  12 us
    pallas_call x1, Pallas kernels, body(): pl.pallas_call(weight_kernel, in_specs=[VMEM, HBM, HBM], out_shape=shaped...  9.87 us
    pallas_call x1, Pallas kernels, body(): pl.pallas_call(functools.partial(index_kernel, members), in_specs=[HBM] *...  4.3 us
    all_to_all x1, starting transfers between devices, body(): feat_parts = lax.all_to_all(feat_parts, 'graph', 0, 0, tiled=True)  3.61 us
  transfers between devices with their start and end apart: 33, of which 20 were waited for; matrix products, arithmetic and copies ran while one was open for 0% of the time, Pallas kernels for 16%

profile of v7, /device:TPU:0, one launch (start us, length us, event | category | flops | bytes accessed | tf_op | source)
XLA Modules:
  0.0 102.3 jit_solution(12924838160575167195)
XLA Ops:
  0.6 1.4 %features.1 = (f32[64,512]{1,0:T(8,128)S(1)}, bf16[64,512]{1,0:T(8,128)(2,1)S(1)}) custom-call(bf16[512,512]{1,0:T(8,128)(2,1)} %bitcast.15, bf16[64,512]{1,0:T(8,128)(2,1)} %bitcast.18), custom_call_target="tpu_custom_call" | custom-call | flops 268435456 | bytes 1048576 | tf_op jit(solution)/shard_map/features/pallas_call | solution.py:524
  2.0 4.1 %collective-permute-start = (bf16[64,512]{1,0:T(8,128)(2,1)S(1)}, bf16[64,512]{1,0:T(8,128)(2,1)S(1)}, u32[]{:S(2)}, u32[]{:S(2)}) collective-permute-start(bf16[64,512]{1,0:T(8,128)(2,1)S(1)} %get-tuple-element.89.refs_13_), channel_id=1, source_target_pairs={{0,4},{1,5},{2,6},{3,7},{4,0},{5,1},{6,2},{7,3},{8,12},{9,13},{10,... | collective-permute-start | bytes 196616 | tf_op jit(solution)/shard_map/ppermute | solution.py:463
  6.1 1.3 %collective-permute-start.1 = (bf16[64,512]{1,0:T(8,128)(2,1)S(1)}, bf16[64,512]{1,0:T(8,128)(2,1)S(1)}, u32[]{:S(2)}, u32[]{:S(2)}) collective-permute-start(bf16[64,512]{1,0:T(8,128)(2,1)S(1)} %get-tuple-element.89.refs_13_), channel_id=1, source_target_pairs={{0,6},{1,7},{2,4},{3,5},{4,2},{5,3},{6,0},{7,1},{8,14},{9,15},{10,... | collective-permute-start | bytes 196616 | tf_op jit(solution)/shard_map/ppermute | solution.py:463
  7.5 0.2 collective-permute-start.2
  7.7 4.3 %slots.1 = (s32[1,16384]{1,0:T(1,128)S(1)}, f32[32,128]{1,0:T(8,128)S(1)}, bf16[64,1024]{1,0:T(8,128)(2,1)S(1)}, s32[1,16384]{1,0:T(1,128)S(1)}, bf16[16,16384]{...) custom-call(s32[1,16384]{1,0:T(1,128)} %in_hbm.1, ...), custom_call_target="tpu_custom_call" | custom-call | flops 2147483648 | bytes 1048576 | tf_op jit(solution)/shard_map/slots/pallas_call | solution.py:542
  12.0 0.0 collective-permute-done.refs_7_
  12.0 0.3 collective-permute-done.1.refs_9_
  12.3 0.1 collective-permute-done.2.refs_11_
  12.4 0.0 collective-permute-start.3
  12.4 0.5 collective-permute-start.4
  12.9 0.0 collective-permute-start.5
  13.0 0.5 collective-permute-start.6
  14.1 0.0 collective-permute-done.3.refs_6_
  14.1 0.1 collective-permute-done.5.refs_10_
  14.2 0.2 collective-permute-done.6.refs_12_
  14.4 13.1 %forward_triplets.1 = (bf16[512,512]{1,0:T(8,128)(2,1)}, bf16[4,32,512]{2,1,0:T(8,128)(2,1)S(1)}, bf16[4,32,512]{2,1,0:T(8,128)(2,1)S(1)}, bf16[64,512]{1,0:T(8,128)(2,1)S(1)}, bf16[64,16384]{1,0:T(8,128)(2,1)}) custom-call(s32[1,1]{1,0:T(1,128)S(6)} %copy.20.count_ref, s32[1,16384]{1,0:T(1,128)S(1)} %get-tuple-element.78.slot_ref, ...), custom_call_target="tpu_custom_call" | custom-call | flops 12884901888 | bytes 1048576 | tf_op jit(solution)/shard_map/forward_triplets/pallas_call | solution.py:565
  27.5 0.4 collective-permute-start.7
  27.9 1.0 collective-permute-done.7.far_ref
  28.9 2.7 %collective-permute-start.8 = (bf16[32,512]{1,0:T(8,128)(2,1)S(1)}, bf16[32,512]{1,0:T(8,128)(2,1)S(1)}, u32[]{:S(2)}, u32[]{:S(2)}) collective-permute-start(bf16[32,512]{1,0:T(8,128)(2,1)S(1)} %get-tuple-element.93), channel_id=1, source_target_pairs={{0,4},{1,5},{2,6},{3,7},{4,0},{5,1},{6,2},{7,3},{8,12},{9,13},{10,... | collective-permute-start | bytes 98312 | tf_op jit(solution)/shard_map/ppermute | solution.py:463
  31.7 1.1 %collective-permute-start.9 = (bf16[32,512]{1,0:T(8,128)(2,1)S(1)}, bf16[32,512]{1,0:T(8,128)(2,1)S(1)}, u32[]{:S(2)}, u32[]{:S(2)}) collective-permute-start(bf16[32,512]{1,0:T(8,128)(2,1)S(1)} %get-tuple-element.94), channel_id=1, source_target_pairs={{0,6},{1,7},{2,4},{3,5},{4,2},{5,3},{6,0},{7,1},{8,14},{9,15},{10,... | collective-permute-start | bytes 98312 | tf_op jit(solution)/shard_map/ppermute | solution.py:463
  32.8 0.5 slopes.1.slope_ref
  33.4 0.4 collective-permute-done.8.refs_0_
  33.8 3.6 %collective-permute-done.9.refs_1_ = bf16[32,512]{1,0:T(8,128)(2,1)S(1)} collective-permute-done((bf16[32,512]{1,0:T(8,128)(2,1)S(1)}, bf16[32,512]{1,0:T(8,128)(2,1)S(1)}, u32[]{:S(2)}, u32[]{:S(2)}) %collective-permute-start.9) | collective-permute-done | bytes 32800 | tf_op jit(solution)/shard_map/ppermute | solution.py:463
  37.4 0.9 atoms.1
  38.2 0.9 collective-permute-start.11
  39.1 1.1 %collective-permute-start.13 = (bf16[2,32,512]{2,1,0:T(8,128)(2,1)S(1)}, bf16[2,32,512]{2,1,0:T(8,128)(2,1)S(1)}, u32[]{:S(2)}, u32[]{:S(2)}) collective-permute-start(bf16[2,32,512]{2,1,0:T(8,128)(2,1)S(1)} %get-tuple-element.105.refs_7_.refs_0_), channel_id=1, source_target_pairs={{0,6},{1,7},{2,4},{3,5},{4,2},{5,3},{6,0},{7,1},{8,14},{9,15},{10,... | collective-permute-start | bytes 196616 | tf_op jit(solution)/shard_map/ppermute | solution.py:463
  40.3 1.4 %collective-permute-start.15 = (bf16[2,32,512]{2,1,0:T(8,128)(2,1)S(1)}, bf16[2,32,512]{2,1,0:T(8,128)(2,1)S(1)}, u32[]{:S(2)}, u32[]{:S(2)}) collective-permute-start(bf16[2,32,512]{2,1,0:T(8,128)(2,1)S(1)} %get-tuple-element.105.refs_7_.refs_0_), channel_id=1, source_target_pairs={{0,2},{1,3},{2,0},{3,1},{4,6},{5,7},{6,4},{7,5},{8,10},{9,11},{10,... | collective-permute-start | bytes 196616 | tf_op jit(solution)/shard_map/ppermute | solution.py:463
  41.7 3.7 %collective-permute-done.11.refs_1_.refs_4_ = bf16[2,32,512]{2,1,0:T(8,128)(2,1)S(1)} collective-permute-done((bf16[2,32,512]{2,1,0:T(8,128)(2,1)S(1)}, bf16[2,32,512]{2,1,0:T(8,128)(2,1)S(1)}, u32[]{:S(2)}, u32[]{:S(2)}) %collective-permute-start.11) | collective-permute-done | bytes 65568 | tf_op jit(solution)/shard_map/ppermute | solution.py:463
  45.4 0.5 collective-permute-start.14
  45.9 0.1 collective-permute-start.16
  46.0 0.7 collective-permute-done.12.refs_0_.refs_5_
  46.7 0.2 collective-permute-done.14.refs_2_.refs_7_
  46.8 0.4 collective-permute-done.16.refs_4_.refs_3_
  47.2 12.0 %backward_triplets.1 = (f32[512,512]{1,0:T(8,128)S(1)}, bf16[64,512]{1,0:T(8,128)(2,1)S(1)}, bf16[64,16384]{1,0:T(8,128)(2,1)}, bf16[8,80,128]{2,1,0:T(8,128)(2,1)}) custom-call(s32[1,1]{1,0:T(1,128)S(6)} %copy.20.count_ref, s32[1,16384]{1,0:T(1,128)S(1)} %get-tuple-element.78.slot_ref, s32[1,16384]{1,0:T(1,128)S(1)} %get-tuple-element.80.refs_0_.out_ref, ...), custom_call_target="tpu_custom_call" | custom-call | flops 12884901888 | bytes 1048576 | tf_op jit(solution)/shard_map/backward_triplets/pallas_call | solution.py:617
  59.2 3.6 %all-to-all-start = ((bf16[8,80,128]{2,1,0:T(8,128)(2,1)}), bf16[8,80,128]{2,1,0:T(8,128)(2,1)S(1)}, u32[]{:S(2)}, u32[]{:S(2)}) async-start(bf16[8,80,128]{2,1,0:T(8,128)(2,1)} %get-tuple-element.106), calls=%async_computation | async-start | bytes 327680 | tf_op jit(solution)/shard_map/all_to_all | solution.py:654
  62.9 0.0 copy-start.4
  62.9 9.9 %bilinear_weights.1.bil_grad_ref = bf16[64,1024]{1,0:T(8,128)(2,1)S(1)} custom-call(bf16[16,16384]{1,0:T(8,128)(2,1)S(1)} %get-tuple-element.81.refs_1_.basis_ref, bf16[64,16384]{1,0:T(8,128)(2,1)} %get-tuple-element.108.picked_hbm, bf16[64,16384]{1,0:T(8,128)(2,1)} %get-tuple-element.109.mixed_hbm), custom_call_target="tpu_custom_call" | custom-call | flops 8589934592 | bytes 1048576 | tf_op jit(solution)/shard_map/bilinear_weights/pallas_call | solution.py:656
  72.8 0.5 edges.1
  73.3 0.0 copy-start.5
  73.3 0.3 collective-permute-start.18
  73.5 0.3 atom_slab.1.slab_ref
  73.9 0.8 collective-permute-done.18.far_ref
  74.7 2.7 %collective-permute-start.19 = (bf16[128,128]{1,0:T(8,128)(2,1)S(1)}, bf16[128,128]{1,0:T(8,128)(2,1)S(1)}, u32[]{:S(2)}, u32[]{:S(2)}) collective-permute-start(bf16[128,128]{1,0:T(8,128)(2,1)S(1)} %get-tuple-element.113), channel_id=1, source_target_pairs={{0,4},{1,5},{2,6},{3,7},{4,0},{5,1},{6,2},{7,3},{8,12},{9,13},{10,... | collective-permute-start | bytes 98312 | tf_op jit(solution)/shard_map/ppermute | solution.py:463
  77.4 1.5 %collective-permute-start.20 = (bf16[128,128]{1,0:T(8,128)(2,1)S(1)}, bf16[128,128]{1,0:T(8,128)(2,1)S(1)}, u32[]{:S(2)}, u32[]{:S(2)}) collective-permute-start(bf16[128,128]{1,0:T(8,128)(2,1)S(1)} %get-tuple-element.114), channel_id=1, source_target_pairs={{0,6},{1,7},{2,4},{3,5},{4,2},{5,3},{6,0},{7,1},{8,14},{9,15},{10,... | collective-permute-start | bytes 98312 | tf_op jit(solution)/shard_map/ppermute | solution.py:463
  78.9 0.0 collective-permute-start.21
  78.9 1.3 %input_grads.1 = f32[512,512]{1,0:T(8,128)} custom-call(bf16[64,512]{1,0:T(8,128)(2,1)S(1)} %get-tuple-element.117.grad_project_ref, bf16[64,512]{1,0:T(8,128)(2,1)S(1)} %bitcast.19, f32[512,512]{1,0:T(8,128)S(1)} %get-tuple-element.118.grad_new_ref), custom_call_target="tpu_custom_call" | custom-call | flops 1073741824 | bytes 1048576 | tf_op jit(solution)/shard_map/input_grads/pallas_call | solution.py:682
  80.2 3.0 %collective-permute-done.20.refs_1_ = bf16[128,128]{1,0:T(8,128)(2,1)S(1)} collective-permute-done((bf16[128,128]{1,0:T(8,128)(2,1)S(1)}, bf16[128,128]{1,0:T(8,128)(2,1)S(1)}, u32[]{:S(2)}, u32[]{:S(2)}) %collective-permute-start.20) | collective-permute-done | bytes 32800 | tf_op jit(solution)/shard_map/ppermute | solution.py:463
  83.2 2.5 %collective-permute-start.22 = (bf16[384,128]{1,0:T(8,128)(2,1)S(1)}, bf16[384,128]{1,0:T(8,128)(2,1)S(1)}, u32[]{:S(2)}, u32[]{:S(2)}) collective-permute-start(bf16[384,128]{1,0:T(8,128)(2,1)S(1)} %share.1.refs_3_), channel_id=1, source_target_pairs={{0,24},{8,16},{16,8},{24,0},{1,25},{9,17},{17,9},{25,1},{2,26},{10... | collective-permute-start | bytes 294920 | tf_op jit(solution)/shard_map/ppermute | solution.py:463
  85.7 0.5 collective-permute-start.23
  86.2 0.5 collective-permute-start.24
  86.7 2.9 %collective-permute-done.22.refs_0_ = bf16[384,128]{1,0:T(8,128)(2,1)S(1)} collective-permute-done((bf16[384,128]{1,0:T(8,128)(2,1)S(1)}, bf16[384,128]{1,0:T(8,128)(2,1)S(1)}, u32[]{:S(2)}, u32[]{:S(2)}) %collective-permute-start.22) | collective-permute-done | bytes 98336 | tf_op jit(solution)/shard_map/ppermute | solution.py:463
  89.6 0.9 collective-permute-done.23.refs_1_
  90.5 0.3 collective-permute-done.24.refs_2_
  90.8 0.1 total.1.refs_7_
  90.8 1.2 %collective-permute-start.25 = (bf16[384,128]{1,0:T(8,128)(2,1)S(1)}, bf16[384,128]{1,0:T(8,128)(2,1)S(1)}, u32[]{:S(2)}, u32[]{:S(2)}) collective-permute-start(bf16[384,128]{1,0:T(8,128)(2,1)S(1)} %total.1.refs_7_), channel_id=1, source_target_pairs={{0,4},{1,5},{2,6},{3,7},{4,0},{5,1},{6,2},{7,3},{8,12},{9,13},{10,... | collective-permute-start | bytes 294920 | tf_op jit(solution)/shard_map/ppermute | solution.py:463
  92.0 1.2 %collective-permute-start.27 = (bf16[384,128]{1,0:T(8,128)(2,1)S(1)}, bf16[384,128]{1,0:T(8,128)(2,1)S(1)}, u32[]{:S(2)}, u32[]{:S(2)}) collective-permute-start(bf16[384,128]{1,0:T(8,128)(2,1)S(1)} %total.1.refs_7_), channel_id=1, source_target_pairs={{0,6},{1,7},{2,4},{3,5},{4,2},{5,3},{6,0},{7,1},{8,14},{9,15},{10,... | collective-permute-start | bytes 294920 | tf_op jit(solution)/shard_map/ppermute | solution.py:463
  93.3 1.1 %collective-permute-start.29 = (bf16[384,128]{1,0:T(8,128)(2,1)S(1)}, bf16[384,128]{1,0:T(8,128)(2,1)S(1)}, u32[]{:S(2)}, u32[]{:S(2)}) collective-permute-start(bf16[384,128]{1,0:T(8,128)(2,1)S(1)} %total.1.refs_7_), channel_id=1, source_target_pairs={{0,2},{1,3},{2,0},{3,1},{4,6},{5,7},{6,4},{7,5},{8,10},{9,11},{10,... | collective-permute-start | bytes 294920 | tf_op jit(solution)/shard_map/ppermute | solution.py:463
  94.4 4.9 %collective-permute-done.25.refs_1_ = bf16[384,128]{1,0:T(8,128)(2,1)S(1)} collective-permute-done((bf16[384,128]{1,0:T(8,128)(2,1)S(1)}, bf16[384,128]{1,0:T(8,128)(2,1)S(1)}, u32[]{:S(2)}, u32[]{:S(2)}) %collective-permute-start.25) | collective-permute-done | bytes 98336 | tf_op jit(solution)/shard_map/ppermute | solution.py:463
  99.3 0.5 collective-permute-start.28
  99.8 0.1 collective-permute-start.30
  99.9 0.7 collective-permute-done.26.refs_0_
  100.6 0.2 collective-permute-done.28.refs_2_
  100.8 0.4 collective-permute-done.30.refs_4_
  101.1 1.2 %weights.1 = (f32[64,512]{1,0:T(8,128)}, f32[64,1024]{1,0:T(8,128)}, f32[64,512]{1,0:T(8,128)}, f32[512,512]{1,0:T(8,128)}) custom-call(bf16[384,128]{1,0:T(8,128)(2,1)S(1)} %collective-permute-done.26.refs_0_, bf16[384,128]{1,0:T(8,128)(2,1)S(1)} %collective-permute-done.25.refs_1_, bf16[384,128]{1,0:T(8,128)(2,1)S(1)} %collective-permute-done.28.refs_2_, ...), custom_call_target="tpu_custom_call" | custom-call | tf_op jit(solution)/shard_map/weights/pallas_call | solution.py:723
  (29 shorter events, 0.1 us)
Async XLA Ops:
  2.0 10.0 %collective-permute-start = (bf16[64,512]{1,0:T(8,128)(2,1)S(1)}, bf16[64,512]{1,0:T(8,128)(2,1)S(1)}, u32[]{:S(2)}, u32[]{:S(2)}) collective-permute-start(bf16[64,512]{1,0:T(8,128)(2,1)S(1)} %get-tuple-element.89.refs_13_), channel_id=1, source_target_pairs={{0,4},{1,5},{2,6},{3,7},{4,0},{5,1},{6,2},{7,3},{8,12},{9,13},{10,... | collective-permute-start | bytes 196616 | tf_op jit(solution)/shard_map/ppermute | solution.py:463
  6.1 6.2 %collective-permute-start.1 = (bf16[64,512]{1,0:T(8,128)(2,1)S(1)}, bf16[64,512]{1,0:T(8,128)(2,1)S(1)}, u32[]{:S(2)}, u32[]{:S(2)}) collective-permute-start(bf16[64,512]{1,0:T(8,128)(2,1)S(1)} %get-tuple-element.89.refs_13_), channel_id=1, source_target_pairs={{0,6},{1,7},{2,4},{3,5},{4,2},{5,3},{6,0},{7,1},{8,14},{9,15},{10,... | collective-permute-start | bytes 196616 | tf_op jit(solution)/shard_map/ppermute | solution.py:463
  7.5 5.0 %collective-permute-start.2 = (bf16[64,512]{1,0:T(8,128)(2,1)S(1)}, bf16[64,512]{1,0:T(8,128)(2,1)S(1)}, u32[]{:S(2)}, u32[]{:S(2)}) collective-permute-start(bf16[64,512]{1,0:T(8,128)(2,1)S(1)} %get-tuple-element.89.refs_13_), channel_id=1, source_target_pairs={{0,2},{1,3},{2,0},{3,1},{4,6},{5,7},{6,4},{7,5},{8,10},{9,11},{10,... | collective-permute-start | bytes 196616 | tf_op jit(solution)/shard_map/ppermute | solution.py:463
  12.4 1.7 %collective-permute-start.3 = (bf16[64,512]{1,0:T(8,128)(2,1)S(1)}, bf16[64,512]{1,0:T(8,128)(2,1)S(1)}, u32[]{:S(2)}, u32[]{:S(2)}) collective-permute-start(bf16[64,512]{1,0:T(8,128)(2,1)S(1)} %collective-permute-done.refs_7_), channel_id=1, source_target_pairs={{0,1},{1,0},{2,3},{3,2},{4,5},{5,4},{6,7},{7,6},{8,9},{9,8},{10,11... | collective-permute-start | bytes 196616 | tf_op jit(solution)/shard_map/ppermute | solution.py:463
  12.4 1.7 %collective-permute-start.4 = (bf16[64,512]{1,0:T(8,128)(2,1)S(1)}, bf16[64,512]{1,0:T(8,128)(2,1)S(1)}, u32[]{:S(2)}, u32[]{:S(2)}) collective-permute-start(bf16[64,512]{1,0:T(8,128)(2,1)S(1)} %collective-permute-done.1.refs_9_), channel_id=1, source_target_pairs={{0,1},{1,0},{2,3},{3,2},{4,5},{5,4},{6,7},{7,6},{8,9},{9,8},{10,11... | collective-permute-start | bytes 196616 | tf_op jit(solution)/shard_map/ppermute | solution.py:463
  12.9 1.3 %collective-permute-start.5 = (bf16[64,512]{1,0:T(8,128)(2,1)S(1)}, bf16[64,512]{1,0:T(8,128)(2,1)S(1)}, u32[]{:S(2)}, u32[]{:S(2)}) collective-permute-start(bf16[64,512]{1,0:T(8,128)(2,1)S(1)} %collective-permute-done.2.refs_11_), channel_id=1, source_target_pairs={{0,1},{1,0},{2,3},{3,2},{4,5},{5,4},{6,7},{7,6},{8,9},{9,8},{10,11... | collective-permute-start | bytes 196616 | tf_op jit(solution)/shard_map/ppermute | solution.py:463
  13.0 1.4 %collective-permute-start.6 = (bf16[64,512]{1,0:T(8,128)(2,1)S(1)}, bf16[64,512]{1,0:T(8,128)(2,1)S(1)}, u32[]{:S(2)}, u32[]{:S(2)}) collective-permute-start(bf16[64,512]{1,0:T(8,128)(2,1)S(1)} %get-tuple-element.89.refs_13_), channel_id=1, source_target_pairs={{0,1},{1,0},{2,3},{3,2},{4,5},{5,4},{6,7},{7,6},{8,9},{9,8},{10,11... | collective-permute-start | bytes 196616 | tf_op jit(solution)/shard_map/ppermute | solution.py:463
  27.5 1.4 %collective-permute-start.7 = (bf16[4,32,512]{2,1,0:T(8,128)(2,1)S(1)}, bf16[4,32,512]{2,1,0:T(8,128)(2,1)S(1)}, u32[]{:S(2)}, u32[]{:S(2)}) collective-permute-start(bf16[4,32,512]{2,1,0:T(8,128)(2,1)S(1)} %get-tuple-element.92), channel_id=1, source_target_pairs={{0,1},{1,0},{2,3},{3,2},{4,5},{5,4},{6,7},{7,6},{8,9},{9,8},{10,11... | collective-permute-start | bytes 393224 | tf_op jit(solution)/shard_map/ppermute | solution.py:463
  28.9 8.5 %copy-start = (bf16[512,512]{1,0:T(8,128)(2,1)S(1)}, bf16[512,512]{1,0:T(8,128)(2,1)}, u32[]{:S(2)}) copy-start(bf16[512,512]{1,0:T(8,128)(2,1)} %atom_weight_ref.1) | copy-start | bytes 1572868
  28.9 8.5 %copy-start.1 = (bf16[1,32,512]{2,1,0:T(8,128)(2,1)S(1)}, bf16[1,32,512]{2,1,0:T(8,128)(2,1)}, u32[]{:S(2)}) copy-start(bf16[1,32,512]{2,1,0:T(8,128)(2,1)} %param.14) | copy-start | bytes 98308
  28.9 8.5 %copy-start.2 = (bf16[1,32,512]{2,1,0:T(8,128)(2,1)S(1)}, bf16[1,32,512]{2,1,0:T(8,128)(2,1)}, u32[]{:S(2)}) copy-start(bf16[1,32,512]{2,1,0:T(8,128)(2,1)} %param.21) | copy-start | bytes 98308
  28.9 4.9 %collective-permute-start.8 = (bf16[32,512]{1,0:T(8,128)(2,1)S(1)}, bf16[32,512]{1,0:T(8,128)(2,1)S(1)}, u32[]{:S(2)}, u32[]{:S(2)}) collective-permute-start(bf16[32,512]{1,0:T(8,128)(2,1)S(1)} %get-tuple-element.93), channel_id=1, source_target_pairs={{0,4},{1,5},{2,6},{3,7},{4,0},{5,1},{6,2},{7,3},{8,12},{9,13},{10,... | collective-permute-start | bytes 98312 | tf_op jit(solution)/shard_map/ppermute | solution.py:463
  31.7 5.7 %collective-permute-start.9 = (bf16[32,512]{1,0:T(8,128)(2,1)S(1)}, bf16[32,512]{1,0:T(8,128)(2,1)S(1)}, u32[]{:S(2)}, u32[]{:S(2)}) collective-permute-start(bf16[32,512]{1,0:T(8,128)(2,1)S(1)} %get-tuple-element.94), channel_id=1, source_target_pairs={{0,6},{1,7},{2,4},{3,5},{4,2},{5,3},{6,0},{7,1},{8,14},{9,15},{10,... | collective-permute-start | bytes 98312 | tf_op jit(solution)/shard_map/ppermute | solution.py:463
  32.8 4.6 %collective-permute-start.10 = (bf16[32,512]{1,0:T(8,128)(2,1)S(1)}, bf16[32,512]{1,0:T(8,128)(2,1)S(1)}, u32[]{:S(2)}, u32[]{:S(2)}) collective-permute-start(bf16[32,512]{1,0:T(8,128)(2,1)S(1)} %get-tuple-element.95), channel_id=1, source_target_pairs={{0,2},{1,3},{2,0},{3,1},{4,6},{5,7},{6,4},{7,5},{8,10},{9,11},{10,... | collective-permute-start | bytes 98312 | tf_op jit(solution)/shard_map/ppermute | solution.py:463
  32.8 14.4 %copy-start.3 = (bf16[1,512,512]{2,1,0:T(8,128)(2,1)S(1)}, bf16[1,512,512]{2,1,0:T(8,128)(2,1)}, u32[]{:S(2)}) copy-start(bf16[1,512,512]{2,1,0:T(8,128)(2,1)} %param.20) | copy-start | bytes 1572868
  38.2 7.2 %collective-permute-start.11 = (bf16[2,32,512]{2,1,0:T(8,128)(2,1)S(1)}, bf16[2,32,512]{2,1,0:T(8,128)(2,1)S(1)}, u32[]{:S(2)}, u32[]{:S(2)}) collective-permute-start(bf16[2,32,512]{2,1,0:T(8,128)(2,1)S(1)} %get-tuple-element.105.refs_7_.refs_0_), channel_id=1, source_target_pairs={{0,4},{1,5},{2,6},{3,7},{4,0},{5,1},{6,2},{7,3},{8,12},{9,13},{10,... | collective-permute-start | bytes 196616 | tf_op jit(solution)/shard_map/ppermute | solution.py:463
  39.1 6.3 %collective-permute-start.13 = (bf16[2,32,512]{2,1,0:T(8,128)(2,1)S(1)}, bf16[2,32,512]{2,1,0:T(8,128)(2,1)S(1)}, u32[]{:S(2)}, u32[]{:S(2)}) collective-permute-start(bf16[2,32,512]{2,1,0:T(8,128)(2,1)S(1)} %get-tuple-element.105.refs_7_.refs_0_), channel_id=1, source_target_pairs={{0,6},{1,7},{2,4},{3,5},{4,2},{5,3},{6,0},{7,1},{8,14},{9,15},{10,... | collective-permute-start | bytes 196616 | tf_op jit(solution)/shard_map/ppermute | solution.py:463
  40.3 5.6 %collective-permute-start.15 = (bf16[2,32,512]{2,1,0:T(8,128)(2,1)S(1)}, bf16[2,32,512]{2,1,0:T(8,128)(2,1)S(1)}, u32[]{:S(2)}, u32[]{:S(2)}) collective-permute-start(bf16[2,32,512]{2,1,0:T(8,128)(2,1)S(1)} %get-tuple-element.105.refs_7_.refs_0_), channel_id=1, source_target_pairs={{0,2},{1,3},{2,0},{3,1},{4,6},{5,7},{6,4},{7,5},{8,10},{9,11},{10,... | collective-permute-start | bytes 196616 | tf_op jit(solution)/shard_map/ppermute | solution.py:463
  41.7 4.3 %collective-permute-start.17 = (bf16[2,32,512]{2,1,0:T(8,128)(2,1)S(1)}, bf16[2,32,512]{2,1,0:T(8,128)(2,1)S(1)}, u32[]{:S(2)}, u32[]{:S(2)}) collective-permute-start(bf16[2,32,512]{2,1,0:T(8,128)(2,1)S(1)} %get-tuple-element.105.refs_7_.refs_0_), channel_id=1, source_target_pairs={{0,1},{1,0},{2,3},{3,2},{4,5},{5,4},{6,7},{7,6},{8,9},{9,8},{10,11... | collective-permute-start | bytes 196616 | tf_op jit(solution)/shard_map/ppermute | solution.py:463
  45.4 1.3 %collective-permute-start.12 = (bf16[2,32,512]{2,1,0:T(8,128)(2,1)S(1)}, bf16[2,32,512]{2,1,0:T(8,128)(2,1)S(1)}, u32[]{:S(2)}, u32[]{:S(2)}) collective-permute-start(bf16[2,32,512]{2,1,0:T(8,128)(2,1)S(1)} %collective-permute-done.11.refs_1_.refs_4_), channel_id=1, source_target_pairs={{0,1},{1,0},{2,3},{3,2},{4,5},{5,4},{6,7},{7,6},{8,9},{9,8},{10,11... | collective-permute-start | bytes 196616 | tf_op jit(solution)/shard_map/ppermute | solution.py:463
  45.4 1.4 %collective-permute-start.14 = (bf16[2,32,512]{2,1,0:T(8,128)(2,1)S(1)}, bf16[2,32,512]{2,1,0:T(8,128)(2,1)S(1)}, u32[]{:S(2)}, u32[]{:S(2)}) collective-permute-start(bf16[2,32,512]{2,1,0:T(8,128)(2,1)S(1)} %collective-permute-done.13.refs_3_.refs_6_), channel_id=1, source_target_pairs={{0,1},{1,0},{2,3},{3,2},{4,5},{5,4},{6,7},{7,6},{8,9},{9,8},{10,11... | collective-permute-start | bytes 196616 | tf_op jit(solution)/shard_map/ppermute | solution.py:463
  45.9 1.3 %collective-permute-start.16 = (bf16[2,32,512]{2,1,0:T(8,128)(2,1)S(1)}, bf16[2,32,512]{2,1,0:T(8,128)(2,1)S(1)}, u32[]{:S(2)}, u32[]{:S(2)}) collective-permute-start(bf16[2,32,512]{2,1,0:T(8,128)(2,1)S(1)} %collective-permute-done.15.refs_5_.refs_2_), channel_id=1, source_target_pairs={{0,1},{1,0},{2,3},{3,2},{4,5},{5,4},{6,7},{7,6},{8,9},{9,8},{10,11... | collective-permute-start | bytes 196616 | tf_op jit(solution)/shard_map/ppermute | solution.py:463
  59.2 13.5 %all-to-all-start = ((bf16[8,80,128]{2,1,0:T(8,128)(2,1)}), bf16[8,80,128]{2,1,0:T(8,128)(2,1)S(1)}, u32[]{:S(2)}, u32[]{:S(2)}) async-start(bf16[8,80,128]{2,1,0:T(8,128)(2,1)} %get-tuple-element.106), calls=%async_computation | async-start | bytes 327680 | tf_op jit(solution)/shard_map/all_to_all | solution.py:654
  62.9 9.9 %copy-start.4 = (bf16[1,512,512]{2,1,0:T(8,128)(2,1)S(1)}, bf16[1,512,512]{2,1,0:T(8,128)(2,1)}, u32[]{:S(2)}) copy-start(bf16[1,512,512]{2,1,0:T(8,128)(2,1)} %param.13) | copy-start | bytes 1572868
  73.3 5.6 %copy-start.5 = (bf16[512,64]{0,1:T(8,128)(2,1)S(1)}, bf16[512,64]{0,1:T(8,128)(2,1)}, u32[]{:S(2)}) copy-start(bf16[512,64]{0,1:T(8,128)(2,1)} %param.22) | copy-start | bytes 196612
  73.3 1.4 %collective-permute-start.18 = (bf16[4,128,128]{2,1,0:T(8,128)(2,1)S(1)}, bf16[4,128,128]{2,1,0:T(8,128)(2,1)S(1)}, u32[]{:S(2)}, u32[]{:S(2)}) collective-permute-start(bf16[4,128,128]{2,1,0:T(8,128)(2,1)S(1)} %get-tuple-element.112), channel_id=1, source_target_pairs={{0,1},{1,0},{2,3},{3,2},{4,5},{5,4},{6,7},{7,6},{8,9},{9,8},{10,11... | collective-permute-start | bytes 393224 | tf_op jit(solution)/shard_map/ppermute | solution.py:463
  74.7 5.4 %collective-permute-start.19 = (bf16[128,128]{1,0:T(8,128)(2,1)S(1)}, bf16[128,128]{1,0:T(8,128)(2,1)S(1)}, u32[]{:S(2)}, u32[]{:S(2)}) collective-permute-start(bf16[128,128]{1,0:T(8,128)(2,1)S(1)} %get-tuple-element.113), channel_id=1, source_target_pairs={{0,4},{1,5},{2,6},{3,7},{4,0},{5,1},{6,2},{7,3},{8,12},{9,13},{10,... | collective-permute-start | bytes 98312 | tf_op jit(solution)/shard_map/ppermute | solution.py:463
  77.4 5.7 %collective-permute-start.20 = (bf16[128,128]{1,0:T(8,128)(2,1)S(1)}, bf16[128,128]{1,0:T(8,128)(2,1)S(1)}, u32[]{:S(2)}, u32[]{:S(2)}) collective-permute-start(bf16[128,128]{1,0:T(8,128)(2,1)S(1)} %get-tuple-element.114), channel_id=1, source_target_pairs={{0,6},{1,7},{2,4},{3,5},{4,2},{5,3},{6,0},{7,1},{8,14},{9,15},{10,... | collective-permute-start | bytes 98312 | tf_op jit(solution)/shard_map/ppermute | solution.py:463
  78.9 4.3 %collective-permute-start.21 = (bf16[128,128]{1,0:T(8,128)(2,1)S(1)}, bf16[128,128]{1,0:T(8,128)(2,1)S(1)}, u32[]{:S(2)}, u32[]{:S(2)}) collective-permute-start(bf16[128,128]{1,0:T(8,128)(2,1)S(1)} %get-tuple-element.115), channel_id=1, source_target_pairs={{0,2},{1,3},{2,0},{3,1},{4,6},{5,7},{6,4},{7,5},{8,10},{9,11},{10,... | collective-permute-start | bytes 98312 | tf_op jit(solution)/shard_map/ppermute | solution.py:463
  83.2 6.4 %collective-permute-start.22 = (bf16[384,128]{1,0:T(8,128)(2,1)S(1)}, bf16[384,128]{1,0:T(8,128)(2,1)S(1)}, u32[]{:S(2)}, u32[]{:S(2)}) collective-permute-start(bf16[384,128]{1,0:T(8,128)(2,1)S(1)} %share.1.refs_3_), channel_id=1, source_target_pairs={{0,24},{8,16},{16,8},{24,0},{1,25},{9,17},{17,9},{25,1},{2,26},{10... | collective-permute-start | bytes 294920 | tf_op jit(solution)/shard_map/ppermute | solution.py:463
  85.7 4.8 %collective-permute-start.23 = (bf16[384,128]{1,0:T(8,128)(2,1)S(1)}, bf16[384,128]{1,0:T(8,128)(2,1)S(1)}, u32[]{:S(2)}, u32[]{:S(2)}) collective-permute-start(bf16[384,128]{1,0:T(8,128)(2,1)S(1)} %share.1.refs_3_), channel_id=1, source_target_pairs={{0,16},{8,24},{16,0},{24,8},{1,17},{9,25},{17,1},{25,9},{2,18},{10... | collective-permute-start | bytes 294920 | tf_op jit(solution)/shard_map/ppermute | solution.py:463
  86.2 4.6 %collective-permute-start.24 = (bf16[384,128]{1,0:T(8,128)(2,1)S(1)}, bf16[384,128]{1,0:T(8,128)(2,1)S(1)}, u32[]{:S(2)}, u32[]{:S(2)}) collective-permute-start(bf16[384,128]{1,0:T(8,128)(2,1)S(1)} %share.1.refs_3_), channel_id=1, source_target_pairs={{0,8},{8,0},{16,24},{24,16},{1,9},{9,1},{17,25},{25,17},{2,10},{10... | collective-permute-start | bytes 294920 | tf_op jit(solution)/shard_map/ppermute | solution.py:463
  90.8 8.4 %collective-permute-start.25 = (bf16[384,128]{1,0:T(8,128)(2,1)S(1)}, bf16[384,128]{1,0:T(8,128)(2,1)S(1)}, u32[]{:S(2)}, u32[]{:S(2)}) collective-permute-start(bf16[384,128]{1,0:T(8,128)(2,1)S(1)} %total.1.refs_7_), channel_id=1, source_target_pairs={{0,4},{1,5},{2,6},{3,7},{4,0},{5,1},{6,2},{7,3},{8,12},{9,13},{10,... | collective-permute-start | bytes 294920 | tf_op jit(solution)/shard_map/ppermute | solution.py:463
  92.0 7.3 %collective-permute-start.27 = (bf16[384,128]{1,0:T(8,128)(2,1)S(1)}, bf16[384,128]{1,0:T(8,128)(2,1)S(1)}, u32[]{:S(2)}, u32[]{:S(2)}) collective-permute-start(bf16[384,128]{1,0:T(8,128)(2,1)S(1)} %total.1.refs_7_), channel_id=1, source_target_pairs={{0,6},{1,7},{2,4},{3,5},{4,2},{5,3},{6,0},{7,1},{8,14},{9,15},{10,... | collective-permute-start | bytes 294920 | tf_op jit(solution)/shard_map/ppermute | solution.py:463
  93.3 6.5 %collective-permute-start.29 = (bf16[384,128]{1,0:T(8,128)(2,1)S(1)}, bf16[384,128]{1,0:T(8,128)(2,1)S(1)}, u32[]{:S(2)}, u32[]{:S(2)}) collective-permute-start(bf16[384,128]{1,0:T(8,128)(2,1)S(1)} %total.1.refs_7_), channel_id=1, source_target_pairs={{0,2},{1,3},{2,0},{3,1},{4,6},{5,7},{6,4},{7,5},{8,10},{9,11},{10,... | collective-permute-start | bytes 294920 | tf_op jit(solution)/shard_map/ppermute | solution.py:463
  94.4 5.5 %collective-permute-start.31 = (bf16[384,128]{1,0:T(8,128)(2,1)S(1)}, bf16[384,128]{1,0:T(8,128)(2,1)S(1)}, u32[]{:S(2)}, u32[]{:S(2)}) collective-permute-start(bf16[384,128]{1,0:T(8,128)(2,1)S(1)} %total.1.refs_7_), channel_id=1, source_target_pairs={{0,1},{1,0},{2,3},{3,2},{4,5},{5,4},{6,7},{7,6},{8,9},{9,8},{10,11... | collective-permute-start | bytes 294920 | tf_op jit(solution)/shard_map/ppermute | solution.py:463
  99.3 1.3 %collective-permute-start.26 = (bf16[384,128]{1,0:T(8,128)(2,1)S(1)}, bf16[384,128]{1,0:T(8,128)(2,1)S(1)}, u32[]{:S(2)}, u32[]{:S(2)}) collective-permute-start(bf16[384,128]{1,0:T(8,128)(2,1)S(1)} %collective-permute-done.25.refs_1_), channel_id=1, source_target_pairs={{0,1},{1,0},{2,3},{3,2},{4,5},{5,4},{6,7},{7,6},{8,9},{9,8},{10,11... | collective-permute-start | bytes 294920 | tf_op jit(solution)/shard_map/ppermute | solution.py:463
  99.3 1.5 %collective-permute-start.28 = (bf16[384,128]{1,0:T(8,128)(2,1)S(1)}, bf16[384,128]{1,0:T(8,128)(2,1)S(1)}, u32[]{:S(2)}, u32[]{:S(2)}) collective-permute-start(bf16[384,128]{1,0:T(8,128)(2,1)S(1)} %collective-permute-done.27.refs_3_), channel_id=1, source_target_pairs={{0,1},{1,0},{2,3},{3,2},{4,5},{5,4},{6,7},{7,6},{8,9},{9,8},{10,11... | collective-permute-start | bytes 294920 | tf_op jit(solution)/shard_map/ppermute | solution.py:463
  99.8 1.3 %collective-permute-start.30 = (bf16[384,128]{1,0:T(8,128)(2,1)S(1)}, bf16[384,128]{1,0:T(8,128)(2,1)S(1)}, u32[]{:S(2)}, u32[]{:S(2)}) collective-permute-start(bf16[384,128]{1,0:T(8,128)(2,1)S(1)} %collective-permute-done.29.refs_5_), channel_id=1, source_target_pairs={{0,1},{1,0},{2,3},{3,2},{4,5},{5,4},{6,7},{7,6},{8,9},{9,8},{10,11... | collective-permute-start | bytes 294920 | tf_op jit(solution)/shard_map/ppermute | solution.py:463

commit v8 on v7

--- a/solution.py
+++ b/solution.py
@@ -718,7 +718,7 @@
         out_shape=shaped((share_rows, CAP), b16),
         compiler_params=params(),
         name="total",
-    )(*[swap(share, batches, mask, "dp") for mask in range(batches - 1, 0, -1)], share)
+    )(*[swap(share, batches, mask, "dp") for mask in sending(batches)[:-1]], share)
     shares, _ = gather_near(share, members)
     grad_wdown, grad_wbil, grad_wup, grad_watom = pl.pallas_call(
         functools.partial(last_kernel, members),

time: 103 us -> 102 us (level)
  transfers between devices with their start and end apart: 33 -> 33, of which waited for: 20 -> 21; matrix products, arithmetic and copies ran while one was open for 0% -> 0% of each run, Pallas kernels for 16% -> 16%
where the time goes in v8:
time: 102 us
  Pallas kernels  45.5 us (45%)
  starting transfers between devices  30.7 us (30%)
  waiting for transfers between devices  24.5 us (24%)
  between operations  1.47 us (1%)
    ppermute x32, starting transfers between devices, swap(): return lax.ppermute(value, axis, [(at, at ^ mask) for at in range(members)])  27.1 us
    ppermute x32, waiting for transfers between devices, swap(): return lax.ppermute(value, axis, [(at, at ^ mask) for at in range(members)])  24.5 us
    pallas_call x1, Pallas kernels, body(): pl.pallas_call(functools.partial(forward_kernel, members), in_specs=[SMEM...  13.1 us
    pallas_call x1, Pallas kernels, body(): pl.pallas_call(functools.partial(backward_kernel, members), in_specs=[SME...  12 us
    pallas_call x1, Pallas kernels, body(): pl.pallas_call(weight_kernel, in_specs=[VMEM, HBM, HBM], out_shape=shaped...  9.87 us
    pallas_call x1, Pallas kernels, body(): pl.pallas_call(functools.partial(index_kernel, members), in_specs=[HBM] *...  4.3 us
    all_to_all x1, starting transfers between devices, body(): feat_parts = lax.all_to_all(feat_parts, 'graph', 0, 0, tiled=True)  3.61 us
  transfers between devices with their start and end apart: 33, of which 21 were waited for; matrix products, arithmetic and copies ran while one was open for 0% of the time, Pallas kernels for 16%

profile of v8, /device:TPU:0, one launch (start us, length us, event | category | flops | bytes accessed | tf_op | source)
XLA Modules:
  0.0 102.2 jit_solution(1765921197078082162)
XLA Ops:
  0.6 1.4 %features.1 = (f32[64,512]{1,0:T(8,128)S(1)}, bf16[64,512]{1,0:T(8,128)(2,1)S(1)}) custom-call(bf16[512,512]{1,0:T(8,128)(2,1)} %bitcast.15, bf16[64,512]{1,0:T(8,128)(2,1)} %bitcast.18), custom_call_target="tpu_custom_call" | custom-call | flops 268435456 | bytes 1048576 | tf_op jit(solution)/shard_map/features/pallas_call | solution.py:524
  2.0 4.1 %collective-permute-start = (bf16[64,512]{1,0:T(8,128)(2,1)S(1)}, bf16[64,512]{1,0:T(8,128)(2,1)S(1)}, u32[]{:S(2)}, u32[]{:S(2)}) collective-permute-start(bf16[64,512]{1,0:T(8,128)(2,1)S(1)} %get-tuple-element.89.refs_13_), channel_id=1, source_target_pairs={{0,4},{1,5},{2,6},{3,7},{4,0},{5,1},{6,2},{7,3},{8,12},{9,13},{10,... | collective-permute-start | bytes 196616 | tf_op jit(solution)/shard_map/ppermute | solution.py:463
  6.1 1.3 %collective-permute-start.1 = (bf16[64,512]{1,0:T(8,128)(2,1)S(1)}, bf16[64,512]{1,0:T(8,128)(2,1)S(1)}, u32[]{:S(2)}, u32[]{:S(2)}) collective-permute-start(bf16[64,512]{1,0:T(8,128)(2,1)S(1)} %get-tuple-element.89.refs_13_), channel_id=1, source_target_pairs={{0,6},{1,7},{2,4},{3,5},{4,2},{5,3},{6,0},{7,1},{8,14},{9,15},{10,... | collective-permute-start | bytes 196616 | tf_op jit(solution)/shard_map/ppermute | solution.py:463
  7.5 0.2 collective-permute-start.2
  7.7 4.3 %slots.1 = (s32[1,16384]{1,0:T(1,128)S(1)}, f32[32,128]{1,0:T(8,128)S(1)}, bf16[64,1024]{1,0:T(8,128)(2,1)S(1)}, s32[1,16384]{1,0:T(1,128)S(1)}, bf16[16,16384]{...) custom-call(s32[1,16384]{1,0:T(1,128)} %in_hbm.1, ...), custom_call_target="tpu_custom_call" | custom-call | flops 2147483648 | bytes 1048576 | tf_op jit(solution)/shard_map/slots/pallas_call | solution.py:542
  12.0 0.0 collective-permute-done.refs_7_
  12.0 0.3 collective-permute-done.1.refs_9_
  12.3 0.1 collective-permute-done.2.refs_11_
  12.4 0.0 collective-permute-start.3
  12.4 0.5 collective-permute-start.4
  12.9 0.0 collective-permute-start.5
  13.0 0.5 collective-permute-start.6
  14.1 0.1 collective-permute-done.5.refs_10_
  14.2 0.2 collective-permute-done.6.refs_12_
  14.4 13.1 %forward_triplets.1 = (bf16[512,512]{1,0:T(8,128)(2,1)}, bf16[4,32,512]{2,1,0:T(8,128)(2,1)S(1)}, bf16[4,32,512]{2,1,0:T(8,128)(2,1)S(1)}, bf16[64,512]{1,0:T(8,128)(2,1)S(1)}, bf16[64,16384]{1,0:T(8,128)(2,1)}) custom-call(s32[1,1]{1,0:T(1,128)S(6)} %copy.20.count_ref, s32[1,16384]{1,0:T(1,128)S(1)} %get-tuple-element.78.slot_ref, ...), custom_call_target="tpu_custom_call" | custom-call | flops 12884901888 | bytes 1048576 | tf_op jit(solution)/shard_map/forward_triplets/pallas_call | solution.py:565
  27.5 0.4 collective-permute-start.7
  27.9 1.0 collective-permute-done.7.far_ref
  28.9 2.7 %collective-permute-start.8 = (bf16[32,512]{1,0:T(8,128)(2,1)S(1)}, bf16[32,512]{1,0:T(8,128)(2,1)S(1)}, u32[]{:S(2)}, u32[]{:S(2)}) collective-permute-start(bf16[32,512]{1,0:T(8,128)(2,1)S(1)} %get-tuple-element.93), channel_id=1, source_target_pairs={{0,4},{1,5},{2,6},{3,7},{4,0},{5,1},{6,2},{7,3},{8,12},{9,13},{10,... | collective-permute-start | bytes 98312 | tf_op jit(solution)/shard_map/ppermute | solution.py:463
  31.7 1.1 %collective-permute-start.9 = (bf16[32,512]{1,0:T(8,128)(2,1)S(1)}, bf16[32,512]{1,0:T(8,128)(2,1)S(1)}, u32[]{:S(2)}, u32[]{:S(2)}) collective-permute-start(bf16[32,512]{1,0:T(8,128)(2,1)S(1)} %get-tuple-element.94), channel_id=1, source_target_pairs={{0,6},{1,7},{2,4},{3,5},{4,2},{5,3},{6,0},{7,1},{8,14},{9,15},{10,... | collective-permute-start | bytes 98312 | tf_op jit(solution)/shard_map/ppermute | solution.py:463
  32.8 0.0 collective-permute-start.10
  32.8 0.5 slopes.1.slope_ref
  33.4 0.4 collective-permute-done.8.refs_0_
  33.8 3.6 %collective-permute-done.9.refs_1_ = bf16[32,512]{1,0:T(8,128)(2,1)S(1)} collective-permute-done((bf16[32,512]{1,0:T(8,128)(2,1)S(1)}, bf16[32,512]{1,0:T(8,128)(2,1)S(1)}, u32[]{:S(2)}, u32[]{:S(2)}) %collective-permute-start.9) | collective-permute-done | bytes 32800 | tf_op jit(solution)/shard_map/ppermute | solution.py:463
  37.4 0.9 atoms.1
  38.2 0.9 collective-permute-start.11
  39.1 1.1 %collective-permute-start.13 = (bf16[2,32,512]{2,1,0:T(8,128)(2,1)S(1)}, bf16[2,32,512]{2,1,0:T(8,128)(2,1)S(1)}, u32[]{:S(2)}, u32[]{:S(2)}) collective-permute-start(bf16[2,32,512]{2,1,0:T(8,128)(2,1)S(1)} %get-tuple-element.105.refs_7_.refs_0_), channel_id=1, source_target_pairs={{0,6},{1,7},{2,4},{3,5},{4,2},{5,3},{6,0},{7,1},{8,14},{9,15},{10,... | collective-permute-start | bytes 196616 | tf_op jit(solution)/shard_map/ppermute | solution.py:463
  40.3 1.4 %collective-permute-start.15 = (bf16[2,32,512]{2,1,0:T(8,128)(2,1)S(1)}, bf16[2,32,512]{2,1,0:T(8,128)(2,1)S(1)}, u32[]{:S(2)}, u32[]{:S(2)}) collective-permute-start(bf16[2,32,512]{2,1,0:T(8,128)(2,1)S(1)} %get-tuple-element.105.refs_7_.refs_0_), channel_id=1, source_target_pairs={{0,2},{1,3},{2,0},{3,1},{4,6},{5,7},{6,4},{7,5},{8,10},{9,11},{10,... | collective-permute-start | bytes 196616 | tf_op jit(solution)/shard_map/ppermute | solution.py:463
  41.7 3.7 %collective-permute-done.11.refs_1_.refs_4_ = bf16[2,32,512]{2,1,0:T(8,128)(2,1)S(1)} collective-permute-done((bf16[2,32,512]{2,1,0:T(8,128)(2,1)S(1)}, bf16[2,32,512]{2,1,0:T(8,128)(2,1)S(1)}, u32[]{:S(2)}, u32[]{:S(2)}) %collective-permute-start.11) | collective-permute-done | bytes 65568 | tf_op jit(solution)/shard_map/ppermute | solution.py:463
  45.4 0.5 collective-permute-start.14
  45.9 0.1 collective-permute-start.16
  46.0 0.7 collective-permute-done.12.refs_0_.refs_5_
  46.7 0.2 collective-permute-done.14.refs_2_.refs_7_
  46.8 0.4 collective-permute-done.16.refs_4_.refs_3_
  47.2 12.0 %backward_triplets.1 = (f32[512,512]{1,0:T(8,128)S(1)}, bf16[64,512]{1,0:T(8,128)(2,1)S(1)}, bf16[64,16384]{1,0:T(8,128)(2,1)}, bf16[8,80,128]{2,1,0:T(8,128)(2,1)}) custom-call(s32[1,1]{1,0:T(1,128)S(6)} %copy.20.count_ref, s32[1,16384]{1,0:T(1,128)S(1)} %get-tuple-element.78.slot_ref, s32[1,16384]{1,0:T(1,128)S(1)} %get-tuple-element.80.refs_0_.out_ref, ...), custom_call_target="tpu_custom_call" | custom-call | flops 12884901888 | bytes 1048576 | tf_op jit(solution)/shard_map/backward_triplets/pallas_call | solution.py:617
  59.2 3.6 %all-to-all-start = ((bf16[8,80,128]{2,1,0:T(8,128)(2,1)}), bf16[8,80,128]{2,1,0:T(8,128)(2,1)S(1)}, u32[]{:S(2)}, u32[]{:S(2)}) async-start(bf16[8,80,128]{2,1,0:T(8,128)(2,1)} %get-tuple-element.106), calls=%async_computation | async-start | bytes 327680 | tf_op jit(solution)/shard_map/all_to_all | solution.py:654
  62.9 0.0 copy-start.4
  62.9 9.9 %bilinear_weights.1.bil_grad_ref = bf16[64,1024]{1,0:T(8,128)(2,1)S(1)} custom-call(bf16[16,16384]{1,0:T(8,128)(2,1)S(1)} %get-tuple-element.81.refs_1_.basis_ref, bf16[64,16384]{1,0:T(8,128)(2,1)} %get-tuple-element.108.picked_hbm, bf16[64,16384]{1,0:T(8,128)(2,1)} %get-tuple-element.109.mixed_hbm), custom_call_target="tpu_custom_call" | custom-call | flops 8589934592 | bytes 1048576 | tf_op jit(solution)/shard_map/bilinear_weights/pallas_call | solution.py:656
  72.8 0.5 edges.1
  73.3 0.0 copy-start.5
  73.3 0.3 collective-permute-start.18
  73.5 0.3 atom_slab.1.slab_ref
  73.9 0.8 collective-permute-done.18.far_ref
  74.7 2.7 %collective-permute-start.19 = (bf16[128,128]{1,0:T(8,128)(2,1)S(1)}, bf16[128,128]{1,0:T(8,128)(2,1)S(1)}, u32[]{:S(2)}, u32[]{:S(2)}) collective-permute-start(bf16[128,128]{1,0:T(8,128)(2,1)S(1)} %get-tuple-element.113), channel_id=1, source_target_pairs={{0,4},{1,5},{2,6},{3,7},{4,0},{5,1},{6,2},{7,3},{8,12},{9,13},{10,... | collective-permute-start | bytes 98312 | tf_op jit(solution)/shard_map/ppermute | solution.py:463
  77.4 1.5 %collective-permute-start.20 = (bf16[128,128]{1,0:T(8,128)(2,1)S(1)}, bf16[128,128]{1,0:T(8,128)(2,1)S(1)}, u32[]{:S(2)}, u32[]{:S(2)}) collective-permute-start(bf16[128,128]{1,0:T(8,128)(2,1)S(1)} %get-tuple-element.114), channel_id=1, source_target_pairs={{0,6},{1,7},{2,4},{3,5},{4,2},{5,3},{6,0},{7,1},{8,14},{9,15},{10,... | collective-permute-start | bytes 98312 | tf_op jit(solution)/shard_map/ppermute | solution.py:463
  78.9 0.0 collective-permute-start.21
  78.9 1.3 %input_grads.1 = f32[512,512]{1,0:T(8,128)} custom-call(bf16[64,512]{1,0:T(8,128)(2,1)S(1)} %get-tuple-element.117.grad_project_ref, bf16[64,512]{1,0:T(8,128)(2,1)S(1)} %bitcast.19, f32[512,512]{1,0:T(8,128)S(1)} %get-tuple-element.118.grad_new_ref), custom_call_target="tpu_custom_call" | custom-call | flops 1073741824 | bytes 1048576 | tf_op jit(solution)/shard_map/input_grads/pallas_call | solution.py:682
  80.2 3.0 %collective-permute-done.20.refs_1_ = bf16[128,128]{1,0:T(8,128)(2,1)S(1)} collective-permute-done((bf16[128,128]{1,0:T(8,128)(2,1)S(1)}, bf16[128,128]{1,0:T(8,128)(2,1)S(1)}, u32[]{:S(2)}, u32[]{:S(2)}) %collective-permute-start.20) | collective-permute-done | bytes 32800 | tf_op jit(solution)/shard_map/ppermute | solution.py:463
  83.2 1.6 %collective-permute-start.22 = (bf16[384,128]{1,0:T(8,128)(2,1)S(1)}, bf16[384,128]{1,0:T(8,128)(2,1)S(1)}, u32[]{:S(2)}, u32[]{:S(2)}) collective-permute-start(bf16[384,128]{1,0:T(8,128)(2,1)S(1)} %share.1.refs_3_), channel_id=1, source_target_pairs={{0,16},{8,24},{16,0},{24,8},{1,17},{9,25},{17,1},{25,9},{2,18},{10... | collective-permute-start | bytes 294920 | tf_op jit(solution)/shard_map/ppermute | solution.py:463
  84.7 1.4 %collective-permute-start.23 = (bf16[384,128]{1,0:T(8,128)(2,1)S(1)}, bf16[384,128]{1,0:T(8,128)(2,1)S(1)}, u32[]{:S(2)}, u32[]{:S(2)}) collective-permute-start(bf16[384,128]{1,0:T(8,128)(2,1)S(1)} %share.1.refs_3_), channel_id=1, source_target_pairs={{0,24},{8,16},{16,8},{24,0},{1,25},{9,17},{17,9},{25,1},{2,26},{10... | collective-permute-start | bytes 294920 | tf_op jit(solution)/shard_map/ppermute | solution.py:463
  86.2 0.5 collective-permute-start.24
  86.7 2.1 %collective-permute-done.22.refs_0_ = bf16[384,128]{1,0:T(8,128)(2,1)S(1)} collective-permute-done((bf16[384,128]{1,0:T(8,128)(2,1)S(1)}, bf16[384,128]{1,0:T(8,128)(2,1)S(1)}, u32[]{:S(2)}, u32[]{:S(2)}) %collective-permute-start.22) | collective-permute-done | bytes 98336 | tf_op jit(solution)/shard_map/ppermute | solution.py:463
  88.8 1.5 %collective-permute-done.23.refs_1_ = bf16[384,128]{1,0:T(8,128)(2,1)S(1)} collective-permute-done((bf16[384,128]{1,0:T(8,128)(2,1)S(1)}, bf16[384,128]{1,0:T(8,128)(2,1)S(1)}, u32[]{:S(2)}, u32[]{:S(2)}) %collective-permute-start.23) | collective-permute-done | bytes 98336 | tf_op jit(solution)/shard_map/ppermute | solution.py:463
  90.3 0.5 collective-permute-done.24.refs_2_
  90.8 0.1 total.1.refs_7_
  90.8 1.2 %collective-permute-start.25 = (bf16[384,128]{1,0:T(8,128)(2,1)S(1)}, bf16[384,128]{1,0:T(8,128)(2,1)S(1)}, u32[]{:S(2)}, u32[]{:S(2)}) collective-permute-start(bf16[384,128]{1,0:T(8,128)(2,1)S(1)} %total.1.refs_7_), channel_id=1, source_target_pairs={{0,4},{1,5},{2,6},{3,7},{4,0},{5,1},{6,2},{7,3},{8,12},{9,13},{10,... | collective-permute-start | bytes 294920 | tf_op jit(solution)/shard_map/ppermute | solution.py:463
  92.0 1.2 %collective-permute-start.27 = (bf16[384,128]{1,0:T(8,128)(2,1)S(1)}, bf16[384,128]{1,0:T(8,128)(2,1)S(1)}, u32[]{:S(2)}, u32[]{:S(2)}) collective-permute-start(bf16[384,128]{1,0:T(8,128)(2,1)S(1)} %total.1.refs_7_), channel_id=1, source_target_pairs={{0,6},{1,7},{2,4},{3,5},{4,2},{5,3},{6,0},{7,1},{8,14},{9,15},{10,... | collective-permute-start | bytes 294920 | tf_op jit(solution)/shard_map/ppermute | solution.py:463
  93.3 1.1 %collective-permute-start.29 = (bf16[384,128]{1,0:T(8,128)(2,1)S(1)}, bf16[384,128]{1,0:T(8,128)(2,1)S(1)}, u32[]{:S(2)}, u32[]{:S(2)}) collective-permute-start(bf16[384,128]{1,0:T(8,128)(2,1)S(1)} %total.1.refs_7_), channel_id=1, source_target_pairs={{0,2},{1,3},{2,0},{3,1},{4,6},{5,7},{6,4},{7,5},{8,10},{9,11},{10,... | collective-permute-start | bytes 294920 | tf_op jit(solution)/shard_map/ppermute | solution.py:463
  94.4 4.7 %collective-permute-done.25.refs_1_ = bf16[384,128]{1,0:T(8,128)(2,1)S(1)} collective-permute-done((bf16[384,128]{1,0:T(8,128)(2,1)S(1)}, bf16[384,128]{1,0:T(8,128)(2,1)S(1)}, u32[]{:S(2)}, u32[]{:S(2)}) %collective-permute-start.25) | collective-permute-done | bytes 98336 | tf_op jit(solution)/shard_map/ppermute | solution.py:463
  99.1 0.5 collective-permute-start.28
  99.6 0.1 collective-permute-done.29.refs_5_
  99.7 0.7 collective-permute-done.26.refs_0_
  100.4 0.2 collective-permute-done.28.refs_2_
  100.6 0.4 collective-permute-done.30.refs_4_
  101.0 1.2 %weights.1 = (f32[64,512]{1,0:T(8,128)}, f32[64,1024]{1,0:T(8,128)}, f32[64,512]{1,0:T(8,128)}, f32[512,512]{1,0:T(8,128)}) custom-call(bf16[384,128]{1,0:T(8,128)(2,1)S(1)} %collective-permute-done.26.refs_0_, bf16[384,128]{1,0:T(8,128)(2,1)S(1)} %collective-permute-done.25.refs_1_, bf16[384,128]{1,0:T(8,128)(2,1)S(1)} %collective-permute-done.28.refs_2_, ...), custom_call_target="tpu_custom_call" | custom-call | tf_op jit(solution)/shard_map/weights/pallas_call | solution.py:723
  (29 shorter events, 0.1 us)
Async XLA Ops:
  2.0 10.0 %collective-permute-start = (bf16[64,512]{1,0:T(8,128)(2,1)S(1)}, bf16[64,512]{1,0:T(8,128)(2,1)S(1)}, u32[]{:S(2)}, u32[]{:S(2)}) collective-permute-start(bf16[64,512]{1,0:T(8,128)(2,1)S(1)} %get-tuple-element.89.refs_13_), channel_id=1, source_target_pairs={{0,4},{1,5},{2,6},{3,7},{4,0},{5,1},{6,2},{7,3},{8,12},{9,13},{10,... | collective-permute-start | bytes 196616 | tf_op jit(solution)/shard_map/ppermute | solution.py:463
  6.1 6.2 %collective-permute-start.1 = (bf16[64,512]{1,0:T(8,128)(2,1)S(1)}, bf16[64,512]{1,0:T(8,128)(2,1)S(1)}, u32[]{:S(2)}, u32[]{:S(2)}) collective-permute-start(bf16[64,512]{1,0:T(8,128)(2,1)S(1)} %get-tuple-element.89.refs_13_), channel_id=1, source_target_pairs={{0,6},{1,7},{2,4},{3,5},{4,2},{5,3},{6,0},{7,1},{8,14},{9,15},{10,... | collective-permute-start | bytes 196616 | tf_op jit(solution)/shard_map/ppermute | solution.py:463
  7.5 5.0 %collective-permute-start.2 = (bf16[64,512]{1,0:T(8,128)(2,1)S(1)}, bf16[64,512]{1,0:T(8,128)(2,1)S(1)}, u32[]{:S(2)}, u32[]{:S(2)}) collective-permute-start(bf16[64,512]{1,0:T(8,128)(2,1)S(1)} %get-tuple-element.89.refs_13_), channel_id=1, source_target_pairs={{0,2},{1,3},{2,0},{3,1},{4,6},{5,7},{6,4},{7,5},{8,10},{9,11},{10,... | collective-permute-start | bytes 196616 | tf_op jit(solution)/shard_map/ppermute | solution.py:463
  12.4 1.7 %collective-permute-start.3 = (bf16[64,512]{1,0:T(8,128)(2,1)S(1)}, bf16[64,512]{1,0:T(8,128)(2,1)S(1)}, u32[]{:S(2)}, u32[]{:S(2)}) collective-permute-start(bf16[64,512]{1,0:T(8,128)(2,1)S(1)} %collective-permute-done.refs_7_), channel_id=1, source_target_pairs={{0,1},{1,0},{2,3},{3,2},{4,5},{5,4},{6,7},{7,6},{8,9},{9,8},{10,11... | collective-permute-start | bytes 196616 | tf_op jit(solution)/shard_map/ppermute | solution.py:463
  12.4 1.7 %collective-permute-start.4 = (bf16[64,512]{1,0:T(8,128)(2,1)S(1)}, bf16[64,512]{1,0:T(8,128)(2,1)S(1)}, u32[]{:S(2)}, u32[]{:S(2)}) collective-permute-start(bf16[64,512]{1,0:T(8,128)(2,1)S(1)} %collective-permute-done.1.refs_9_), channel_id=1, source_target_pairs={{0,1},{1,0},{2,3},{3,2},{4,5},{5,4},{6,7},{7,6},{8,9},{9,8},{10,11... | collective-permute-start | bytes 196616 | tf_op jit(solution)/shard_map/ppermute | solution.py:463
  12.9 1.3 %collective-permute-start.5 = (bf16[64,512]{1,0:T(8,128)(2,1)S(1)}, bf16[64,512]{1,0:T(8,128)(2,1)S(1)}, u32[]{:S(2)}, u32[]{:S(2)}) collective-permute-start(bf16[64,512]{1,0:T(8,128)(2,1)S(1)} %collective-permute-done.2.refs_11_), channel_id=1, source_target_pairs={{0,1},{1,0},{2,3},{3,2},{4,5},{5,4},{6,7},{7,6},{8,9},{9,8},{10,11... | collective-permute-start | bytes 196616 | tf_op jit(solution)/shard_map/ppermute | solution.py:463
  13.0 1.4 %collective-permute-start.6 = (bf16[64,512]{1,0:T(8,128)(2,1)S(1)}, bf16[64,512]{1,0:T(8,128)(2,1)S(1)}, u32[]{:S(2)}, u32[]{:S(2)}) collective-permute-start(bf16[64,512]{1,0:T(8,128)(2,1)S(1)} %get-tuple-element.89.refs_13_), channel_id=1, source_target_pairs={{0,1},{1,0},{2,3},{3,2},{4,5},{5,4},{6,7},{7,6},{8,9},{9,8},{10,11... | collective-permute-start | bytes 196616 | tf_op jit(solution)/shard_map/ppermute | solution.py:463
  27.5 1.4 %collective-permute-start.7 = (bf16[4,32,512]{2,1,0:T(8,128)(2,1)S(1)}, bf16[4,32,512]{2,1,0:T(8,128)(2,1)S(1)}, u32[]{:S(2)}, u32[]{:S(2)}) collective-permute-start(bf16[4,32,512]{2,1,0:T(8,128)(2,1)S(1)} %get-tuple-element.92), channel_id=1, source_target_pairs={{0,1},{1,0},{2,3},{3,2},{4,5},{5,4},{6,7},{7,6},{8,9},{9,8},{10,11... | collective-permute-start | bytes 393224 | tf_op jit(solution)/shard_map/ppermute | solution.py:463
  28.9 8.5 %copy-start = (bf16[512,512]{1,0:T(8,128)(2,1)S(1)}, bf16[512,512]{1,0:T(8,128)(2,1)}, u32[]{:S(2)}) copy-start(bf16[512,512]{1,0:T(8,128)(2,1)} %atom_weight_ref.1) | copy-start | bytes 1572868
  28.9 8.5 %copy-start.1 = (bf16[1,32,512]{2,1,0:T(8,128)(2,1)S(1)}, bf16[1,32,512]{2,1,0:T(8,128)(2,1)}, u32[]{:S(2)}) copy-start(bf16[1,32,512]{2,1,0:T(8,128)(2,1)} %param.14) | copy-start | bytes 98308
  28.9 8.5 %copy-start.2 = (bf16[1,32,512]{2,1,0:T(8,128)(2,1)S(1)}, bf16[1,32,512]{2,1,0:T(8,128)(2,1)}, u32[]{:S(2)}) copy-start(bf16[1,32,512]{2,1,0:T(8,128)(2,1)} %param.21) | copy-start | bytes 98308
  28.9 4.9 %collective-permute-start.8 = (bf16[32,512]{1,0:T(8,128)(2,1)S(1)}, bf16[32,512]{1,0:T(8,128)(2,1)S(1)}, u32[]{:S(2)}, u32[]{:S(2)}) collective-permute-start(bf16[32,512]{1,0:T(8,128)(2,1)S(1)} %get-tuple-element.93), channel_id=1, source_target_pairs={{0,4},{1,5},{2,6},{3,7},{4,0},{5,1},{6,2},{7,3},{8,12},{9,13},{10,... | collective-permute-start | bytes 98312 | tf_op jit(solution)/shard_map/ppermute | solution.py:463
  31.7 5.7 %collective-permute-start.9 = (bf16[32,512]{1,0:T(8,128)(2,1)S(1)}, bf16[32,512]{1,0:T(8,128)(2,1)S(1)}, u32[]{:S(2)}, u32[]{:S(2)}) collective-permute-start(bf16[32,512]{1,0:T(8,128)(2,1)S(1)} %get-tuple-element.94), channel_id=1, source_target_pairs={{0,6},{1,7},{2,4},{3,5},{4,2},{5,3},{6,0},{7,1},{8,14},{9,15},{10,... | collective-permute-start | bytes 98312 | tf_op jit(solution)/shard_map/ppermute | solution.py:463
  32.8 4.6 %collective-permute-start.10 = (bf16[32,512]{1,0:T(8,128)(2,1)S(1)}, bf16[32,512]{1,0:T(8,128)(2,1)S(1)}, u32[]{:S(2)}, u32[]{:S(2)}) collective-permute-start(bf16[32,512]{1,0:T(8,128)(2,1)S(1)} %get-tuple-element.95), channel_id=1, source_target_pairs={{0,2},{1,3},{2,0},{3,1},{4,6},{5,7},{6,4},{7,5},{8,10},{9,11},{10,... | collective-permute-start | bytes 98312 | tf_op jit(solution)/shard_map/ppermute | solution.py:463
  32.8 14.4 %copy-start.3 = (bf16[1,512,512]{2,1,0:T(8,128)(2,1)S(1)}, bf16[1,512,512]{2,1,0:T(8,128)(2,1)}, u32[]{:S(2)}) copy-start(bf16[1,512,512]{2,1,0:T(8,128)(2,1)} %param.20) | copy-start | bytes 1572868
  38.2 7.2 %collective-permute-start.11 = (bf16[2,32,512]{2,1,0:T(8,128)(2,1)S(1)}, bf16[2,32,512]{2,1,0:T(8,128)(2,1)S(1)}, u32[]{:S(2)}, u32[]{:S(2)}) collective-permute-start(bf16[2,32,512]{2,1,0:T(8,128)(2,1)S(1)} %get-tuple-element.105.refs_7_.refs_0_), channel_id=1, source_target_pairs={{0,4},{1,5},{2,6},{3,7},{4,0},{5,1},{6,2},{7,3},{8,12},{9,13},{10,... | collective-permute-start | bytes 196616 | tf_op jit(solution)/shard_map/ppermute | solution.py:463
  39.1 6.3 %collective-permute-start.13 = (bf16[2,32,512]{2,1,0:T(8,128)(2,1)S(1)}, bf16[2,32,512]{2,1,0:T(8,128)(2,1)S(1)}, u32[]{:S(2)}, u32[]{:S(2)}) collective-permute-start(bf16[2,32,512]{2,1,0:T(8,128)(2,1)S(1)} %get-tuple-element.105.refs_7_.refs_0_), channel_id=1, source_target_pairs={{0,6},{1,7},{2,4},{3,5},{4,2},{5,3},{6,0},{7,1},{8,14},{9,15},{10,... | collective-permute-start | bytes 196616 | tf_op jit(solution)/shard_map/ppermute | solution.py:463
  40.3 5.6 %collective-permute-start.15 = (bf16[2,32,512]{2,1,0:T(8,128)(2,1)S(1)}, bf16[2,32,512]{2,1,0:T(8,128)(2,1)S(1)}, u32[]{:S(2)}, u32[]{:S(2)}) collective-permute-start(bf16[2,32,512]{2,1,0:T(8,128)(2,1)S(1)} %get-tuple-element.105.refs_7_.refs_0_), channel_id=1, source_target_pairs={{0,2},{1,3},{2,0},{3,1},{4,6},{5,7},{6,4},{7,5},{8,10},{9,11},{10,... | collective-permute-start | bytes 196616 | tf_op jit(solution)/shard_map/ppermute | solution.py:463
  41.7 4.3 %collective-permute-start.17 = (bf16[2,32,512]{2,1,0:T(8,128)(2,1)S(1)}, bf16[2,32,512]{2,1,0:T(8,128)(2,1)S(1)}, u32[]{:S(2)}, u32[]{:S(2)}) collective-permute-start(bf16[2,32,512]{2,1,0:T(8,128)(2,1)S(1)} %get-tuple-element.105.refs_7_.refs_0_), channel_id=1, source_target_pairs={{0,1},{1,0},{2,3},{3,2},{4,5},{5,4},{6,7},{7,6},{8,9},{9,8},{10,11... | collective-permute-start | bytes 196616 | tf_op jit(solution)/shard_map/ppermute | solution.py:463
  45.4 1.3 %collective-permute-start.12 = (bf16[2,32,512]{2,1,0:T(8,128)(2,1)S(1)}, bf16[2,32,512]{2,1,0:T(8,128)(2,1)S(1)}, u32[]{:S(2)}, u32[]{:S(2)}) collective-permute-start(bf16[2,32,512]{2,1,0:T(8,128)(2,1)S(1)} %collective-permute-done.11.refs_1_.refs_4_), channel_id=1, source_target_pairs={{0,1},{1,0},{2,3},{3,2},{4,5},{5,4},{6,7},{7,6},{8,9},{9,8},{10,11... | collective-permute-start | bytes 196616 | tf_op jit(solution)/shard_map/ppermute | solution.py:463
  45.4 1.4 %collective-permute-start.14 = (bf16[2,32,512]{2,1,0:T(8,128)(2,1)S(1)}, bf16[2,32,512]{2,1,0:T(8,128)(2,1)S(1)}, u32[]{:S(2)}, u32[]{:S(2)}) collective-permute-start(bf16[2,32,512]{2,1,0:T(8,128)(2,1)S(1)} %collective-permute-done.13.refs_3_.refs_6_), channel_id=1, source_target_pairs={{0,1},{1,0},{2,3},{3,2},{4,5},{5,4},{6,7},{7,6},{8,9},{9,8},{10,11... | collective-permute-start | bytes 196616 | tf_op jit(solution)/shard_map/ppermute | solution.py:463
  45.9 1.3 %collective-permute-start.16 = (bf16[2,32,512]{2,1,0:T(8,128)(2,1)S(1)}, bf16[2,32,512]{2,1,0:T(8,128)(2,1)S(1)}, u32[]{:S(2)}, u32[]{:S(2)}) collective-permute-start(bf16[2,32,512]{2,1,0:T(8,128)(2,1)S(1)} %collective-permute-done.15.refs_5_.refs_2_), channel_id=1, source_target_pairs={{0,1},{1,0},{2,3},{3,2},{4,5},{5,4},{6,7},{7,6},{8,9},{9,8},{10,11... | collective-permute-start | bytes 196616 | tf_op jit(solution)/shard_map/ppermute | solution.py:463
  59.2 13.5 %all-to-all-start = ((bf16[8,80,128]{2,1,0:T(8,128)(2,1)}), bf16[8,80,128]{2,1,0:T(8,128)(2,1)S(1)}, u32[]{:S(2)}, u32[]{:S(2)}) async-start(bf16[8,80,128]{2,1,0:T(8,128)(2,1)} %get-tuple-element.106), calls=%async_computation | async-start | bytes 327680 | tf_op jit(solution)/shard_map/all_to_all | solution.py:654
  62.9 9.9 %copy-start.4 = (bf16[1,512,512]{2,1,0:T(8,128)(2,1)S(1)}, bf16[1,512,512]{2,1,0:T(8,128)(2,1)}, u32[]{:S(2)}) copy-start(bf16[1,512,512]{2,1,0:T(8,128)(2,1)} %param.13) | copy-start | bytes 1572868
  73.3 5.6 %copy-start.5 = (bf16[512,64]{0,1:T(8,128)(2,1)S(1)}, bf16[512,64]{0,1:T(8,128)(2,1)}, u32[]{:S(2)}) copy-start(bf16[512,64]{0,1:T(8,128)(2,1)} %param.22) | copy-start | bytes 196612
  73.3 1.4 %collective-permute-start.18 = (bf16[4,128,128]{2,1,0:T(8,128)(2,1)S(1)}, bf16[4,128,128]{2,1,0:T(8,128)(2,1)S(1)}, u32[]{:S(2)}, u32[]{:S(2)}) collective-permute-start(bf16[4,128,128]{2,1,0:T(8,128)(2,1)S(1)} %get-tuple-element.112), channel_id=1, source_target_pairs={{0,1},{1,0},{2,3},{3,2},{4,5},{5,4},{6,7},{7,6},{8,9},{9,8},{10,11... | collective-permute-start | bytes 393224 | tf_op jit(solution)/shard_map/ppermute | solution.py:463
  74.7 5.4 %collective-permute-start.19 = (bf16[128,128]{1,0:T(8,128)(2,1)S(1)}, bf16[128,128]{1,0:T(8,128)(2,1)S(1)}, u32[]{:S(2)}, u32[]{:S(2)}) collective-permute-start(bf16[128,128]{1,0:T(8,128)(2,1)S(1)} %get-tuple-element.113), channel_id=1, source_target_pairs={{0,4},{1,5},{2,6},{3,7},{4,0},{5,1},{6,2},{7,3},{8,12},{9,13},{10,... | collective-permute-start | bytes 98312 | tf_op jit(solution)/shard_map/ppermute | solution.py:463
  77.4 5.7 %collective-permute-start.20 = (bf16[128,128]{1,0:T(8,128)(2,1)S(1)}, bf16[128,128]{1,0:T(8,128)(2,1)S(1)}, u32[]{:S(2)}, u32[]{:S(2)}) collective-permute-start(bf16[128,128]{1,0:T(8,128)(2,1)S(1)} %get-tuple-element.114), channel_id=1, source_target_pairs={{0,6},{1,7},{2,4},{3,5},{4,2},{5,3},{6,0},{7,1},{8,14},{9,15},{10,... | collective-permute-start | bytes 98312 | tf_op jit(solution)/shard_map/ppermute | solution.py:463
  78.9 4.3 %collective-permute-start.21 = (bf16[128,128]{1,0:T(8,128)(2,1)S(1)}, bf16[128,128]{1,0:T(8,128)(2,1)S(1)}, u32[]{:S(2)}, u32[]{:S(2)}) collective-permute-start(bf16[128,128]{1,0:T(8,128)(2,1)S(1)} %get-tuple-element.115), channel_id=1, source_target_pairs={{0,2},{1,3},{2,0},{3,1},{4,6},{5,7},{6,4},{7,5},{8,10},{9,11},{10,... | collective-permute-start | bytes 98312 | tf_op jit(solution)/shard_map/ppermute | solution.py:463
  83.2 5.6 %collective-permute-start.22 = (bf16[384,128]{1,0:T(8,128)(2,1)S(1)}, bf16[384,128]{1,0:T(8,128)(2,1)S(1)}, u32[]{:S(2)}, u32[]{:S(2)}) collective-permute-start(bf16[384,128]{1,0:T(8,128)(2,1)S(1)} %share.1.refs_3_), channel_id=1, source_target_pairs={{0,16},{8,24},{16,0},{24,8},{1,17},{9,25},{17,1},{25,9},{2,18},{10... | collective-permute-start | bytes 294920 | tf_op jit(solution)/shard_map/ppermute | solution.py:463
  84.7 5.5 %collective-permute-start.23 = (bf16[384,128]{1,0:T(8,128)(2,1)S(1)}, bf16[384,128]{1,0:T(8,128)(2,1)S(1)}, u32[]{:S(2)}, u32[]{:S(2)}) collective-permute-start(bf16[384,128]{1,0:T(8,128)(2,1)S(1)} %share.1.refs_3_), channel_id=1, source_target_pairs={{0,24},{8,16},{16,8},{24,0},{1,25},{9,17},{17,9},{25,1},{2,26},{10... | collective-permute-start | bytes 294920 | tf_op jit(solution)/shard_map/ppermute | solution.py:463
  86.2 4.6 %collective-permute-start.24 = (bf16[384,128]{1,0:T(8,128)(2,1)S(1)}, bf16[384,128]{1,0:T(8,128)(2,1)S(1)}, u32[]{:S(2)}, u32[]{:S(2)}) collective-permute-start(bf16[384,128]{1,0:T(8,128)(2,1)S(1)} %share.1.refs_3_), channel_id=1, source_target_pairs={{0,8},{8,0},{16,24},{24,16},{1,9},{9,1},{17,25},{25,17},{2,10},{10... | collective-permute-start | bytes 294920 | tf_op jit(solution)/shard_map/ppermute | solution.py:463
  90.8 8.2 %collective-permute-start.25 = (bf16[384,128]{1,0:T(8,128)(2,1)S(1)}, bf16[384,128]{1,0:T(8,128)(2,1)S(1)}, u32[]{:S(2)}, u32[]{:S(2)}) collective-permute-start(bf16[384,128]{1,0:T(8,128)(2,1)S(1)} %total.1.refs_7_), channel_id=1, source_target_pairs={{0,4},{1,5},{2,6},{3,7},{4,0},{5,1},{6,2},{7,3},{8,12},{9,13},{10,... | collective-permute-start | bytes 294920 | tf_op jit(solution)/shard_map/ppermute | solution.py:463
  92.0 7.1 %collective-permute-start.27 = (bf16[384,128]{1,0:T(8,128)(2,1)S(1)}, bf16[384,128]{1,0:T(8,128)(2,1)S(1)}, u32[]{:S(2)}, u32[]{:S(2)}) collective-permute-start(bf16[384,128]{1,0:T(8,128)(2,1)S(1)} %total.1.refs_7_), channel_id=1, source_target_pairs={{0,6},{1,7},{2,4},{3,5},{4,2},{5,3},{6,0},{7,1},{8,14},{9,15},{10,... | collective-permute-start | bytes 294920 | tf_op jit(solution)/shard_map/ppermute | solution.py:463
  93.3 6.4 %collective-permute-start.29 = (bf16[384,128]{1,0:T(8,128)(2,1)S(1)}, bf16[384,128]{1,0:T(8,128)(2,1)S(1)}, u32[]{:S(2)}, u32[]{:S(2)}) collective-permute-start(bf16[384,128]{1,0:T(8,128)(2,1)S(1)} %total.1.refs_7_), channel_id=1, source_target_pairs={{0,2},{1,3},{2,0},{3,1},{4,6},{5,7},{6,4},{7,5},{8,10},{9,11},{10,... | collective-permute-start | bytes 294920 | tf_op jit(solution)/shard_map/ppermute | solution.py:463
  94.4 5.3 %collective-permute-start.31 = (bf16[384,128]{1,0:T(8,128)(2,1)S(1)}, bf16[384,128]{1,0:T(8,128)(2,1)S(1)}, u32[]{:S(2)}, u32[]{:S(2)}) collective-permute-start(bf16[384,128]{1,0:T(8,128)(2,1)S(1)} %total.1.refs_7_), channel_id=1, source_target_pairs={{0,1},{1,0},{2,3},{3,2},{4,5},{5,4},{6,7},{7,6},{8,9},{9,8},{10,11... | collective-permute-start | bytes 294920 | tf_op jit(solution)/shard_map/ppermute | solution.py:463
  99.1 1.3 %collective-permute-start.26 = (bf16[384,128]{1,0:T(8,128)(2,1)S(1)}, bf16[384,128]{1,0:T(8,128)(2,1)S(1)}, u32[]{:S(2)}, u32[]{:S(2)}) collective-permute-start(bf16[384,128]{1,0:T(8,128)(2,1)S(1)} %collective-permute-done.25.refs_1_), channel_id=1, source_target_pairs={{0,1},{1,0},{2,3},{3,2},{4,5},{5,4},{6,7},{7,6},{8,9},{9,8},{10,11... | collective-permute-start | bytes 294920 | tf_op jit(solution)/shard_map/ppermute | solution.py:463
  99.1 1.5 %collective-permute-start.28 = (bf16[384,128]{1,0:T(8,128)(2,1)S(1)}, bf16[384,128]{1,0:T(8,128)(2,1)S(1)}, u32[]{:S(2)}, u32[]{:S(2)}) collective-permute-start(bf16[384,128]{1,0:T(8,128)(2,1)S(1)} %collective-permute-done.27.refs_3_), channel_id=1, source_target_pairs={{0,1},{1,0},{2,3},{3,2},{4,5},{5,4},{6,7},{7,6},{8,9},{9,8},{10,11... | collective-permute-start | bytes 294920 | tf_op jit(solution)/shard_map/ppermute | solution.py:463
  99.7 1.3 %collective-permute-start.30 = (bf16[384,128]{1,0:T(8,128)(2,1)S(1)}, bf16[384,128]{1,0:T(8,128)(2,1)S(1)}, u32[]{:S(2)}, u32[]{:S(2)}) collective-permute-start(bf16[384,128]{1,0:T(8,128)(2,1)S(1)} %collective-permute-done.29.refs_5_), channel_id=1, source_target_pairs={{0,1},{1,0},{2,3},{3,2},{4,5},{5,4},{6,7},{7,6},{8,9},{9,8},{10,11... | collective-permute-start | bytes 294920 | tf_op jit(solution)/shard_map/ppermute | solution.py:463
